TPU v7x, 32 devices: a whole 2x2x4 slice. The times are simulated.
32 devices in a mesh: src: 2 (over x), snk: 4 (over z), mom: 4 (over y, core).
Axes of the slice: x: 2, y: 2, z: 4, core: 2. Of those that a mesh axis runs over, the one named last changes fastest.
Arguments:
- peram_blocks: bfloat16 [8, 8, 2, 512, 512], P('src', 'snk'), may hold values from -5 to 5
- projections: bfloat16 [8, 4, 4, 2, 128, 128], P('src', 'mom'), may hold values from -0.5 to 0.5
- gamma_index: int32 [4, 4], replicated, may hold values from 0 to 15
- partner: int32 [4], P('mom'), may hold values from 0 to 3, each once
- separations: int32 [4], replicated, may hold values from 1 to 7, as said below
Outputs:
- correlator: float32 [8, 4, 4, 2], P(None, None, 'mom')
Inputs may be any that keep to these rules, and one draw needn't show every extreme that they name: Each operator appears once as the partner of a source operator. separations count source time slices; sink slices are taken modulo 8.
All inputs are finite; a program needn't handle non-finite values.
Results may differ from a plain program's by a relative error of at most 0.007.
Values may be sent and summed in bfloat16 or wider, within the bound.
No kernel may reach another device: no remote copies, remote signals or barrier semaphores. Data moves between devices by JAX's collectives and lax.ppermute only.
A program may use at most 128 MiB of HBM per device.

v0:
```python
import jax
import jax.numpy as jnp
import numpy as np
from jax import lax
from jax.sharding import PartitionSpec as P

NSEP = 4


def dirac_table():
    zero_matrix = np.zeros((4, 4))
    unit_real = np.eye(4)
    gamma_one = (
        zero_matrix,
        np.array([[0, 0, 0, 1], [0, 0, 1, 0], [0, -1, 0, 0], [-1, 0, 0, 0]], dtype=np.float32),
    )
    gamma_two = (
        np.array([[0, 0, 0, -1], [0, 0, 1, 0], [0, 1, 0, 0], [-1, 0, 0, 0]], dtype=np.float32),
        zero_matrix,
    )
    gamma_three = (
        zero_matrix,
        np.array([[0, 0, 1, 0], [0, 0, 0, -1], [-1, 0, 0, 0], [0, 1, 0, 0]], dtype=np.float32),
    )
    gamma_four = (
        np.array([[0, 0, 1, 0], [0, 0, 0, 1], [1, 0, 0, 0], [0, 1, 0, 0]], dtype=np.float32),
        zero_matrix,
    )
    factors = (gamma_one, gamma_two, gamma_three, gamma_four)
    real_list = []
    imag_list = []
    for gamma_code in range(16):
        real_now = unit_real
        imag_now = zero_matrix
        for position in range(4):
            if gamma_code >> position & 1:
                factor_real, factor_imag = factors[position]
                next_real = real_now @ factor_real - imag_now @ factor_imag
                next_imag = real_now @ factor_imag + imag_now @ factor_real
                real_now = next_real
                imag_now = next_imag
        real_list.append(real_now)
        imag_list.append(imag_now)
    return np.stack([np.stack(real_list), np.stack(imag_list)], axis=1).astype(np.float32)


def build_elementals(projections, gamma_index):
    codes = jnp.arange(16, dtype=jnp.int32)
    one_hot = (gamma_index[:, :, None] == codes[None, None, :]).astype(jnp.float32)
    spin_part = jnp.einsum(
        "prg,gcst->prcst", one_hot, jnp.asarray(dirac_table()).astype(jnp.float32)
    )
    proj_real = projections[:, :, :, 0].astype(jnp.float32)
    proj_imag = projections[:, :, :, 1].astype(jnp.float32)
    form = "prst,wpref->wpsetf"
    real_part = jnp.einsum(form, spin_part[:, :, 0], proj_real) - jnp.einsum(
        form, spin_part[:, :, 1], proj_imag
    )
    imag_part = jnp.einsum(form, spin_part[:, :, 0], proj_imag) + jnp.einsum(
        form, spin_part[:, :, 1], proj_real
    )
    full_width = 4 * projections.shape[-1]
    shape_out = (projections.shape[0], projections.shape[1], full_width, full_width)
    stacked = jnp.stack([real_part.reshape(shape_out), imag_part.reshape(shape_out)], axis=2)
    return stacked.astype(jnp.bfloat16)


def complex_products(blocks, elementals, form):
    real_part = jnp.einsum(
        form, blocks[:, :, 0], elementals[:, :, 0], preferred_element_type=jnp.float32
    )
    real_part = real_part - jnp.einsum(
        form, blocks[:, :, 1], elementals[:, :, 1], preferred_element_type=jnp.float32
    )
    imag_part = jnp.einsum(
        form, blocks[:, :, 0], elementals[:, :, 1], preferred_element_type=jnp.float32
    )
    imag_part = imag_part + jnp.einsum(
        form, blocks[:, :, 1], elementals[:, :, 0], preferred_element_type=jnp.float32
    )
    return jnp.stack([real_part, imag_part], axis=3).astype(jnp.bfloat16)


def sink_products(blocks, elementals):
    return complex_products(blocks, elementals, "woyc,wpcx->wopxy")


def source_products(blocks, elementals):
    return complex_products(blocks, elementals, "woxc,wpcy->wopxy")


def align_sources(backward_raw, shifts):
    source_count = backward_raw.shape[0]
    columns = []
    for sep_index in range(backward_raw.shape[1]):
        targets = (jnp.arange(source_count, dtype=jnp.int32) + shifts[sep_index]) % source_count
        columns.append(jnp.take(backward_raw[:, sep_index], targets, axis=0))
    return jnp.stack(columns, axis=1)


def pair_traces(forward, backward):
    form = "tkpxy,tkpxy->tkp"
    real_part = jnp.einsum(
        form, forward[:, :, :, 0], backward[:, :, :, 0], preferred_element_type=jnp.float32
    )
    real_part = real_part - jnp.einsum(
        form, forward[:, :, :, 1], backward[:, :, :, 1], preferred_element_type=jnp.float32
    )
    imag_part = jnp.einsum(
        form, forward[:, :, :, 0], backward[:, :, :, 1], preferred_element_type=jnp.float32
    )
    imag_part = imag_part + jnp.einsum(
        form, forward[:, :, :, 1], backward[:, :, :, 0], preferred_element_type=jnp.float32
    )
    return jnp.stack([real_part, imag_part], axis=-1)


def shards(peram_blocks, projections, gamma_index, partner, separations):
    src_count = lax.axis_size("src")
    snk_count = lax.axis_size("snk")
    slices_dev = peram_blocks.shape[0]
    offsets_dev = peram_blocks.shape[1]
    full_width = peram_blocks.shape[-1]
    ops_dev = projections.shape[1]
    time_count = slices_dev * src_count
    is_back = lax.axis_index("snk") * offsets_dev >= NSEP
    own_gamma = lax.dynamic_slice_in_dim(gamma_index, lax.axis_index("mom") * ops_dev, ops_dev, 0)
    arrived = lax.all_gather(projections, "mom", axis=1, tiled=True)
    codes = jnp.arange(arrived.shape[1], dtype=jnp.int32)
    selector = (partner[:, None] == codes[None, :]).astype(jnp.bfloat16)
    partner_proj = jnp.einsum(
        "pq,wqrcef->wprcef", selector, arrived, preferred_element_type=jnp.float32
    ).astype(jnp.bfloat16)
    all_codes = jnp.arange(gamma_index.shape[0], dtype=jnp.int32)
    matches = (partner[:, None] == all_codes[None, :]).astype(jnp.int32)
    partner_gamma = jnp.sum(matches[:, :, None] * gamma_index[None, :, :], axis=1)
    chosen_proj = jnp.where(is_back, partner_proj, projections)
    chosen_gamma = jnp.where(is_back, partner_gamma, own_gamma)
    elementals = build_elementals(chosen_proj, chosen_gamma)
    own_products = lax.cond(is_back, sink_products, source_products, peram_blocks, elementals)
    grid_count = src_count * snk_count
    rows_dev = full_width // grid_count
    shaped = own_products.reshape(
        slices_dev, offsets_dev, ops_dev, 2, grid_count, rows_dev, full_width
    )
    received = lax.all_to_all(shaped, ("src", "snk"), split_axis=4, concat_axis=0, tiled=True)
    received = received.reshape(
        src_count, snk_count, slices_dev, offsets_dev, ops_dev, 2, rows_dev, full_width
    )

    def offset_column(offset):
        picked = received[:, offset // offsets_dev, :, offset % offsets_dev]
        return picked.reshape(time_count, ops_dev, 2, rows_dev, full_width)

    forward = jnp.stack([offset_column(sep_index) for sep_index in range(NSEP)], axis=1)
    backward_raw = jnp.stack([offset_column(NSEP + sep_index) for sep_index in range(NSEP)], axis=1)
    backward = align_sources(backward_raw, separations)
    traces = pair_traces(forward, backward)
    return lax.psum(traces * (1.0 / full_width), ("src", "snk"))


def solution(mesh):
    placed = (
        P("src", "snk", None, None, None),
        P("src", "mom", None, None, None, None),
        P(),
        P("mom"),
        P(),
    )
    return jax.shard_map(
        shards, mesh=mesh, in_specs=placed, out_specs=P(None, None, "mom", None), check_vma=False
    )
```

profile of v0, /device:TPU:0, one launch (start us, length us, event | category | flops | bytes accessed | tf_op | source)
XLA Modules:
  0.0 384.3 jit_solution(9049846587515761939)
XLA Ops:
  6.5 0.7 all-gather.2.cloned.1.call-update
  7.9 0.8 multiply_reduce_fusion
  8.7 0.7 fusion.31
  9.4 0.9 fusion.25
  10.6 35.6 %all-gather.2.cloned.1.call-done = bf16[4,4,4,2,128,128]{5,4,3,2,1,0:T(8,128)(2,1)} async-done(((bf16[4,1,4,2,128,128]{5,4,3,2,1,0:T(8,128)(2,1)}), bf16[4,4,4,2,128,128]{5,4,3,2,1,0:T(8,128)(2,1)}) %all-gather.2.cloned.1.call-update) | async-done | bytes 4194320 | tf_op jit(solution)/shard_map/all_gather | solution.py:128
  46.1 5.6 %fusion.12 = bf16[1,4,4,2,128,128]{5,0,4,3,2,1:T(2,128)(2,1)S(1)} fusion(bf16[4,4,4,2,128,128]{5,4,3,2,1,0:T(8,128)(2,1)} %all-gather.2.cloned.1.call-done, s32[]{:T(128)} %bitcast.229), kind=kOutput, calls=%fused_computation.39 | convolution fusion | flops 4194308 | bytes 5242884 | tf_op jit(solution)/shard_map/pq,wqrcef->wprcef/dot_general | solution.py:131
  51.8 1.9 fusion.17
  53.7 1.2 fusion.22
  54.9 3.2 fusion.23
  58.0 1.2 fusion.14
  59.3 1.0 copy.61
  60.3 2.4 stack.52
  62.7 3.4 fusion.15
  66.1 1.0 copy.64
  67.1 2.3 stack.53
  69.4 4.5 %pad_maximum_fusion.2 = bf16[4,1,2,512,512]{4,3,0,2,1:T(8,128)(2,1)} fusion(bf16[4,1,1,512,512]{4,3,0,2,1:T(8,128)(2,1)} %stack.53, bf16[4,1,1,512,512]{4,3,0,2,1:T(8,128)(2,1)} %stack.52), kind=kLoop, calls=%fused_computation.34 | loop fusion | flops 2097152 | bytes 8388608 | tf_op jit(solution)/shard_map/stack | solution.py:64
  73.9 41.5 %conditional.2 = (bf16[4,2,1,2,512,512]{4,5,1,0,3,2:T(8,128)(2,1)}) conditional(s32[]{:T(128)} %convert_element_type.40, (bf16[4,1,2,512,512]{4,3,0,2,1:T(8,128)(2,1)}, bf16[4,2,2,512,512]{4,3,2,1,0:T(8,128)(2,1)}) %tuple.15, (bf16[4,1,2,512,512]{4,3,0,2,1:T(8,128)(2,1)}, bf16[4,2,2,512,512]{4,3,2,1,0:T(8,128)(2,1)}) %tuple.15), branch_computations={%region_1.2_spmd, %region_2.3_spmd} | conditional | flops 8602517504 | bytes 159383616
  73.9 7.3 %copy.65 = bf16[4,1,2,512,512]{3,4,0,2,1:T(8,128)(2,1)} copy(bf16[4,1,2,512,512]{4,3,0,2,1:T(8,128)(2,1)} %get-tuple-element.35) | data formatting | bytes 8388608 | tf_op jit(solution)/shard_map
  81.2 8.6 %fusion.1 = f32[4,512,2,512]{3,1,2,0:T(8,128)} fusion(bf16[4,1,2,512,512]{3,4,0,2,1:T(8,128)(2,1)} %copy.65, bf16[4,2,2,512,512]{4,3,2,1,0:T(8,128)(2,1)} %get-tuple-element.36), kind=kOutput, calls=%fused_computation.10 | convolution fusion | flops 2147483648 | bytes 14680064 | tf_op jit(solution)/shard_map/cond/branch_0_fun/woxc,wpcy->wopxy/dot_general | solution.py:69
  89.8 6.2 %subtract_bitcast_fusion = bf16[4,2,1,1,512,512]{4,5,1,0,3,2:T(8,128)(2,1)} fusion(f32[4,512,2,512]{3,1,2,0:T(8,128)} %fusion.1, bf16[4,1,2,512,512]{3,4,0,2,1:T(8,128)(2,1)S(1)} %copy-done.2, bf16[4,2,2,512,512]{4,3,2,1,0:T(8,128)(2,1)S(1)} %copy-done), kind=kOutput, calls=%fused_computation.6 | convolution fusion | flops 2151677952 | bytes 18874368 | tf_op jit(solution)/shard_map/cond/branch_0_fun/woxc,wpcy->wopxy/dot_general | solution.py:72
  96.1 5.6 %fusion = f32[4,512,2,512]{3,1,2,0:T(8,128)} fusion(bf16[4,1,2,512,512]{3,4,0,2,1:T(8,128)(2,1)S(1)} %copy-done.2, bf16[4,2,2,512,512]{4,3,2,1,0:T(8,128)(2,1)S(1)} %copy-done), kind=kOutput, calls=%fused_computation.9 | convolution fusion | flops 2147483648 | bytes 14680064 | tf_op jit(solution)/shard_map/cond/branch_0_fun/woxc,wpcy->wopxy/dot_general | solution.py:75
  101.7 6.2 %add_bitcast_fusion = bf16[4,2,1,1,512,512]{4,5,1,0,3,2:T(8,128)(2,1)} fusion(f32[4,512,2,512]{3,1,2,0:T(8,128)} %fusion, bf16[4,1,2,512,512]{3,4,0,2,1:T(8,128)(2,1)S(1)} %copy-done.2, bf16[4,2,2,512,512]{4,3,2,1,0:T(8,128)(2,1)S(1)} %copy-done), kind=kOutput, calls=%fused_computation.5 | convolution fusion | flops 2151677952 | bytes 18874368 | tf_op jit(solution)/shard_map/cond/branch_0_fun/woxc,wpcy->wopxy/dot_general | solution.py:78
  107.9 7.5 %pad_maximum_fusion = bf16[4,2,1,2,512,512]{4,5,1,0,3,2:T(8,128)(2,1)} fusion(bf16[4,2,1,1,512,512]{4,5,1,0,3,2:T(8,128)(2,1)} %add_bitcast_fusion, bf16[4,2,1,1,512,512]{4,5,1,0,3,2:T(8,128)(2,1)} %subtract_bitcast_fusion), kind=kLoop, calls=%fused_computation.4 | loop fusion | flops 4194304 | bytes 16777216 | tf_op jit(solution)/shard_map/cond/branch_0_fun/stack | solution.py:81
  115.4 13.3 %copy.69 = bf16[4,2,1,2,512,512]{5,4,3,1,0,2:T(8,128)(2,1)} copy(bf16[4,2,1,2,512,512]{4,5,1,0,3,2:T(8,128)(2,1)} %get-tuple-element.61) | data formatting | bytes 16777216 | tf_op jit(solution)/shard_map/conditional
  128.7 7.7 %copy.70 = bf16[4,2,1,2,8,64,512]{6,5,3,1,0,2,4:T(8,128)(2,1)} copy(bf16[4,2,1,2,8,64,512]{6,5,4,3,1,0,2:T(8,128)(2,1)} %bitcast.231) | data formatting | bytes 16777216 | tf_op jit(solution)/shard_map/reshape | solution.py:143
  136.5 18.8 %all-to-all-start = ((bf16[4,2,1,2,8,64,512]{6,5,3,1,0,2,4:T(8,128)(2,1)}), bf16[4,2,1,2,8,64,512]{6,5,3,1,0,2,4:T(8,128)(2,1)}, u32[]{:S(2)}, u32[]{:S(2)}) async-start(bf16[4,2,1,2,8,64,512]{6,5,3,1,0,2,4:T(8,128)(2,1)} %copy.70), calls=%async_computation | async-start | bytes 16777216 | tf_op jit(solution)/shard_map/all_to_all | solution.py:146
  155.3 0.7 fusion.38
  156.0 0.6 compare_select_fusion.2
  156.5 0.6 compare_and_fusion.2
  157.1 0.7 compare_select_fusion.3
  157.8 0.7 compare_and_fusion.3
  158.5 0.7 compare_select_fusion
  159.2 0.7 compare_and_fusion
  159.9 0.6 compare_select_fusion.1
  160.4 0.6 compare_and_fusion.1
  161.0 178.7 %all-to-all-done = bf16[4,2,1,2,8,64,512]{6,5,3,1,0,2,4:T(8,128)(2,1)} async-done(((bf16[4,2,1,2,8,64,512]{6,5,3,1,0,2,4:T(8,128)(2,1)}), bf16[4,2,1,2,8,64,512]{6,5,3,1,0,2,4:T(8,128)(2,1)}, u32[]{:S(2)}, u32[]{:S(2)}) %all-to-all-start) | async-done | bytes 8388640 | tf_op jit(solution)/shard_map/all_to_all | solution.py:146
  339.7 5.8 %fusion.37 = (bf16[2,1,4,1,1,2,64,512]{7,6,5,3,2,1,0,4:T(8,128)(2,1)}, bf16[2,1,4,1,1,2,64,512]{7,6,5,3,2,1,0,4:T(8,128)(2,1)S(1)}, bf16[2,1,4,1,1,2,64,512]{7,6...) fusion(bf16[2,4,4,2,1,2,64,512]{7,6,5,3,2,1,0,4:T(8,128)(2,1)} , ...), kind=kLoop, calls=%fused_computation.108 | loop fusion | bytes 16777216 | tf_op jit(solution)/shard_map/slice | solution.py:152
  345.5 1.8 gather_fusion
  347.4 1.6 gather_fusion.1
  349.0 1.8 gather_fusion.2
  350.8 1.7 gather_fusion.3
  352.5 1.6 fusion.20
  354.4 0.6 pad_maximum_fusion.4
  355.0 0.6 copy-done.6
  356.5 0.5 pad_maximum_fusion.3
  357.1 2.5 fusion.10
  359.6 17.2 %psum.7 = f32[8,4,1,2]{0,1,3,2:T(4,128)S(1)} all-reduce(f32[8,4,1,2]{0,1,3,2:T(4,128)S(1)} %maximum_multiply_fusion), channel_id=1, replica_groups=mesh['src'=2,'snk'=4,'mom'=4] {'src','snk'}, use_global_device_ids=true, to_apply=%region_3.5 | all-reduce | flops 64 | bytes 512 | tf_op jit(solution)/shard_map/psum | solution.py:159
  376.8 0.6 copy.71
  (31 shorter events, 1.6 us)
Async XLA Ops:
  6.5 39.6 %all-gather.2.cloned.1.call-start = ((), (), s32[]{:S(2)}) async-start(), calls=%async_computation.1 | async-start | bytes 5242880 | tf_op jit(solution)/shard_map/all_gather | solution.py:128
  46.1 5.6 %copy-start.5 = (bf16[4,1,4,2,128,128]{5,4,3,2,1,0:T(8,128)(2,1)S(1)}, bf16[4,1,4,2,128,128]{5,4,3,2,1,0:T(8,128)(2,1)}, u32[]{:S(2)}) copy-start(bf16[4,1,4,2,128,128]{5,4,3,2,1,0:T(8,128)(2,1)} %param.11) | copy-start | bytes 3145732
  81.2 8.6 %copy-start = (bf16[4,2,2,512,512]{4,3,2,1,0:T(8,128)(2,1)S(1)}, bf16[4,2,2,512,512]{4,3,2,1,0:T(8,128)(2,1)}, u32[]{:S(2)}) copy-start(bf16[4,2,2,512,512]{4,3,2,1,0:T(8,128)(2,1)} %get-tuple-element.36) | copy-start | bytes 25165828 | tf_op jit(solution)/shard_map/conditional
  81.2 8.6 %copy-start.2 = (bf16[4,1,2,512,512]{3,4,0,2,1:T(8,128)(2,1)S(1)}, bf16[4,1,2,512,512]{3,4,0,2,1:T(8,128)(2,1)}, u32[]{:S(2)}) copy-start(bf16[4,1,2,512,512]{3,4,0,2,1:T(8,128)(2,1)} %copy.65) | copy-start | bytes 12582916 | tf_op jit(solution)/shard_map/conditional
  136.5 18.8 %copy-start.10 = (s32[4]{0:T(128)S(1)}, s32[4]{0:T(128)}, u32[]{:S(2)}) copy-start(s32[4]{0:T(128)} %param.14) | copy-start | bytes 52
  136.5 203.3 %all-to-all-start = ((bf16[4,2,1,2,8,64,512]{6,5,3,1,0,2,4:T(8,128)(2,1)}), bf16[4,2,1,2,8,64,512]{6,5,3,1,0,2,4:T(8,128)(2,1)}, u32[]{:S(2)}, u32[]{:S(2)}) async-start(bf16[4,2,1,2,8,64,512]{6,5,3,1,0,2,4:T(8,128)(2,1)} %copy.70), calls=%async_computation | async-start | bytes 16777216 | tf_op jit(solution)/shard_map/all_to_all | solution.py:146
  352.5 1.6 copy-start.4
  354.3 1.2 copy-start.6
  354.3 1.5 copy-start.7
  354.4 1.8 copy-start.8
  354.4 2.1 copy-start.9
Sparse Core Ops, SparseCore 0:
  8.9 37.1 all-gather.1
where the time goes:
time: 386 us; the launch traced here: 384 us
  waiting for transfers between devices  215 us (56%)
  local copies, waits for them, and re-layouts  50.9 us (13%)
  matrix products  42.2 us (11%)
  other arithmetic  25.9 us (7%)
  starting transfers between devices  18.8 us (5%)
  blocking collectives  17.2 us (4%)
  between operations  14.3 us (4%)
    all_to_all x1, waiting for transfers between devices, shards(): lax.all_to_all(shaped, ('src', 'snk'), split_axis=4, concat_axis=0, tiled...  179 us
    all_gather x1, waiting for transfers between devices, shards(): arrived = lax.all_gather(projections, 'mom', axis=1, tiled=True)  35.6 us
    another operation x9, local copies, waits for them, and re-layouts  20.9 us
    all_to_all x1, starting transfers between devices, shards(): lax.all_to_all(shaped, ('src', 'snk'), split_axis=4, concat_axis=0, tiled...  18.8 us
    psum x1, blocking collectives, shards(): return lax.psum(traces * (1.0 / full_width), ('src', 'snk'))  17.2 us
    dot_general x1, matrix products, complex_products(): jnp.einsum(form, blocks[:, :, 0], elementals[:, :, 0], preferred_element_...  8.61 us
    reshape x1, local copies, waits for them, and re-layouts, shards(): own_products.reshape(slices_dev, offsets_dev, ops_dev, 2, grid_count, row...  7.72 us
  transfers between devices with their start and end apart: 2, of which 2 were waited for; matrix products, arithmetic and copies ran while one was open for 2% of the time, Pallas kernels for 0%

commit v1 on v0

v1 whole, which is shorter than its diff:
```python
import functools

import jax
import jax.numpy as jnp
import numpy as np
from jax import lax
from jax.experimental import pallas as pl
from jax.experimental.pallas import tpu as pltpu
from jax.sharding import PartitionSpec as P

NSPIN = 4
NCODE = 16
NT_DIMS = (((1,), (1,)), ((), ()))
TILE = 256
STRIP = 32
VMEM_LIMIT = 48 * 1024 * 1024


def dirac_table():
    zero = np.zeros((4, 4))
    one = (zero, np.array([[0, 0, 0, 1], [0, 0, 1, 0], [0, -1, 0, 0], [-1, 0, 0, 0]]))
    two = (np.array([[0, 0, 0, -1], [0, 0, 1, 0], [0, 1, 0, 0], [-1, 0, 0, 0]]), zero)
    three = (zero, np.array([[0, 0, 1, 0], [0, 0, 0, -1], [-1, 0, 0, 0], [0, 1, 0, 0]]))
    four = (np.array([[0, 0, 1, 0], [0, 0, 0, 1], [1, 0, 0, 0], [0, 1, 0, 0]]), zero)
    out = []
    for code in range(NCODE):
        real, imag = np.eye(4), zero
        for position, (fr, fi) in enumerate((one, two, three, four)):
            if code >> position & 1:
                real, imag = real @ fr - imag @ fi, real @ fi + imag @ fr
        out.append(np.stack([real, imag]))
    return np.stack(out).astype(np.float32)


def build(table, code_of, planes, store, transposed):
    nterm = 4
    nev = 128
    codes = [code_of(r) for r in range(nterm)]

    def coefficient(r, plane, left, right):
        if transposed:
            left, right = right, left
        return table[codes[r] * 32 + (plane * 16 + left * 4 + right)]

    coeffs = {}
    for left in range(NSPIN):
        for right in range(NSPIN):
            for r in range(nterm):
                for plane in range(2):
                    coeffs[r, plane, left, right] = coefficient(r, plane, left, right)

    def step(index, carry):
        row = pl.multiple_of(index * STRIP, STRIP)
        parts = [(planes(r, 0, row), planes(r, 1, row)) for r in range(nterm)]
        for left in range(NSPIN):
            for right in range(NSPIN):
                re = im = None
                for r in range(nterm):
                    cr, ci = coeffs[r, 0, left, right], coeffs[r, 1, left, right]
                    pr, pi = parts[r]
                    add_re, add_im = cr * pr - ci * pi, cr * pi + ci * pr
                    re = add_re if re is None else re + add_re
                    im = add_im if im is None else im + add_im
                store(left, right, row, re, im)
        return carry

    lax.fori_loop(0, nev // STRIP, step, 0)


def own_kernel(scal, gamma, table, x_ref, *refs):
    count = (len(refs) - 4) // 1
    pieces, (ht_ref, y_ref, u_ref, tr_ref) = refs[:count], refs[count:]
    mom = scal[0]
    width = x_ref.shape[-1]
    real, imag = x_ref[0, 0, 0], x_ref[0, 0, 1]
    y_ref[:width, :width] = real
    y_ref[:width, width:] = -imag
    y_ref[width:, :width] = imag
    y_ref[width:, width:] = real
    nev = tr_ref.shape[-1]

    for p, piece in enumerate(pieces):
        view = piece
        for r in range(4):
            for plane in range(2):
                source = view[0, 0, r, plane] if p == 0 else view[r, plane]
                tr_ref[p, r, plane] = source.astype(jnp.float32).T

    def product(p, carry):
        op = mom ^ p

        def planes(r, plane, row):
            return tr_ref[p, r, plane, pl.ds(row, STRIP), :]

        def store(left, right, row, re, im):
            rows = pl.ds(pl.multiple_of(left * nev + row, STRIP), STRIP)
            u_ref[rows, right * nev : (right + 1) * nev] = re.astype(jnp.bfloat16)
            u_ref[rows, width + right * nev : width + (right + 1) * nev] = im.astype(jnp.bfloat16)

        build(table, lambda r: gamma[op, r], planes, store, True)

        def tile(n, inner):
            rows = pl.ds(pl.multiple_of(n * TILE, TILE), TILE)
            out = lax.dot_general(
                u_ref[...], y_ref[rows, :], NT_DIMS, preferred_element_type=jnp.float32
            )
            ht_ref[p, :, rows] = out.astype(jnp.bfloat16)
            return inner

        return lax.fori_loop(0, 2 * width // TILE, tile, carry)

    lax.fori_loop(0, count, product, 0)


def other_kernel(scal, gamma, table, bsel, ht_ref, *refs):
    count = (len(refs) - 3) // 2
    here, away = refs[:count], refs[count : 2 * count]
    k_ref, v_ref, p_ref = refs[2 * count :]
    mom, cross = scal[0], scal[1]
    width = ht_ref.shape[1]
    nev = p_ref.shape[-1]

    @pl.when(cross == 0)
    def _():
        for p in range(count):
            p_ref[p] = here[p][...]

    @pl.when(cross != 0)
    def _():
        for p in range(count):
            p_ref[p] = away[p][...]

    def product(p, carry):
        op = mom ^ p

        def planes(r, plane, row):
            return p_ref[p, r, plane, pl.ds(row, STRIP), :].astype(jnp.float32)

        def store(left, right, row, re, im):
            top = pl.ds(pl.multiple_of(left * nev + row, STRIP), STRIP)
            low = pl.ds(pl.multiple_of(width + left * nev + row, STRIP), STRIP)
            near = slice(right * nev, (right + 1) * nev)
            far = slice(width + right * nev, width + (right + 1) * nev)
            re, im = re.astype(jnp.bfloat16), im.astype(jnp.bfloat16)
            v_ref[top, near] = re
            v_ref[top, far] = -im
            v_ref[low, near] = im
            v_ref[low, far] = re

        build(table, lambda r: gamma[op, r], planes, store, False)
        left = bsel[p]

        def tile(n, inner):
            rows = pl.ds(pl.multiple_of(n * TILE, TILE), TILE)
            k_ref[p, :, rows] = lax.dot_general(
                ht_ref[left], v_ref[rows, :], NT_DIMS, preferred_element_type=jnp.float32
            )
            return inner

        return lax.fori_loop(0, 2 * width // TILE, tile, carry)

    lax.fori_loop(0, count, product, 0)


def trace_kernel(scal, label, k_ref, near_ref, far_ref, rest_ref, *refs):
    outs = refs
    count = len(outs)
    mom, cross = scal[0], scal[1]
    width = k_ref.shape[1]
    half = near_ref.shape[1]
    rows = 16

    def part(source, offset, totals):
        def step(index, totals):
            row = pl.multiple_of(index * rows, rows)
            real = source[0, pl.ds(row, rows), :].astype(jnp.float32)
            imag = source[1, pl.ds(row, rows), :].astype(jnp.float32)
            new = []
            for p in range(count):
                here = pl.ds(pl.multiple_of(offset + row, rows), rows)
                kr, ki = k_ref[p, here, :width], k_ref[p, here, width:]
                re, im = real * kr - imag * ki, real * ki + imag * kr
                new.append(totals[2 * p] + re)
                new.append(totals[2 * p + 1] + im)
            return tuple(new)

        return lax.fori_loop(0, source.shape[1] // rows, step, totals)

    zero = jnp.zeros((rows, width), jnp.float32)
    totals = tuple(zero for _ in range(2 * count))
    totals = lax.cond(
        cross != 0, lambda t: part(far_ref, 0, t), lambda t: part(near_ref, 0, t), totals
    )
    totals = part(rest_ref, half, totals)
    sums = [jnp.sum(total) * (1.0 / width) for total in totals]
    lane = lax.broadcasted_iota(jnp.int32, (1, 128), 1)
    for i, out in enumerate(outs):
        line = jnp.zeros((1, 128), jnp.float32)
        for p in range(count):
            mine = label[p] == (mom ^ i)
            re = jnp.where(mine, sums[2 * p], 0.0)
            im = jnp.where(mine, sums[2 * p + 1], 0.0)
            line = line + jnp.where(lane % 2 == 0, re, im)
        out[...] = line


def place_kernel(scal, times, *refs):
    lines, out = refs[:-1], refs[-1]
    sep_index, live = scal[2], scal[3]
    time = lax.broadcasted_iota(jnp.int32, out.shape, 0)
    lane = lax.broadcasted_iota(jnp.int32, out.shape, 1)
    total = jnp.zeros(out.shape, jnp.float32)
    for i, line in enumerate(lines):
        here = (time == times[i]) & (lane // 2 == sep_index) & (live != 0)
        total = total + jnp.where(here, line[...], 0.0)
    out[...] = total


def smem():
    return pl.BlockSpec(memory_space=pltpu.SMEM)


def vmem():
    return pl.BlockSpec(memory_space=pltpu.VMEM)


def params():
    return pltpu.CompilerParams(vmem_limit_bytes=VMEM_LIMIT)


def shards(peram_blocks, projections, gamma_index, partner, separations):
    src_count, snk_count = lax.axis_size("src"), lax.axis_size("snk")
    mom_count = lax.axis_size("mom")
    slices, offsets = peram_blocks.shape[:2]
    width = peram_blocks.shape[-1]
    nterm, nev = projections.shape[2], projections.shape[-1]
    time_count = slices * src_count
    sep_count = separations.shape[0]
    half_snk = snk_count // 2
    src, snk, mom = lax.axis_index("src"), lax.axis_index("snk"), lax.axis_index("mom")
    is_forward = snk < half_snk
    plane = snk % half_snk
    keep = jnp.where(is_forward, 0, offsets - 1)
    give = jnp.where(is_forward, offsets - 1, 0)
    sep_index = plane * offsets + keep
    shift = jnp.where(is_forward, 1, -1) * separations[sep_index]
    peer_shift = jnp.where(is_forward, -1, 1) * separations[plane * offsets + give]

    def local(place, amount):
        return (place + amount) % slices

    def hops(place, amount):
        return ((place + amount) % time_count) // slices

    def swap_mom(array, i):
        return lax.ppermute(array, "mom", [(a, a ^ i) for a in range(mom_count)])

    def swap_snk(array):
        pairs = [(a, (a + half_snk) % snk_count) for a in range(snk_count)]
        return lax.ppermute(array, "snk", pairs)

    def along_src(array, amount):
        step, near = 1, array
        while True:
            if step >= src_count:
                return near, near, jnp.int32(0)
            pairs = [((a + step) % src_count, a) for a in range(src_count)]
            far = lax.ppermute(near, "src", pairs)
            flag = (amount // step) % 2
            step *= 2
            if step >= src_count:
                return near, far, flag
            near = jnp.where(flag != 0, far, near)

    half_rows = width // 2
    peer_local, peer_hops = local(mom, peer_shift), hops(mom, peer_shift)
    own_hops = hops(mom, shift)

    def rows_of(start):
        return lax.dynamic_slice(
            peram_blocks, (peer_local, give, 0, start, 0), (1, 1, 2, half_rows, width)
        ).reshape(2, half_rows, width)

    first = swap_snk(rows_of(0))
    near, far, flag = along_src(rows_of(half_rows), peer_hops)
    rest = swap_snk(jnp.where(flag != 0, far, near))

    def projection(index):
        return lax.dynamic_index_in_dim(projections, index, 0, keepdims=False)[0]

    partners = jnp.stack(
        [partner[0]] + [swap_mom(partner, i)[0] for i in range(1, mom_count)]
    )
    here, away = [], []
    for i in range(mom_count):
        piece = projection(local(mom ^ i, shift))
        if i:
            piece = swap_mom(piece, i)
        near, far, _ = along_src(piece, own_hops)
        here.append(near)
        away.append(far)
    own = [projections]
    for i in range(1, mom_count):
        own.append(swap_mom(projection(mom ^ i), i))

    first_near, first_far, cross = along_src(first, own_hops)

    pieces = jnp.arange(mom_count, dtype=jnp.int32)
    inverse = jnp.sum(
        jnp.where(partners[None, :] == (mom ^ pieces)[:, None], (mom ^ pieces)[None, :], 0), axis=1
    )
    label = jnp.where(is_forward, inverse, mom ^ pieces).astype(jnp.int32)
    bsel = (jnp.where(is_forward, inverse, partners) ^ mom).astype(jnp.int32)
    live = jnp.where(is_forward, 1, int(offsets > 1))
    scal = jnp.stack([mom, cross, sep_index, live]).astype(jnp.int32)
    table = jnp.asarray(dirac_table().reshape(-1))
    where_own = jnp.stack([mom, keep]).astype(jnp.int32)

    ht = pl.pallas_call(
        own_kernel,
        grid_spec=pltpu.PrefetchScalarGridSpec(
            num_scalar_prefetch=1,
            grid=(1,),
            in_specs=[
                smem(),
                smem(),
                pl.BlockSpec((1, 1, 2, width, width), lambda g, at: (at[0], at[1], 0, 0, 0)),
                pl.BlockSpec((1, 1, nterm, 2, nev, nev), lambda g, at: (at[0], 0, 0, 0, 0, 0)),
            ]
            + [pl.BlockSpec((nterm, 2, nev, nev), lambda g, at: (0, 0, 0, 0))] * (mom_count - 1),
            out_specs=pl.BlockSpec((mom_count, width, 2 * width), lambda g, at: (0, 0, 0)),
            scratch_shapes=[
                pltpu.VMEM((2 * width, 2 * width), jnp.bfloat16),
                pltpu.VMEM((width, 2 * width), jnp.bfloat16),
                pltpu.VMEM((mom_count, nterm, 2, nev, nev), jnp.float32),
            ],
        ),
        out_shape=jax.ShapeDtypeStruct((mom_count, width, 2 * width), jnp.bfloat16),
        compiler_params=params(),
        name="own_products",
    )(where_own, gamma_index, table, peram_blocks, *own)

    k = pl.pallas_call(
        other_kernel,
        in_specs=[smem()] * 4 + [vmem()] * (1 + 2 * mom_count),
        out_specs=vmem(),
        out_shape=jax.ShapeDtypeStruct((mom_count, width, 2 * width), jnp.float32),
        scratch_shapes=[
            pltpu.VMEM((2 * width, 2 * width), jnp.bfloat16),
            pltpu.VMEM((mom_count, nterm, 2, nev, nev), jnp.bfloat16),
        ],
        compiler_params=params(),
        name="other_products",
    )(scal, gamma_index, table, bsel, ht, *here, *away)

    lines = pl.pallas_call(
        trace_kernel,
        in_specs=[smem()] * 2 + [vmem()] * 4,
        out_specs=[vmem()] * mom_count,
        out_shape=[jax.ShapeDtypeStruct((1, 128), jnp.float32)] * mom_count,
        compiler_params=params(),
        name="traces",
    )(scal, label, k, first_near, first_far, rest)

    got = [lines[0]] + [swap_mom(lines[i], i) for i in range(1, mom_count)]
    own_time = src * slices + (mom ^ pieces)
    times = jnp.where(is_forward, own_time, own_time + shift) % time_count
    total = pl.pallas_call(
        place_kernel,
        in_specs=[smem()] * 2 + [vmem()] * mom_count,
        out_specs=vmem(),
        out_shape=jax.ShapeDtypeStruct((time_count, 128), jnp.float32),
        name="placed",
    )(scal, times.astype(jnp.int32), *got)

    for axis, count in (("src", src_count), ("snk", snk_count)):
        step = 1
        while step < count:
            total = total + lax.ppermute(total, axis, [(a, a ^ step) for a in range(count)])
            step *= 2
    return total[:, : 2 * sep_count].reshape(time_count, sep_count, 1, 2)


def solution(mesh):
    placed = (
        P("src", "snk", None, None, None),
        P("src", "mom", None, None, None, None),
        P(),
        P("mom"),
        P(),
    )
    return jax.shard_map(
        shards, mesh=mesh, in_specs=placed, out_specs=P(None, None, "mom", None), check_vma=False
    )
```

time: 386 us -> 143 us (0.37)
  waiting for transfers between devices: 215 us -> 58.1 us
  matrix products: 42.2 us -> 0 us
  Pallas kernels: 0 us -> 41.1 us
  local copies, waits for them, and re-layouts: 50.9 us -> 10.7 us
  other arithmetic: 25.9 us -> 6.44 us
  blocking collectives: 17.2 us -> 0 us
  between operations: 14.3 us -> 2.36 us
  starting transfers between devices: 18.8 us -> 23.5 us
    all_to_all x1 -> x0, waiting for transfers between devices: 179 us -> none  [shards(): lax.all_to_all(shaped, ('src', 'snk'), split_axis=4, concat_axis=0, tiled...]
    ppermute x0 -> x23, waiting for transfers between devices: none -> 58.1 us  [the longest x2 31.3 us: swap_snk(): return lax.ppermute(array, 'snk', pairs)]
    dot_general x10 -> x0, matrix products: 42.2 us -> none  [the longest x1 8.61 us: complex_products(): jnp.einsum(form, blocks[:, :, 0], elementals[:, :, 0], preferred_element_...]
    pallas_call x0 -> x4, Pallas kernels: none -> 41.1 us  [the longest x1 19 us: shards(): pl.pallas_call(other_kernel, in_specs=[smem()] * 4 + [vmem()] * (1 + 2 *...]
    all_gather x1 -> x0, waiting for transfers between devices: 35.6 us -> none  [shards(): arrived = lax.all_gather(projections, 'mom', axis=1, tiled=True)]
    another operation x11 -> x0, local copies, waits for them, and re-layouts: 25.6 us -> none
    ppermute x0 -> x23, starting transfers between devices: none -> 23.5 us  [the longest x12 8.74 us: swap_mom(): return lax.ppermute(array, 'mom', [(a, a ^ i) for a in range(mom_count)])]
    all_to_all x1 -> x0, starting transfers between devices: 18.8 us -> none  [shards(): lax.all_to_all(shaped, ('src', 'snk'), split_axis=4, concat_axis=0, tiled...]
  transfers between devices with their start and end apart: 2 -> 23, of which waited for: 2 -> 10; matrix products, arithmetic and copies ran while one was open for 2% -> 6% of each run, Pallas kernels for 0% -> 24%
where the time goes in v1:
time: 143 us; the launch traced here: 142 us
  waiting for transfers between devices  58.1 us (41%)
  Pallas kernels  41.1 us (29%)
  starting transfers between devices  23.5 us (16%)
  local copies, waits for them, and re-layouts  10.7 us (7%)
  other arithmetic  6.44 us (5%)
  between operations  2.36 us (2%)
    ppermute x2, waiting for transfers between devices, swap_snk(): return lax.ppermute(array, 'snk', pairs)  31.3 us
    pallas_call x1, Pallas kernels, shards(): pl.pallas_call(other_kernel, in_specs=[smem()] * 4 + [vmem()] * (1 + 2 *...  19 us
    ppermute x12, waiting for transfers between devices, swap_mom(): return lax.ppermute(array, 'mom', [(a, a ^ i) for a in range(mom_count)])  16.5 us
    pallas_call x1, Pallas kernels, shards(): pl.pallas_call(own_kernel, grid_spec=pltpu.PrefetchScalarGridSpec(num_sca...  15 us
    ppermute x12, starting transfers between devices, swap_mom(): return lax.ppermute(array, 'mom', [(a, a ^ i) for a in range(mom_count)])  8.74 us
    ppermute x6, starting transfers between devices, along_src(): far = lax.ppermute(near, 'src', pairs)  7.54 us
    ppermute x3, waiting for transfers between devices, shards(): lax.ppermute(total, axis, [(a, a ^ step) for a in range(count)])  7.39 us
    pallas_call x1, Pallas kernels, shards(): pl.pallas_call(trace_kernel, in_specs=[smem()] * 2 + [vmem()] * 4, out_sp...  5.67 us
  transfers between devices with their start and end apart: 23, of which 10 were waited for; matrix products, arithmetic and copies ran while one was open for 6% of the time, Pallas kernels for 24%

profile of v1, /device:TPU:0, one launch (start us, length us, event | category | flops | bytes accessed | tf_op | source)
XLA Modules:
  0.0 142.2 jit_solution(15362029386471134130)
XLA Ops:
  0.0 1.4 %fusion.2 = (s32[1]{0:T(128)}, s32[1]{0:T(128)}) fusion(s32[4]{0:T(128)} %param.10, s32[]{:T(128)S(6)} %select_n.160, s32[]{:T(128)S(6)} %select_n.137), kind=kLoop, calls=%fused_computation.23 | loop fusion | bytes 24 | tf_op jit(solution)/shard_map/dynamic_slice | solution.py:247
  2.1 2.1 %dynamic-slice_bitcast_fusion = (bf16[2,256,512]{2,1,0:T(8,128)(2,1)S(1)}, bf16[2,256,512]{2,1,0:T(8,128)(2,1)}) fusion(bf16[4,2,2,512,512]{4,3,2,1,0:T(8,128)(2,1)} %x_ref.1, s32[]{:T(128)S(6)} %select_n.162, s32[]{:T(128)S(6)} %select_n.159), kind=kLoop, calls=%fused_computation | loop fusion | bytes 2097160 | tf_op jit(solution)/shard_map/reshape | solution.py:282
  4.2 2.9 %collective-permute-start.15 = (bf16[2,256,512]{2,1,0:T(8,128)(2,1)S(1)}, bf16[2,256,512]{2,1,0:T(8,128)(2,1)}, u32[]{:S(2)}, u32[]{:S(2)}) collective-permute-start(bf16[2,256,512]{2,1,0:T(8,128)(2,1)S(1)} %get-tuple-element.13), channel_id=1, source_target_pairs={{16,0},{0,16},{17,1},{1,17},{18,2},{2,18},{19,3},{3,19},{20,4},{4,... | collective-permute-start | bytes 1572872 | tf_op jit(solution)/shard_map/ppermute | solution.py:268
  8.0 2.6 %dynamic-slice_bitcast_fusion.2 = (bf16[4,2,128,128]{3,2,1,0:T(8,128)(2,1)S(1)}, bf16[4,2,128,128]{3,2,1,0:T(8,128)(2,1)}, bf16[4,2,128,128]{3,2,1,0:T(8,128)(2,...) fusion(bf16[4,1,4,2,128,128]{5,4,3,2,1,0:T(8,128)(2,1)} %refs_0, ...), kind=kLoop, calls=%fused_computation.3 | loop fusion | bytes 3670044 | tf_op jit(solution)/shard_map/squeeze | solution.py:289
  10.6 1.6 %collective-permute-start.4 = (bf16[4,2,128,128]{3,2,1,0:T(8,128)(2,1)}, bf16[4,2,128,128]{3,2,1,0:T(8,128)(2,1)S(1)}, u32[]{:S(2)}, u32[]{:S(2)}) collective-permute-start(bf16[4,2,128,128]{3,2,1,0:T(8,128)(2,1)} %get-tuple-element.19), channel_id=1, source_target_pairs={{0,2},{1,3},{2,0},{3,1},{4,6},{5,7},{6,4},{7,5},{8,10},{9,11},{10,... | collective-permute-start | bytes 786440 | tf_op jit(solution)/shard_map/ppermute | solution.py:256
  12.2 0.3 collective-permute-start.5
  12.5 1.5 %collective-permute-start.2 = (s32[1]{0:T(128)}, s32[1]{0:T(128)}, u32[]{:S(2)}, u32[]{:S(2)}) collective-permute-start(s32[1]{0:T(128)} %param.9), channel_id=1, source_target_pairs={{0,3},{1,2},{2,1},{3,0},{4,7},{5,6},{6,5},{7,4},{8,11},{9,10},{10,... | collective-permute-start | bytes 20 | tf_op jit(solution)/shard_map/ppermute | solution.py:256
  14.0 10.8 %collective-permute-done.2 = s32[1]{0:T(128)} collective-permute-done((s32[1]{0:T(128)}, s32[1]{0:T(128)}, u32[]{:S(2)}, u32[]{:S(2)}) %collective-permute-start.2) | collective-permute-done | bytes 36 | tf_op jit(solution)/shard_map/ppermute | solution.py:256
  24.8 1.5 %collective-permute-start.1 = (s32[1]{0:T(128)}, s32[1]{0:T(128)}, u32[]{:S(2)}, u32[]{:S(2)}) collective-permute-start(s32[1]{0:T(128)} %param.9), channel_id=1, source_target_pairs={{0,2},{1,3},{2,0},{3,1},{4,6},{5,7},{6,4},{7,5},{8,10},{9,11},{10,... | collective-permute-start | bytes 20 | tf_op jit(solution)/shard_map/ppermute | solution.py:256
  26.3 2.2 %collective-permute-done.1 = s32[1]{0:T(128)} collective-permute-done((s32[1]{0:T(128)}, s32[1]{0:T(128)}, u32[]{:S(2)}, u32[]{:S(2)}) %collective-permute-start.1) | collective-permute-done | bytes 36 | tf_op jit(solution)/shard_map/ppermute | solution.py:256
  28.6 1.2 collective-permute-done
  29.8 2.6 %collective-permute-start.13 = (bf16[2,256,512]{2,1,0:T(8,128)(2,1)}, bf16[2,256,512]{2,1,0:T(8,128)(2,1)S(1)}, u32[]{:S(2)}, u32[]{:S(2)}) collective-permute-start(bf16[2,256,512]{2,1,0:T(8,128)(2,1)} %get-tuple-element.14), channel_id=1, source_target_pairs={{0,8},{4,12},{8,0},{12,4},{1,9},{5,13},{9,1},{13,5},{2,10},{6,14},... | collective-permute-start | bytes 1572872 | tf_op jit(solution)/shard_map/ppermute | solution.py:260
  33.1 0.1 pad_add_fusion.2.scal
  33.3 1.6 %collective-permute-start.7 = (bf16[4,2,128,128]{3,2,1,0:T(8,128)(2,1)}, bf16[4,2,128,128]{3,2,1,0:T(8,128)(2,1)S(1)}, u32[]{:S(2)}, u32[]{:S(2)}) collective-permute-start(bf16[4,2,128,128]{3,2,1,0:T(8,128)(2,1)} %get-tuple-element.21), channel_id=1, source_target_pairs={{0,2},{1,3},{2,0},{3,1},{4,6},{5,7},{6,4},{7,5},{8,10},{9,11},{10,... | collective-permute-start | bytes 786440 | tf_op jit(solution)/shard_map/ppermute | solution.py:256
  34.9 0.3 collective-permute-start.8
  35.1 0.5 collective-permute-start.9
  35.7 1.1 broadcast_select_fusion
  36.8 31.3 %collective-permute-done.13.near_ref = bf16[2,256,512]{2,1,0:T(8,128)(2,1)S(1)} collective-permute-done((bf16[2,256,512]{2,1,0:T(8,128)(2,1)}, bf16[2,256,512]{2,1,0:T(8,128)(2,1)S(1)}, u32[]{:S(2)}, u32[]{:S(2)}) %collective-permute-start.13) | collective-permute-done | bytes 524320 | tf_op jit(solution)/shard_map/ppermute | solution.py:260
  68.2 0.5 collective-permute-start.14
  68.7 0.1 pad_add_fusion.scal
  68.8 1.9 %pad_add_fusion.1 = s32[4]{0:T(128)S(1)} fusion(s32[1]{0:T(128)} %collective-permute-done.2, s32[1]{0:T(128)} %collective-permute-done.1, s32[1]{0:T(128)} %collective-permute-done, s32[1]{0:T(128)S(6)} %copy.11), kind=kLoop, calls=%fused_computation.20 | loop fusion | flops 12 | bytes 32 | tf_op jit(solution)/shard_map/stack | solution.py:291
  70.6 1.5 %collective-permute-start.10 = (bf16[4,2,128,128]{3,2,1,0:T(8,128)(2,1)S(1)}, bf16[4,2,128,128]{3,2,1,0:T(8,128)(2,1)S(1)}, u32[]{:S(2)}, u32[]{:S(2)}) collective-permute-start(bf16[4,2,128,128]{3,2,1,0:T(8,128)(2,1)S(1)} %collective-permute-done.6.refs_1_), channel_id=1, source_target_pairs={{16,0},{0,16},{17,1},{1,17},{18,2},{2,18},{19,3},{3,19},{20,4},{4,... | collective-permute-start | bytes 786440 | tf_op jit(solution)/shard_map/ppermute | solution.py:268
  72.2 0.5 collective-permute-start.11
  72.7 1.5 %collective-permute-start.12 = (bf16[4,2,128,128]{3,2,1,0:T(8,128)(2,1)S(1)}, bf16[4,2,128,128]{3,2,1,0:T(8,128)(2,1)S(1)}, u32[]{:S(2)}, u32[]{:S(2)}) collective-permute-start(bf16[4,2,128,128]{3,2,1,0:T(8,128)(2,1)S(1)} %collective-permute-done.8.refs_3_), channel_id=1, source_target_pairs={{16,0},{0,16},{17,1},{1,17},{18,2},{2,18},{19,3},{3,19},{20,4},{4,... | collective-permute-start | bytes 786440 | tf_op jit(solution)/shard_map/ppermute | solution.py:268
  74.2 0.2 select_reduce_fusion
  74.4 1.9 %fusion = (s32[4]{0:T(128)S(1)}, s32[4]{0:T(128)S(1)}) fusion(s32[4]{0:T(128)S(1)} %select_reduce_fusion, pred[]{:T(512)S(6)} %lt.85, s32[]{:T(128)} %axis_index.32, s32[1]{0:T(128)} %collective-permute-done.2, s32[1]{0:T(128)} %collective-permute-done.1, s32[1]{0:T(128)} %collective-permute-done, s32[1]{0:T(128)S(6)} %copy.11), kind=kLoop, calls=%fused_computation.17 | loop fusion | flops 28 | bytes 69 | tf_op jit(solution)/shard_map/xor | solution.py:313
  76.2 0.7 copy-done.2
  76.9 0.7 copy-done.4
  77.6 15.0 %own_products.1.ht_ref = bf16[4,512,1024]{2,1,0:T(8,128)(2,1)S(1)} custom-call(s32[2]{0:T(128)S(1)} %pad_add_fusion.2.scal, s32[4,4]{1,0:T(4,128)S(1)} %copy-done.2, f32[512]{0:T(512)S(1)} %copy-done.4, bf16[4,2,2,512,512]{4,3,2,1,0:T(8,128)(2,1)} %x_ref.1, bf16[4,1,4,2,128,128]{5,4,3,2,1,0:T(8,128)(2,1)S(1)} %copy-done.1, ...), custom_call_target="tpu_custom_call" | custom-call | tf_op jit(solution)/shard_map/own_products/pallas_call | solution.py:319
  92.7 2.0 %copy-done = bf16[4,512,1024]{2,1,0:T(8,128)(2,1)} copy-done((bf16[4,512,1024]{2,1,0:T(8,128)(2,1)}, bf16[4,512,1024]{2,1,0:T(8,128)(2,1)S(1)}, u32[]{:S(2)}) %copy-start) | copy-done | bytes 4194328
  94.7 2.9 %collective-permute-done.12.refs_7_ = bf16[4,2,128,128]{3,2,1,0:T(8,128)(2,1)S(1)} collective-permute-done((bf16[4,2,128,128]{3,2,1,0:T(8,128)(2,1)S(1)}, bf16[4,2,128,128]{3,2,1,0:T(8,128)(2,1)S(1)}, u32[]{:S(2)}, u32[]{:S(2)}) %collective-permute-start.12) | collective-permute-done | bytes 262176 | tf_op jit(solution)/shard_map/ppermute | solution.py:268
  97.6 19.0 %other_products.1.k_ref = f32[4,512,1024]{2,1,0:T(8,128)} custom-call(s32[4]{0:T(128)S(1)} %pad_add_fusion.scal, s32[4,4]{1,0:T(4,128)S(1)} %copy-done.3, f32[512]{0:T(512)S(1)} %copy-done.5, s32[4]{0:T(128)S(1)} %get-tuple-element.24.bsel, bf16[4,512,1024]{2,1,0:T(8,128)(2,1)} %copy-done, bf16[4,2,128,128]{3,2,1,0:T(8,128)(2,1)S(1)} %get-tuple-element.17.refs_0_, ...), custom_call_target="tpu_custom_call" | custom-call | tf_op jit(solution)/shard_map/other_products/pallas_call | solution.py:343
  116.5 5.7 %traces.1 = (f32[1,128]{1,0:T(1,128)S(1)}, f32[1,128]{1,0:T(1,128)S(1)}, f32[1,128]{1,0:T(1,128)S(1)}, f32[1,128]{1,0:T(1,128)S(1)}) custom-call(s32[4]{0:T(128)S(1)} %pad_add_fusion.scal, s32[4]{0:T(128)S(1)} %get-tuple-element.25.label, f32[4,512,1024]{2,1,0:T(8,128)} %other_products.1.k_ref, bf16[2,256,512]{2,1,0:T(8,128)(2,1)S(1)} %collective-permute-done.13.near_ref, ...), custom_call_target="tpu_custom_call" | custom-call | tf_op jit(solution)/shard_map/traces/pallas_call | solution.py:356
  122.3 1.6 %collective-permute-start.18 = (f32[1,128]{1,0:T(1,128)S(1)}, f32[1,128]{1,0:T(1,128)S(1)}, u32[]{:S(2)}, u32[]{:S(2)}) collective-permute-start(f32[1,128]{1,0:T(1,128)S(1)} %get-tuple-element.11), channel_id=1, source_target_pairs={{0,2},{1,3},{2,0},{3,1},{4,6},{5,7},{6,4},{7,5},{8,10},{9,11},{10,... | collective-permute-start | bytes 1544 | tf_op jit(solution)/shard_map/ppermute | solution.py:256
  123.9 0.2 collective-permute-start.19
  124.2 0.6 and_select_fusion.times
  124.8 1.2 collective-permute-done.18.refs_2_
  125.9 1.0 collective-permute-done.19.refs_3_
  126.9 0.6 copy-done.10
  127.5 1.4 placed.1
  128.9 0.5 collective-permute-start.20
  129.4 3.3 %collective-permute-done.20 = f32[8,128]{1,0:T(8,128)S(1)} collective-permute-done((f32[8,128]{1,0:T(8,128)}, f32[8,128]{1,0:T(8,128)S(1)}, u32[]{:S(2)}, u32[]{:S(2)}) %collective-permute-start.20) | collective-permute-done | bytes 4128 | tf_op jit(solution)/shard_map/ppermute | solution.py:379
  132.7 0.7 add.151
  133.4 1.4 collective-permute-start.21
  134.8 2.2 %collective-permute-done.21 = f32[8,128]{1,0:T(8,128)S(1)} collective-permute-done((f32[8,128]{1,0:T(8,128)S(1)}, f32[8,128]{1,0:T(8,128)S(1)}, u32[]{:S(2)}, u32[]{:S(2)}) %collective-permute-start.21) | collective-permute-done | bytes 4128 | tf_op jit(solution)/shard_map/ppermute | solution.py:379
  137.0 2.6 %collective-permute-start.22 = (f32[8,128]{1,0:T(8,128)S(1)}, f32[8,128]{1,0:T(8,128)S(1)}, u32[]{:S(2)}, u32[]{:S(2)}) collective-permute-start(f32[8,128]{1,0:T(8,128)S(1)} %add.152), channel_id=1, source_target_pairs={{0,8},{4,12},{8,0},{12,4},{1,9},{5,13},{9,1},{13,5},{2,10},{6,14},... | collective-permute-start | bytes 12296 | tf_op jit(solution)/shard_map/ppermute | solution.py:379
  139.7 1.9 %collective-permute-done.22 = f32[8,128]{1,0:T(8,128)S(1)} collective-permute-done((f32[8,128]{1,0:T(8,128)S(1)}, f32[8,128]{1,0:T(8,128)S(1)}, u32[]{:S(2)}, u32[]{:S(2)}) %collective-permute-start.22) | collective-permute-done | bytes 4128 | tf_op jit(solution)/shard_map/ppermute | solution.py:379
  141.5 0.7 copy.9
  (39 shorter events, 0.3 us)
Async XLA Ops:
  0.0 76.2 %copy-start.1 = (bf16[4,1,4,2,128,128]{5,4,3,2,1,0:T(8,128)(2,1)S(1)}, bf16[4,1,4,2,128,128]{5,4,3,2,1,0:T(8,128)(2,1)}, u32[]{:S(2)}) copy-start(bf16[4,1,4,2,128,128]{5,4,3,2,1,0:T(8,128)(2,1)} %refs_0_.1) | copy-start | bytes 3145732
  4.2 30.9 %collective-permute-start.15 = (bf16[2,256,512]{2,1,0:T(8,128)(2,1)S(1)}, bf16[2,256,512]{2,1,0:T(8,128)(2,1)}, u32[]{:S(2)}, u32[]{:S(2)}) collective-permute-start(bf16[2,256,512]{2,1,0:T(8,128)(2,1)S(1)} %get-tuple-element.13), channel_id=1, source_target_pairs={{16,0},{0,16},{17,1},{1,17},{18,2},{2,18},{19,3},{3,19},{20,4},{4,... | collective-permute-start | bytes 1572872 | tf_op jit(solution)/shard_map/ppermute | solution.py:268
  10.6 87.0 %copy-start.3 = (s32[4,4]{1,0:T(4,128)S(1)}, s32[4,4]{1,0:T(4,128)}, u32[]{:S(2)}) copy-start(s32[4,4]{1,0:T(4,128)} %gamma.3) | copy-start | bytes 196
  10.6 87.0 %copy-start.5 = (f32[512]{0:T(512)S(1)}, f32[512]{0:T(512)}, u32[]{:S(2)}) copy-start(f32[512]{0:T(512)} %constant.142.clone.table) | copy-start | bytes 6148
  10.6 22.7 %collective-permute-start.3 = (bf16[4,2,128,128]{3,2,1,0:T(8,128)(2,1)}, bf16[4,2,128,128]{3,2,1,0:T(8,128)(2,1)S(1)}, u32[]{:S(2)}, u32[]{:S(2)}) collective-permute-start(bf16[4,2,128,128]{3,2,1,0:T(8,128)(2,1)} %get-tuple-element.20), channel_id=1, source_target_pairs={{0,1},{1,0},{2,3},{3,2},{4,5},{5,4},{6,7},{7,6},{8,9},{9,8},{10,11... | collective-permute-start | bytes 786440 | tf_op jit(solution)/shard_map/ppermute | solution.py:256
  10.6 22.6 %collective-permute-start.4 = (bf16[4,2,128,128]{3,2,1,0:T(8,128)(2,1)}, bf16[4,2,128,128]{3,2,1,0:T(8,128)(2,1)S(1)}, u32[]{:S(2)}, u32[]{:S(2)}) collective-permute-start(bf16[4,2,128,128]{3,2,1,0:T(8,128)(2,1)} %get-tuple-element.19), channel_id=1, source_target_pairs={{0,2},{1,3},{2,0},{3,1},{4,6},{5,7},{6,4},{7,5},{8,10},{9,11},{10,... | collective-permute-start | bytes 786440 | tf_op jit(solution)/shard_map/ppermute | solution.py:256
  12.2 22.6 %collective-permute-start.5 = (bf16[4,2,128,128]{3,2,1,0:T(8,128)(2,1)}, bf16[4,2,128,128]{3,2,1,0:T(8,128)(2,1)S(1)}, u32[]{:S(2)}, u32[]{:S(2)}) collective-permute-start(bf16[4,2,128,128]{3,2,1,0:T(8,128)(2,1)} %get-tuple-element.18), channel_id=1, source_target_pairs={{0,3},{1,2},{2,1},{3,0},{4,7},{5,6},{6,5},{7,4},{8,11},{9,10},{10,... | collective-permute-start | bytes 786440 | tf_op jit(solution)/shard_map/ppermute | solution.py:256
  12.5 12.3 %collective-permute-start.2 = (s32[1]{0:T(128)}, s32[1]{0:T(128)}, u32[]{:S(2)}, u32[]{:S(2)}) collective-permute-start(s32[1]{0:T(128)} %param.9), channel_id=1, source_target_pairs={{0,3},{1,2},{2,1},{3,0},{4,7},{5,6},{6,5},{7,4},{8,11},{9,10},{10,... | collective-permute-start | bytes 20 | tf_op jit(solution)/shard_map/ppermute | solution.py:256
  24.8 3.8 %collective-permute-start.1 = (s32[1]{0:T(128)}, s32[1]{0:T(128)}, u32[]{:S(2)}, u32[]{:S(2)}) collective-permute-start(s32[1]{0:T(128)} %param.9), channel_id=1, source_target_pairs={{0,2},{1,3},{2,0},{3,1},{4,6},{5,7},{6,4},{7,5},{8,10},{9,11},{10,... | collective-permute-start | bytes 20 | tf_op jit(solution)/shard_map/ppermute | solution.py:256
  28.6 1.2 collective-permute-start
  29.8 38.3 %collective-permute-start.13 = (bf16[2,256,512]{2,1,0:T(8,128)(2,1)}, bf16[2,256,512]{2,1,0:T(8,128)(2,1)S(1)}, u32[]{:S(2)}, u32[]{:S(2)}) collective-permute-start(bf16[2,256,512]{2,1,0:T(8,128)(2,1)} %get-tuple-element.14), channel_id=1, source_target_pairs={{0,8},{4,12},{8,0},{12,4},{1,9},{5,13},{9,1},{13,5},{2,10},{6,14},... | collective-permute-start | bytes 1572872 | tf_op jit(solution)/shard_map/ppermute | solution.py:260
  33.2 3.5 %collective-permute-start.6 = (bf16[4,2,128,128]{3,2,1,0:T(8,128)(2,1)}, bf16[4,2,128,128]{3,2,1,0:T(8,128)(2,1)S(1)}, u32[]{:S(2)}, u32[]{:S(2)}) collective-permute-start(bf16[4,2,128,128]{3,2,1,0:T(8,128)(2,1)} %get-tuple-element.16), channel_id=1, source_target_pairs={{0,1},{1,0},{2,3},{3,2},{4,5},{5,4},{6,7},{7,6},{8,9},{9,8},{10,11... | collective-permute-start | bytes 786440 | tf_op jit(solution)/shard_map/ppermute | solution.py:256
  33.3 37.4 %collective-permute-start.7 = (bf16[4,2,128,128]{3,2,1,0:T(8,128)(2,1)}, bf16[4,2,128,128]{3,2,1,0:T(8,128)(2,1)S(1)}, u32[]{:S(2)}, u32[]{:S(2)}) collective-permute-start(bf16[4,2,128,128]{3,2,1,0:T(8,128)(2,1)} %get-tuple-element.21), channel_id=1, source_target_pairs={{0,2},{1,3},{2,0},{3,1},{4,6},{5,7},{6,4},{7,5},{8,10},{9,11},{10,... | collective-permute-start | bytes 786440 | tf_op jit(solution)/shard_map/ppermute | solution.py:256
  34.9 37.3 %collective-permute-start.8 = (bf16[4,2,128,128]{3,2,1,0:T(8,128)(2,1)S(1)}, bf16[4,2,128,128]{3,2,1,0:T(8,128)(2,1)S(1)}, u32[]{:S(2)}, u32[]{:S(2)}) collective-permute-start(bf16[4,2,128,128]{3,2,1,0:T(8,128)(2,1)S(1)} %get-tuple-element.15), channel_id=1, source_target_pairs={{0,3},{1,2},{2,1},{3,0},{4,7},{5,6},{6,5},{7,4},{8,11},{9,10},{10,... | collective-permute-start | bytes 786440 | tf_op jit(solution)/shard_map/ppermute | solution.py:256
  35.1 37.5 %collective-permute-start.9 = (bf16[4,2,128,128]{3,2,1,0:T(8,128)(2,1)S(1)}, bf16[4,2,128,128]{3,2,1,0:T(8,128)(2,1)S(1)}, u32[]{:S(2)}, u32[]{:S(2)}) collective-permute-start(bf16[4,2,128,128]{3,2,1,0:T(8,128)(2,1)S(1)} %get-tuple-element.17.refs_0_), channel_id=1, source_target_pairs={{16,0},{0,16},{17,1},{1,17},{18,2},{2,18},{19,3},{3,19},{20,4},{4,... | collective-permute-start | bytes 786440 | tf_op jit(solution)/shard_map/ppermute | solution.py:268
  36.8 79.8 %collective-permute-start.16 = (bf16[2,256,512]{2,1,0:T(8,128)(2,1)S(1)}, bf16[2,256,512]{2,1,0:T(8,128)(2,1)S(1)}, u32[]{:S(2)}, u32[]{:S(2)}) collective-permute-start(bf16[2,256,512]{2,1,0:T(8,128)(2,1)S(1)} %broadcast_select_fusion), channel_id=1, source_target_pairs={{0,8},{4,12},{8,0},{12,4},{1,9},{5,13},{9,1},{13,5},{2,10},{6,14},... | collective-permute-start | bytes 1572872 | tf_op jit(solution)/shard_map/ppermute | solution.py:260
  68.2 48.4 %collective-permute-start.14 = (bf16[2,256,512]{2,1,0:T(8,128)(2,1)S(1)}, bf16[2,256,512]{2,1,0:T(8,128)(2,1)S(1)}, u32[]{:S(2)}, u32[]{:S(2)}) collective-permute-start(bf16[2,256,512]{2,1,0:T(8,128)(2,1)S(1)} %collective-permute-done.13.near_ref), channel_id=1, source_target_pairs={{16,0},{0,16},{17,1},{1,17},{18,2},{2,18},{19,3},{3,19},{20,4},{4,... | collective-permute-start | bytes 1572872 | tf_op jit(solution)/shard_map/ppermute | solution.py:268
  68.8 47.8 %copy-start.6 = (s32[4]{0:T(128)}, s32[4]{0:T(128)S(1)}, u32[]{:S(2)}) copy-start(s32[4]{0:T(128)S(1)} %pad_add_fusion.scal) | copy-start | bytes 52
  70.6 24.0 %collective-permute-start.10 = (bf16[4,2,128,128]{3,2,1,0:T(8,128)(2,1)S(1)}, bf16[4,2,128,128]{3,2,1,0:T(8,128)(2,1)S(1)}, u32[]{:S(2)}, u32[]{:S(2)}) collective-permute-start(bf16[4,2,128,128]{3,2,1,0:T(8,128)(2,1)S(1)} %collective-permute-done.6.refs_1_), channel_id=1, source_target_pairs={{16,0},{0,16},{17,1},{1,17},{18,2},{2,18},{19,3},{3,19},{20,4},{4,... | collective-permute-start | bytes 786440 | tf_op jit(solution)/shard_map/ppermute | solution.py:268
  72.2 22.5 %collective-permute-start.11 = (bf16[4,2,128,128]{3,2,1,0:T(8,128)(2,1)S(1)}, bf16[4,2,128,128]{3,2,1,0:T(8,128)(2,1)S(1)}, u32[]{:S(2)}, u32[]{:S(2)}) collective-permute-start(bf16[4,2,128,128]{3,2,1,0:T(8,128)(2,1)S(1)} %collective-permute-done.7.refs_2_), channel_id=1, source_target_pairs={{16,0},{0,16},{17,1},{1,17},{18,2},{2,18},{19,3},{3,19},{20,4},{4,... | collective-permute-start | bytes 786440 | tf_op jit(solution)/shard_map/ppermute | solution.py:268
  72.7 24.9 %collective-permute-start.12 = (bf16[4,2,128,128]{3,2,1,0:T(8,128)(2,1)S(1)}, bf16[4,2,128,128]{3,2,1,0:T(8,128)(2,1)S(1)}, u32[]{:S(2)}, u32[]{:S(2)}) collective-permute-start(bf16[4,2,128,128]{3,2,1,0:T(8,128)(2,1)S(1)} %collective-permute-done.8.refs_3_), channel_id=1, source_target_pairs={{16,0},{0,16},{17,1},{1,17},{18,2},{2,18},{19,3},{3,19},{20,4},{4,... | collective-permute-start | bytes 786440 | tf_op jit(solution)/shard_map/ppermute | solution.py:268
  76.2 0.7 copy-start.2
  76.9 0.7 copy-start.4
  92.7 2.0 %copy-start = (bf16[4,512,1024]{2,1,0:T(8,128)(2,1)}, bf16[4,512,1024]{2,1,0:T(8,128)(2,1)S(1)}, u32[]{:S(2)}) copy-start(bf16[4,512,1024]{2,1,0:T(8,128)(2,1)S(1)} %own_products.1.ht_ref) | copy-start | bytes 12582916
  122.2 4.7 %copy-start.7 = (f32[1,128]{1,0:T(1,128)}, f32[1,128]{1,0:T(1,128)S(1)}, u32[]{:S(2)}) copy-start(f32[1,128]{1,0:T(1,128)S(1)} %get-tuple-element.9.refs_0_) | copy-start | bytes 1540
  122.2 2.5 %collective-permute-start.17 = (f32[1,128]{1,0:T(1,128)S(1)}, f32[1,128]{1,0:T(1,128)S(1)}, u32[]{:S(2)}, u32[]{:S(2)}) collective-permute-start(f32[1,128]{1,0:T(1,128)S(1)} %get-tuple-element.10), channel_id=1, source_target_pairs={{0,1},{1,0},{2,3},{3,2},{4,5},{5,4},{6,7},{7,6},{8,9},{9,8},{10,11... | collective-permute-start | bytes 1544 | tf_op jit(solution)/shard_map/ppermute | solution.py:256
  122.3 3.6 %collective-permute-start.18 = (f32[1,128]{1,0:T(1,128)S(1)}, f32[1,128]{1,0:T(1,128)S(1)}, u32[]{:S(2)}, u32[]{:S(2)}) collective-permute-start(f32[1,128]{1,0:T(1,128)S(1)} %get-tuple-element.11), channel_id=1, source_target_pairs={{0,2},{1,3},{2,0},{3,1},{4,6},{5,7},{6,4},{7,5},{8,10},{9,11},{10,... | collective-permute-start | bytes 1544 | tf_op jit(solution)/shard_map/ppermute | solution.py:256
  123.9 3.0 %collective-permute-start.19 = (f32[1,128]{1,0:T(1,128)S(1)}, f32[1,128]{1,0:T(1,128)S(1)}, u32[]{:S(2)}, u32[]{:S(2)}) collective-permute-start(f32[1,128]{1,0:T(1,128)S(1)} %get-tuple-element.12), channel_id=1, source_target_pairs={{0,3},{1,2},{2,1},{3,0},{4,7},{5,6},{6,5},{7,4},{8,11},{9,10},{10,... | collective-permute-start | bytes 1544 | tf_op jit(solution)/shard_map/ppermute | solution.py:256
  124.8 2.1 %copy-start.8 = (f32[1,128]{1,0:T(1,128)}, f32[1,128]{1,0:T(1,128)S(1)}, u32[]{:S(2)}) copy-start(f32[1,128]{1,0:T(1,128)S(1)} %collective-permute-done.17.refs_1_) | copy-start | bytes 1540
  125.9 1.0 copy-start.9
  126.9 0.6 copy-start.10
  128.9 3.8 %collective-permute-start.20 = (f32[8,128]{1,0:T(8,128)}, f32[8,128]{1,0:T(8,128)S(1)}, u32[]{:S(2)}, u32[]{:S(2)}) collective-permute-start(f32[8,128]{1,0:T(8,128)} %placed.1), channel_id=1, source_target_pairs={{0,16},{16,0},{1,17},{17,1},{2,18},{18,2},{3,19},{19,3},{4,20},{20... | collective-permute-start | bytes 12296 | tf_op jit(solution)/shard_map/ppermute | solution.py:379
  133.4 3.6 %collective-permute-start.21 = (f32[8,128]{1,0:T(8,128)S(1)}, f32[8,128]{1,0:T(8,128)S(1)}, u32[]{:S(2)}, u32[]{:S(2)}) collective-permute-start(f32[8,128]{1,0:T(8,128)S(1)} %add.151), channel_id=1, source_target_pairs={{0,4},{4,0},{8,12},{12,8},{1,5},{5,1},{9,13},{13,9},{2,6},{6,2},{1... | collective-permute-start | bytes 12296 | tf_op jit(solution)/shard_map/ppermute | solution.py:379
  137.0 4.5 %collective-permute-start.22 = (f32[8,128]{1,0:T(8,128)S(1)}, f32[8,128]{1,0:T(8,128)S(1)}, u32[]{:S(2)}, u32[]{:S(2)}) collective-permute-start(f32[8,128]{1,0:T(8,128)S(1)} %add.152), channel_id=1, source_target_pairs={{0,8},{4,12},{8,0},{12,4},{1,9},{5,13},{9,1},{13,5},{2,10},{6,14},... | collective-permute-start | bytes 12296 | tf_op jit(solution)/shard_map/ppermute | solution.py:379

commit v2 on v0

v2 whole, which is shorter than its diff:
```python
import jax
import jax.numpy as jnp
from jax import lax
from jax.experimental import pallas as pl
from jax.experimental.pallas import tpu as pltpu
from jax.sharding import PartitionSpec as P

NSPIN = 4
NT_DIMS = (((1,), (1,)), ((), ()))
MIB = 1024 * 1024
TAG_ROWS = 16
GAMMAS = (
    (3, 1 | 1 << 2 | 3 << 4 | 3 << 6),
    (3, 2 | 0 << 2 | 0 << 4 | 2 << 6),
    (2, 1 | 3 << 2 | 3 << 4 | 1 << 6),
    (2, 0),
)


def spin_entry(code, row):
    phase = row * 0
    for bit, (flip, phases) in enumerate(GAMMAS):
        on = (code >> bit) & 1
        phase = phase + on * ((phases >> (2 * row)) & 3)
        row = row ^ (on * flip)
    return row, phase & 3


def spin_column_entry(code, column):
    row = column
    for bit, (flip, _) in enumerate(GAMMAS):
        row = row ^ (((code >> bit) & 1) * flip)
    return row, spin_entry(code, row)[1]


def phase_blocks(block_ref, r, real, imag):
    nev = real.shape[0]
    for phase, (a, b) in enumerate(((real, imag), (-imag, real), (-real, -imag), (imag, -real))):
        slot = 4 * r + phase
        block_ref[slot, :nev, :nev] = a
        block_ref[slot, :nev, nev:] = -b
        block_ref[slot, nev:, :nev] = b
        block_ref[slot, nev:, nev:] = a


def position():
    return lax.axis_index("src"), lax.axis_index("snk"), lax.axis_index("mom")


def pair_plan(separations, snk, offsets, half_snk):
    forward = snk < half_snk
    base = lax.rem(snk, half_snk) * offsets
    keep = jnp.where(forward, 0, offsets - 1)
    give = offsets - 1 - keep
    sign = jnp.where(forward, 1, -1)
    return forward, keep, give, base + keep, sign * separations[base + keep], -sign * separations[base + give]


def pack_kernel(place, seps, partner, peram, proj, *refs):
    outs, (tag, sems) = refs[:-2], refs[-2:]
    first, rest, here = outs[:3]
    count = (len(outs) - 3) // 2
    other, own = outs[3 : 3 + count], outs[3 + count :]
    slices, offsets = peram.shape[:2]
    time_count, half_snk = place[3], place[4]
    snk, mom = place[1], place[2]
    _, _, give, _, shift, peer_shift = pair_plan(seps, snk, offsets, half_snk)

    def local(amount):
        return lax.rem(amount + time_count, slices)

    half = first.shape[1]
    rows = own[0].shape[0] - TAG_ROWS
    peer = local(mom + peer_shift)
    tag[...] = jnp.full(tag.shape, partner[0].astype(jnp.float32)).astype(jnp.bfloat16)
    copies = [
        (peram.at[peer, give, :, pl.ds(0, half)], first),
        (peram.at[peer, give, :, pl.ds(half, half)], rest),
    ]
    for i in range(count):
        copies.append((proj.at[local((mom ^ (i + 1)) + shift)], other[i]))
    copies.append((proj.at[local(mom + shift)], here))
    for i in range(count):
        copies.append((proj.at[mom ^ (i + 1)], own[i].at[pl.ds(0, rows)]))
        copies.append((tag, own[i].at[pl.ds(rows, TAG_ROWS)]))
    handles = [
        pltpu.make_async_copy(source, target, sems.at[n])
        for n, (source, target) in enumerate(copies)
    ]
    for handle in handles:
        handle.start()
    for handle in handles:
        handle.wait()


def own_kernel(place, gamma, x_ref, *refs):
    pieces, (ht_ref, xb_ref, block_ref, tr_ref) = refs[:-4], refs[-4:]
    mom = place[0]
    nev = tr_ref.shape[-1]
    for spin in range(NSPIN):
        lanes = slice(spin * nev, (spin + 1) * nev)
        xb_ref[spin, :, :nev] = x_ref[0, 0, 0, :, lanes]
        xb_ref[spin, :, nev:] = x_ref[0, 0, 1, :, lanes]
    nterm = tr_ref.shape[1] // 2
    for p, piece in enumerate(pieces):
        for n in range(2 * nterm):
            rows = slice(n * nev, (n + 1) * nev)
            source = piece[0, rows] if p == 0 else piece[rows]
            tr_ref[p, n] = source.T

    def product(p, carry):
        for r in range(nterm):
            phase_blocks(block_ref, r, tr_ref[p, 2 * r], tr_ref[p, 2 * r + 1])

        def spin_rows(spin, inner):
            total = None
            for r in range(nterm):
                source, phase = spin_column_entry(gamma[mom ^ p, r], spin)
                term = lax.dot_general(
                    block_ref[4 * r + phase],
                    xb_ref[source],
                    NT_DIMS,
                    preferred_element_type=jnp.float32,
                )
                total = term if total is None else total + term
            total = total.astype(jnp.bfloat16)
            rows = pl.ds(pl.multiple_of(spin * nev, nev), nev)
            for column in range(NSPIN):
                lanes = slice(column * nev, (column + 1) * nev)
                ht_ref[p, column, rows, :nev] = total[:nev, lanes]
                ht_ref[p, column, rows, nev:] = total[nev:, lanes]
            return inner

        return lax.fori_loop(0, NSPIN, spin_rows, carry)

    lax.fori_loop(0, len(pieces), product, 0)


def other_kernel(place, gamma, partner, ht_ref, *refs):
    count = place_count = ht_ref.shape[0]
    tags = refs[: count - 1]
    here, away = refs[count - 1 : 2 * count - 1], refs[2 * count - 1 : 3 * count - 1]
    k_ref, label_ref, p_ref, block_ref = refs[3 * count - 1 :]
    mom, cross, forward = place[0], place[1], place[2]
    nev = block_ref.shape[-1] // 2
    nterm = block_ref.shape[0] // 4
    partners = [partner[0]] + [
        jnp.max(tag[tag.shape[0] - TAG_ROWS :].astype(jnp.float32)).astype(jnp.int32)
        for tag in tags
    ]
    for p in range(place_count):
        back = jnp.int32(0)
        for i in range(count):
            back = back + jnp.where(partners[i] == (mom ^ p), mom ^ i, 0)
        label_ref[p] = jnp.where(forward != 0, back, mom ^ p)
        label_ref[count + p] = jnp.where(forward != 0, back, partners[p]) ^ mom

    @pl.when(cross == 0)
    def _():
        for p in range(count):
            p_ref[p] = here[p][...]

    @pl.when(cross != 0)
    def _():
        for p in range(count):
            p_ref[p] = away[p][...]

    def product(p, carry):
        for r in range(nterm):
            real = p_ref[p, 2 * r * nev : (2 * r + 1) * nev]
            imag = p_ref[p, (2 * r + 1) * nev : (2 * r + 2) * nev]
            phase_blocks(block_ref, r, real, imag)
        left = label_ref[count + p]

        def spin_columns(spin, inner):
            total = None
            for r in range(nterm):
                source, phase = spin_entry(gamma[mom ^ p, r], spin)
                term = lax.dot_general(
                    ht_ref[left, source],
                    block_ref[4 * r + phase],
                    NT_DIMS,
                    preferred_element_type=jnp.float32,
                )
                total = term if total is None else total + term
            k_ref[p, spin] = total
            return inner

        return lax.fori_loop(0, NSPIN, spin_columns, carry)

    lax.fori_loop(0, count, product, 0)


def row_sums(k_ref, source, offset, totals):
    rows = 16
    count = len(totals) // 2
    nev = source.shape[-1] // NSPIN

    def step(index, totals):
        row = pl.multiple_of(index * rows, rows)
        here = pl.ds(pl.multiple_of(offset + row, rows), rows)
        totals = list(totals)
        for spin in range(NSPIN):
            lanes = slice(spin * nev, (spin + 1) * nev)
            real = source[0, pl.ds(row, rows), lanes].astype(jnp.float32)
            imag = source[1, pl.ds(row, rows), lanes].astype(jnp.float32)
            for p in range(count):
                kr, ki = k_ref[p, spin, here, :nev], k_ref[p, spin, here, nev:]
                totals[2 * p] += real * kr - imag * ki
                totals[2 * p + 1] += real * ki + imag * kr
        return tuple(totals)

    return lax.fori_loop(0, source.shape[1] // rows, step, totals)


def early_kernel(place, k_ref, near_ref, far_ref, sums_ref):
    cross = place[1]
    count = sums_ref.shape[0]
    zero = tuple(jnp.zeros(sums_ref.shape[1:], jnp.float32) for _ in range(count))

    @pl.when(cross == 0)
    def _():
        for n, total in enumerate(row_sums(k_ref, near_ref, 0, zero)):
            sums_ref[n] = total

    @pl.when(cross != 0)
    def _():
        for n, total in enumerate(row_sums(k_ref, far_ref, 0, zero)):
            sums_ref[n] = total


def late_kernel(place, label, k_ref, rest_ref, sums_ref, *outs):
    count = len(outs)
    mom, time, sep_index, live = place[0], place[3], place[4], place[5]
    width = rest_ref.shape[-1]
    half = k_ref.shape[2] - rest_ref.shape[1]
    totals = row_sums(k_ref, rest_ref, half, tuple(sums_ref[n] for n in range(2 * count)))
    sums = [jnp.sum(total, axis=0, keepdims=True) for total in totals]
    sums = [jnp.sum(total, axis=1, keepdims=True) * (1.0 / width) for total in sums]
    shape = outs[0].shape
    row = lax.broadcasted_iota(jnp.int32, shape, 0)
    lane = lax.broadcasted_iota(jnp.int32, shape, 1)
    here = (row == time) & (lane // 2 == sep_index) & (live != 0)
    values = [jnp.where(lane % 2 == 0, sums[2 * p], sums[2 * p + 1]) for p in range(count)]
    for i, out in enumerate(outs):
        line = jnp.zeros(shape, jnp.float32)
        for p in range(count):
            line = jnp.where(label[p] == (mom ^ i), values[p], line)
        out[...] = jnp.where(here, line, 0.0)


def smem():
    return pl.BlockSpec(memory_space=pltpu.SMEM)


def vmem():
    return pl.BlockSpec(memory_space=pltpu.VMEM)


def anywhere():
    return pl.BlockSpec(memory_space=pl.ANY)


def limit(mib):
    return pltpu.CompilerParams(vmem_limit_bytes=mib * MIB)


def shards(peram_blocks, projections, gamma_index, partner, separations):
    src_count, snk_count = lax.axis_size("src"), lax.axis_size("snk")
    mom_count = lax.axis_size("mom")
    slices, offsets = peram_blocks.shape[:2]
    width = peram_blocks.shape[-1]
    nterm, nev = projections.shape[2], projections.shape[-1]
    time_count = slices * src_count
    sep_count = separations.shape[0]
    half_snk = snk_count // 2
    half_rows = width // 2
    src, snk, mom = position()
    forward, keep, _, sep_index, shift, peer_shift = pair_plan(separations, snk, offsets, half_snk)
    own_hops = ((mom + shift) % time_count) // slices
    peer_hops = ((mom + peer_shift) % time_count) // slices
    own_time = src * slices + mom
    pair_time = jnp.where(forward, own_time, own_time + shift) % time_count
    live = jnp.where(forward, 1, int(offsets > 1))

    def swap_mom(array, i):
        return lax.ppermute(array, "mom", [(a, a ^ i) for a in range(mom_count)])

    def swap_snk(array):
        pairs = [(a, (a + half_snk) % snk_count) for a in range(snk_count)]
        return lax.ppermute(array, "snk", pairs)

    def along_src(array, amount):
        step, near = 1, array
        while True:
            if step >= src_count:
                return near, near, jnp.int32(0)
            pairs = [((a + step) % src_count, a) for a in range(src_count)]
            far = lax.ppermute(near, "src", pairs)
            flag = (amount // step) % 2
            step *= 2
            if step >= src_count:
                return near, far, flag
            near = jnp.where(flag != 0, far, near)

    rows = nterm * 2 * nev
    proj_rows = projections.reshape(slices, rows, nev)
    block_half = jax.ShapeDtypeStruct((2, half_rows, width), jnp.bfloat16)
    piece = jax.ShapeDtypeStruct((rows, nev), jnp.bfloat16)
    tagged = jax.ShapeDtypeStruct((rows + TAG_ROWS, nev), jnp.bfloat16)
    others = mom_count - 1
    place_pack = jnp.stack([src, snk, mom, time_count, half_snk]).astype(jnp.int32)
    packed = pl.pallas_call(
        pack_kernel,
        in_specs=[smem()] * 3 + [anywhere()] * 2,
        out_specs=[anywhere()] * (3 + 2 * others),
        out_shape=[block_half, block_half, piece] + [piece] * others + [tagged] * others,
        scratch_shapes=[
            pltpu.VMEM((TAG_ROWS, nev), jnp.bfloat16),
            pltpu.SemaphoreType.DMA((3 + 3 * others,)),
        ],
        compiler_params=limit(4),
        name="pack",
    )(place_pack, separations, partner, peram_blocks, proj_rows)
    first, rest, piece_here = packed[:3]
    other, own = packed[3 : 3 + others], packed[3 + others :]

    first = swap_snk(first)
    rest_near, rest_far, flag = along_src(rest, peer_hops)
    other = [piece_here] + [swap_mom(array, i + 1) for i, array in enumerate(other)]
    own = [swap_mom(array, i + 1) for i, array in enumerate(own)]
    rest = swap_snk(jnp.where(flag != 0, rest_far, rest_near))
    here, away = [], []
    for array in other:
        near, far, _ = along_src(array, own_hops)
        here.append(near)
        away.append(far)
    first_near, first_far, cross = along_src(first, own_hops)

    scal = jnp.stack([mom, cross, forward, pair_time, sep_index, live]).astype(jnp.int32)
    where_own = jnp.stack([mom, keep]).astype(jnp.int32)
    blocks = (mom_count, NSPIN, width, 2 * nev)

    ht = pl.pallas_call(
        own_kernel,
        grid_spec=pltpu.PrefetchScalarGridSpec(
            num_scalar_prefetch=1,
            grid=(1,),
            in_specs=[
                smem(),
                pl.BlockSpec((1, 1, 2, width, width), lambda g, at: (at[0], at[1], 0, 0, 0)),
                pl.BlockSpec((1, rows, nev), lambda g, at: (at[0], 0, 0)),
            ]
            + [vmem()] * others,
            out_specs=vmem(),
            scratch_shapes=[
                pltpu.VMEM((NSPIN, width, 2 * nev), jnp.bfloat16),
                pltpu.VMEM((4 * nterm, 2 * nev, 2 * nev), jnp.bfloat16),
                pltpu.VMEM((mom_count, 2 * nterm, nev, nev), jnp.bfloat16),
            ],
        ),
        out_shape=jax.ShapeDtypeStruct(blocks, jnp.bfloat16),
        compiler_params=limit(20),
        name="own_products",
    )(where_own, gamma_index, peram_blocks, proj_rows, *own)

    k, label = pl.pallas_call(
        other_kernel,
        in_specs=[smem()] * 3 + [vmem()] * (1 + others + 2 * mom_count),
        out_specs=[vmem(), smem()],
        out_shape=[
            jax.ShapeDtypeStruct(blocks, jnp.float32),
            jax.ShapeDtypeStruct((2 * mom_count,), jnp.int32),
        ],
        scratch_shapes=[
            pltpu.VMEM((mom_count, rows, nev), jnp.bfloat16),
            pltpu.VMEM((4 * nterm, 2 * nev, 2 * nev), jnp.bfloat16),
        ],
        compiler_params=limit(24),
        name="other_products",
    )(scal, gamma_index, partner, ht, *own, *here, *away)

    sums = pl.pallas_call(
        early_kernel,
        in_specs=[smem()] + [vmem()] * 3,
        out_specs=vmem(),
        out_shape=jax.ShapeDtypeStruct((2 * mom_count, 16, nev), jnp.float32),
        compiler_params=limit(16),
        name="early_traces",
    )(scal, k, first_near, first_far)
    lines = pl.pallas_call(
        late_kernel,
        in_specs=[smem()] * 2 + [vmem()] * 3,
        out_specs=[vmem()] * mom_count,
        out_shape=[jax.ShapeDtypeStruct((time_count, 128), jnp.float32)] * mom_count,
        compiler_params=limit(16),
        name="late_traces",
    )(scal, label, k, rest, sums)

    total = lines[0]
    for i in range(1, mom_count):
        total = total + swap_mom(lines[i], i)
    step = 1
    while step < src_count:
        pairs = [(a, a ^ step) for a in range(src_count)]
        total = total + lax.ppermute(total, "src", pairs)
        step *= 2
    whole = total
    for step in range(1, snk_count):
        pairs = [(a, (a + step) % snk_count) for a in range(snk_count)]
        whole = whole + lax.ppermute(total, "snk", pairs)
    return whole[:, : 2 * sep_count].reshape(time_count, sep_count, 1, 2)


def solution(mesh):
    placed = (
        P("src", "snk", None, None, None),
        P("src", "mom", None, None, None, None),
        P(),
        P("mom"),
        P(),
    )
    return jax.shard_map(
        shards, mesh=mesh, in_specs=placed, out_specs=P(None, None, "mom", None), check_vma=False
    )
```

time: 386 us -> 104 us (0.27)
  waiting for transfers between devices: 215 us -> 34.7 us
  matrix products: 42.2 us -> 0 us
  local copies, waits for them, and re-layouts: 50.9 us -> 15.1 us
  Pallas kernels: 0 us -> 25.4 us
  other arithmetic: 25.9 us -> 0.97 us
  blocking collectives: 17.2 us -> 0 us
  between operations: 14.3 us -> 2.34 us
  starting transfers between devices: 18.8 us -> 25.3 us
    all_to_all x1 -> x0, waiting for transfers between devices: 179 us -> none  [shards(): lax.all_to_all(shaped, ('src', 'snk'), split_axis=4, concat_axis=0, tiled...]
    dot_general x10 -> x0, matrix products: 42.2 us -> none  [the longest x1 8.61 us: complex_products(): jnp.einsum(form, blocks[:, :, 0], elementals[:, :, 0], preferred_element_...]
    all_gather x1 -> x0, waiting for transfers between devices: 35.6 us -> none  [shards(): arrived = lax.all_gather(projections, 'mom', axis=1, tiled=True)]
    ppermute x0 -> x21, waiting for transfers between devices: none -> 34.7 us  [the longest x6 14.1 us: along_src(): far = lax.ppermute(near, 'src', pairs)]
    another operation x11 -> x2, local copies, waits for them, and re-layouts: 25.6 us -> 0.17 us  [the longest x1 0.09 us: shards(): jnp.stack([mom, cross, forward, pair_time, sep_index, live])]
    pallas_call x0 -> x5, Pallas kernels: none -> 25.4 us  [the longest x1 10.8 us: shards(): pl.pallas_call(other_kernel, in_specs=[smem()] * 3 + [vmem()] * (1 + othe...]
    ppermute x0 -> x21, starting transfers between devices: none -> 25.3 us  [the longest x9 7.61 us: swap_mom(): return lax.ppermute(array, 'mom', [(a, a ^ i) for a in range(mom_count)])]
    all_to_all x1 -> x0, starting transfers between devices: 18.8 us -> none  [shards(): lax.all_to_all(shaped, ('src', 'snk'), split_axis=4, concat_axis=0, tiled...]
  transfers between devices with their start and end apart: 2 -> 21, of which waited for: 2 -> 12; matrix products, arithmetic and copies ran while one was open for 2% -> 2% of each run, Pallas kernels for 0% -> 21%
where the time goes in v2:
time: 104 us
  waiting for transfers between devices  34.7 us (33%)
  Pallas kernels  25.4 us (24%)
  starting transfers between devices  25.3 us (24%)
  local copies, waits for them, and re-layouts  15.1 us (15%)
  between operations  2.34 us (2%)
    ppermute x6, waiting for transfers between devices, along_src(): far = lax.ppermute(near, 'src', pairs)  14.1 us
    unnamed x36, local copies, waits for them, and re-layouts  13.6 us
    pallas_call x1, Pallas kernels, shards(): pl.pallas_call(other_kernel, in_specs=[smem()] * 3 + [vmem()] * (1 + othe...  10.8 us
    pallas_call x1, Pallas kernels, shards(): pl.pallas_call(own_kernel, grid_spec=pltpu.PrefetchScalarGridSpec(num_sca...  10.3 us
    ppermute x9, waiting for transfers between devices, swap_mom(): return lax.ppermute(array, 'mom', [(a, a ^ i) for a in range(mom_count)])  10.2 us
    ppermute x9, starting transfers between devices, swap_mom(): return lax.ppermute(array, 'mom', [(a, a ^ i) for a in range(mom_count)])  7.61 us
    ppermute x6, starting transfers between devices, along_src(): far = lax.ppermute(near, 'src', pairs)  7.09 us
    ppermute x3, starting transfers between devices, shards(): whole = whole + lax.ppermute(total, 'snk', pairs)  5.08 us
  transfers between devices with their start and end apart: 21, of which 12 were waited for; matrix products, arithmetic and copies ran while one was open for 2% of the time, Pallas kernels for 21%

profile of v2, /device:TPU:0, one launch (start us, length us, event | category | flops | bytes accessed | tf_op | source)
XLA Modules:
  0.0 103.9 jit_solution(5453181003225703167)
XLA Ops:
  0.8 3.4 %copy-done = bf16[4,2,2,512,512]{4,3,2,1,0:T(8,128)(2,1)S(1)} copy-done((bf16[4,2,2,512,512]{4,3,2,1,0:T(8,128)(2,1)S(1)}, bf16[4,2,2,512,512]{4,3,2,1,0:T(8,128)(2,1)}, u32[]{:S(2)}) %copy-start) | copy-done | bytes 8388632
  4.2 1.2 %copy-done.2 = bf16[4,1,4,2,128,128]{5,4,3,2,1,0:T(8,128)(2,1)S(1)} copy-done((bf16[4,1,4,2,128,128]{5,4,3,2,1,0:T(8,128)(2,1)S(1)}, bf16[4,1,4,2,128,128]{5,4,3,2,1,0:T(8,128)(2,1)}, u32[]{:S(2)}) %copy-start.2) | copy-done | bytes 1048600
  5.4 0.7 copy-done.13
  6.0 1.7 %pack.1 = (bf16[2,256,512]{2,1,0:T(8,128)(2,1)S(1)}, bf16[2,256,512]{2,1,0:T(8,128)(2,1)S(1)}, bf16[1024,128]{1,0:T(8,128)(2,1)}, bf16[1024,128]{1,0:T(8,128)(2,...) custom-call(s32[5]{0:T(128)S(1)} %stack.50.place, ...), custom_call_target="tpu_custom_call" | custom-call | tf_op jit(solution)/shard_map/pack/pallas_call | solution.py:313
  7.8 0.7 copy-done.15
  8.5 0.7 copy-done.16
  9.2 0.7 copy-done.17
  9.9 4.0 %collective-permute-start.12 = (bf16[2,256,512]{2,1,0:T(8,128)(2,1)S(1)}, bf16[2,256,512]{2,1,0:T(8,128)(2,1)S(1)}, u32[]{:S(2)}, u32[]{:S(2)}) collective-permute-start(bf16[2,256,512]{2,1,0:T(8,128)(2,1)S(1)} %get-tuple-element.30), channel_id=1, source_target_pairs={{0,8},{4,12},{8,0},{12,4},{1,9},{5,13},{9,1},{13,5},{2,10},{6,14},... | collective-permute-start | bytes 1572872 | tf_op jit(solution)/shard_map/ppermute | solution.py:291
  13.9 1.5 %collective-permute-start.10 = (bf16[2,256,512]{2,1,0:T(8,128)(2,1)S(1)}, bf16[2,256,512]{2,1,0:T(8,128)(2,1)}, u32[]{:S(2)}, u32[]{:S(2)}) collective-permute-start(bf16[2,256,512]{2,1,0:T(8,128)(2,1)S(1)} %get-tuple-element.29), channel_id=1, source_target_pairs={{16,0},{0,16},{17,1},{1,17},{18,2},{2,18},{19,3},{3,19},{20,4},{4,... | collective-permute-start | bytes 1572872 | tf_op jit(solution)/shard_map/ppermute | solution.py:299
  15.4 1.5 %collective-permute-start.4 = (bf16[1024,128]{1,0:T(8,128)(2,1)}, bf16[1024,128]{1,0:T(8,128)(2,1)S(1)}, u32[]{:S(2)}, u32[]{:S(2)}) collective-permute-start(bf16[1024,128]{1,0:T(8,128)(2,1)} %get-tuple-element.25), channel_id=1, source_target_pairs={{0,2},{1,3},{2,0},{3,1},{4,6},{5,7},{6,4},{7,5},{8,10},{9,11},{10,... | collective-permute-start | bytes 786440 | tf_op jit(solution)/shard_map/ppermute | solution.py:287
  17.0 0.3 collective-permute-start.5
  17.3 0.7 fusion
  18.7 0.7 copy-done.4
  19.4 0.3 collective-permute-start
  19.7 5.0 %collective-permute-done.4.refs_5_ = bf16[1024,128]{1,0:T(8,128)(2,1)S(1)} collective-permute-done((bf16[1024,128]{1,0:T(8,128)(2,1)}, bf16[1024,128]{1,0:T(8,128)(2,1)S(1)}, u32[]{:S(2)}, u32[]{:S(2)}) %collective-permute-start.4) | collective-permute-done | bytes 262176 | tf_op jit(solution)/shard_map/ppermute | solution.py:287
  24.8 0.7 copy-done.6
  25.5 1.5 %collective-permute-start.1 = (bf16[1040,128]{1,0:T(8,128)(2,1)}, bf16[1040,128]{1,0:T(8,128)(2,1)S(1)}, u32[]{:S(2)}, u32[]{:S(2)}) collective-permute-start(bf16[1040,128]{1,0:T(8,128)(2,1)} %copy-done.16), channel_id=1, source_target_pairs={{0,2},{1,3},{2,0},{3,1},{4,6},{5,7},{6,4},{7,5},{8,10},{9,11},{10,... | collective-permute-start | bytes 798728 | tf_op jit(solution)/shard_map/ppermute | solution.py:287
  27.0 2.6 %collective-permute-done.5.refs_6_ = bf16[1024,128]{1,0:T(8,128)(2,1)S(1)} collective-permute-done((bf16[1024,128]{1,0:T(8,128)(2,1)}, bf16[1024,128]{1,0:T(8,128)(2,1)S(1)}, u32[]{:S(2)}, u32[]{:S(2)}) %collective-permute-start.5) | collective-permute-done | bytes 262176 | tf_op jit(solution)/shard_map/ppermute | solution.py:287
  29.6 0.7 copy-done.8
  30.3 2.0 %collective-permute-start.2 = (bf16[1040,128]{1,0:T(8,128)(2,1)}, bf16[1040,128]{1,0:T(8,128)(2,1)S(1)}, u32[]{:S(2)}, u32[]{:S(2)}) collective-permute-start(bf16[1040,128]{1,0:T(8,128)(2,1)} %copy-done.15), channel_id=1, source_target_pairs={{0,3},{1,2},{2,1},{3,0},{4,7},{5,6},{6,5},{7,4},{8,11},{9,10},{10,... | collective-permute-start | bytes 798728 | tf_op jit(solution)/shard_map/ppermute | solution.py:287
  32.3 4.8 %collective-permute-done.12.near_ref = bf16[2,256,512]{2,1,0:T(8,128)(2,1)S(1)} collective-permute-done((bf16[2,256,512]{2,1,0:T(8,128)(2,1)S(1)}, bf16[2,256,512]{2,1,0:T(8,128)(2,1)S(1)}, u32[]{:S(2)}, u32[]{:S(2)}) %collective-permute-start.12) | collective-permute-done | bytes 524320 | tf_op jit(solution)/shard_map/ppermute | solution.py:291
  37.1 1.5 %collective-permute-start.6 = (bf16[1024,128]{1,0:T(8,128)(2,1)}, bf16[1024,128]{1,0:T(8,128)(2,1)S(1)}, u32[]{:S(2)}, u32[]{:S(2)}) collective-permute-start(bf16[1024,128]{1,0:T(8,128)(2,1)} %get-tuple-element.23.refs_3_), channel_id=1, source_target_pairs={{16,0},{0,16},{17,1},{1,17},{18,2},{2,18},{19,3},{3,19},{20,4},{4,... | collective-permute-start | bytes 786440 | tf_op jit(solution)/shard_map/ppermute | solution.py:299
  38.6 0.5 collective-permute-start.13
  39.1 0.9 broadcast_select_fusion
  40.0 6.5 %collective-permute-done.6.refs_7_ = bf16[1024,128]{1,0:T(8,128)(2,1)S(1)} collective-permute-done((bf16[1024,128]{1,0:T(8,128)(2,1)}, bf16[1024,128]{1,0:T(8,128)(2,1)S(1)}, u32[]{:S(2)}, u32[]{:S(2)}) %collective-permute-start.6) | collective-permute-done | bytes 262176 | tf_op jit(solution)/shard_map/ppermute | solution.py:299
  46.6 0.7 copy-done.10
  47.3 1.5 %collective-permute-start.7 = (bf16[1024,128]{1,0:T(8,128)(2,1)}, bf16[1024,128]{1,0:T(8,128)(2,1)}, u32[]{:S(2)}, u32[]{:S(2)}) collective-permute-start(bf16[1024,128]{1,0:T(8,128)(2,1)} %copy-done.4), channel_id=1, source_target_pairs={{16,0},{0,16},{17,1},{1,17},{18,2},{2,18},{19,3},{3,19},{20,4},{4,... | collective-permute-start | bytes 786440 | tf_op jit(solution)/shard_map/ppermute | solution.py:299
  48.8 0.5 collective-permute-start.8
  49.3 1.5 %collective-permute-start.9 = (bf16[1024,128]{1,0:T(8,128)(2,1)}, bf16[1024,128]{1,0:T(8,128)(2,1)}, u32[]{:S(2)}, u32[]{:S(2)}) collective-permute-start(bf16[1024,128]{1,0:T(8,128)(2,1)} %copy-done.8), channel_id=1, source_target_pairs={{16,0},{0,16},{17,1},{1,17},{18,2},{2,18},{19,3},{3,19},{20,4},{4,... | collective-permute-start | bytes 786440 | tf_op jit(solution)/shard_map/ppermute | solution.py:299
  51.8 3.4 %copy-done.1 = bf16[4,2,2,512,512]{4,3,2,1,0:T(8,128)(2,1)S(1)} copy-done((bf16[4,2,2,512,512]{4,3,2,1,0:T(8,128)(2,1)S(1)}, bf16[4,2,2,512,512]{4,3,2,1,0:T(8,128)(2,1)}, u32[]{:S(2)}) %copy-start.1) | copy-done | bytes 8388632
  55.2 10.3 %own_products.1.ht_ref = bf16[4,4,512,256]{3,2,1,0:T(8,128)(2,1)S(1)} custom-call(s32[2]{0:T(128)S(1)} %pad_add_fusion.place, s32[4,4]{1,0:T(4,128)S(1)} %copy-done.12, bf16[4,2,2,512,512]{4,3,2,1,0:T(8,128)(2,1)S(1)} %copy-done.1, bf16[4,1024,128]{2,1,0:T(8,128)(2,1)S(1)} %bitcast.16, bf16[1040,128]{1,0:T(8,128)(2,1)S(1)} %collective-permute-done.refs_1_.refs_0_, ...), custom_call_target="tpu_custom_call" | custom-call | tf_op jit(solution)/shard_map/own_products/pallas_call | solution.py:344
  65.5 3.7 %collective-permute-done.8.refs_9_ = bf16[1024,128]{1,0:T(8,128)(2,1)} collective-permute-done((bf16[1024,128]{1,0:T(8,128)(2,1)}, bf16[1024,128]{1,0:T(8,128)(2,1)}, u32[]{:S(2)}, u32[]{:S(2)}) %collective-permute-start.8) | collective-permute-done | bytes 262176 | tf_op jit(solution)/shard_map/ppermute | solution.py:299
  69.1 3.9 %collective-permute-done.9.refs_10_ = bf16[1024,128]{1,0:T(8,128)(2,1)} collective-permute-done((bf16[1024,128]{1,0:T(8,128)(2,1)}, bf16[1024,128]{1,0:T(8,128)(2,1)}, u32[]{:S(2)}, u32[]{:S(2)}) %collective-permute-start.9) | collective-permute-done | bytes 262176 | tf_op jit(solution)/shard_map/ppermute | solution.py:299
  73.0 10.8 %other_products.1 = (f32[4,4,512,256]{3,2,1,0:T(8,128)S(1)}, s32[8]{0:T(128)S(1)}) custom-call(s32[6]{0:T(128)S(1)} %stack.45.place, s32[4,4]{1,0:T(4,128)S(1)} %copy-done.12, s32[1]{0:T(128)S(6)} %copy.8.partner, bf16[4,4,512,256]{3,2,1,0:T(8,128)(2,1)S(1)} %own_products.1.ht_ref, bf16[1040,128]{1,0:T(8,128)(2,1)S(1)} %collective-permute-done.refs_1_.refs_0_, ...), custom_call_target="tpu_custom_call" | custom-call | tf_op jit(solution)/shard_map/other_products/pallas_call | solution.py:367
  83.9 1.2 %early_traces.1.sums_ref = f32[8,16,128]{2,1,0:T(8,128)S(1)} custom-call(s32[6]{0:T(128)S(1)} %stack.45.place, f32[4,4,512,256]{3,2,1,0:T(8,128)S(1)} %get-tuple-element.28.k_ref, bf16[2,256,512]{2,1,0:T(8,128)(2,1)S(1)} %collective-permute-done.12.near_ref, bf16[2,256,512]{2,1,0:T(8,128)(2,1)S(1)} %collective-permute-done.13.far_ref), custom_call_target="tpu_custom_call" | custom-call | tf_op jit(solution)/shard_map/early_traces/pallas_call | solution.py:383
  85.1 1.3 %late_traces.1 = (f32[8,128]{1,0:T(8,128)S(1)}, f32[8,128]{1,0:T(8,128)S(1)}, f32[8,128]{1,0:T(8,128)S(1)}, f32[8,128]{1,0:T(8,128)S(1)}) custom-call(s32[6]{0:T(128)S(1)} %stack.45.place, s32[8]{0:T(128)S(1)} %get-tuple-element.27.label, f32[4,4,512,256]{3,2,1,0:T(8,128)S(1)} %get-tuple-element.28.k_ref, ...), custom_call_target="tpu_custom_call" | custom-call | tf_op jit(solution)/shard_map/late_traces/pallas_call | solution.py:391
  86.5 1.3 %collective-permute-start.15 = (f32[8,128]{1,0:T(8,128)S(1)}, f32[8,128]{1,0:T(8,128)S(1)}, u32[]{:S(2)}, u32[]{:S(2)}) collective-permute-start(f32[8,128]{1,0:T(8,128)S(1)} %get-tuple-element.33), channel_id=1, source_target_pairs={{0,2},{1,3},{2,0},{3,1},{4,6},{5,7},{6,4},{7,5},{8,10},{9,11},{10,... | collective-permute-start | bytes 12296 | tf_op jit(solution)/shard_map/ppermute | solution.py:287
  87.8 0.5 collective-permute-start.16
  88.4 1.8 %collective-permute-done.15 = f32[8,128]{1,0:T(8,128)S(1)} collective-permute-done((f32[8,128]{1,0:T(8,128)S(1)}, f32[8,128]{1,0:T(8,128)S(1)}, u32[]{:S(2)}, u32[]{:S(2)}) %collective-permute-start.15) | collective-permute-done | bytes 4128 | tf_op jit(solution)/shard_map/ppermute | solution.py:287
  90.2 0.7 collective-permute-done.16
  90.9 1.5 %collective-permute-start.17 = (f32[8,128]{1,0:T(8,128)S(1)}, f32[8,128]{1,0:T(8,128)S(1)}, u32[]{:S(2)}, u32[]{:S(2)}) collective-permute-start(f32[8,128]{1,0:T(8,128)S(1)} %add_add_fusion.1), channel_id=1, source_target_pairs={{0,16},{16,0},{1,17},{17,1},{2,18},{18,2},{3,19},{19,3},{4,20},{20... | collective-permute-start | bytes 12296 | tf_op jit(solution)/shard_map/ppermute | solution.py:406
  92.4 2.1 %collective-permute-done.17 = f32[8,128]{1,0:T(8,128)S(1)} collective-permute-done((f32[8,128]{1,0:T(8,128)S(1)}, f32[8,128]{1,0:T(8,128)S(1)}, u32[]{:S(2)}, u32[]{:S(2)}) %collective-permute-start.17) | collective-permute-done | bytes 4128 | tf_op jit(solution)/shard_map/ppermute | solution.py:406
  94.5 1.7 %collective-permute-start.18 = (f32[8,128]{1,0:T(8,128)S(1)}, f32[8,128]{1,0:T(8,128)S(1)}, u32[]{:S(2)}, u32[]{:S(2)}) collective-permute-start(f32[8,128]{1,0:T(8,128)S(1)} %add.82), channel_id=1, source_target_pairs={{0,4},{4,8},{8,12},{12,0},{1,5},{5,9},{9,13},{13,1},{2,6},{6,10},{... | collective-permute-start | bytes 12296 | tf_op jit(solution)/shard_map/ppermute | solution.py:411
  96.2 3.4 %collective-permute-start.19 = (f32[8,128]{1,0:T(8,128)S(1)}, f32[8,128]{1,0:T(8,128)S(1)}, u32[]{:S(2)}, u32[]{:S(2)}) collective-permute-start(f32[8,128]{1,0:T(8,128)S(1)} %add.82), channel_id=1, source_target_pairs={{0,8},{4,12},{8,0},{12,4},{1,9},{5,13},{9,1},{13,5},{2,10},{6,14},... | collective-permute-start | bytes 12296 | tf_op jit(solution)/shard_map/ppermute | solution.py:411
  99.6 1.0 collective-permute-done.18
  100.6 0.6 collective-permute-done.19
  101.2 2.0 %collective-permute-done.20 = f32[8,128]{1,0:T(8,128)S(1)} collective-permute-done((f32[8,128]{1,0:T(8,128)S(1)}, f32[8,128]{1,0:T(8,128)S(1)}, u32[]{:S(2)}, u32[]{:S(2)}) %collective-permute-start.20) | collective-permute-done | bytes 4128 | tf_op jit(solution)/shard_map/ppermute | solution.py:411
  103.2 0.7 copy.6
  (44 shorter events, 0.4 us)
Async XLA Ops:
  0.0 17.3 %copy-start.14 = (s32[4]{0:T(128)S(1)}, s32[4]{0:T(128)}, u32[]{:S(2)}) copy-start(s32[4]{0:T(128)} %seps.1) | copy-start | bytes 52
  0.0 51.8 %copy-start.12 = (s32[4,4]{1,0:T(4,128)S(1)}, s32[4,4]{1,0:T(4,128)}, u32[]{:S(2)}) copy-start(s32[4,4]{1,0:T(4,128)} %gamma.3) | copy-start | bytes 196
  0.8 3.4 %copy-start = (bf16[4,2,2,512,512]{4,3,2,1,0:T(8,128)(2,1)S(1)}, bf16[4,2,2,512,512]{4,3,2,1,0:T(8,128)(2,1)}, u32[]{:S(2)}) copy-start(bf16[4,2,2,512,512]{4,3,2,1,0:T(8,128)(2,1)} %x_ref.1) | copy-start | bytes 25165828
  4.2 1.2 %copy-start.2 = (bf16[4,1,4,2,128,128]{5,4,3,2,1,0:T(8,128)(2,1)S(1)}, bf16[4,1,4,2,128,128]{5,4,3,2,1,0:T(8,128)(2,1)}, u32[]{:S(2)}) copy-start(bf16[4,1,4,2,128,128]{5,4,3,2,1,0:T(8,128)(2,1)} %param.6) | copy-start | bytes 3145732
  5.4 0.7 copy-start.13
  6.0 45.8 %copy-start.3 = (bf16[4,1,4,2,128,128]{5,4,3,2,1,0:T(8,128)(2,1)S(1)}, bf16[4,1,4,2,128,128]{5,4,3,2,1,0:T(8,128)(2,1)}, u32[]{:S(2)}) copy-start(bf16[4,1,4,2,128,128]{5,4,3,2,1,0:T(8,128)(2,1)} %param.6) | copy-start | bytes 3145732
  7.8 0.7 copy-start.15
  8.5 0.7 copy-start.16
  9.2 0.7 copy-start.17
  9.9 27.2 %collective-permute-start.12 = (bf16[2,256,512]{2,1,0:T(8,128)(2,1)S(1)}, bf16[2,256,512]{2,1,0:T(8,128)(2,1)S(1)}, u32[]{:S(2)}, u32[]{:S(2)}) collective-permute-start(bf16[2,256,512]{2,1,0:T(8,128)(2,1)S(1)} %get-tuple-element.30), channel_id=1, source_target_pairs={{0,8},{4,12},{8,0},{12,4},{1,9},{5,13},{9,1},{13,5},{2,10},{6,14},... | collective-permute-start | bytes 1572872 | tf_op jit(solution)/shard_map/ppermute | solution.py:291
  13.9 24.7 %collective-permute-start.10 = (bf16[2,256,512]{2,1,0:T(8,128)(2,1)S(1)}, bf16[2,256,512]{2,1,0:T(8,128)(2,1)}, u32[]{:S(2)}, u32[]{:S(2)}) collective-permute-start(bf16[2,256,512]{2,1,0:T(8,128)(2,1)S(1)} %get-tuple-element.29), channel_id=1, source_target_pairs={{16,0},{0,16},{17,1},{1,17},{18,2},{2,18},{19,3},{3,19},{20,4},{4,... | collective-permute-start | bytes 1572872 | tf_op jit(solution)/shard_map/ppermute | solution.py:299
  15.4 3.3 %collective-permute-start.3 = (bf16[1024,128]{1,0:T(8,128)(2,1)}, bf16[1024,128]{1,0:T(8,128)(2,1)S(1)}, u32[]{:S(2)}, u32[]{:S(2)}) collective-permute-start(bf16[1024,128]{1,0:T(8,128)(2,1)} %get-tuple-element.24), channel_id=1, source_target_pairs={{0,1},{1,0},{2,3},{3,2},{4,5},{5,4},{6,7},{7,6},{8,9},{9,8},{10,11... | collective-permute-start | bytes 786440 | tf_op jit(solution)/shard_map/ppermute | solution.py:287
  15.4 9.3 %collective-permute-start.4 = (bf16[1024,128]{1,0:T(8,128)(2,1)}, bf16[1024,128]{1,0:T(8,128)(2,1)S(1)}, u32[]{:S(2)}, u32[]{:S(2)}) collective-permute-start(bf16[1024,128]{1,0:T(8,128)(2,1)} %get-tuple-element.25), channel_id=1, source_target_pairs={{0,2},{1,3},{2,0},{3,1},{4,6},{5,7},{6,4},{7,5},{8,10},{9,11},{10,... | collective-permute-start | bytes 786440 | tf_op jit(solution)/shard_map/ppermute | solution.py:287
  17.0 12.6 %collective-permute-start.5 = (bf16[1024,128]{1,0:T(8,128)(2,1)}, bf16[1024,128]{1,0:T(8,128)(2,1)S(1)}, u32[]{:S(2)}, u32[]{:S(2)}) collective-permute-start(bf16[1024,128]{1,0:T(8,128)(2,1)} %get-tuple-element.26), channel_id=1, source_target_pairs={{0,3},{1,2},{2,1},{3,0},{4,7},{5,6},{6,5},{7,4},{8,11},{9,10},{10,... | collective-permute-start | bytes 786440 | tf_op jit(solution)/shard_map/ppermute | solution.py:287
  18.7 0.7 copy-start.4
  19.4 27.8 %collective-permute-start = (bf16[1040,128]{1,0:T(8,128)(2,1)}, bf16[1040,128]{1,0:T(8,128)(2,1)S(1)}, u32[]{:S(2)}, u32[]{:S(2)}) collective-permute-start(bf16[1040,128]{1,0:T(8,128)(2,1)} %copy-done.17), channel_id=1, source_target_pairs={{0,1},{1,0},{2,3},{3,2},{4,5},{5,4},{6,7},{7,6},{8,9},{9,8},{10,11... | collective-permute-start | bytes 798728 | tf_op jit(solution)/shard_map/ppermute | solution.py:287
  24.8 0.7 copy-start.6
  25.5 23.3 %collective-permute-start.1 = (bf16[1040,128]{1,0:T(8,128)(2,1)}, bf16[1040,128]{1,0:T(8,128)(2,1)S(1)}, u32[]{:S(2)}, u32[]{:S(2)}) collective-permute-start(bf16[1040,128]{1,0:T(8,128)(2,1)} %copy-done.16), channel_id=1, source_target_pairs={{0,2},{1,3},{2,0},{3,1},{4,6},{5,7},{6,4},{7,5},{8,10},{9,11},{10,... | collective-permute-start | bytes 798728 | tf_op jit(solution)/shard_map/ppermute | solution.py:287
  29.6 0.7 copy-start.8
  30.3 19.0 %collective-permute-start.2 = (bf16[1040,128]{1,0:T(8,128)(2,1)}, bf16[1040,128]{1,0:T(8,128)(2,1)S(1)}, u32[]{:S(2)}, u32[]{:S(2)}) collective-permute-start(bf16[1040,128]{1,0:T(8,128)(2,1)} %copy-done.15), channel_id=1, source_target_pairs={{0,3},{1,2},{2,1},{3,0},{4,7},{5,6},{6,5},{7,4},{8,11},{9,10},{10,... | collective-permute-start | bytes 798728 | tf_op jit(solution)/shard_map/ppermute | solution.py:287
  37.1 9.5 %collective-permute-start.6 = (bf16[1024,128]{1,0:T(8,128)(2,1)}, bf16[1024,128]{1,0:T(8,128)(2,1)S(1)}, u32[]{:S(2)}, u32[]{:S(2)}) collective-permute-start(bf16[1024,128]{1,0:T(8,128)(2,1)} %get-tuple-element.23.refs_3_), channel_id=1, source_target_pairs={{16,0},{0,16},{17,1},{1,17},{18,2},{2,18},{19,3},{3,19},{20,4},{4,... | collective-permute-start | bytes 786440 | tf_op jit(solution)/shard_map/ppermute | solution.py:299
  38.6 45.2 %collective-permute-start.13 = (bf16[2,256,512]{2,1,0:T(8,128)(2,1)S(1)}, bf16[2,256,512]{2,1,0:T(8,128)(2,1)S(1)}, u32[]{:S(2)}, u32[]{:S(2)}) collective-permute-start(bf16[2,256,512]{2,1,0:T(8,128)(2,1)S(1)} %collective-permute-done.12.near_ref), channel_id=1, source_target_pairs={{16,0},{0,16},{17,1},{1,17},{18,2},{2,18},{19,3},{3,19},{20,4},{4,... | collective-permute-start | bytes 1572872 | tf_op jit(solution)/shard_map/ppermute | solution.py:299
  46.6 0.7 copy-start.10
  47.3 37.8 %collective-permute-start.11 = (bf16[2,256,512]{2,1,0:T(8,128)(2,1)}, bf16[2,256,512]{2,1,0:T(8,128)(2,1)S(1)}, u32[]{:S(2)}, u32[]{:S(2)}) collective-permute-start(bf16[2,256,512]{2,1,0:T(8,128)(2,1)} %broadcast_select_fusion), channel_id=1, source_target_pairs={{0,8},{4,12},{8,0},{12,4},{1,9},{5,13},{9,1},{13,5},{2,10},{6,14},... | collective-permute-start | bytes 1572872 | tf_op jit(solution)/shard_map/ppermute | solution.py:291
  47.3 18.2 %collective-permute-start.7 = (bf16[1024,128]{1,0:T(8,128)(2,1)}, bf16[1024,128]{1,0:T(8,128)(2,1)}, u32[]{:S(2)}, u32[]{:S(2)}) collective-permute-start(bf16[1024,128]{1,0:T(8,128)(2,1)} %copy-done.4), channel_id=1, source_target_pairs={{16,0},{0,16},{17,1},{1,17},{18,2},{2,18},{19,3},{3,19},{20,4},{4,... | collective-permute-start | bytes 786440 | tf_op jit(solution)/shard_map/ppermute | solution.py:299
  48.8 20.3 %collective-permute-start.8 = (bf16[1024,128]{1,0:T(8,128)(2,1)}, bf16[1024,128]{1,0:T(8,128)(2,1)}, u32[]{:S(2)}, u32[]{:S(2)}) collective-permute-start(bf16[1024,128]{1,0:T(8,128)(2,1)} %copy-done.6), channel_id=1, source_target_pairs={{16,0},{0,16},{17,1},{1,17},{18,2},{2,18},{19,3},{3,19},{20,4},{4,... | collective-permute-start | bytes 786440 | tf_op jit(solution)/shard_map/ppermute | solution.py:299
  49.3 23.7 %collective-permute-start.9 = (bf16[1024,128]{1,0:T(8,128)(2,1)}, bf16[1024,128]{1,0:T(8,128)(2,1)}, u32[]{:S(2)}, u32[]{:S(2)}) collective-permute-start(bf16[1024,128]{1,0:T(8,128)(2,1)} %copy-done.8), channel_id=1, source_target_pairs={{16,0},{0,16},{17,1},{1,17},{18,2},{2,18},{19,3},{3,19},{20,4},{4,... | collective-permute-start | bytes 786440 | tf_op jit(solution)/shard_map/ppermute | solution.py:299
  51.8 3.4 %copy-start.1 = (bf16[4,2,2,512,512]{4,3,2,1,0:T(8,128)(2,1)S(1)}, bf16[4,2,2,512,512]{4,3,2,1,0:T(8,128)(2,1)}, u32[]{:S(2)}) copy-start(bf16[4,2,2,512,512]{4,3,2,1,0:T(8,128)(2,1)} %x_ref.1) | copy-start | bytes 25165828
  55.2 17.8 %copy-start.5 = (bf16[1024,128]{1,0:T(8,128)(2,1)S(1)}, bf16[1024,128]{1,0:T(8,128)(2,1)}, u32[]{:S(2)}) copy-start(bf16[1024,128]{1,0:T(8,128)(2,1)} %copy-done.4) | copy-start | bytes 786436
  55.2 17.8 %copy-start.7 = (bf16[1024,128]{1,0:T(8,128)(2,1)S(1)}, bf16[1024,128]{1,0:T(8,128)(2,1)}, u32[]{:S(2)}) copy-start(bf16[1024,128]{1,0:T(8,128)(2,1)} %copy-done.6) | copy-start | bytes 786436
  55.2 17.8 %copy-start.9 = (bf16[1024,128]{1,0:T(8,128)(2,1)S(1)}, bf16[1024,128]{1,0:T(8,128)(2,1)}, u32[]{:S(2)}) copy-start(bf16[1024,128]{1,0:T(8,128)(2,1)} %copy-done.8) | copy-start | bytes 786436
  55.2 17.8 %copy-start.11 = (bf16[1024,128]{1,0:T(8,128)(2,1)S(1)}, bf16[1024,128]{1,0:T(8,128)(2,1)}, u32[]{:S(2)}) copy-start(bf16[1024,128]{1,0:T(8,128)(2,1)} %copy-done.10) | copy-start | bytes 786436
  86.4 1.9 %collective-permute-start.14 = (f32[8,128]{1,0:T(8,128)S(1)}, f32[8,128]{1,0:T(8,128)S(1)}, u32[]{:S(2)}, u32[]{:S(2)}) collective-permute-start(f32[8,128]{1,0:T(8,128)S(1)} %get-tuple-element.32), channel_id=1, source_target_pairs={{0,1},{1,0},{2,3},{3,2},{4,5},{5,4},{6,7},{7,6},{8,9},{9,8},{10,11... | collective-permute-start | bytes 12296 | tf_op jit(solution)/shard_map/ppermute | solution.py:287
  86.5 3.7 %collective-permute-start.15 = (f32[8,128]{1,0:T(8,128)S(1)}, f32[8,128]{1,0:T(8,128)S(1)}, u32[]{:S(2)}, u32[]{:S(2)}) collective-permute-start(f32[8,128]{1,0:T(8,128)S(1)} %get-tuple-element.33), channel_id=1, source_target_pairs={{0,2},{1,3},{2,0},{3,1},{4,6},{5,7},{6,4},{7,5},{8,10},{9,11},{10,... | collective-permute-start | bytes 12296 | tf_op jit(solution)/shard_map/ppermute | solution.py:287
  87.8 3.0 %collective-permute-start.16 = (f32[8,128]{1,0:T(8,128)S(1)}, f32[8,128]{1,0:T(8,128)S(1)}, u32[]{:S(2)}, u32[]{:S(2)}) collective-permute-start(f32[8,128]{1,0:T(8,128)S(1)} %get-tuple-element.34), channel_id=1, source_target_pairs={{0,3},{1,2},{2,1},{3,0},{4,7},{5,6},{6,5},{7,4},{8,11},{9,10},{10,... | collective-permute-start | bytes 12296 | tf_op jit(solution)/shard_map/ppermute | solution.py:287
  90.9 3.6 %collective-permute-start.17 = (f32[8,128]{1,0:T(8,128)S(1)}, f32[8,128]{1,0:T(8,128)S(1)}, u32[]{:S(2)}, u32[]{:S(2)}) collective-permute-start(f32[8,128]{1,0:T(8,128)S(1)} %add_add_fusion.1), channel_id=1, source_target_pairs={{0,16},{16,0},{1,17},{17,1},{2,18},{18,2},{3,19},{19,3},{4,20},{20... | collective-permute-start | bytes 12296 | tf_op jit(solution)/shard_map/ppermute | solution.py:406
  94.5 6.1 %collective-permute-start.18 = (f32[8,128]{1,0:T(8,128)S(1)}, f32[8,128]{1,0:T(8,128)S(1)}, u32[]{:S(2)}, u32[]{:S(2)}) collective-permute-start(f32[8,128]{1,0:T(8,128)S(1)} %add.82), channel_id=1, source_target_pairs={{0,4},{4,8},{8,12},{12,0},{1,5},{5,9},{9,13},{13,1},{2,6},{6,10},{... | collective-permute-start | bytes 12296 | tf_op jit(solution)/shard_map/ppermute | solution.py:411
  96.2 5.0 %collective-permute-start.19 = (f32[8,128]{1,0:T(8,128)S(1)}, f32[8,128]{1,0:T(8,128)S(1)}, u32[]{:S(2)}, u32[]{:S(2)}) collective-permute-start(f32[8,128]{1,0:T(8,128)S(1)} %add.82), channel_id=1, source_target_pairs={{0,8},{4,12},{8,0},{12,4},{1,9},{5,13},{9,1},{13,5},{2,10},{6,14},... | collective-permute-start | bytes 12296 | tf_op jit(solution)/shard_map/ppermute | solution.py:411
  99.6 3.6 %collective-permute-start.20 = (f32[8,128]{1,0:T(8,128)S(1)}, f32[8,128]{1,0:T(8,128)S(1)}, u32[]{:S(2)}, u32[]{:S(2)}) collective-permute-start(f32[8,128]{1,0:T(8,128)S(1)} %add.82), channel_id=1, source_target_pairs={{0,12},{4,0},{8,4},{12,8},{1,13},{5,1},{9,5},{13,9},{2,14},{6,2},{... | collective-permute-start | bytes 12296 | tf_op jit(solution)/shard_map/ppermute | solution.py:411

commit v3 on v2

v3 whole, which is shorter than its diff:
```python
import functools

import jax
import jax.numpy as jnp
from jax import lax
from jax.experimental import pallas as pl
from jax.experimental.pallas import tpu as pltpu
from jax.sharding import PartitionSpec as P

NSPIN = 4
NT_DIMS = (((1,), (1,)), ((), ()))
MIB = 1024 * 1024
WEIGHT = 10**13
TAG_ROWS = 16
GAMMAS = (
    (3, 1 | 1 << 2 | 3 << 4 | 3 << 6),
    (3, 2 | 0 << 2 | 0 << 4 | 2 << 6),
    (2, 1 | 3 << 2 | 3 << 4 | 1 << 6),
    (2, 0),
)


def spin_entry(code, row):
    phase = row * 0
    for bit, (flip, phases) in enumerate(GAMMAS):
        on = (code >> bit) & 1
        phase = phase + on * ((phases >> (2 * row)) & 3)
        row = row ^ (on * flip)
    return row, phase & 3


def spin_column_entry(code, column):
    row = column
    for bit, (flip, _) in enumerate(GAMMAS):
        row = row ^ (((code >> bit) & 1) * flip)
    return row, spin_entry(code, row)[1]


def phase_blocks(block_ref, r, real, imag):
    nev = real.shape[0]
    for phase, (a, b) in enumerate(((real, imag), (-imag, real), (-real, -imag), (imag, -real))):
        slot = 4 * r + phase
        block_ref[slot, :nev, :nev] = a
        block_ref[slot, :nev, nev:] = -b
        block_ref[slot, nev:, :nev] = b
        block_ref[slot, nev:, nev:] = a


class Plan:
    def __init__(self, place, seps, sizes):
        slices, offsets, src_count, snk_count = sizes
        src, snk, self.mom = place[0], place[1], place[2]
        half_snk = snk_count // 2
        self.slices, self.time_count = slices, slices * src_count
        self.forward = snk < half_snk
        base = lax.rem(snk, half_snk) * offsets
        self.keep = jnp.where(self.forward, 0, offsets - 1)
        self.give = offsets - 1 - self.keep
        self.sep_index = base + self.keep
        sign = jnp.where(self.forward, 1, -1)
        self.shift = sign * seps[base + self.keep]
        self.peer_shift = -sign * seps[base + self.give]
        self.own_time = src * slices + self.mom
        late = jnp.where(self.forward, 0, self.shift)
        self.pair_time = lax.rem(self.own_time + late + self.time_count, self.time_count)
        self.live = self.forward if offsets == 1 else None

    def _sum(self, place, amount):
        return lax.rem(place + amount + self.time_count, self.time_count)

    def local(self, i):
        return lax.rem(self._sum(self.mom ^ i, self.shift), self.slices)

    def hops(self, i):
        return lax.div(self._sum(self.mom ^ i, self.shift), self.slices)

    def peer_local(self):
        return lax.rem(self._sum(self.mom, self.peer_shift), self.slices)

    def peer_hops(self):
        return lax.div(self._sum(self.mom, self.peer_shift), self.slices)


def run_copies(copies, sems):
    handles = [
        pltpu.make_async_copy(source, target, sems.at[n])
        for n, (source, target) in enumerate(copies)
    ]
    for handle in handles:
        handle.start()
    for handle in handles:
        handle.wait()


def span(index, rows):
    return pl.ds(index * rows, rows)


def first_pack(sizes, place, seps, partner, peram, proj, first, rest, near, tag, sems):
    plan = Plan(place, seps, sizes)
    half, rows = first.shape[1], proj.shape[1]
    tag[...] = jnp.full(tag.shape, partner[0].astype(jnp.float32)).astype(jnp.bfloat16)
    peer, give, mom = plan.peer_local(), plan.give, plan.mom
    run_copies(
        [
            (peram.at[peer, give, :, pl.ds(0, half)], first),
            (peram.at[peer, give, :, pl.ds(half, half)], rest),
            (proj.at[plan.local(2)], near.at[span(0, rows)]),
            (proj.at[plan.local(3)], near.at[span(1, rows)]),
            (proj.at[mom ^ 2], near.at[span(2, rows)]),
            (proj.at[mom ^ 3], near.at[span(3, rows)]),
            (tag, near.at[pl.ds(4 * rows, TAG_ROWS)]),
        ],
        sems,
    )


def second_pack(sizes, place, seps, peram, proj, rest_near, rest_far, *refs):
    rest, far_same, far_cross, x_ref, sems = refs
    plan = Plan(place, seps, sizes)
    rows = proj.shape[1]
    flag = lax.rem(plan.peer_hops(), 2)

    @pl.when(flag == 0)
    def _():
        run_copies([(rest_near, rest)], sems)

    @pl.when(flag != 0)
    def _():
        run_copies([(rest_far, rest)], sems)

    run_copies(
        [
            (proj.at[plan.local(0)], far_same.at[span(0, rows)]),
            (proj.at[plan.local(1)], far_same.at[span(1, rows)]),
            (proj.at[plan.local(2)], far_cross.at[span(0, rows)]),
            (proj.at[plan.local(3)], far_cross.at[span(1, rows)]),
            (peram.at[plan.mom, plan.keep], x_ref),
        ],
        sems,
    )


def own_pack(place, partner, proj, near, out, tag, sems):
    rows = proj.shape[1]
    mom = place[2]
    tag[...] = jnp.full(tag.shape, partner[0].astype(jnp.float32)).astype(jnp.bfloat16)
    run_copies(
        [
            (proj.at[mom ^ 1], out.at[span(0, rows)]),
            (near.at[span(3, rows)], out.at[span(1, rows)]),
            (tag, out.at[pl.ds(2 * rows, TAG_ROWS)]),
            (near.at[pl.ds(4 * rows, TAG_ROWS)], out.at[pl.ds(2 * rows + TAG_ROWS, TAG_ROWS)]),
        ],
        sems,
    )


def other_pack(sizes, place, seps, proj, near, far_same, far_cross, after, out, sems):
    plan = Plan(place, seps, sizes)
    rows = proj.shape[1]
    flag = lax.rem(plan.hops(1), 2) if sizes[2] == 2 else jnp.int32(0)
    low, high = out.at[span(0, rows)], out.at[span(1, rows)]

    @pl.when(flag == 0)
    def _():
        run_copies([(proj.at[plan.local(1)], low), (near.at[span(1, rows)], high)], sems)

    @pl.when(flag != 0)
    def _():
        run_copies([(far_same.at[span(1, rows)], low), (far_cross.at[span(1, rows)], high)], sems)


def own_products(mom, gamma, pieces, p_ref, xb_ref, ht_ref, block_ref, tr_ref):
    nev = tr_ref.shape[-1]
    nterm = tr_ref.shape[0] // 2
    first, step = pieces[0], pieces[1] - pieces[0]

    def product(n, carry):
        for m in range(2 * nterm):
            tr_ref[m] = p_ref[n, m * nev : (m + 1) * nev].T
        for r in range(nterm):
            phase_blocks(block_ref, r, tr_ref[2 * r], tr_ref[2 * r + 1])

        def spin_rows(spin, inner):
            total = None
            for r in range(nterm):
                source, phase = spin_column_entry(gamma[mom ^ (first + n * step), r], spin)
                term = lax.dot_general(
                    block_ref[4 * r + phase],
                    xb_ref[source],
                    NT_DIMS,
                    preferred_element_type=jnp.float32,
                )
                total = term if total is None else total + term
            total = total.astype(jnp.bfloat16)
            rows = pl.ds(pl.multiple_of(spin * nev, nev), nev)
            for column in range(NSPIN):
                lanes = slice(column * nev, (column + 1) * nev)
                ht_ref[n, column, rows, :nev] = total[:nev, lanes]
                ht_ref[n, column, rows, nev:] = total[nev:, lanes]
            return inner

        return lax.fori_loop(0, NSPIN, spin_rows, carry)

    lax.fori_loop(0, len(pieces), product, 0)


def own_kernel_a(place, gamma, block, proj, near, *refs):
    ht_ref, xb_ref, x_ref, p_ref, block_ref, tr_ref, sems = refs[-7:]
    mom = place[2]
    nev = tr_ref.shape[-1]
    rows = proj.shape[1]
    run_copies(
        [
            (block, x_ref),
            (proj.at[mom], p_ref.at[0]),
            (near.at[span(2, rows)], p_ref.at[1]),
        ],
        sems,
    )
    for spin in range(NSPIN):
        lanes = slice(spin * nev, (spin + 1) * nev)
        xb_ref[spin, :, :nev] = x_ref[0, :, lanes]
        xb_ref[spin, :, nev:] = x_ref[1, :, lanes]
    own_products(mom, gamma, (0, 2), p_ref, xb_ref, ht_ref, block_ref, tr_ref)


def own_kernel_b(place, gamma, xb_ref, traded, ht_ref, p_ref, block_ref, tr_ref, sems):
    rows = p_ref.shape[1]
    run_copies([(traded.at[span(n, rows)], p_ref.at[n]) for n in range(2)], sems)
    own_products(place[2], gamma, (1, 3), p_ref, xb_ref, ht_ref, block_ref, tr_ref)


def other_products(mom, forward, gamma, partner, near_tag, own_tag, pieces, hts, p_ref, refs):
    k_ref, label_ref, ht_ref, block_ref = refs
    nev = block_ref.shape[-1] // 2
    nterm = block_ref.shape[0] // 4

    def number(tag):
        return jnp.max(tag.astype(jnp.float32)).astype(jnp.int32)

    partners = [
        partner[0],
        number(own_tag[:TAG_ROWS]),
        number(near_tag[...]),
        number(own_tag[TAG_ROWS:]),
    ]
    lefts = []
    for n, p in enumerate(pieces):
        back = jnp.int32(0)
        for i, value in enumerate(partners):
            back = back + jnp.where(value == (mom ^ p), mom ^ i, 0)
        label_ref[n] = jnp.where(forward, back, mom ^ p)
        lefts.append(jnp.where(forward, back, partners[p]) ^ mom)
    first, step = pieces[0], pieces[1] - pieces[0]

    def product(n, carry):
        for r in range(nterm):
            real = p_ref[n, 2 * r * nev : (2 * r + 1) * nev]
            imag = p_ref[n, (2 * r + 1) * nev : (2 * r + 2) * nev]
            phase_blocks(block_ref, r, real, imag)
        left = jnp.where(n == 0, lefts[0], lefts[1])
        for odd in range(2):

            @pl.when((left & 1) == odd)
            def _():
                ht_ref[...] = hts[odd][left >> 1]

        def spin_columns(spin, inner):
            total = None
            for r in range(nterm):
                source, phase = spin_entry(gamma[mom ^ (first + n * step), r], spin)
                term = lax.dot_general(
                    ht_ref[source],
                    block_ref[4 * r + phase],
                    NT_DIMS,
                    preferred_element_type=jnp.float32,
                )
                total = term if total is None else total + term
            k_ref[n, spin] = total
            return inner

        return lax.fori_loop(0, NSPIN, spin_columns, carry)

    lax.fori_loop(0, len(pieces), product, 0)


def read_tags(near, own, near_tag, own_tag, rows, sems):
    run_copies(
        [
            (near.at[pl.ds(4 * rows, TAG_ROWS)], near_tag),
            (own.at[pl.ds(2 * rows, 2 * TAG_ROWS)], own_tag),
        ],
        sems,
    )


def other_kernel_a(sizes, place, seps, gamma, partner, hta, htb, proj, near, own, *refs):
    far_same, far_cross = refs[:2]
    k_ref, label_ref, ht_ref, block_ref, p_ref, near_tag, own_tag, sems = refs[-8:]
    plan = Plan(place, seps, sizes)
    rows = proj.shape[1]
    read_tags(near, own, near_tag, own_tag, rows, sems)
    flag = lax.rem(plan.hops(0), 2) if sizes[2] == 2 else jnp.int32(1)

    @pl.when(flag == 0)
    def _():
        run_copies(
            [(proj.at[plan.local(0)], p_ref.at[0]), (near.at[span(0, rows)], p_ref.at[1])], sems
        )

    @pl.when(flag != 0)
    def _():
        run_copies(
            [(far_same.at[span(0, rows)], p_ref.at[0]), (far_cross.at[span(0, rows)], p_ref.at[1])],
            sems,
        )

    out = (k_ref, label_ref, ht_ref, block_ref)
    other_products(
        plan.mom, plan.forward, gamma, partner, near_tag, own_tag, (0, 2), (hta, htb), p_ref, out
    )


def other_kernel_b(sizes, place, seps, gamma, partner, hta, htb, near, own, traded, *refs):
    k_ref, label_ref, ht_ref, block_ref, p_ref, near_tag, own_tag, sems = refs
    plan = Plan(place, seps, sizes)
    rows = p_ref.shape[1]
    read_tags(near, own, near_tag, own_tag, rows, sems)
    run_copies([(traded.at[span(n, rows)], p_ref.at[n]) for n in range(2)], sems)
    out = (k_ref, label_ref, ht_ref, block_ref)
    other_products(
        plan.mom, plan.forward, gamma, partner, near_tag, own_tag, (1, 3), (hta, htb), p_ref, out
    )


def row_sums(k_refs, source, offset, totals):
    rows = 16
    each = k_refs[0].shape[0]
    nev = source.shape[-1] // NSPIN

    def step(index, totals):
        row = pl.multiple_of(index * rows, rows)
        here = pl.ds(pl.multiple_of(offset + row, rows), rows)
        totals = list(totals)
        for spin in range(NSPIN):
            lanes = slice(spin * nev, (spin + 1) * nev)
            real = source[0, pl.ds(row, rows), lanes].astype(jnp.float32)
            imag = source[1, pl.ds(row, rows), lanes].astype(jnp.float32)
            for n in range(len(totals) // 2):
                k_ref, p = k_refs[n // each], n % each
                kr, ki = k_ref[p, spin, here, :nev], k_ref[p, spin, here, nev:]
                totals[2 * n] += real * kr - imag * ki
                totals[2 * n + 1] += real * ki + imag * kr
        return tuple(totals)

    return lax.fori_loop(0, source.shape[1] // rows, step, totals)


def early_kernel(sizes, place, seps, ka, kb, near, far, sums_ref, part_ref, sems):
    plan = Plan(place, seps, sizes)
    count = sums_ref.shape[0]
    flag = lax.rem(lax.div(plan.hops(0), max(sizes[2] // 2, 1)), 2)

    @pl.when(flag == 0)
    def _():
        run_copies([(near, part_ref)], sems)

    @pl.when(flag != 0)
    def _():
        run_copies([(far, part_ref)], sems)

    zero = tuple(jnp.zeros(sums_ref.shape[1:], jnp.float32) for _ in range(count))
    for n, total in enumerate(row_sums((ka, kb), part_ref, 0, zero)):
        sums_ref[n] = total


def late_kernel(sizes, sep_count, place, seps, label_a, label_b, ka, kb, rest_ref, sums_ref, out_ref):
    plan = Plan(place, seps, sizes)
    count = sums_ref.shape[0] // 2
    width = rest_ref.shape[-1]
    half = ka.shape[2] - rest_ref.shape[1]
    totals = row_sums((ka, kb), rest_ref, half, tuple(sums_ref[n] for n in range(2 * count)))
    sums = [jnp.sum(total, axis=0, keepdims=True) for total in totals]
    sums = [jnp.sum(total, axis=1, keepdims=True) * (1.0 / width) for total in sums]
    shape = out_ref.shape[1:]
    spot = lax.broadcasted_iota(jnp.int32, shape, 0) * shape[1]
    spot = spot + lax.broadcasted_iota(jnp.int32, shape, 1)
    here = spot // 2 == plan.pair_time * sep_count + plan.sep_index
    if plan.live is not None:
        here = here & plan.live
    values = [jnp.where(spot % 2 == 0, sums[2 * p], sums[2 * p + 1]) for p in range(count)]
    labels = [label_a[0], label_a[1], label_b[0], label_b[1]]
    lines = []
    for op in range(count):
        line = jnp.zeros(shape, jnp.float32)
        for p in range(count):
            line = jnp.where(labels[p] == op, values[p], line)
        lines.append(jnp.where(here, line, 0.0))
    for n in range(out_ref.shape[0]):
        out_ref[n] = lines[n % count]


def smem():
    return pl.BlockSpec(memory_space=pltpu.SMEM)


def vmem():
    return pl.BlockSpec(memory_space=pltpu.VMEM)


def hbm():
    return pl.BlockSpec(memory_space=pltpu.HBM)


def limit(mib):
    return pltpu.CompilerParams(vmem_limit_bytes=mib * MIB)


def shards(peram_blocks, projections, gamma_index, partner, separations):
    src_count, snk_count = lax.axis_size("src"), lax.axis_size("snk")
    mom_count = lax.axis_size("mom")
    slices, offsets = peram_blocks.shape[:2]
    width = peram_blocks.shape[-1]
    nterm, nev = projections.shape[2], projections.shape[-1]
    time_count = slices * src_count
    sep_count = separations.shape[0]
    half_snk = snk_count // 2
    half_rows = width // 2
    rows = nterm * 2 * nev
    sizes = (slices, offsets, src_count, snk_count)
    place = jnp.stack([lax.axis_index(name) for name in ("src", "snk", "mom")]).astype(jnp.int32)
    proj = projections.reshape(slices, rows, nev)

    def swap_mom(array, i):
        return lax.ppermute(array, "mom", [(a, a ^ i) for a in range(mom_count)])

    def swap_snk(array):
        pairs = [(a, (a + half_snk) % snk_count) for a in range(snk_count)]
        return lax.ppermute(array, "snk", pairs)

    def next_src(array, step=1, i=0):
        pairs = [
            (((a + step) % src_count) * mom_count + (b ^ i), a * mom_count + b)
            for a in range(src_count)
            for b in range(mom_count)
        ]
        return lax.ppermute(array, ("src", "mom"), pairs)

    def most_of(array, amount):
        step = 1
        while 2 * step < src_count:
            array = jnp.where((amount // step) % 2 != 0, next_src(array, step), array)
            step *= 2
        return array, next_src(array, step)

    def call(kernel, name, in_specs, out_specs, out_shape, scratch, mib):
        cost = pl.CostEstimate(flops=WEIGHT, bytes_accessed=WEIGHT // 1000, transcendentals=0)
        return pl.pallas_call(
            kernel,
            in_specs=in_specs,
            out_specs=out_specs,
            out_shape=out_shape,
            scratch_shapes=scratch,
            compiler_params=limit(mib),
            cost_estimate=cost,
            name=name,
        )

    def bf16(*shape):
        return jax.ShapeDtypeStruct(shape, jnp.bfloat16)

    def dma(count):
        return pltpu.SemaphoreType.DMA((count,))

    part = functools.partial
    tag = pltpu.VMEM((TAG_ROWS, nev), jnp.bfloat16)
    half_block = bf16(2, half_rows, width)
    two = bf16(2 * rows, nev)

    first, rest, near = call(
        part(first_pack, sizes),
        "first_pack",
        [smem()] * 3 + [hbm()] * 2,
        [hbm()] * 3,
        [half_block, half_block, bf16(4 * rows + TAG_ROWS, nev)],
        [tag, dma(7)],
        58,
    )(place, separations, partner, peram_blocks, proj)

    plan = Plan(place, separations, sizes)
    first = swap_snk(first)
    rest_near, rest_far = most_of(rest, plan.peer_hops())
    near = swap_mom(near, 2)
    if src_count > 2:
        rest_near = jnp.where(plan.peer_hops() // (src_count // 2) != 0, rest_far, rest_near)
        rest_far = rest_near
    rest, far_same, far_cross, x = call(
        part(second_pack, sizes),
        "second_pack",
        [smem()] * 2 + [hbm()] * 4,
        [hbm()] * 4,
        [half_block, two, two, bf16(2, width, width)],
        [dma(5)],
        58,
    )(place, separations, peram_blocks, proj, rest_near, rest_far)
    rest = swap_snk(rest)
    if src_count == 2:
        far_same, far_cross = next_src(far_same), next_src(far_cross, 1, 2)

    own_trade = call(
        own_pack,
        "own_pack",
        [smem()] * 2 + [hbm()] * 2,
        hbm(),
        bf16(2 * (rows + TAG_ROWS), nev),
        [tag, dma(4)],
        16,
    )(place, partner, proj, near)
    own_got = swap_mom(own_trade, 1)
    first_near, first_far = most_of(first, plan.hops(0))

    blocks = (mom_count // 2, NSPIN, width, 2 * nev)
    weights = pltpu.VMEM((4 * nterm, 2 * nev, 2 * nev), jnp.bfloat16)
    pieces = pltpu.VMEM((2, rows, nev), jnp.bfloat16)
    turned = pltpu.VMEM((2 * nterm, nev, nev), jnp.bfloat16)
    hta, xb = call(
        own_kernel_a,
        "own_products_a",
        [smem()] * 2 + [hbm()] * 5,
        [vmem()] * 2,
        [bf16(*blocks), bf16(NSPIN, width, 2 * nev)],
        [pltpu.VMEM((2, width, width), jnp.bfloat16), pieces, weights, turned, dma(3)],
        16,
    )(place, gamma_index, x, proj, near, own_trade, first)
    htb = call(
        own_kernel_b,
        "own_products_b",
        [smem()] * 2 + [vmem(), hbm()],
        vmem(),
        bf16(*blocks),
        [pieces, weights, turned, dma(2)],
        16,
    )(place, gamma_index, xb, own_got)

    other_trade = call(
        part(other_pack, sizes),
        "other_pack",
        [smem()] * 2 + [hbm()] * 5,
        hbm(),
        two,
        [dma(2)],
        16,
    )(place, separations, proj, near, far_same, far_cross, htb)
    other_got = swap_mom(other_trade, 1)
    if src_count != 2:

        def moved(array):
            if src_count == 1:
                return array
            array, far = most_of(array, plan.hops(0))
            return jnp.where(plan.hops(0) // (src_count // 2) != 0, far, array)

        far_same = moved(lax.dynamic_index_in_dim(proj, plan.local(0), 0, keepdims=False))
        far_cross, other_got = moved(near[:rows]), moved(other_got)

    chosen = pltpu.VMEM((NSPIN, width, 2 * nev), jnp.bfloat16)
    own_tag = pltpu.VMEM((2 * TAG_ROWS, nev), jnp.bfloat16)
    k_out = [
        jax.ShapeDtypeStruct(blocks, jnp.float32),
        jax.ShapeDtypeStruct((mom_count // 2,), jnp.int32),
    ]
    scratch = [chosen, weights, pieces, tag, own_tag, dma(2)]
    ka, label_a = call(
        part(other_kernel_a, sizes),
        "other_products_a",
        [smem()] * 4 + [vmem()] * 2 + [hbm()] * 6,
        [vmem(), smem()],
        k_out,
        scratch,
        24,
    )(
        place, separations, gamma_index, partner, hta, htb,
        proj, near, own_got, far_same, far_cross, other_trade,
    )
    kb, label_b = call(
        part(other_kernel_b, sizes),
        "other_products_b",
        [smem()] * 4 + [vmem()] * 2 + [hbm()] * 3,
        [vmem(), smem()],
        k_out,
        scratch,
        24,
    )(place, separations, gamma_index, partner, hta, htb, near, own_got, other_got)

    sums = call(
        part(early_kernel, sizes),
        "early_traces",
        [smem()] * 2 + [vmem()] * 2 + [hbm()] * 2,
        vmem(),
        jax.ShapeDtypeStruct((2 * mom_count, 16, nev), jnp.float32),
        [pltpu.VMEM((2, half_rows, width), jnp.bfloat16), dma(1)],
        20,
    )(place, separations, ka, kb, first_near, first_far)
    device_count = src_count * snk_count * mom_count
    values = time_count * sep_count * 2
    lines = (values + 127) // 128
    out = call(
        part(late_kernel, sizes, sep_count),
        "late_traces",
        [smem()] * 4 + [vmem()] * 4,
        vmem(),
        jax.ShapeDtypeStruct((device_count, lines, 128), jnp.float32),
        [],
        20,
    )(place, separations, label_a, label_b, ka, kb, rest, sums)
    out = lax.all_to_all(out, ("src", "snk", "mom"), split_axis=0, concat_axis=0, tiled=True)
    out = jnp.sum(out, axis=0).reshape(lines * 128)[:values]
    return out.reshape(time_count, sep_count, 1, 2)


def solution(mesh):
    placed = (
        P("src", "snk", None, None, None),
        P("src", "mom", None, None, None, None),
        P(),
        P("mom"),
        P(),
    )
    return jax.shard_map(
        shards, mesh=mesh, in_specs=placed, out_specs=P(None, None, "mom", None), check_vma=False
    )
```

time: 104 us -> 243 us (2.34)
  Pallas kernels: 25.4 us -> 199 us
  waiting for transfers between devices: 34.7 us -> 8.04 us
  blocking collectives: 0 us -> 16.9 us
  local copies, waits for them, and re-layouts: 15.1 us -> 1.66 us
  starting transfers between devices: 25.3 us -> 15.1 us
    pallas_call x5 -> x10, Pallas kernels: 25.4 us -> 199 us  [the longest x1 82.5 us: shards(): call(part(second_pack, sizes), 'second_pack', [smem()] * 2 + [hbm()] * 4,...]
    all_to_all x0 -> x1, blocking collectives: none -> 16.9 us  [shards(): lax.all_to_all(out, ('src', 'snk', 'mom'), split_axis=0, concat_axis=0, t...]
    unnamed x36 -> x14, local copies, waits for them, and re-layouts: 13.6 us -> 0.82 us
    ppermute x10 -> x4, waiting for transfers between devices: 19.8 us -> 8.03 us  [next_src(): return lax.ppermute(array, ('src', 'mom'), pairs)]
    ppermute x9 -> x3, waiting for transfers between devices: 10.2 us -> 0.01 us  [swap_mom(): return lax.ppermute(array, 'mom', [(a, a ^ i) for a in range(mom_count)])]
    ppermute x10 -> x4, starting transfers between devices: 13.7 us -> 7.79 us  [next_src(): return lax.ppermute(array, ('src', 'mom'), pairs)]
    ppermute x9 -> x3, starting transfers between devices: 7.61 us -> 2.14 us  [swap_mom(): return lax.ppermute(array, 'mom', [(a, a ^ i) for a in range(mom_count)])]
    ppermute x2, waiting for transfers between devices: 4.79 us -> 0.01 us  [swap_snk(): return lax.ppermute(array, 'snk', pairs)]
  transfers between devices with their start and end apart: 21 -> 9, of which waited for: 12 -> 1; matrix products, arithmetic and copies ran while one was open for 2% -> 0% of each run, Pallas kernels for 21% -> 54%
where the time goes in v3:
time: 243 us; the launch traced here: 242 us
  Pallas kernels  199 us (82%)
  blocking collectives  16.9 us (7%)
  starting transfers between devices  15.1 us (6%)
  waiting for transfers between devices  8.04 us (3%)
    pallas_call x1, Pallas kernels, shards(): call(part(second_pack, sizes), 'second_pack', [smem()] * 2 + [hbm()] * 4,...  82.5 us
    pallas_call x1, Pallas kernels, shards(): call(part(first_pack, sizes), 'first_pack', [smem()] * 3 + [hbm()] * 2, [...  65.4 us
    all_to_all x1, blocking collectives, shards(): lax.all_to_all(out, ('src', 'snk', 'mom'), split_axis=0, concat_axis=0, t...  16.9 us
    pallas_call x1, Pallas kernels, shards(): call(own_pack, 'own_pack', [smem()] * 2 + [hbm()] * 2, hbm(), bf16(2 * (r...  9.75 us
    pallas_call x1, Pallas kernels, shards(): call(part(other_pack, sizes), 'other_pack', [smem()] * 2 + [hbm()] * 5, h...  9.62 us
    ppermute x4, waiting for transfers between devices, next_src(): return lax.ppermute(array, ('src', 'mom'), pairs)  8.03 us
    ppermute x4, starting transfers between devices, next_src(): return lax.ppermute(array, ('src', 'mom'), pairs)  7.79 us
    pallas_call x1, Pallas kernels, shards(): call(part(other_kernel_b, sizes), 'other_products_b', [smem()] * 4 + [vme...  7.65 us
  transfers between devices with their start and end apart: 9, of which 1 were waited for; matrix products, arithmetic and copies ran while one was open for 0% of the time, Pallas kernels for 54%

profile of v3, /device:TPU:0, one launch (start us, length us, event | category | flops | bytes accessed | tf_op | source)
XLA Modules:
  0.0 242.5 jit_solution(1147802511966214786)
XLA Ops:
  0.7 0.6 pad_add_fusion.place
  1.3 65.4 %first_pack.1 = (bf16[2,256,512]{2,1,0:T(8,128)(2,1)}, bf16[2,256,512]{2,1,0:T(8,128)(2,1)}, bf16[4112,128]{1,0:T(8,128)(2,1)}) custom-call(s32[3]{0:T(128)} %pad_add_fusion.place, s32[4]{0:T(128)} %seps.13, s32[1]{0:T(128)S(6)} %copy.8.partner, bf16[4,2,2,512,512]{4,3,2,1,0:T(8,128)(2,1)} %peram.3, bf16[4,1024,128]{2,1,0:T(8,128)(2,1)} %bitcast.5), custom_call_target="tpu_custom_call" | custom-call | flops 9999999827968 | bytes 10000000000 | tf_op jit(solution)/shard_map/first_pack/pallas_call | solution.py:482
  66.7 3.0 %collective-permute-start = (bf16[2,256,512]{2,1,0:T(8,128)(2,1)}, bf16[2,256,512]{2,1,0:T(8,128)(2,1)S(1)}, u32[]{:S(2)}, u32[]{:S(2)}) collective-permute-start(bf16[2,256,512]{2,1,0:T(8,128)(2,1)} %get-tuple-element.18.rest_near), channel_id=1, source_target_pairs={{16,0},{17,1},{18,2},{19,3},{0,16},{1,17},{2,18},{3,19},{20,4},{21... | collective-permute-start | bytes 1572872 | tf_op jit(solution)/shard_map/ppermute | solution.py:449
  69.7 1.5 collective-permute-start.1
  71.2 2.6 %collective-permute-start.2 = (bf16[2,256,512]{2,1,0:T(8,128)(2,1)}, bf16[2,256,512]{2,1,0:T(8,128)(2,1)}, u32[]{:S(2)}, u32[]{:S(2)}) collective-permute-start(bf16[2,256,512]{2,1,0:T(8,128)(2,1)} %get-tuple-element.21), channel_id=1, source_target_pairs={{0,8},{4,12},{8,0},{12,4},{1,9},{5,13},{9,1},{13,5},{2,10},{6,14},... | collective-permute-start | bytes 1572872 | tf_op jit(solution)/shard_map/ppermute | solution.py:441
  73.8 8.0 %collective-permute-done.rest_far = bf16[2,256,512]{2,1,0:T(8,128)(2,1)S(1)} collective-permute-done((bf16[2,256,512]{2,1,0:T(8,128)(2,1)}, bf16[2,256,512]{2,1,0:T(8,128)(2,1)S(1)}, u32[]{:S(2)}, u32[]{:S(2)}) %collective-permute-start) | collective-permute-done | bytes 524320 | tf_op jit(solution)/shard_map/ppermute | solution.py:449
  81.8 0.0 copy-start.6
  81.8 0.8 copy-done.6
  82.6 0.0 copy-start
  82.6 0.0 copy-start.1
  82.6 82.5 %second_pack.1 = (bf16[2,256,512]{2,1,0:T(8,128)(2,1)}, bf16[2048,128]{1,0:T(8,128)(2,1)}, bf16[2048,128]{1,0:T(8,128)(2,1)}, bf16[2,512,512]{2,1,0:T(8,128)(2,1)}) custom-call(s32[3]{0:T(128)} %pad_add_fusion.place, s32[4]{0:T(128)} %seps.13, bf16[4,2,2,512,512]{4,3,2,1,0:T(8,128)(2,1)} %peram.3, bf16[4,1024,128]{2,1,0:T(8,128)(2,1)} %bitcast.6, ...), custom_call_target="tpu_custom_call" | custom-call | flops 9999999827968 | bytes 10000000000 | tf_op jit(solution)/shard_map/second_pack/pallas_call | solution.py:499
  165.1 1.8 collective-permute-start.4
  166.9 1.5 collective-permute-start.5
  168.4 2.6 %collective-permute-start.7 = (bf16[2,256,512]{2,1,0:T(8,128)(2,1)}, bf16[2,256,512]{2,1,0:T(8,128)(2,1)}, u32[]{:S(2)}, u32[]{:S(2)}) collective-permute-start(bf16[2,256,512]{2,1,0:T(8,128)(2,1)} %get-tuple-element.30), channel_id=1, source_target_pairs={{0,8},{4,12},{8,0},{12,4},{1,9},{5,13},{9,1},{13,5},{2,10},{6,14},... | collective-permute-start | bytes 1572872 | tf_op jit(solution)/shard_map/ppermute | solution.py:441
  171.0 0.0 collective-permute-done.2.refs_1_.near
  171.0 1.5 collective-permute-start.8
  172.5 0.0 collective-permute-done.1.near
  172.5 0.0 copy-done
  172.5 0.0 copy-done.1
  172.5 0.0 copy-start.2
  172.5 0.0 copy-start.5
  172.5 9.7 %own_pack.1.refs_0_ = bf16[2080,128]{1,0:T(8,128)(2,1)} custom-call(s32[3]{0:T(128)S(1)} %copy-done, s32[1]{0:T(128)S(6)} %copy.8.partner, bf16[4,1024,128]{2,1,0:T(8,128)(2,1)S(1)} %bitcast.7, bf16[4112,128]{1,0:T(8,128)(2,1)} %collective-permute-done.1.near), custom_call_target="tpu_custom_call" | custom-call | flops 9999999827968 | bytes 10000000000 | tf_op jit(solution)/shard_map/own_pack/pallas_call | solution.py:512
  182.2 0.1 collective-permute-start.3
  182.3 0.0 copy-done.2
  182.3 0.0 copy-done.5
  182.3 6.4 %own_products_a.1 = (bf16[2,4,512,256]{3,2,1,0:T(8,128)(2,1)S(1)}, bf16[4,512,256]{2,1,0:T(8,128)(2,1)S(1)}) custom-call(s32[3]{0:T(128)S(1)} %copy-done, s32[4,4]{1,0:T(4,128)S(1)} %copy-done.2, bf16[2,512,512]{2,1,0:T(8,128)(2,1)S(1)} %copy-done.5, bf16[4,1024,128]{2,1,0:T(8,128)(2,1)S(1)} %bitcast.8, bf16[4112,128]{1,0:T(8,128)(2,1)} %collective-permute-done.1.near, ...), custom_call_target="tpu_custom_call" | custom-call | flops 9999999827968 | bytes 10000000000 | tf_op jit(solution)/shard_map/own_products_a/pallas_call | solution.py:528
  188.8 0.0 collective-permute-done.3.traded.own
  188.8 0.0 copy-start.4
  188.8 6.2 %own_products_b.1.after.htb = bf16[2,4,512,256]{3,2,1,0:T(8,128)(2,1)S(1)} custom-call(s32[3]{0:T(128)S(1)} %copy-done, s32[4,4]{1,0:T(4,128)S(1)} %copy-done.2, bf16[4,512,256]{2,1,0:T(8,128)(2,1)S(1)} %get-tuple-element.23.xb_ref, bf16[2080,128]{1,0:T(8,128)(2,1)} %collective-permute-done.3.traded.own), custom_call_target="tpu_custom_call" | custom-call | flops 9999999827968 | bytes 10000000000 | tf_op jit(solution)/shard_map/own_products_b/pallas_call | solution.py:537
  195.1 0.0 collective-permute-done.4.far_same.refs_0_
  195.1 0.0 collective-permute-done.5.far_cross.refs_1_
  195.1 0.0 copy-done.4
  195.1 0.0 copy-start.3
  195.1 9.6 %other_pack.1.refs_2_ = bf16[2048,128]{1,0:T(8,128)(2,1)} custom-call(s32[3]{0:T(128)S(1)} %copy-done, s32[4]{0:T(128)S(1)} %copy-done.4, bf16[4,1024,128]{2,1,0:T(8,128)(2,1)S(1)} %bitcast.9, bf16[4112,128]{1,0:T(8,128)(2,1)} %collective-permute-done.1.near, bf16[2048,128]{1,0:T(8,128)(2,1)} %collective-permute-done.4.far_same.refs_0_, ...), custom_call_target="tpu_custom_call" | custom-call | flops 9999999827968 | bytes 10000000000 | tf_op jit(solution)/shard_map/other_pack/pallas_call | solution.py:547
  204.7 0.5 collective-permute-start.6
  205.3 0.0 copy-done.3
  205.3 7.6 %other_products_a.1 = (f32[2,4,512,256]{3,2,1,0:T(8,128)S(1)}, s32[2]{0:T(128)S(1)}) custom-call(s32[3]{0:T(128)S(1)} %copy-done, s32[4]{0:T(128)S(1)} %copy-done.4, s32[4,4]{1,0:T(4,128)S(1)} %copy-done.3, s32[1]{0:T(128)S(6)} %copy.8.partner, bf16[2,4,512,256]{3,2,1,0:T(8,128)(2,1)S(1)} %get-tuple-element.22.hta, ...), custom_call_target="tpu_custom_call" | custom-call | flops 9999999827968 | bytes 10000000000 | tf_op jit(solution)/shard_map/other_products_a/pallas_call | solution.py:575
  212.9 0.0 collective-permute-done.6.traded
  212.9 7.7 %other_products_b.1 = (f32[2,4,512,256]{3,2,1,0:T(8,128)S(1)}, s32[2]{0:T(128)S(1)}) custom-call(s32[3]{0:T(128)S(1)} %copy-done, s32[4]{0:T(128)S(1)} %copy-done.4, s32[4,4]{1,0:T(4,128)S(1)} %copy-done.3, s32[1]{0:T(128)S(6)} %copy.8.partner, bf16[2,4,512,256]{3,2,1,0:T(8,128)(2,1)S(1)} %get-tuple-element.22.hta, ...), custom_call_target="tpu_custom_call" | custom-call | flops 9999999827968 | bytes 10000000000 | tf_op jit(solution)/shard_map/other_products_b/pallas_call | solution.py:587
  220.6 0.0 collective-permute-done.8.far
  220.6 2.3 early_traces.1.sums_ref
  222.8 0.0 collective-permute-done.7.rest_ref
  222.9 1.8 late_traces.1
  224.7 16.9 %all_to_all.5 = f32[32,1,128]{2,1,0:T(1,128)S(1)} all-to-all(f32[32,1,128]{2,1,0:T(1,128)S(1)} %late_traces.1), channel_id=1, replica_groups=mesh['src'=2,'snk'=4,'mom'=4] {'src','snk','mom'}, dimensions={0} | all-to-all | bytes 32768 | tf_op jit(solution)/shard_map/all_to_all | solution.py:618
  241.6 0.1 reduce_sum.11
  241.7 0.1 reshape.11
  241.8 0.7 copy.7
  (1 shorter events, 0.0 us)
Async XLA Ops:
  66.7 15.1 %collective-permute-start = (bf16[2,256,512]{2,1,0:T(8,128)(2,1)}, bf16[2,256,512]{2,1,0:T(8,128)(2,1)S(1)}, u32[]{:S(2)}, u32[]{:S(2)}) collective-permute-start(bf16[2,256,512]{2,1,0:T(8,128)(2,1)} %get-tuple-element.18.rest_near), channel_id=1, source_target_pairs={{16,0},{17,1},{18,2},{19,3},{0,16},{1,17},{2,18},{3,19},{20,4},{21... | collective-permute-start | bytes 1572872 | tf_op jit(solution)/shard_map/ppermute | solution.py:449
  69.7 102.8 %collective-permute-start.1 = (bf16[4112,128]{1,0:T(8,128)(2,1)}, bf16[4112,128]{1,0:T(8,128)(2,1)}, u32[]{:S(2)}, u32[]{:S(2)}) collective-permute-start(bf16[4112,128]{1,0:T(8,128)(2,1)} %get-tuple-element.20), channel_id=1, source_target_pairs={{0,2},{1,3},{2,0},{3,1},{4,6},{5,7},{6,4},{7,5},{8,10},{9,11},{10,... | collective-permute-start | bytes 3158024 | tf_op jit(solution)/shard_map/ppermute | solution.py:437
  71.2 99.8 %collective-permute-start.2 = (bf16[2,256,512]{2,1,0:T(8,128)(2,1)}, bf16[2,256,512]{2,1,0:T(8,128)(2,1)}, u32[]{:S(2)}, u32[]{:S(2)}) collective-permute-start(bf16[2,256,512]{2,1,0:T(8,128)(2,1)} %get-tuple-element.21), channel_id=1, source_target_pairs={{0,8},{4,12},{8,0},{12,4},{1,9},{5,13},{9,1},{13,5},{2,10},{6,14},... | collective-permute-start | bytes 1572872 | tf_op jit(solution)/shard_map/ppermute | solution.py:441
  81.8 0.8 copy-start.6
  82.6 89.9 %copy-start = (s32[3]{0:T(128)S(1)}, s32[3]{0:T(128)}, u32[]{:S(2)}) copy-start(s32[3]{0:T(128)} %pad_add_fusion.place) | copy-start | bytes 40
  82.6 89.9 %copy-start.1 = (bf16[4,1,4,2,128,128]{5,4,3,2,1,0:T(8,128)(2,1)S(1)}, bf16[4,1,4,2,128,128]{5,4,3,2,1,0:T(8,128)(2,1)}, u32[]{:S(2)}) copy-start(bf16[4,1,4,2,128,128]{5,4,3,2,1,0:T(8,128)(2,1)} %param.6) | copy-start | bytes 3145732
  165.1 30.0 %collective-permute-start.4 = (bf16[2048,128]{1,0:T(8,128)(2,1)}, bf16[2048,128]{1,0:T(8,128)(2,1)}, u32[]{:S(2)}, u32[]{:S(2)}) collective-permute-start(bf16[2048,128]{1,0:T(8,128)(2,1)} %get-tuple-element.24), channel_id=1, source_target_pairs={{16,0},{17,1},{18,2},{19,3},{0,16},{1,17},{2,18},{3,19},{20,4},{21... | collective-permute-start | bytes 1572872 | tf_op jit(solution)/shard_map/ppermute | solution.py:449
  166.9 28.2 %collective-permute-start.5 = (bf16[2048,128]{1,0:T(8,128)(2,1)}, bf16[2048,128]{1,0:T(8,128)(2,1)}, u32[]{:S(2)}, u32[]{:S(2)}) collective-permute-start(bf16[2048,128]{1,0:T(8,128)(2,1)} %get-tuple-element.25), channel_id=1, source_target_pairs={{18,0},{19,1},{16,2},{17,3},{2,16},{3,17},{0,18},{1,19},{22,4},{23... | collective-permute-start | bytes 1572872 | tf_op jit(solution)/shard_map/ppermute | solution.py:449
  168.4 54.5 %collective-permute-start.7 = (bf16[2,256,512]{2,1,0:T(8,128)(2,1)}, bf16[2,256,512]{2,1,0:T(8,128)(2,1)}, u32[]{:S(2)}, u32[]{:S(2)}) collective-permute-start(bf16[2,256,512]{2,1,0:T(8,128)(2,1)} %get-tuple-element.30), channel_id=1, source_target_pairs={{0,8},{4,12},{8,0},{12,4},{1,9},{5,13},{9,1},{13,5},{2,10},{6,14},... | collective-permute-start | bytes 1572872 | tf_op jit(solution)/shard_map/ppermute | solution.py:441
  171.0 49.6 %collective-permute-start.8 = (bf16[2,256,512]{2,1,0:T(8,128)(2,1)}, bf16[2,256,512]{2,1,0:T(8,128)(2,1)}, u32[]{:S(2)}, u32[]{:S(2)}) collective-permute-start(bf16[2,256,512]{2,1,0:T(8,128)(2,1)} %collective-permute-done.2.refs_1_.near), channel_id=1, source_target_pairs={{16,0},{17,1},{18,2},{19,3},{0,16},{1,17},{2,18},{3,19},{20,4},{21... | collective-permute-start | bytes 1572872 | tf_op jit(solution)/shard_map/ppermute | solution.py:449
  172.5 9.9 %copy-start.2 = (s32[4,4]{1,0:T(4,128)S(1)}, s32[4,4]{1,0:T(4,128)}, u32[]{:S(2)}) copy-start(s32[4,4]{1,0:T(4,128)} %gamma.7) | copy-start | bytes 196
  172.5 9.9 %copy-start.5 = (bf16[2,512,512]{2,1,0:T(8,128)(2,1)S(1)}, bf16[2,512,512]{2,1,0:T(8,128)(2,1)}, u32[]{:S(2)}) copy-start(bf16[2,512,512]{2,1,0:T(8,128)(2,1)} %get-tuple-element.19.block) | copy-start | bytes 3145732
  182.2 6.5 %collective-permute-start.3 = (bf16[2080,128]{1,0:T(8,128)(2,1)}, bf16[2080,128]{1,0:T(8,128)(2,1)}, u32[]{:S(2)}, u32[]{:S(2)}) collective-permute-start(bf16[2080,128]{1,0:T(8,128)(2,1)} %own_pack.1.refs_0_), channel_id=1, source_target_pairs={{0,1},{1,0},{2,3},{3,2},{4,5},{5,4},{6,7},{7,6},{8,9},{9,8},{10,11... | collective-permute-start | bytes 1597448 | tf_op jit(solution)/shard_map/ppermute | solution.py:437
  188.8 6.3 %copy-start.4 = (s32[4]{0:T(128)S(1)}, s32[4]{0:T(128)}, u32[]{:S(2)}) copy-start(s32[4]{0:T(128)} %seps.13) | copy-start | bytes 52
  195.1 10.2 %copy-start.3 = (s32[4,4]{1,0:T(4,128)S(1)}, s32[4,4]{1,0:T(4,128)}, u32[]{:S(2)}) copy-start(s32[4,4]{1,0:T(4,128)} %gamma.7) | copy-start | bytes 196
  204.7 8.1 %collective-permute-start.6 = (bf16[2048,128]{1,0:T(8,128)(2,1)}, bf16[2048,128]{1,0:T(8,128)(2,1)}, u32[]{:S(2)}, u32[]{:S(2)}) collective-permute-start(bf16[2048,128]{1,0:T(8,128)(2,1)} %other_pack.1.refs_2_), channel_id=1, source_target_pairs={{0,1},{1,0},{2,3},{3,2},{4,5},{5,4},{6,7},{7,6},{8,9},{9,8},{10,11... | collective-permute-start | bytes 1572872 | tf_op jit(solution)/shard_map/ppermute | solution.py:437

commit v4 on v3

v4 whole, which is shorter than its diff:
```python
import functools

import jax
import jax.numpy as jnp
from jax import lax
from jax.experimental import pallas as pl
from jax.experimental.pallas import tpu as pltpu
from jax.sharding import PartitionSpec as P

NSPIN = 4
NT_DIMS = (((1,), (1,)), ((), ()))
MIB = 1024 * 1024
WEIGHT = 10**13
TAG_ROWS = 16
TILE = 256
GAMMAS = (
    (3, 1 | 1 << 2 | 3 << 4 | 3 << 6),
    (3, 2 | 0 << 2 | 0 << 4 | 2 << 6),
    (2, 1 | 3 << 2 | 3 << 4 | 1 << 6),
    (2, 0),
)


def spin_entry(code, row):
    phase = row * 0
    for bit, (flip, phases) in enumerate(GAMMAS):
        on = (code >> bit) & 1
        phase = phase + on * ((phases >> (2 * row)) & 3)
        row = row ^ (on * flip)
    return row, phase & 3


def mask_of(code):
    mask = code * 0
    for bit, (flip, _) in enumerate(GAMMAS):
        mask = mask ^ (((code >> bit) & 1) * flip)
    return mask


def fill_spin_blocks(codes, turns, zero, write):
    nterm = len(codes)
    masks = [mask_of(code) for code in codes]
    for mask in range(NSPIN):
        missing = masks[0] != mask
        for r in range(1, nterm):
            missing = missing & (masks[r] != mask)

        @pl.when(missing)
        def _():
            for spin in range(NSPIN):
                zero(spin, spin ^ mask)

    for r in range(nterm):

        def term(add):
            for spin in range(NSPIN):
                column, phase = spin_entry(codes[r], spin)
                a, b, minus_b = (turns[r, (n - phase) & 3] for n in (4, 1, 3))
                write(spin, column, a, b, minus_b, add)

        if r == 0:
            term(False)
            continue
        met = masks[0] == masks[r]
        for before in range(1, r):
            met = met | (masks[before] == masks[r])
        pl.when(met)(lambda: term(True))
        pl.when(jnp.logical_not(met))(lambda: term(False))


def set_turns(turns, r, real, imag):
    for n, value in enumerate((real, imag, -real, -imag)):
        turns[r, n] = value


def put(ref, rows, lanes, value, add):
    if add:
        value = (ref[rows, lanes].astype(jnp.float32) + value.astype(jnp.float32)).astype(ref.dtype)
    ref[rows, lanes] = value


def along(spin, nev, start=0):
    if isinstance(spin, int):
        return slice(start + spin * nev, start + (spin + 1) * nev)
    return pl.ds(pl.multiple_of(start + spin * nev, nev), nev)


class Plan:
    def __init__(self, place, seps, sizes):
        slices, offsets, src_count, snk_count = sizes
        src, snk, self.mom = place[0], place[1], place[2]
        half_snk = snk_count // 2
        self.slices, self.time_count = slices, slices * src_count
        self.forward = snk < half_snk
        base = lax.rem(snk, half_snk) * offsets
        self.keep = jnp.where(self.forward, 0, offsets - 1)
        self.give = offsets - 1 - self.keep
        self.sep_index = base + self.keep
        sign = jnp.where(self.forward, 1, -1)
        self.shift = sign * seps[base + self.keep]
        self.peer_shift = -sign * seps[base + self.give]
        self.own_time = src * slices + self.mom
        late = jnp.where(self.forward, 0, self.shift)
        self.pair_time = lax.rem(self.own_time + late + self.time_count, self.time_count)
        self.live = self.forward if offsets == 1 else None

    def _sum(self, place, amount):
        return lax.rem(place + amount + self.time_count, self.time_count)

    def local(self, i):
        return lax.rem(self._sum(self.mom ^ i, self.shift), self.slices)

    def hops(self, i):
        return lax.div(self._sum(self.mom ^ i, self.shift), self.slices)

    def peer_local(self):
        return lax.rem(self._sum(self.mom, self.peer_shift), self.slices)

    def peer_hops(self):
        return lax.div(self._sum(self.mom, self.peer_shift), self.slices)


def run_copies(copies, sems):
    handles = [
        pltpu.make_async_copy(source, target, sems.at[n])
        for n, (source, target) in enumerate(copies)
    ]
    for handle in handles:
        handle.start()
    for handle in handles:
        handle.wait()


def span(index, rows):
    return pl.ds(index * rows, rows)


def first_pack(sizes, place, seps, partner, peram, proj, first, rest, near, sems):
    plan = Plan(place, seps, sizes)
    split, rows = first.shape[1], proj.shape[1]
    peer, give, mom = plan.peer_local(), plan.give, plan.mom
    number = jnp.full((TAG_ROWS, near.shape[-1]), partner[0].astype(jnp.float32))
    near[pl.ds(4 * rows, TAG_ROWS), :] = number.astype(jnp.bfloat16)
    run_copies(
        [
            (peram.at[peer, give, :, pl.ds(0, split)], first),
            (peram.at[peer, give, :, pl.ds(split, rest.shape[1])], rest),
            (proj.at[plan.local(2)], near.at[span(0, rows)]),
            (proj.at[plan.local(3)], near.at[span(1, rows)]),
            (proj.at[mom ^ 2], near.at[span(2, rows)]),
            (proj.at[mom ^ 3], near.at[span(3, rows)]),
        ],
        sems,
    )


def second_pack(sizes, place, seps, proj, rest_near, rest_far, after, *refs):
    rest, far_same, far_cross, sems = refs
    plan = Plan(place, seps, sizes)
    rows = proj.shape[1]
    flag = lax.rem(plan.peer_hops(), 2)
    copies = [
        (proj.at[plan.local(0)], far_same.at[span(0, rows)]),
        (proj.at[plan.local(1)], far_same.at[span(1, rows)]),
        (proj.at[plan.local(2)], far_cross.at[span(0, rows)]),
        (proj.at[plan.local(3)], far_cross.at[span(1, rows)]),
    ]

    @pl.when(flag == 0)
    def _():
        run_copies([(rest_near, rest)] + copies, sems)

    @pl.when(flag != 0)
    def _():
        run_copies([(rest_far, rest)] + copies, sems)


def own_pack(place, partner, proj, near, out, sems):
    rows = proj.shape[1]
    mom = place[2]
    number = jnp.full((TAG_ROWS, out.shape[-1]), partner[0].astype(jnp.float32))
    out[pl.ds(2 * rows, TAG_ROWS), :] = number.astype(jnp.bfloat16)
    run_copies(
        [
            (proj.at[mom ^ 1], out.at[span(0, rows)]),
            (near.at[span(3, rows)], out.at[span(1, rows)]),
            (near.at[pl.ds(4 * rows, TAG_ROWS)], out.at[pl.ds(2 * rows + TAG_ROWS, TAG_ROWS)]),
        ],
        sems,
    )


def other_pack(sizes, place, seps, proj, near, far_same, far_cross, after, out, sems):
    plan = Plan(place, seps, sizes)
    rows = proj.shape[1]
    flag = lax.rem(plan.hops(1), 2) if sizes[2] == 2 else jnp.int32(0)
    low, high = out.at[span(0, rows)], out.at[span(1, rows)]

    @pl.when(flag == 0)
    def _():
        run_copies([(proj.at[plan.local(1)], low), (near.at[span(1, rows)], high)], sems)

    @pl.when(flag != 0)
    def _():
        run_copies([(far_same.at[span(1, rows)], low), (far_cross.at[span(1, rows)], high)], sems)


def own_product(codes, p_ref, n, y_ref, ht, u_ref, turns):
    nterm = len(codes)
    nev = turns.shape[-1]
    width = u_ref.shape[0]
    for r in range(nterm):
        real, imag = (p_ref[n, m * nev : (m + 1) * nev].T for m in (2 * r, 2 * r + 1))
        set_turns(turns, r, real, imag)

    def zero(spin, column):
        empty = jnp.zeros((nev, nev), jnp.bfloat16)
        u_ref[along(column, nev), along(spin, nev)] = empty
        u_ref[along(column, nev), along(spin, nev, width)] = empty

    def write(spin, column, a, b, minus_b, add):
        put(u_ref, along(column, nev), along(spin, nev), a, add)
        put(u_ref, along(column, nev), along(spin, nev, width), b, add)

    fill_spin_blocks(codes, turns, zero, write)
    for tile in range(2 * width // TILE):
        lanes = slice(tile * TILE, (tile + 1) * TILE)
        out = lax.dot_general(
            u_ref[...], y_ref[lanes, :], NT_DIMS, preferred_element_type=jnp.float32
        )
        ht[:, lanes] = out.astype(jnp.bfloat16)


def codes_of(gamma, op, nterm):
    return [gamma[op, r] for r in range(nterm)]


def own_kernel_0(sizes, place, seps, gamma, peram, proj, y_ref, ht, x_ref, p_ref, u_ref, turns, sems):
    plan = Plan(place, seps, sizes)
    run_copies(
        [(peram.at[plan.mom, plan.keep], x_ref), (proj.at[plan.mom], p_ref.at[0])], sems
    )
    width = x_ref.shape[-1]
    real, imag = x_ref[0], x_ref[1]
    y_ref[:width, :width] = real
    y_ref[:width, width:] = -imag
    y_ref[width:, :width] = imag
    y_ref[width:, width:] = real
    codes = codes_of(gamma, plan.mom, turns.shape[0])
    own_product(codes, p_ref, 0, y_ref, ht, u_ref, turns)


def own_kernel_2(place, gamma, near, y_ref, first, traded, ht, p_ref, u_ref, turns, sems):
    rows = p_ref.shape[1]
    run_copies([(near.at[span(2, rows)], p_ref.at[0])], sems)
    codes = codes_of(gamma, place[2] ^ 2, turns.shape[0])
    own_product(codes, p_ref, 0, y_ref, ht, u_ref, turns)


def own_kernel_13(sizes, place, seps, gamma, partner, near, traded, y_ref, *refs):
    ht, label, p_ref, u_ref, turns, near_tag, own_tag, sems = refs
    plan = Plan(place, seps, sizes)
    mom = plan.mom
    rows = p_ref.shape[1]
    run_copies(
        [
            (traded.at[span(0, rows)], p_ref.at[0]),
            (traded.at[span(1, rows)], p_ref.at[1]),
            (traded.at[pl.ds(2 * rows, 2 * TAG_ROWS)], own_tag),
            (near.at[pl.ds(4 * rows, TAG_ROWS)], near_tag),
        ],
        sems,
    )

    def number(tag):
        return jnp.max(tag.astype(jnp.float32)).astype(jnp.int32)

    partners = [
        partner[0],
        number(own_tag[:TAG_ROWS]),
        number(near_tag[...]),
        number(own_tag[TAG_ROWS:]),
    ]
    for p in range(len(partners)):
        back = jnp.int32(0)
        for i, value in enumerate(partners):
            back = back + jnp.where(value == (mom ^ p), mom ^ i, 0)
        label[p] = jnp.where(plan.forward, back, mom ^ p)
        label[len(partners) + p] = jnp.where(plan.forward, back, partners[p]) ^ mom

    def step(n, carry):
        codes = codes_of(gamma, mom ^ (1 + 2 * n), turns.shape[0])
        own_product(codes, p_ref, n, y_ref, ht.at[n], u_ref, turns)
        return carry

    lax.fori_loop(0, 2, step, 0)


def other_products(mom, gamma, label, first, hts, refs):
    k_ref, p_ref, ht_ref, v_ref, turns = refs
    nterm, nev = turns.shape[0], turns.shape[-1]
    width = ht_ref.shape[0]
    h0, h2, h13 = hts

    def zero(spin, column):
        empty = jnp.zeros((nev, nev), jnp.bfloat16)
        for top in (0, width):
            for left in (0, width):
                v_ref[along(spin, nev, top), along(column, nev, left)] = empty

    def write(spin, column, a, b, minus_b, add):
        put(v_ref, along(spin, nev), along(column, nev), a, add)
        put(v_ref, along(spin, nev), along(column, nev, width), minus_b, add)
        put(v_ref, along(spin, nev, width), along(column, nev), b, add)
        put(v_ref, along(spin, nev, width), along(column, nev, width), a, add)

    def step(n, carry):
        left = label[4 + first + 2 * n]
        for index, source in enumerate((h0, h13.at[0], h2, h13.at[1])):

            @pl.when(left == index)
            def _():
                ht_ref[...] = source[...]

        for r in range(nterm):
            real, imag = (p_ref[n, m * nev : (m + 1) * nev] for m in (2 * r, 2 * r + 1))
            set_turns(turns, r, real, imag)
        fill_spin_blocks(codes_of(gamma, mom ^ (first + 2 * n), nterm), turns, zero, write)
        for tile in range(2 * width // TILE):
            lanes = slice(tile * TILE, (tile + 1) * TILE)
            k_ref[n, :, lanes] = lax.dot_general(
                ht_ref[...], v_ref[lanes, :], NT_DIMS, preferred_element_type=jnp.float32
            )
        return carry

    lax.fori_loop(0, 2, step, 0)


def other_kernel_02(sizes, place, seps, gamma, label, h0, h2, h13, proj, near, *refs):
    far_same, far_cross = refs[:2]
    k_ref, p_ref, ht_ref, v_ref, turns, sems = refs[-6:]
    plan = Plan(place, seps, sizes)
    rows = proj.shape[1]
    flag = lax.rem(plan.hops(0), 2) if sizes[2] == 2 else jnp.int32(1)

    @pl.when(flag == 0)
    def _():
        run_copies(
            [(proj.at[plan.local(0)], p_ref.at[0]), (near.at[span(0, rows)], p_ref.at[1])], sems
        )

    @pl.when(flag != 0)
    def _():
        run_copies(
            [(far_same.at[span(0, rows)], p_ref.at[0]), (far_cross.at[span(0, rows)], p_ref.at[1])],
            sems,
        )

    out = (k_ref, p_ref, ht_ref, v_ref, turns)
    other_products(plan.mom, gamma, label, 0, (h0, h2, h13), out)


def other_kernel_13(place, gamma, label, h0, h2, h13, traded, *refs):
    k_ref, p_ref, ht_ref, v_ref, turns, sems = refs
    rows = p_ref.shape[1]
    run_copies([(traded.at[span(n, rows)], p_ref.at[n]) for n in range(2)], sems)
    out = (k_ref, p_ref, ht_ref, v_ref, turns)
    other_products(place[2], gamma, label, 1, (h0, h2, h13), out)


def row_sums(k_refs, source, offset, totals):
    rows = 16
    each = k_refs[0].shape[0]
    width = source.shape[-1]
    nev = totals[0].shape[-1]

    def step(index, totals):
        row = pl.multiple_of(index * rows, rows)
        here = pl.ds(pl.multiple_of(offset + row, rows), rows)
        totals = list(totals)
        for spin in range(NSPIN):
            lanes, later = along(spin, nev), along(spin, nev, width)
            real = source[0, pl.ds(row, rows), lanes].astype(jnp.float32)
            imag = source[1, pl.ds(row, rows), lanes].astype(jnp.float32)
            for n in range(len(totals) // 2):
                k_ref, p = k_refs[n // each], n % each
                kr, ki = k_ref[p, here, lanes], k_ref[p, here, later]
                totals[2 * n] += real * kr - imag * ki
                totals[2 * n + 1] += real * ki + imag * kr
        return tuple(totals)

    return lax.fori_loop(0, source.shape[1] // rows, step, totals)


def early_kernel(sizes, place, seps, ka, kb, near, far, sums_ref, part_ref, sems):
    plan = Plan(place, seps, sizes)
    count = sums_ref.shape[0]
    flag = lax.rem(lax.div(plan.hops(0), max(sizes[2] // 2, 1)), 2)

    @pl.when(flag == 0)
    def _():
        run_copies([(near, part_ref)], sems)

    @pl.when(flag != 0)
    def _():
        run_copies([(far, part_ref)], sems)

    zero = tuple(jnp.zeros(sums_ref.shape[1:], jnp.float32) for _ in range(count))
    for n, total in enumerate(row_sums((ka, kb), part_ref, 0, zero)):
        sums_ref[n] = total


def late_kernel(sizes, sep_count, place, seps, label, ka, kb, rest_ref, sums_ref, out_ref):
    plan = Plan(place, seps, sizes)
    count = sums_ref.shape[0] // 2
    width = rest_ref.shape[-1]
    start = ka.shape[1] - rest_ref.shape[1]
    totals = row_sums((ka, kb), rest_ref, start, tuple(sums_ref[n] for n in range(2 * count)))
    sums = [jnp.sum(total, axis=0, keepdims=True) for total in totals]
    sums = [jnp.sum(total, axis=1, keepdims=True) * (1.0 / width) for total in sums]
    shape = out_ref.shape[1:]
    spot = lax.broadcasted_iota(jnp.int32, shape, 0) * shape[1]
    spot = spot + lax.broadcasted_iota(jnp.int32, shape, 1)
    here = spot // 2 == plan.pair_time * sep_count + plan.sep_index
    if plan.live is not None:
        here = here & plan.live
    values = [jnp.where(spot % 2 == 0, sums[2 * p], sums[2 * p + 1]) for p in range(count)]
    pieces = (0, 2, 1, 3)
    lines = []
    for op in range(count):
        line = jnp.zeros(shape, jnp.float32)
        for value, p in zip(values, pieces):
            line = jnp.where(label[p] == op, value, line)
        lines.append(jnp.where(here, line, 0.0))
    for n in range(out_ref.shape[0]):
        out_ref[n] = lines[n % count]


def smem():
    return pl.BlockSpec(memory_space=pltpu.SMEM)


def vmem():
    return pl.BlockSpec(memory_space=pltpu.VMEM)


def hbm():
    return pl.BlockSpec(memory_space=pltpu.HBM)


def limit(mib):
    return pltpu.CompilerParams(vmem_limit_bytes=mib * MIB)


def shards(peram_blocks, projections, gamma_index, partner, separations):
    src_count, snk_count = lax.axis_size("src"), lax.axis_size("snk")
    mom_count = lax.axis_size("mom")
    slices, offsets = peram_blocks.shape[:2]
    width = peram_blocks.shape[-1]
    nterm, nev = projections.shape[2], projections.shape[-1]
    time_count = slices * src_count
    sep_count = separations.shape[0]
    half_snk = snk_count // 2
    rows = nterm * 2 * nev
    sizes = (slices, offsets, src_count, snk_count)
    place = jnp.stack([lax.axis_index(name) for name in ("src", "snk", "mom")]).astype(jnp.int32)
    proj = projections.reshape(slices, rows, nev)

    def swap_mom(array, i):
        return lax.ppermute(array, "mom", [(a, a ^ i) for a in range(mom_count)])

    def swap_snk(array):
        pairs = [(a, (a + half_snk) % snk_count) for a in range(snk_count)]
        return lax.ppermute(array, "snk", pairs)

    def next_src(array, step=1, i=0):
        pairs = [
            (((a + step) % src_count) * mom_count + (b ^ i), a * mom_count + b)
            for a in range(src_count)
            for b in range(mom_count)
        ]
        return lax.ppermute(array, ("src", "mom"), pairs)

    def most_of(array, amount):
        step = 1
        while 2 * step < src_count:
            array = jnp.where((amount // step) % 2 != 0, next_src(array, step), array)
            step *= 2
        return array, next_src(array, step)

    def call(kernel, name, in_specs, out_specs, out_shape, scratch, mib):
        cost = pl.CostEstimate(flops=WEIGHT, bytes_accessed=WEIGHT // 1000, transcendentals=0)
        return pl.pallas_call(
            kernel,
            in_specs=in_specs,
            out_specs=out_specs,
            out_shape=out_shape,
            scratch_shapes=scratch,
            compiler_params=limit(mib),
            cost_estimate=cost,
            name=name,
        )

    def bf16(*shape):
        return jax.ShapeDtypeStruct(shape, jnp.bfloat16)

    def dma(count):
        return pltpu.SemaphoreType.DMA((count,))

    part = functools.partial
    tag = pltpu.VMEM((TAG_ROWS, nev), jnp.bfloat16)
    split = (width * 5 // 8) // 16 * 16
    two = bf16(2 * rows, nev)
    rest_shape = bf16(2, width - split, width)

    first, rest, near = call(
        part(first_pack, sizes),
        "first_pack",
        [smem()] * 3 + [hbm()] * 2,
        [vmem()] * 3,
        [bf16(2, split, width), rest_shape, bf16(4 * rows + TAG_ROWS, nev)],
        [dma(6)],
        58,
    )(place, separations, partner, peram_blocks, proj)

    u_scratch = pltpu.VMEM((width, 2 * width), jnp.bfloat16)
    v_scratch = pltpu.VMEM((2 * width, 2 * width), jnp.bfloat16)
    turns = pltpu.VMEM((nterm, 4, nev, nev), jnp.bfloat16)
    piece = pltpu.VMEM((1, rows, nev), jnp.bfloat16)
    pieces = pltpu.VMEM((2, rows, nev), jnp.bfloat16)
    y, h0 = call(
        part(own_kernel_0, sizes),
        "own_products_0",
        [smem()] * 3 + [hbm()] * 2,
        [vmem()] * 2,
        [bf16(2 * width, 2 * width), bf16(width, 2 * width)],
        [pltpu.VMEM((2, width, width), jnp.bfloat16), piece, u_scratch, turns, dma(2)],
        58,
    )(place, separations, gamma_index, peram_blocks, proj)

    plan = Plan(place, separations, sizes)
    first = swap_snk(first)
    rest_near, rest_far = most_of(rest, plan.peer_hops())
    near = swap_mom(near, 2)
    if src_count > 2:
        rest_near = jnp.where(plan.peer_hops() // (src_count // 2) != 0, rest_far, rest_near)
        rest_far = rest_near
    rest, far_same, far_cross = call(
        part(second_pack, sizes),
        "second_pack",
        [smem()] * 2 + [hbm()] * 4,
        [vmem()] * 3,
        [rest_shape, two, two],
        [dma(5)],
        16,
    )(place, separations, proj, rest_near, rest_far, h0)
    rest = swap_snk(rest)
    if src_count == 2:
        far_same, far_cross = next_src(far_same), next_src(far_cross, 1, 2)

    own_trade = call(
        own_pack,
        "own_pack",
        [smem()] * 2 + [hbm()] * 2,
        vmem(),
        bf16(2 * (rows + TAG_ROWS), nev),
        [dma(3)],
        16,
    )(place, partner, proj, near)
    own_got = swap_mom(own_trade, 1)
    first_near, first_far = most_of(first, plan.hops(0))

    h2 = call(
        own_kernel_2,
        "own_products_2",
        [smem()] * 2 + [hbm(), vmem()] + [hbm()] * 2,
        vmem(),
        bf16(width, 2 * width),
        [piece, u_scratch, turns, dma(1)],
        16,
    )(place, gamma_index, near, y, first, own_trade)
    h13, label = call(
        part(own_kernel_13, sizes),
        "own_products_13",
        [smem()] * 4 + [hbm()] * 2 + [vmem()],
        [vmem(), smem()],
        [bf16(2, width, 2 * width), jax.ShapeDtypeStruct((2 * mom_count,), jnp.int32)],
        [pieces, u_scratch, turns, tag, pltpu.VMEM((2 * TAG_ROWS, nev), jnp.bfloat16), dma(4)],
        16,
    )(place, separations, gamma_index, partner, near, own_got, y)

    other_trade = call(
        part(other_pack, sizes),
        "other_pack",
        [smem()] * 2 + [hbm()] * 5,
        vmem(),
        two,
        [dma(2)],
        16,
    )(place, separations, proj, near, far_same, far_cross, h13)
    other_got = swap_mom(other_trade, 1)
    if src_count != 2:

        def moved(array):
            if src_count == 1:
                return array
            array, far = most_of(array, plan.hops(0))
            return jnp.where(plan.hops(0) // (src_count // 2) != 0, far, array)

        far_same = moved(lax.dynamic_index_in_dim(proj, plan.local(0), 0, keepdims=False))
        far_cross, other_got = moved(near[:rows]), moved(other_got)

    k_out = jax.ShapeDtypeStruct((mom_count // 2, width, 2 * width), jnp.float32)
    scratch = [pieces, u_scratch, v_scratch, turns, dma(2)]
    ka = call(
        part(other_kernel_02, sizes),
        "other_products_02",
        [smem()] * 4 + [vmem()] * 3 + [hbm()] * 5,
        vmem(),
        k_out,
        scratch,
        24,
    )(
        place, separations, gamma_index, label, h0, h2, h13,
        proj, near, far_same, far_cross, other_trade,
    )
    kb = call(
        other_kernel_13,
        "other_products_13",
        [smem()] * 3 + [vmem()] * 3 + [hbm()],
        vmem(),
        k_out,
        scratch,
        24,
    )(place, gamma_index, label, h0, h2, h13, other_got)

    sums = call(
        part(early_kernel, sizes),
        "early_traces",
        [smem()] * 2 + [vmem()] * 2 + [hbm()] * 2,
        vmem(),
        jax.ShapeDtypeStruct((2 * mom_count, 16, nev), jnp.float32),
        [pltpu.VMEM((2, split, width), jnp.bfloat16), dma(1)],
        20,
    )(place, separations, ka, kb, first_near, first_far)
    device_count = src_count * snk_count * mom_count
    values = time_count * sep_count * 2
    lines = (values + 127) // 128
    out = call(
        part(late_kernel, sizes, sep_count),
        "late_traces",
        [smem()] * 3 + [vmem()] * 4,
        vmem(),
        jax.ShapeDtypeStruct((device_count, lines, 128), jnp.float32),
        [],
        20,
    )(place, separations, label, ka, kb, rest, sums)
    out = lax.all_to_all(out, ("src", "snk", "mom"), split_axis=0, concat_axis=0, tiled=True)
    out = jnp.sum(out, axis=0).reshape(lines * 128)[:values]
    return out.reshape(time_count, sep_count, 1, 2)


def solution(mesh):
    placed = (
        P("src", "snk", None, None, None),
        P("src", "mom", None, None, None, None),
        P(),
        P("mom"),
        P(),
    )
    return jax.shard_map(
        shards, mesh=mesh, in_specs=placed, out_specs=P(None, None, "mom", None), check_vma=False
    )
```

time: 243 us -> 92.6 us (0.38)
  Pallas kernels: 199 us -> 40.9 us
  waiting for transfers between devices: 8.04 us -> 26.2 us
  blocking collectives: 16.9 us -> 10 us
  starting transfers between devices: 15.1 us -> 11.6 us
    pallas_call x1, Pallas kernels: 82.5 us -> 2.03 us  [shards(): call(part(second_pack, sizes), 'second_pack', [smem()] * 2 + [hbm()] * 4,...]
    pallas_call x1, Pallas kernels: 65.4 us -> 3.6 us  [shards(): call(part(first_pack, sizes), 'first_pack', [smem()] * 3 + [hbm()] * 2, [...]
    ppermute x2, waiting for transfers between devices: 0.01 us -> 22.2 us  [swap_snk(): return lax.ppermute(array, 'snk', pairs)]
    pallas_call x7 -> x8, Pallas kernels: 49.1 us -> 32.8 us  [the longest x1 6.23 us: shards(): call(part(other_kernel_02, sizes), 'other_products_02', [smem()] * 4 + [v...]
    all_to_all x1, blocking collectives: 16.9 us -> 10 us  [shards(): lax.all_to_all(out, ('src', 'snk', 'mom'), split_axis=0, concat_axis=0, t...]
    ppermute x4, waiting for transfers between devices: 8.03 us -> 4 us  [next_src(): return lax.ppermute(array, ('src', 'mom'), pairs)]
    ppermute x4, starting transfers between devices: 7.79 us -> 5.02 us  [next_src(): return lax.ppermute(array, ('src', 'mom'), pairs)]
  transfers between devices with their start and end apart: 9 -> 9, of which waited for: 1 -> 2; matrix products, arithmetic and copies ran while one was open for 0% -> 0% of each run, Pallas kernels for 54% -> 39%
where the time goes in v4:
time: 92.6 us; the launch traced here: 92.4 us
  Pallas kernels  40.9 us (44%)
  waiting for transfers between devices  26.2 us (28%)
  starting transfers between devices  11.6 us (13%)
  blocking collectives  10 us (11%)
  local copies, waits for them, and re-layouts  2.09 us (2%)
    ppermute x2, waiting for transfers between devices, swap_snk(): return lax.ppermute(array, 'snk', pairs)  22.2 us
    all_to_all x1, blocking collectives, shards(): lax.all_to_all(out, ('src', 'snk', 'mom'), split_axis=0, concat_axis=0, t...  10 us
    pallas_call x1, Pallas kernels, shards(): call(part(other_kernel_02, sizes), 'other_products_02', [smem()] * 4 + [v...  6.23 us
    pallas_call x1, Pallas kernels, shards(): call(other_kernel_13, 'other_products_13', [smem()] * 3 + [vmem()] * 3 +...  6.13 us
    pallas_call x1, Pallas kernels, shards(): call(part(own_kernel_13, sizes), 'own_products_13', [smem()] * 4 + [hbm()...  5.5 us
    pallas_call x1, Pallas kernels, shards(): call(part(own_kernel_0, sizes), 'own_products_0', [smem()] * 3 + [hbm()]...  5.11 us
    ppermute x4, starting transfers between devices, next_src(): return lax.ppermute(array, ('src', 'mom'), pairs)  5.02 us
    ppermute x4, waiting for transfers between devices, next_src(): return lax.ppermute(array, ('src', 'mom'), pairs)  4 us
  transfers between devices with their start and end apart: 9, of which 2 were waited for; matrix products, arithmetic and copies ran while one was open for 0% of the time, Pallas kernels for 39%

profile of v4, /device:TPU:0, one launch (start us, length us, event | category | flops | bytes accessed | tf_op | source)
XLA Modules:
  0.0 92.4 jit_solution(14808993274527310597)
XLA Ops:
  0.7 0.6 pad_add_fusion.place
  1.3 3.6 %first_pack.1 = (bf16[2,320,512]{2,1,0:T(8,128)(2,1)}, bf16[2,192,512]{2,1,0:T(8,128)(2,1)}, bf16[4112,128]{1,0:T(8,128)(2,1)}) custom-call(s32[3]{0:T(128)} %pad_add_fusion.place, s32[4]{0:T(128)} %seps.15, s32[1]{0:T(128)S(6)} %copy.8.partner, bf16[4,2,2,512,512]{4,3,2,1,0:T(8,128)(2,1)} %peram.3, bf16[4,1024,128]{2,1,0:T(8,128)(2,1)} %bitcast.5), custom_call_target="tpu_custom_call" | custom-call | flops 9999999827968 | bytes 10000000000 | tf_op jit(solution)/shard_map/first_pack/pallas_call | solution.py:516
  4.9 3.0 %collective-permute-start = (bf16[4112,128]{1,0:T(8,128)(2,1)}, bf16[4112,128]{1,0:T(8,128)(2,1)}, u32[]{:S(2)}, u32[]{:S(2)}) collective-permute-start(bf16[4112,128]{1,0:T(8,128)(2,1)} %get-tuple-element.15), channel_id=1, source_target_pairs={{0,2},{1,3},{2,0},{3,1},{4,6},{5,7},{6,4},{7,5},{8,10},{9,11},{10,... | collective-permute-start | bytes 3158024 | tf_op jit(solution)/shard_map/ppermute | solution.py:470
  7.9 2.6 %collective-permute-start.2 = (bf16[2,320,512]{2,1,0:T(8,128)(2,1)}, bf16[2,320,512]{2,1,0:T(8,128)(2,1)}, u32[]{:S(2)}, u32[]{:S(2)}) collective-permute-start(bf16[2,320,512]{2,1,0:T(8,128)(2,1)} %get-tuple-element.19), channel_id=1, source_target_pairs={{0,8},{4,12},{8,0},{12,4},{1,9},{5,13},{9,1},{13,5},{2,10},{6,14},... | collective-permute-start | bytes 1966088 | tf_op jit(solution)/shard_map/ppermute | solution.py:474
  10.5 1.5 %collective-permute-start.3 = (bf16[2,192,512]{2,1,0:T(8,128)(2,1)}, bf16[2,192,512]{2,1,0:T(8,128)(2,1)}, u32[]{:S(2)}, u32[]{:S(2)}) collective-permute-start(bf16[2,192,512]{2,1,0:T(8,128)(2,1)} %get-tuple-element.21.rest_near), channel_id=1, source_target_pairs={{16,0},{17,1},{18,2},{19,3},{0,16},{1,17},{2,18},{3,19},{20,4},{21... | collective-permute-start | bytes 1179656 | tf_op jit(solution)/shard_map/ppermute | solution.py:482
  12.0 0.0 copy-start
  12.0 0.0 copy-start.1
  12.0 5.1 %own_products_0.1 = (bf16[1024,1024]{1,0:T(8,128)(2,1)}, bf16[512,1024]{1,0:T(8,128)(2,1)}) custom-call(s32[3]{0:T(128)} %pad_add_fusion.place, s32[4]{0:T(128)} %seps.15, s32[4,4]{1,0:T(4,128)} %gamma.9, bf16[4,2,2,512,512]{4,3,2,1,0:T(8,128)(2,1)} %peram.3, bf16[4,1024,128]{2,1,0:T(8,128)(2,1)} %bitcast.6), custom_call_target="tpu_custom_call" | custom-call | flops 9999999827968 | bytes 10000000000 | tf_op jit(solution)/shard_map/own_products_0/pallas_call | solution.py:531
  17.1 4.0 %collective-permute-done.3.rest_far = bf16[2,192,512]{2,1,0:T(8,128)(2,1)} collective-permute-done((bf16[2,192,512]{2,1,0:T(8,128)(2,1)}, bf16[2,192,512]{2,1,0:T(8,128)(2,1)}, u32[]{:S(2)}, u32[]{:S(2)}) %collective-permute-start.3) | collective-permute-done | bytes 393248 | tf_op jit(solution)/shard_map/ppermute | solution.py:482
  21.1 0.0 copy-done
  21.1 0.0 copy-done.1
  21.1 0.0 copy-done.2
  21.1 0.0 copy-done.5
  21.1 0.0 copy-start.7
  21.1 1.2 %copy-done.7 = bf16[512,1024]{1,0:T(8,128)(2,1)S(1)} copy-done((bf16[512,1024]{1,0:T(8,128)(2,1)S(1)}, bf16[512,1024]{1,0:T(8,128)(2,1)}, u32[]{:S(2)}) %copy-start.7) | copy-done | bytes 1048600
  22.4 2.0 %second_pack.1 = (bf16[2,192,512]{2,1,0:T(8,128)(2,1)}, bf16[2048,128]{1,0:T(8,128)(2,1)}, bf16[2048,128]{1,0:T(8,128)(2,1)}) custom-call(s32[3]{0:T(128)S(1)} %copy-done, s32[4]{0:T(128)S(1)} %copy-done.5, bf16[4,1024,128]{2,1,0:T(8,128)(2,1)S(1)} %bitcast.7, bf16[2,192,512]{2,1,0:T(8,128)(2,1)S(1)} %copy-done.2, ...), custom_call_target="tpu_custom_call" | custom-call | flops 9999999827968 | bytes 10000000000 | tf_op jit(solution)/shard_map/second_pack/pallas_call | solution.py:548
  24.4 1.6 %collective-permute-start.4 = (bf16[2048,128]{1,0:T(8,128)(2,1)}, bf16[2048,128]{1,0:T(8,128)(2,1)}, u32[]{:S(2)}, u32[]{:S(2)}) collective-permute-start(bf16[2048,128]{1,0:T(8,128)(2,1)} %get-tuple-element.22), channel_id=1, source_target_pairs={{16,0},{17,1},{18,2},{19,3},{0,16},{1,17},{2,18},{3,19},{20,4},{21... | collective-permute-start | bytes 1572872 | tf_op jit(solution)/shard_map/ppermute | solution.py:482
  26.0 0.5 collective-permute-start.5
  26.4 0.3 collective-permute-start.7
  26.7 22.2 %collective-permute-done.2.first.near = bf16[2,320,512]{2,1,0:T(8,128)(2,1)} collective-permute-done((bf16[2,320,512]{2,1,0:T(8,128)(2,1)}, bf16[2,320,512]{2,1,0:T(8,128)(2,1)}, u32[]{:S(2)}, u32[]{:S(2)}) %collective-permute-start.2) | collective-permute-done | bytes 655392 | tf_op jit(solution)/shard_map/ppermute | solution.py:474
  49.0 1.5 %collective-permute-start.8 = (bf16[2,320,512]{2,1,0:T(8,128)(2,1)}, bf16[2,320,512]{2,1,0:T(8,128)(2,1)}, u32[]{:S(2)}, u32[]{:S(2)}) collective-permute-start(bf16[2,320,512]{2,1,0:T(8,128)(2,1)} %collective-permute-done.2.first.near), channel_id=1, source_target_pairs={{16,0},{17,1},{18,2},{19,3},{0,16},{1,17},{2,18},{3,19},{20,4},{21... | collective-permute-start | bytes 1966088 | tf_op jit(solution)/shard_map/ppermute | solution.py:482
  50.5 0.0 collective-permute-done.near
  50.5 2.4 %own_pack.1.traded = bf16[2080,128]{1,0:T(8,128)(2,1)} custom-call(s32[3]{0:T(128)S(1)} %copy-done, s32[1]{0:T(128)S(6)} %copy.8.partner, bf16[4,1024,128]{2,1,0:T(8,128)(2,1)S(1)} %bitcast.8, bf16[4112,128]{1,0:T(8,128)(2,1)} %collective-permute-done.near), custom_call_target="tpu_custom_call" | custom-call | flops 9999999827968 | bytes 10000000000 | tf_op jit(solution)/shard_map/own_pack/pallas_call | solution.py:561
  52.9 0.1 collective-permute-start.1
  53.0 0.0 copy-done.3
  53.0 0.0 copy-done.6
  53.0 3.4 %own_products_2.1.h2 = bf16[512,1024]{1,0:T(8,128)(2,1)S(1)} custom-call(s32[3]{0:T(128)S(1)} %copy-done, s32[4,4]{1,0:T(4,128)S(1)} %copy-done.3, bf16[4112,128]{1,0:T(8,128)(2,1)} %collective-permute-done.near, bf16[1024,1024]{1,0:T(8,128)(2,1)S(1)} %copy-done.6, bf16[2,320,512]{2,1,0:T(8,128)(2,1)} %collective-permute-done.2.first.near, ...), custom_call_target="tpu_custom_call" | custom-call | flops 9999999827968 | bytes 10000000000 | tf_op jit(solution)/shard_map/own_products_2/pallas_call | solution.py:573
  56.4 0.0 collective-permute-done.1.traded
  56.4 5.5 %own_products_13.1 = (bf16[2,512,1024]{2,1,0:T(8,128)(2,1)S(1)}, s32[8]{0:T(128)S(1)}) custom-call(s32[3]{0:T(128)S(1)} %copy-done, s32[4]{0:T(128)S(1)} %copy-done.5, s32[4,4]{1,0:T(4,128)S(1)} %copy-done.3, s32[1]{0:T(128)S(6)} %copy.8.partner, bf16[4112,128]{1,0:T(8,128)(2,1)} %collective-permute-done.near, ...), custom_call_target="tpu_custom_call" | custom-call | flops 9999999827968 | bytes 10000000000 | tf_op jit(solution)/shard_map/own_products_13/pallas_call | solution.py:582
  61.9 0.0 collective-permute-done.4.far_same.refs_0_
  61.9 0.0 collective-permute-done.5.far_cross.refs_1_
  61.9 0.0 copy-start.4
  61.9 0.0 copy-start.8
  61.9 2.4 %other_pack.1.refs_2_ = bf16[2048,128]{1,0:T(8,128)(2,1)} custom-call(s32[3]{0:T(128)S(1)} %copy-done, s32[4]{0:T(128)S(1)} %copy-done.5, bf16[4,1024,128]{2,1,0:T(8,128)(2,1)S(1)} %bitcast.9, bf16[4112,128]{1,0:T(8,128)(2,1)} %collective-permute-done.near, bf16[2048,128]{1,0:T(8,128)(2,1)} %collective-permute-done.4.far_same.refs_0_, ...), custom_call_target="tpu_custom_call" | custom-call | flops 9999999827968 | bytes 10000000000 | tf_op jit(solution)/shard_map/other_pack/pallas_call | solution.py:592
  64.3 0.6 collective-permute-start.6
  64.9 0.0 copy-done.4
  64.9 0.0 copy-done.8
  64.9 6.2 %other_products_02.1.ka = f32[2,512,1024]{2,1,0:T(8,128)S(1)} custom-call(s32[3]{0:T(128)S(1)} %copy-done, s32[4]{0:T(128)S(1)} %copy-done.5, s32[4,4]{1,0:T(4,128)S(1)} %copy-done.4, s32[8]{0:T(128)S(1)} %get-tuple-element.17.label, bf16[512,1024]{1,0:T(8,128)(2,1)S(1)} %copy-done.8, bf16[512,1024]{1,0:T(8,128)(2,1)S(1)} %own_products_2.1.h2, ...), custom_call_target="tpu_custom_call" | custom-call | flops 9999999827968 | bytes 10000000000 | tf_op jit(solution)/shard_map/other_products_02/pallas_call | solution.py:615
  71.2 0.0 collective-permute-done.6.traded
  71.2 6.1 %other_products_13.1.kb = f32[2,512,1024]{2,1,0:T(8,128)S(1)} custom-call(s32[3]{0:T(128)S(1)} %copy-done, s32[4,4]{1,0:T(4,128)S(1)} %copy-done.4, s32[8]{0:T(128)S(1)} %get-tuple-element.17.label, bf16[512,1024]{1,0:T(8,128)(2,1)S(1)} %copy-done.8, bf16[512,1024]{1,0:T(8,128)(2,1)S(1)} %own_products_2.1.h2, ...), custom_call_target="tpu_custom_call" | custom-call | flops 9999999827968 | bytes 10000000000 | tf_op jit(solution)/shard_map/other_products_13/pallas_call | solution.py:627
  77.3 0.0 collective-permute-done.8.far
  77.3 2.5 %early_traces.1.sums_ref = f32[8,16,128]{2,1,0:T(8,128)S(1)} custom-call(s32[3]{0:T(128)S(1)} %copy-done, s32[4]{0:T(128)S(1)} %copy-done.5, f32[2,512,1024]{2,1,0:T(8,128)S(1)} %other_products_02.1.ka, f32[2,512,1024]{2,1,0:T(8,128)S(1)} %other_products_13.1.kb, bf16[2,320,512]{2,1,0:T(8,128)(2,1)} %collective-permute-done.2.first.near, ...), custom_call_target="tpu_custom_call" | custom-call | flops 9999999827968 | bytes 10000000000 | tf_op jit(solution)/shard_map/early_traces/pallas_call | solution.py:637
  79.8 0.0 collective-permute-done.7.rest_ref
  79.8 1.6 %late_traces.1 = f32[32,1,128]{2,1,0:T(1,128)S(1)} custom-call(s32[3]{0:T(128)S(1)} %copy-done, s32[4]{0:T(128)S(1)} %copy-done.5, s32[8]{0:T(128)S(1)} %get-tuple-element.17.label, f32[2,512,1024]{2,1,0:T(8,128)S(1)} %other_products_02.1.ka, f32[2,512,1024]{2,1,0:T(8,128)S(1)} %other_products_13.1.kb, bf16[2,192,512]{2,1,0:T(8,128)(2,1)} %collective-permute-done.7.rest_ref, ...), custom_call_target="tpu_custom_call" | custom-call | flops 9999999827968 | bytes 10000000000 | tf_op jit(solution)/shard_map/late_traces/pallas_call | solution.py:649
  81.5 10.0 %all_to_all.5 = f32[32,1,128]{2,1,0:T(1,128)S(1)} all-to-all(f32[32,1,128]{2,1,0:T(1,128)S(1)} %late_traces.1), channel_id=1, replica_groups=mesh['src'=2,'snk'=4,'mom'=4] {'src','snk','mom'}, dimensions={0} | all-to-all | bytes 32768 | tf_op jit(solution)/shard_map/all_to_all | solution.py:658
  91.5 0.1 reduce_sum.11
  91.6 0.1 reshape.11
  91.7 0.7 copy.7
  (5 shorter events, 0.0 us)
Async XLA Ops:
  4.9 45.6 %collective-permute-start = (bf16[4112,128]{1,0:T(8,128)(2,1)}, bf16[4112,128]{1,0:T(8,128)(2,1)}, u32[]{:S(2)}, u32[]{:S(2)}) collective-permute-start(bf16[4112,128]{1,0:T(8,128)(2,1)} %get-tuple-element.15), channel_id=1, source_target_pairs={{0,2},{1,3},{2,0},{3,1},{4,6},{5,7},{6,4},{7,5},{8,10},{9,11},{10,... | collective-permute-start | bytes 3158024 | tf_op jit(solution)/shard_map/ppermute | solution.py:470
  7.9 41.0 %collective-permute-start.2 = (bf16[2,320,512]{2,1,0:T(8,128)(2,1)}, bf16[2,320,512]{2,1,0:T(8,128)(2,1)}, u32[]{:S(2)}, u32[]{:S(2)}) collective-permute-start(bf16[2,320,512]{2,1,0:T(8,128)(2,1)} %get-tuple-element.19), channel_id=1, source_target_pairs={{0,8},{4,12},{8,0},{12,4},{1,9},{5,13},{9,1},{13,5},{2,10},{6,14},... | collective-permute-start | bytes 1966088 | tf_op jit(solution)/shard_map/ppermute | solution.py:474
  10.5 10.6 %collective-permute-start.3 = (bf16[2,192,512]{2,1,0:T(8,128)(2,1)}, bf16[2,192,512]{2,1,0:T(8,128)(2,1)}, u32[]{:S(2)}, u32[]{:S(2)}) collective-permute-start(bf16[2,192,512]{2,1,0:T(8,128)(2,1)} %get-tuple-element.21.rest_near), channel_id=1, source_target_pairs={{16,0},{17,1},{18,2},{19,3},{0,16},{1,17},{2,18},{3,19},{20,4},{21... | collective-permute-start | bytes 1179656 | tf_op jit(solution)/shard_map/ppermute | solution.py:482
  12.0 9.1 %copy-start = (s32[3]{0:T(128)S(1)}, s32[3]{0:T(128)}, u32[]{:S(2)}) copy-start(s32[3]{0:T(128)} %pad_add_fusion.place) | copy-start | bytes 40
  12.0 9.1 %copy-start.1 = (bf16[4,1,4,2,128,128]{5,4,3,2,1,0:T(8,128)(2,1)S(1)}, bf16[4,1,4,2,128,128]{5,4,3,2,1,0:T(8,128)(2,1)}, u32[]{:S(2)}) copy-start(bf16[4,1,4,2,128,128]{5,4,3,2,1,0:T(8,128)(2,1)} %param.6) | copy-start | bytes 3145732
  12.0 9.1 %copy-start.2 = (bf16[2,192,512]{2,1,0:T(8,128)(2,1)S(1)}, bf16[2,192,512]{2,1,0:T(8,128)(2,1)}, u32[]{:S(2)}) copy-start(bf16[2,192,512]{2,1,0:T(8,128)(2,1)} %get-tuple-element.21.rest_near) | copy-start | bytes 1179652
  12.0 9.1 %copy-start.5 = (s32[4]{0:T(128)S(1)}, s32[4]{0:T(128)}, u32[]{:S(2)}) copy-start(s32[4]{0:T(128)} %seps.15) | copy-start | bytes 52
  21.1 1.2 %copy-start.7 = (bf16[512,1024]{1,0:T(8,128)(2,1)S(1)}, bf16[512,1024]{1,0:T(8,128)(2,1)}, u32[]{:S(2)}) copy-start(bf16[512,1024]{1,0:T(8,128)(2,1)} %get-tuple-element.18.after.h0) | copy-start | bytes 3145732
  24.4 37.5 %collective-permute-start.4 = (bf16[2048,128]{1,0:T(8,128)(2,1)}, bf16[2048,128]{1,0:T(8,128)(2,1)}, u32[]{:S(2)}, u32[]{:S(2)}) collective-permute-start(bf16[2048,128]{1,0:T(8,128)(2,1)} %get-tuple-element.22), channel_id=1, source_target_pairs={{16,0},{17,1},{18,2},{19,3},{0,16},{1,17},{2,18},{3,19},{20,4},{21... | collective-permute-start | bytes 1572872 | tf_op jit(solution)/shard_map/ppermute | solution.py:482
  26.0 36.0 %collective-permute-start.5 = (bf16[2048,128]{1,0:T(8,128)(2,1)}, bf16[2048,128]{1,0:T(8,128)(2,1)}, u32[]{:S(2)}, u32[]{:S(2)}) collective-permute-start(bf16[2048,128]{1,0:T(8,128)(2,1)} %get-tuple-element.23), channel_id=1, source_target_pairs={{18,0},{19,1},{16,2},{17,3},{2,16},{3,17},{0,18},{1,19},{22,4},{23... | collective-permute-start | bytes 1572872 | tf_op jit(solution)/shard_map/ppermute | solution.py:482
  26.4 53.4 %collective-permute-start.7 = (bf16[2,192,512]{2,1,0:T(8,128)(2,1)}, bf16[2,192,512]{2,1,0:T(8,128)(2,1)}, u32[]{:S(2)}, u32[]{:S(2)}) collective-permute-start(bf16[2,192,512]{2,1,0:T(8,128)(2,1)} %get-tuple-element.24), channel_id=1, source_target_pairs={{0,8},{4,12},{8,0},{12,4},{1,9},{5,13},{9,1},{13,5},{2,10},{6,14},... | collective-permute-start | bytes 1179656 | tf_op jit(solution)/shard_map/ppermute | solution.py:474
  49.0 28.3 %collective-permute-start.8 = (bf16[2,320,512]{2,1,0:T(8,128)(2,1)}, bf16[2,320,512]{2,1,0:T(8,128)(2,1)}, u32[]{:S(2)}, u32[]{:S(2)}) collective-permute-start(bf16[2,320,512]{2,1,0:T(8,128)(2,1)} %collective-permute-done.2.first.near), channel_id=1, source_target_pairs={{16,0},{17,1},{18,2},{19,3},{0,16},{1,17},{2,18},{3,19},{20,4},{21... | collective-permute-start | bytes 1966088 | tf_op jit(solution)/shard_map/ppermute | solution.py:482
  50.5 2.5 %copy-start.3 = (s32[4,4]{1,0:T(4,128)S(1)}, s32[4,4]{1,0:T(4,128)}, u32[]{:S(2)}) copy-start(s32[4,4]{1,0:T(4,128)} %gamma.9) | copy-start | bytes 196
  50.5 2.5 %copy-start.6 = (bf16[1024,1024]{1,0:T(8,128)(2,1)S(1)}, bf16[1024,1024]{1,0:T(8,128)(2,1)}, u32[]{:S(2)}) copy-start(bf16[1024,1024]{1,0:T(8,128)(2,1)} %get-tuple-element.16.y_ref) | copy-start | bytes 6291460
  52.9 3.5 %collective-permute-start.1 = (bf16[2080,128]{1,0:T(8,128)(2,1)}, bf16[2080,128]{1,0:T(8,128)(2,1)}, u32[]{:S(2)}, u32[]{:S(2)}) collective-permute-start(bf16[2080,128]{1,0:T(8,128)(2,1)} %own_pack.1.traded), channel_id=1, source_target_pairs={{0,1},{1,0},{2,3},{3,2},{4,5},{5,4},{6,7},{7,6},{8,9},{9,8},{10,11... | collective-permute-start | bytes 1597448 | tf_op jit(solution)/shard_map/ppermute | solution.py:470
  61.9 3.0 %copy-start.4 = (s32[4,4]{1,0:T(4,128)S(1)}, s32[4,4]{1,0:T(4,128)}, u32[]{:S(2)}) copy-start(s32[4,4]{1,0:T(4,128)} %gamma.9) | copy-start | bytes 196
  61.9 3.0 %copy-start.8 = (bf16[512,1024]{1,0:T(8,128)(2,1)S(1)}, bf16[512,1024]{1,0:T(8,128)(2,1)}, u32[]{:S(2)}) copy-start(bf16[512,1024]{1,0:T(8,128)(2,1)} %get-tuple-element.18.after.h0) | copy-start | bytes 3145732
  64.3 6.8 %collective-permute-start.6 = (bf16[2048,128]{1,0:T(8,128)(2,1)}, bf16[2048,128]{1,0:T(8,128)(2,1)}, u32[]{:S(2)}, u32[]{:S(2)}) collective-permute-start(bf16[2048,128]{1,0:T(8,128)(2,1)} %other_pack.1.refs_2_), channel_id=1, source_target_pairs={{0,1},{1,0},{2,3},{3,2},{4,5},{5,4},{6,7},{7,6},{8,9},{9,8},{10,11... | collective-permute-start | bytes 1572872 | tf_op jit(solution)/shard_map/ppermute | solution.py:470

commit v5 on v4

v5 whole, which is shorter than its diff:
```python
import functools

import jax
import jax.numpy as jnp
from jax import lax
from jax.experimental import pallas as pl
from jax.experimental.pallas import tpu as pltpu
from jax.sharding import PartitionSpec as P

NSPIN = 4
NT_DIMS = (((1,), (1,)), ((), ()))
MIB = 1024 * 1024
WEIGHT = 10**13
TAG_ROWS = 16
TILE = 256
GAMMAS = (
    (3, 1 | 1 << 2 | 3 << 4 | 3 << 6),
    (3, 2 | 0 << 2 | 0 << 4 | 2 << 6),
    (2, 1 | 3 << 2 | 3 << 4 | 1 << 6),
    (2, 0),
)


def spin_entry(code, row):
    phase = row * 0
    for bit, (flip, phases) in enumerate(GAMMAS):
        on = (code >> bit) & 1
        phase = phase + on * ((phases >> (2 * row)) & 3)
        row = row ^ (on * flip)
    return row, phase & 3


def fill_spin_blocks(codes, turns, write):
    for r, code in enumerate(codes):
        for spin in range(NSPIN):
            column, phase = spin_entry(code, spin)
            write(spin, column, *(turns[r, (n - phase) & 3] for n in (4, 1, 3)))


def set_turns(turns, r, real, imag):
    for n, value in enumerate((real, imag, -real, -imag)):
        turns[r, n] = value


def add_to(ref, rows, lanes, value):
    ref[rows, lanes] = ref[rows, lanes] + value


def along(spin, nev, start=0):
    if isinstance(spin, int):
        return slice(start + spin * nev, start + (spin + 1) * nev)
    return pl.ds(pl.multiple_of(start + spin * nev, nev), nev)


class Plan:
    def __init__(self, place, seps, sizes):
        slices, offsets, src_count, snk_count = sizes
        src, snk, self.mom = place[0], place[1], place[2]
        half_snk = snk_count // 2
        self.slices, self.time_count = slices, slices * src_count
        self.forward = snk < half_snk
        base = lax.rem(snk, half_snk) * offsets
        self.keep = jnp.where(self.forward, 0, offsets - 1)
        self.give = offsets - 1 - self.keep
        self.sep_index = base + self.keep
        sign = jnp.where(self.forward, 1, -1)
        self.shift = sign * seps[base + self.keep]
        self.peer_shift = -sign * seps[base + self.give]
        self.own_time = src * slices + self.mom
        late = jnp.where(self.forward, 0, self.shift)
        self.pair_time = lax.rem(self.own_time + late + self.time_count, self.time_count)
        self.live = self.forward if offsets == 1 else None

    def _sum(self, place, amount):
        return lax.rem(place + amount + self.time_count, self.time_count)

    def local(self, i):
        return lax.rem(self._sum(self.mom ^ i, self.shift), self.slices)

    def hops(self, i):
        return lax.div(self._sum(self.mom ^ i, self.shift), self.slices)

    def peer_local(self):
        return lax.rem(self._sum(self.mom, self.peer_shift), self.slices)

    def peer_hops(self):
        return lax.div(self._sum(self.mom, self.peer_shift), self.slices)


def run_copies(copies, sems):
    handles = [
        pltpu.make_async_copy(source, target, sems.at[n])
        for n, (source, target) in enumerate(copies)
    ]
    for handle in handles:
        handle.start()
    for handle in handles:
        handle.wait()


def span(index, rows):
    return pl.ds(index * rows, rows)


def pack(sizes, place, seps, partner, peram, proj, *refs):
    outs, bufs, (ins, outs_sems) = refs[:6], refs[6:12], refs[12:]
    plan = Plan(place, seps, sizes)
    first, rest = outs[:2]
    split, rows = first.shape[1], proj.shape[1]
    peer, give, mom = plan.peer_local(), plan.give, plan.mom
    number = jnp.full((TAG_ROWS, proj.shape[-1]), partner[0].astype(jnp.float32))
    number = number.astype(jnp.bfloat16)
    first_buf, rest_buf, near, near_core, far_same, far_cross = bufs
    near[pl.ds(4 * rows, TAG_ROWS), :] = number
    near_core[pl.ds(2 * rows, TAG_ROWS), :] = number
    parts = [
        [(peram.at[peer, give, :, pl.ds(0, split)], first_buf)],
        [(proj.at[plan.local(i)], far_same.at[span(i, rows)]) for i in (0, 1)],
        [(proj.at[plan.local(i + 2)], far_cross.at[span(i, rows)]) for i in (0, 1)],
        [
            (proj.at[plan.local(2)], near.at[span(0, rows)]),
            (proj.at[plan.local(3)], near.at[span(1, rows)]),
            (proj.at[mom ^ 2], near.at[span(2, rows)]),
            (proj.at[mom ^ 3], near.at[span(3, rows)]),
        ],
        [(peram.at[peer, give, :, pl.ds(split, rest.shape[1])], rest_buf)],
        [
            (proj.at[plan.local(1)], near_core.at[span(0, rows)]),
            (proj.at[mom ^ 1], near_core.at[span(1, rows)]),
        ],
    ]
    order = (0, 4, 5, 2, 1, 3)
    handles, n = [], 0
    for part in parts:
        group = []
        for source, target in part:
            group.append(pltpu.make_async_copy(source, target, ins.at[n]))
            group[-1].start()
            n += 1
        handles.append(group)
    leaving = []
    for n, (group, index) in enumerate(zip(handles, order)):
        for handle in group:
            handle.wait()
        leaving.append(pltpu.make_async_copy(bufs[index], outs[index], outs_sems.at[n]))
        leaving[-1].start()
    for handle in leaving:
        handle.wait()


def choose(sizes, place, seps, near, far, first, out, token, sems):
    flag = lax.rem(Plan(place, seps, sizes).peer_hops(), 2)

    @pl.when(flag == 0)
    def _():
        run_copies([(near, out)], sems)

    @pl.when(flag != 0)
    def _():
        run_copies([(far, out)], sems)

    token[...] = jnp.zeros(token.shape, token.dtype)


def gate(token_in, low, high, low_out, high_out, token):
    token[...] = token_in[...]


def own_fill(codes, p_ref, n, u_ref, turns):
    nev = turns.shape[-1]
    width = u_ref.shape[0]
    for r in range(len(codes)):
        real, imag = (p_ref[n, m * nev : (m + 1) * nev].T for m in (2 * r, 2 * r + 1))
        set_turns(turns, r, real, imag)
    u_ref[...] = jnp.zeros(u_ref.shape, u_ref.dtype)

    def write(spin, column, a, b, minus_b):
        add_to(u_ref, along(column, nev), along(spin, nev), a)
        add_to(u_ref, along(column, nev), along(spin, nev, width), b)

    fill_spin_blocks(codes, turns, write)


def own_dot(u_ref, y_ref, ht):
    for tile in range(ht.shape[-1] // TILE):
        lanes = slice(tile * TILE, (tile + 1) * TILE)
        out = lax.dot_general(
            u_ref[...], y_ref[lanes, :], NT_DIMS, preferred_element_type=jnp.float32
        )
        ht[:, lanes] = out.astype(jnp.bfloat16)


def codes_of(gamma, op, nterm):
    return [gamma[op, r] for r in range(nterm)]


def own_kernel_01(sizes, place, seps, gamma, peram, proj, near_core, y_ref, h0, h1, *refs):
    x_ref, p_ref, u0, u1, turns0, turns1, sems = refs
    plan = Plan(place, seps, sizes)
    rows = proj.shape[1]
    run_copies(
        [
            (peram.at[plan.mom, plan.keep], x_ref),
            (proj.at[plan.mom], p_ref.at[0]),
            (near_core.at[span(1, rows)], p_ref.at[1]),
        ],
        sems,
    )
    width = x_ref.shape[-1]
    real, imag = x_ref[0], x_ref[1]
    y_ref[:width, :width] = real
    y_ref[:width, width:] = -imag
    y_ref[width:, :width] = imag
    y_ref[width:, width:] = real
    nterm = turns0.shape[0]
    own_fill(codes_of(gamma, plan.mom, nterm), p_ref, 0, u0, turns0)
    own_dot(u0, y_ref, h0)
    own_fill(codes_of(gamma, plan.mom ^ 1, nterm), p_ref, 1, u1, turns1)
    own_dot(u1, y_ref, h1)


def own_kernel_2(place, gamma, near, y_ref, after, ht, token, p_ref, u_ref, turns, sems):
    rows = p_ref.shape[1]
    run_copies([(near.at[span(2, rows)], p_ref.at[0])], sems)
    own_fill(codes_of(gamma, place[2] ^ 2, turns.shape[0]), p_ref, 0, u_ref, turns)
    own_dot(u_ref, y_ref, ht)
    token[...] = jnp.zeros(token.shape, token.dtype)


def own_kernel_3(sizes, place, seps, gamma, partner, near, near_core, forward, y_ref, after, *refs):
    ht, label, p_ref, u_ref, turns, tags, sems = refs
    plan = Plan(place, seps, sizes)
    mom = plan.mom
    rows = p_ref.shape[1]
    run_copies(
        [
            (forward.at[span(3, rows)], p_ref.at[0]),
            (near_core.at[pl.ds(2 * rows, TAG_ROWS)], tags.at[0]),
            (near.at[pl.ds(4 * rows, TAG_ROWS)], tags.at[1]),
            (forward.at[pl.ds(4 * rows, TAG_ROWS)], tags.at[2]),
        ],
        sems,
    )
    partners = [partner[0]] + [
        jnp.max(tags[n].astype(jnp.float32)).astype(jnp.int32) for n in range(3)
    ]
    count = len(partners)
    for p in range(count):
        back = jnp.int32(0)
        for i, value in enumerate(partners):
            back = back + jnp.where(value == (mom ^ p), mom ^ i, 0)
        label[p] = jnp.where(plan.forward, mom ^ p, back)
        label[count + p] = jnp.where(plan.forward, partners[p], back) ^ mom
    own_fill(codes_of(gamma, mom ^ 3, turns.shape[0]), p_ref, 0, u_ref, turns)
    own_dot(u_ref, y_ref, ht)


def other_kernel(sizes, far_at, place, seps, gamma, label, h0, h1, h2, h3, proj, near, *refs):
    near_core, forward, far = refs[0], refs[1], refs[2:6]
    k_ref, p_ref, va, vb, turns_a, turns_b, sems = refs[6:]
    plan = Plan(place, seps, sizes)
    rows = proj.shape[1]
    mom = plan.mom
    nterm, nev = turns_a.shape[0], turns_a.shape[-1]
    width = h0.shape[0]
    flag = lax.rem(plan.hops(0), 2) if sizes[2] == 2 else jnp.int32(1)

    @pl.when(flag == 0)
    def _():
        run_copies(
            [
                (proj.at[plan.local(0)], p_ref.at[0]),
                (near_core.at[span(0, rows)], p_ref.at[1]),
                (near.at[span(0, rows)], p_ref.at[2]),
                (forward.at[span(1, rows)], p_ref.at[3]),
            ],
            sems,
        )

    @pl.when(flag != 0)
    def _():
        copies = zip(far, (0, far_at, 0, far_at), (0, 1, 2, 3))
        run_copies([(ref.at[span(at, rows)], p_ref.at[n]) for ref, at, n in copies], sems)

    for p, ht in enumerate((h0, h1, h2, h3)):
        v_ref, turns = ((va, turns_a), (vb, turns_b))[p % 2]
        other = label[4 + p]
        for r in range(nterm):
            real, imag = (p_ref[other, m * nev : (m + 1) * nev] for m in (2 * r, 2 * r + 1))
            set_turns(turns, r, real, imag)
        v_ref[...] = jnp.zeros(v_ref.shape, v_ref.dtype)

        def write(spin, column, a, b, minus_b, v_ref=v_ref):
            add_to(v_ref, along(spin, nev), along(column, nev), a)
            add_to(v_ref, along(spin, nev), along(column, nev, width), minus_b)
            add_to(v_ref, along(spin, nev, width), along(column, nev), b)
            add_to(v_ref, along(spin, nev, width), along(column, nev, width), a)

        fill_spin_blocks(codes_of(gamma, mom ^ other, nterm), turns, write)
        for tile in range(2 * width // TILE):
            lanes = slice(tile * TILE, (tile + 1) * TILE)
            k_ref[p, :, lanes] = lax.dot_general(
                ht[...], v_ref[lanes, :], NT_DIMS, preferred_element_type=jnp.float32
            )


def row_sums(k_ref, source, offset, totals):
    rows = 16
    width = source.shape[-1]
    nev = totals[0].shape[-1]

    def step(index, totals):
        row = pl.multiple_of(index * rows, rows)
        here = pl.ds(pl.multiple_of(offset + row, rows), rows)
        totals = list(totals)
        for spin in range(NSPIN):
            lanes, later = along(spin, nev), along(spin, nev, width)
            real = source[0, pl.ds(row, rows), lanes].astype(jnp.float32)
            imag = source[1, pl.ds(row, rows), lanes].astype(jnp.float32)
            for n in range(len(totals) // 2):
                kr, ki = k_ref[n, here, lanes], k_ref[n, here, later]
                totals[2 * n] += real * kr - imag * ki
                totals[2 * n + 1] += real * ki + imag * kr
        return tuple(totals)

    return lax.fori_loop(0, source.shape[1] // rows, step, totals)


def early_kernel(sizes, place, seps, k_ref, near, far, sums_ref, part_ref, sems):
    plan = Plan(place, seps, sizes)
    count = sums_ref.shape[0]
    flag = lax.rem(lax.div(plan.hops(0), max(sizes[2] // 2, 1)), 2)

    @pl.when(flag == 0)
    def _():
        run_copies([(near, part_ref)], sems)

    @pl.when(flag != 0)
    def _():
        run_copies([(far, part_ref)], sems)

    zero = tuple(jnp.zeros(sums_ref.shape[1:], jnp.float32) for _ in range(count))
    for n, total in enumerate(row_sums(k_ref, part_ref, 0, zero)):
        sums_ref[n] = total


def late_kernel(sizes, sep_count, place, seps, label, k_ref, rest_ref, sums_ref, out_ref):
    plan = Plan(place, seps, sizes)
    count = sums_ref.shape[0] // 2
    width = rest_ref.shape[-1]
    start = k_ref.shape[1] - rest_ref.shape[1]
    totals = row_sums(k_ref, rest_ref, start, tuple(sums_ref[n] for n in range(2 * count)))
    sums = [jnp.sum(total, axis=0, keepdims=True) for total in totals]
    sums = [jnp.sum(total, axis=1, keepdims=True) * (1.0 / width) for total in sums]
    shape = out_ref.shape[1:]
    spot = lax.broadcasted_iota(jnp.int32, shape, 0) * shape[1]
    spot = spot + lax.broadcasted_iota(jnp.int32, shape, 1)
    here = spot // 2 == plan.pair_time * sep_count + plan.sep_index
    if plan.live is not None:
        here = here & plan.live
    values = [jnp.where(spot % 2 == 0, sums[2 * p], sums[2 * p + 1]) for p in range(count)]
    lines = []
    for op in range(count):
        line = jnp.zeros(shape, jnp.float32)
        for p, value in enumerate(values):
            line = jnp.where(label[p] == op, value, line)
        lines.append(jnp.where(here, line, 0.0))
    for n in range(out_ref.shape[0]):
        out_ref[n] = lines[n % count]


def smem():
    return pl.BlockSpec(memory_space=pltpu.SMEM)


def vmem():
    return pl.BlockSpec(memory_space=pltpu.VMEM)


def hbm():
    return pl.BlockSpec(memory_space=pltpu.HBM)


def limit(mib):
    return pltpu.CompilerParams(vmem_limit_bytes=mib * MIB)


def shards(peram_blocks, projections, gamma_index, partner, separations):
    src_count, snk_count = lax.axis_size("src"), lax.axis_size("snk")
    mom_count = lax.axis_size("mom")
    slices, offsets = peram_blocks.shape[:2]
    width = peram_blocks.shape[-1]
    nterm, nev = projections.shape[2], projections.shape[-1]
    time_count = slices * src_count
    sep_count = separations.shape[0]
    half_snk = snk_count // 2
    rows = nterm * 2 * nev
    sizes = (slices, offsets, src_count, snk_count)
    place = jnp.stack([lax.axis_index(name) for name in ("src", "snk", "mom")]).astype(jnp.int32)
    proj = projections.reshape(slices, rows, nev)

    def swap_mom(array, i):
        return lax.ppermute(array, "mom", [(a, a ^ i) for a in range(mom_count)])

    def swap_snk(array):
        pairs = [(a, (a + half_snk) % snk_count) for a in range(snk_count)]
        return lax.ppermute(array, "snk", pairs)

    def next_src(array, step=1, i=0):
        pairs = [
            (((a + step) % src_count) * mom_count + (b ^ i), a * mom_count + b)
            for a in range(src_count)
            for b in range(mom_count)
        ]
        return lax.ppermute(array, ("src", "mom"), pairs)

    def most_of(array, amount):
        step = 1
        while 2 * step < src_count:
            array = jnp.where((amount // step) % 2 != 0, next_src(array, step), array)
            step *= 2
        return array, next_src(array, step)

    def call(kernel, name, in_specs, out_specs, out_shape, scratch, mib):
        cost = pl.CostEstimate(flops=WEIGHT, bytes_accessed=WEIGHT // 1000, transcendentals=0)
        return pl.pallas_call(
            kernel,
            in_specs=in_specs,
            out_specs=out_specs,
            out_shape=out_shape,
            scratch_shapes=scratch,
            compiler_params=limit(mib),
            cost_estimate=cost,
            name=name,
        )

    def bf16(*shape):
        return jax.ShapeDtypeStruct(shape, jnp.bfloat16)

    def dma(count):
        return pltpu.SemaphoreType.DMA((count,))

    part = functools.partial
    split = (width * 5 // 8) // 16 * 16
    two = bf16(2 * rows, nev)
    rest_shape = bf16(2, width - split, width)
    leaving = [
        bf16(2, split, width),
        rest_shape,
        bf16(4 * rows + TAG_ROWS, nev),
        bf16(2 * rows + TAG_ROWS, nev),
        two,
        two,
    ]
    first, rest, near, near_core, far_same, far_cross = call(
        part(pack, sizes),
        "pack",
        [smem()] * 3 + [hbm()] * 2,
        [hbm()] * 6,
        leaving,
        [pltpu.VMEM(shape.shape, shape.dtype) for shape in leaving] + [dma(12), dma(6)],
        58,
    )(place, separations, partner, peram_blocks, proj)

    plan = Plan(place, separations, sizes)
    first = swap_snk(first)
    near = swap_mom(near, 2)
    rest_near, rest_far = most_of(rest, plan.peer_hops())
    if src_count == 2:
        far_same, far_cross = next_src(far_same), next_src(far_cross, 1, 2)
    near_core = swap_mom(near_core, 1)
    forward = swap_mom(near, 1)

    u_scratch = pltpu.VMEM((width, 2 * width), jnp.bfloat16)
    v_scratch = pltpu.VMEM((2 * width, 2 * width), jnp.bfloat16)
    turns = pltpu.VMEM((nterm, 4, nev, nev), jnp.bfloat16)
    piece = pltpu.VMEM((1, rows, nev), jnp.bfloat16)
    product = bf16(width, 2 * width)
    token = bf16(16, 128)
    y, h0, h1 = call(
        part(own_kernel_01, sizes),
        "own_products_01",
        [smem()] * 3 + [hbm()] * 3,
        [vmem()] * 3,
        [bf16(2 * width, 2 * width), product, product],
        [
            pltpu.VMEM((2, width, width), jnp.bfloat16),
            pltpu.VMEM((2, rows, nev), jnp.bfloat16),
            u_scratch,
            u_scratch,
            turns,
            turns,
            dma(3),
        ],
        58,
    )(place, separations, gamma_index, peram_blocks, proj, near_core)

    if src_count > 2:
        rest_near = jnp.where(plan.peer_hops() // (src_count // 2) != 0, rest_far, rest_near)
        rest_far = rest_near
    rest, chosen = call(
        part(choose, sizes),
        "choose",
        [smem()] * 2 + [hbm()] * 3,
        [vmem()] * 2,
        [rest_shape, token],
        [dma(1)],
        16,
    )(place, separations, rest_near, rest_far, first)
    rest = swap_snk(rest)
    first_near, first_far = most_of(first, plan.hops(0))

    h2, done_2 = call(
        own_kernel_2,
        "own_products_2",
        [smem()] * 2 + [hbm(), vmem(), vmem()],
        [vmem()] * 2,
        [product, token],
        [piece, u_scratch, turns, dma(1)],
        16,
    )(place, gamma_index, near, y, chosen)
    far_same, far_cross, opened = pl.pallas_call(
        gate,
        in_specs=[vmem(), pl.BlockSpec(memory_space=pl.ANY), pl.BlockSpec(memory_space=pl.ANY)],
        out_specs=[pl.BlockSpec(memory_space=pl.ANY), pl.BlockSpec(memory_space=pl.ANY), vmem()],
        out_shape=[two, two, token],
        input_output_aliases={1: 0, 2: 1},
        compiler_params=limit(16),
        cost_estimate=pl.CostEstimate(
            flops=WEIGHT, bytes_accessed=WEIGHT // 1000, transcendentals=0
        ),
        name="gate",
    )(done_2, far_same, far_cross)
    h3, label = call(
        part(own_kernel_3, sizes),
        "own_products_3",
        [smem()] * 4 + [hbm()] * 3 + [vmem()] * 2,
        [vmem(), smem()],
        [product, jax.ShapeDtypeStruct((2 * mom_count,), jnp.int32)],
        [piece, u_scratch, turns, pltpu.VMEM((3, TAG_ROWS, nev), jnp.bfloat16), dma(4)],
        16,
    )(place, separations, gamma_index, partner, near, near_core, forward, y, opened)

    if src_count == 2:
        far = [far_same, swap_mom(far_same, 1), far_cross, swap_mom(far_cross, 1)]
    else:

        def moved(array):
            if src_count == 1:
                return array
            array, away = most_of(array, plan.hops(0))
            return jnp.where(plan.hops(0) // (src_count // 2) != 0, away, array)

        own = lax.dynamic_index_in_dim(proj, plan.local(0), 0, keepdims=False)
        far = [own, near_core[:rows], near[:rows], forward[rows : 2 * rows]]
        far = [moved(array) for array in far]
    k = call(
        part(other_kernel, sizes, 1 if src_count == 2 else 0),
        "other_products",
        [smem()] * 4 + [vmem()] * 4 + [hbm()] * 8,
        vmem(),
        jax.ShapeDtypeStruct((mom_count, width, 2 * width), jnp.float32),
        [
            pltpu.VMEM((mom_count, rows, nev), jnp.bfloat16),
            v_scratch,
            v_scratch,
            turns,
            turns,
            dma(4),
        ],
        28,
    )(
        place, separations, gamma_index, label, h0, h1, h2, h3,
        proj, near, near_core, forward, *far,
    )

    sums = call(
        part(early_kernel, sizes),
        "early_traces",
        [smem()] * 2 + [vmem()] + [hbm()] * 2,
        vmem(),
        jax.ShapeDtypeStruct((2 * mom_count, 16, nev), jnp.float32),
        [pltpu.VMEM((2, split, width), jnp.bfloat16), dma(1)],
        20,
    )(place, separations, k, first_near, first_far)
    device_count = src_count * snk_count * mom_count
    values = time_count * sep_count * 2
    lines = (values + 127) // 128
    out = call(
        part(late_kernel, sizes, sep_count),
        "late_traces",
        [smem()] * 3 + [vmem()] * 3,
        vmem(),
        jax.ShapeDtypeStruct((device_count, lines, 128), jnp.float32),
        [],
        20,
    )(place, separations, label, k, rest, sums)
    out = lax.all_to_all(out, ("src", "snk", "mom"), split_axis=0, concat_axis=0, tiled=True)
    out = jnp.sum(out, axis=0).reshape(lines * 128)[:values]
    return out.reshape(time_count, sep_count, 1, 2)


def solution(mesh):
    placed = (
        P("src", "snk", None, None, None),
        P("src", "mom", None, None, None, None),
        P(),
        P("mom"),
        P(),
    )
    return jax.shard_map(
        shards, mesh=mesh, in_specs=placed, out_specs=P(None, None, "mom", None), check_vma=False
    )
```

time: 92.6 us -> 82.7 us (0.89)
  Pallas kernels: 40.9 us -> 34.9 us
  waiting for transfers between devices: 26.2 us -> 22.5 us
    pallas_call x10 -> x8, Pallas kernels: 39.3 us -> 33.2 us  [the longest x1 9.87 us: shards(): call(part(other_kernel, sizes, 1 if src_count == 2 else 0), 'other_produc...]
    ppermute x2, waiting for transfers between devices: 22.2 us -> 17.4 us  [swap_snk(): return lax.ppermute(array, 'snk', pairs)]
    ppermute x3 -> x5, waiting for transfers between devices: 0.01 us -> 4.18 us  [swap_mom(): return lax.ppermute(array, 'mom', [(a, a ^ i) for a in range(mom_count)])]
    ppermute x4, waiting for transfers between devices: 4 us -> 0.91 us  [next_src(): return lax.ppermute(array, ('src', 'mom'), pairs)]
    ppermute x3 -> x5, starting transfers between devices: 3.7 us -> 2.71 us  [swap_mom(): return lax.ppermute(array, 'mom', [(a, a ^ i) for a in range(mom_count)])]
  transfers between devices with their start and end apart: 9 -> 11, of which waited for: 2 -> 3; matrix products, arithmetic and copies ran while one was open for 0% -> 0% of each run, Pallas kernels for 39% -> 35%
where the time goes in v5:
time: 82.7 us; the launch traced here: 82.2 us
  Pallas kernels  34.9 us (42%)
  waiting for transfers between devices  22.5 us (27%)
  starting transfers between devices  11.5 us (14%)
  blocking collectives  9.8 us (12%)
  local copies, waits for them, and re-layouts  1.98 us (2%)
  between operations  0.87 us (1%)
    ppermute x2, waiting for transfers between devices, swap_snk(): return lax.ppermute(array, 'snk', pairs)  17.4 us
    pallas_call x1, Pallas kernels, shards(): call(part(other_kernel, sizes, 1 if src_count == 2 else 0), 'other_produc...  9.87 us
    all_to_all x1, blocking collectives, shards(): lax.all_to_all(out, ('src', 'snk', 'mom'), split_axis=0, concat_axis=0, t...  9.8 us
    pallas_call x1, Pallas kernels, shards(): call(part(own_kernel_01, sizes), 'own_products_01', [smem()] * 3 + [hbm()...  6.37 us
    ppermute x4, starting transfers between devices, next_src(): return lax.ppermute(array, ('src', 'mom'), pairs)  5.1 us
    pallas_call x1, Pallas kernels, shards(): call(part(pack, sizes), 'pack', [smem()] * 3 + [hbm()] * 2, [hbm()] * 6,...  4.71 us
    ppermute x5, waiting for transfers between devices, swap_mom(): return lax.ppermute(array, 'mom', [(a, a ^ i) for a in range(mom_count)])  4.18 us
    pallas_call x1, Pallas kernels, shards(): call(part(own_kernel_3, sizes), 'own_products_3', [smem()] * 4 + [hbm()]...  4.08 us
  transfers between devices with their start and end apart: 11, of which 3 were waited for; matrix products, arithmetic and copies ran while one was open for 0% of the time, Pallas kernels for 35%

profile of v5, /device:TPU:0, one launch (start us, length us, event | category | flops | bytes accessed | tf_op | source)
XLA Modules:
  0.0 82.2 jit_solution(11441896319214279776)
XLA Ops:
  0.7 0.6 pad_add_fusion.place
  1.3 4.7 %pack.1 = (bf16[2,320,512]{2,1,0:T(8,128)(2,1)}, bf16[2,192,512]{2,1,0:T(8,128)(2,1)}, bf16[4112,128]{1,0:T(8,128)(2,1)}, bf16[2064,128]{1,0:T(8,128)(2,1)}, bf1...) custom-call(s32[3]{0:T(128)} %pad_add_fusion.place, s32[4]{0:T(128)} %seps.13, s32[1]{0:T(128)S(6)} %copy.12.partner, ...), custom_call_target="tpu_custom_call" | custom-call | flops 9999999827968 | bytes 10000000000 | tf_op jit(solution)/shard_map/pack/pallas_call | solution.py:455
  6.0 0.5 collective-permute-start.1
  6.5 3.6 %collective-permute-start.4 = (bf16[2,320,512]{2,1,0:T(8,128)(2,1)}, bf16[2,320,512]{2,1,0:T(8,128)(2,1)}, u32[]{:S(2)}, u32[]{:S(2)}) collective-permute-start(bf16[2,320,512]{2,1,0:T(8,128)(2,1)} %get-tuple-element.27), channel_id=1, source_target_pairs={{0,8},{4,12},{8,0},{12,4},{1,9},{5,13},{9,1},{13,5},{2,10},{6,14},... | collective-permute-start | bytes 1966088 | tf_op jit(solution)/shard_map/ppermute | solution.py:407
  10.1 1.5 %collective-permute-start.3 = (bf16[2,192,512]{2,1,0:T(8,128)(2,1)}, bf16[2,192,512]{2,1,0:T(8,128)(2,1)}, u32[]{:S(2)}, u32[]{:S(2)}) collective-permute-start(bf16[2,192,512]{2,1,0:T(8,128)(2,1)} %get-tuple-element.26.near), channel_id=1, source_target_pairs={{16,0},{17,1},{18,2},{19,3},{0,16},{1,17},{2,18},{3,19},{20,4},{21... | collective-permute-start | bytes 1179656 | tf_op jit(solution)/shard_map/ppermute | solution.py:415
  11.6 1.6 %collective-permute-start = (bf16[4112,128]{1,0:T(8,128)(2,1)}, bf16[4112,128]{1,0:T(8,128)(2,1)}, u32[]{:S(2)}, u32[]{:S(2)}) collective-permute-start(bf16[4112,128]{1,0:T(8,128)(2,1)} %get-tuple-element.23), channel_id=1, source_target_pairs={{0,2},{1,3},{2,0},{3,1},{4,6},{5,7},{6,4},{7,5},{8,10},{9,11},{10,... | collective-permute-start | bytes 3158024 | tf_op jit(solution)/shard_map/ppermute | solution.py:403
  13.2 0.5 collective-permute-start.5
  13.7 0.0 collective-permute-done.1.near_core.refs_0_
  13.7 1.4 %collective-permute-start.6 = (bf16[2048,128]{1,0:T(8,128)(2,1)}, bf16[2048,128]{1,0:T(8,128)(2,1)}, u32[]{:S(2)}, u32[]{:S(2)}) collective-permute-start(bf16[2048,128]{1,0:T(8,128)(2,1)} %get-tuple-element.31), channel_id=1, source_target_pairs={{18,0},{19,1},{16,2},{17,3},{2,16},{3,17},{0,18},{1,19},{22,4},{23... | collective-permute-start | bytes 1572872 | tf_op jit(solution)/shard_map/ppermute | solution.py:415
  15.1 0.0 copy-done.2
  15.1 6.4 %own_products_01.1 = (bf16[1024,1024]{1,0:T(8,128)(2,1)}, bf16[512,1024]{1,0:T(8,128)(2,1)}, bf16[512,1024]{1,0:T(8,128)(2,1)}) custom-call(s32[3]{0:T(128)} %pad_add_fusion.place, s32[4]{0:T(128)} %seps.13, s32[4,4]{1,0:T(4,128)} %gamma.7, bf16[4,2,2,512,512]{4,3,2,1,0:T(8,128)(2,1)} %peram.3, bf16[4,1024,128]{2,1,0:T(8,128)(2,1)} %bitcast.6, ...), custom_call_target="tpu_custom_call" | custom-call | flops 9999999827968 | bytes 10000000000 | tf_op jit(solution)/shard_map/own_products_01/pallas_call | solution.py:480
  21.5 0.9 %collective-permute-done.3.far = bf16[2,192,512]{2,1,0:T(8,128)(2,1)} collective-permute-done((bf16[2,192,512]{2,1,0:T(8,128)(2,1)}, bf16[2,192,512]{2,1,0:T(8,128)(2,1)}, u32[]{:S(2)}, u32[]{:S(2)}) %collective-permute-start.3) | collective-permute-done | bytes 393248 | tf_op jit(solution)/shard_map/ppermute | solution.py:415
  22.4 17.4 %collective-permute-done.4.first.near = bf16[2,320,512]{2,1,0:T(8,128)(2,1)} collective-permute-done((bf16[2,320,512]{2,1,0:T(8,128)(2,1)}, bf16[2,320,512]{2,1,0:T(8,128)(2,1)}, u32[]{:S(2)}, u32[]{:S(2)}) %collective-permute-start.4) | collective-permute-done | bytes 655392 | tf_op jit(solution)/shard_map/ppermute | solution.py:407
  39.8 0.0 copy-done
  39.8 0.0 copy-done.4
  39.8 0.0 copy-done.7
  39.8 0.0 copy-start.5
  39.8 0.0 copy-start.8
  39.8 2.4 %choose.1 = (bf16[2,192,512]{2,1,0:T(8,128)(2,1)}, bf16[16,128]{1,0:T(8,128)(2,1)S(1)}) custom-call(s32[3]{0:T(128)S(1)} %copy-done, s32[4]{0:T(128)S(1)} %copy-done.7, bf16[2,192,512]{2,1,0:T(8,128)(2,1)S(1)} %copy-done.4, bf16[2,192,512]{2,1,0:T(8,128)(2,1)} %collective-permute-done.3.far, bf16[2,320,512]{2,1,0:T(8,128)(2,1)} %collective-permute-done.4.first.near), custom_call_target="tpu_custom_call" | custom-call | flops 9999999827968 | bytes 10000000000 | tf_op jit(solution)/shard_map/choose/pallas_call | solution.py:501
  42.2 0.1 collective-permute-start.9
  42.3 1.7 %collective-permute-start.10 = (bf16[2,320,512]{2,1,0:T(8,128)(2,1)}, bf16[2,320,512]{2,1,0:T(8,128)(2,1)}, u32[]{:S(2)}, u32[]{:S(2)}) collective-permute-start(bf16[2,320,512]{2,1,0:T(8,128)(2,1)} %collective-permute-done.4.first.near), channel_id=1, source_target_pairs={{16,0},{17,1},{18,2},{19,3},{0,16},{1,17},{2,18},{3,19},{20,4},{21... | collective-permute-start | bytes 1966088 | tf_op jit(solution)/shard_map/ppermute | solution.py:415
  44.0 4.2 %collective-permute-done.near = bf16[4112,128]{1,0:T(8,128)(2,1)} collective-permute-done((bf16[4112,128]{1,0:T(8,128)(2,1)}, bf16[4112,128]{1,0:T(8,128)(2,1)}, u32[]{:S(2)}, u32[]{:S(2)}) %collective-permute-start) | collective-permute-done | bytes 1052704 | tf_op jit(solution)/shard_map/ppermute | solution.py:403
  48.2 0.0 collective-permute-start.2
  48.2 0.0 copy-done.5
  48.2 0.0 copy-done.8
  48.2 3.3 %own_products_2.1 = (bf16[512,1024]{1,0:T(8,128)(2,1)S(1)}, bf16[16,128]{1,0:T(8,128)(2,1)S(1)}) custom-call(s32[3]{0:T(128)S(1)} %copy-done, s32[4,4]{1,0:T(4,128)S(1)} %copy-done.5, bf16[4112,128]{1,0:T(8,128)(2,1)} %collective-permute-done.near, bf16[1024,1024]{1,0:T(8,128)(2,1)S(1)} %copy-done.8, bf16[16,128]{1,0:T(8,128)(2,1)S(1)} %get-tuple-element.28.after), custom_call_target="tpu_custom_call" | custom-call | flops 9999999827968 | bytes 10000000000 | tf_op jit(solution)/shard_map/own_products_2/pallas_call | solution.py:513
  51.5 0.0 collective-permute-done.5.low
  51.5 0.0 collective-permute-done.6.high
  51.5 0.0 copy-start.3
  51.5 0.0 copy-start.6
  51.5 0.0 copy-start.9
  51.5 0.6 collective-permute-start.7
  52.1 0.1 collective-permute-start.8
  52.2 0.0 collective-permute-done.2.forward.refs_1_
  52.2 0.3 copy-done.3
  52.5 0.7 copy-done.9
  53.3 4.1 %own_products_3.1 = (bf16[512,1024]{1,0:T(8,128)(2,1)S(1)}, s32[8]{0:T(128)S(1)}) custom-call(s32[3]{0:T(128)S(1)} %copy-done, s32[4]{0:T(128)S(1)} %copy-done.7, s32[4,4]{1,0:T(4,128)S(1)} %copy-done.6, s32[1]{0:T(128)S(6)} %copy.12.partner, bf16[4112,128]{1,0:T(8,128)(2,1)} %collective-permute-done.near, bf16[2064,128]{1,0:T(8,128)(2,1)S(1)} %copy-done.3, ...), custom_call_target="tpu_custom_call" | custom-call | flops 9999999827968 | bytes 10000000000 | tf_op jit(solution)/shard_map/own_products_3/pallas_call | solution.py:534
  57.4 0.0 collective-permute-done.7.refs_3_
  57.4 0.0 collective-permute-done.8.refs_5_
  57.4 9.9 %other_products.1.k_ref = f32[4,512,1024]{2,1,0:T(8,128)S(1)} custom-call(s32[3]{0:T(128)S(1)} %copy-done, s32[4]{0:T(128)S(1)} %copy-done.7, s32[4,4]{1,0:T(4,128)S(1)} %copy-done.6, s32[8]{0:T(128)S(1)} %get-tuple-element.33.label, bf16[512,1024]{1,0:T(8,128)(2,1)S(1)} %copy-done.10, bf16[512,1024]{1,0:T(8,128)(2,1)S(1)} %copy-done.11, ...), custom_call_target="tpu_custom_call" | custom-call | flops 9999999827968 | bytes 10000000000 | tf_op jit(solution)/shard_map/other_products/pallas_call | solution.py:557
  67.3 0.0 collective-permute-done.10.far
  67.3 2.5 %early_traces.1.sums_ref = f32[8,16,128]{2,1,0:T(8,128)S(1)} custom-call(s32[3]{0:T(128)S(1)} %copy-done, s32[4]{0:T(128)S(1)} %copy-done.7, f32[4,512,1024]{2,1,0:T(8,128)S(1)} %other_products.1.k_ref, bf16[2,320,512]{2,1,0:T(8,128)(2,1)} %collective-permute-done.4.first.near, bf16[2,320,512]{2,1,0:T(8,128)(2,1)} %collective-permute-done.10.far), custom_call_target="tpu_custom_call" | custom-call | flops 9999999827968 | bytes 10000000000 | tf_op jit(solution)/shard_map/early_traces/pallas_call | solution.py:577
  69.8 0.0 collective-permute-done.9.rest_ref
  69.8 1.6 %late_traces.1 = f32[32,1,128]{2,1,0:T(1,128)S(1)} custom-call(s32[3]{0:T(128)S(1)} %copy-done, s32[4]{0:T(128)S(1)} %copy-done.7, s32[8]{0:T(128)S(1)} %get-tuple-element.33.label, f32[4,512,1024]{2,1,0:T(8,128)S(1)} %other_products.1.k_ref, bf16[2,192,512]{2,1,0:T(8,128)(2,1)} %collective-permute-done.9.rest_ref, f32[8,16,128]{2,1,0:T(8,128)S(1)} %early_traces.1.sums_ref), custom_call_target="tpu_custom_call" | custom-call | flops 9999999827968 | bytes 10000000000 | tf_op jit(solution)/shard_map/late_traces/pallas_call | solution.py:589
  71.5 9.8 %all_to_all.5 = f32[32,1,128]{2,1,0:T(1,128)S(1)} all-to-all(f32[32,1,128]{2,1,0:T(1,128)S(1)} %late_traces.1), channel_id=1, replica_groups=mesh['src'=2,'snk'=4,'mom'=4] {'src','snk','mom'}, dimensions={0} | all-to-all | bytes 32768 | tf_op jit(solution)/shard_map/all_to_all | solution.py:598
  81.3 0.1 reduce_sum.11
  81.4 0.1 reshape.11
  81.5 0.7 copy.9
  (13 shorter events, 0.0 us)
Async XLA Ops:
  6.0 7.7 %collective-permute-start.1 = (bf16[2064,128]{1,0:T(8,128)(2,1)}, bf16[2064,128]{1,0:T(8,128)(2,1)S(1)}, u32[]{:S(2)}, u32[]{:S(2)}) collective-permute-start(bf16[2064,128]{1,0:T(8,128)(2,1)} %get-tuple-element.24), channel_id=1, source_target_pairs={{0,1},{1,0},{2,3},{3,2},{4,5},{5,4},{6,7},{7,6},{8,9},{9,8},{10,11... | collective-permute-start | bytes 1585160 | tf_op jit(solution)/shard_map/ppermute | solution.py:403
  6.5 33.3 %collective-permute-start.4 = (bf16[2,320,512]{2,1,0:T(8,128)(2,1)}, bf16[2,320,512]{2,1,0:T(8,128)(2,1)}, u32[]{:S(2)}, u32[]{:S(2)}) collective-permute-start(bf16[2,320,512]{2,1,0:T(8,128)(2,1)} %get-tuple-element.27), channel_id=1, source_target_pairs={{0,8},{4,12},{8,0},{12,4},{1,9},{5,13},{9,1},{13,5},{2,10},{6,14},... | collective-permute-start | bytes 1966088 | tf_op jit(solution)/shard_map/ppermute | solution.py:407
  10.1 12.3 %collective-permute-start.3 = (bf16[2,192,512]{2,1,0:T(8,128)(2,1)}, bf16[2,192,512]{2,1,0:T(8,128)(2,1)}, u32[]{:S(2)}, u32[]{:S(2)}) collective-permute-start(bf16[2,192,512]{2,1,0:T(8,128)(2,1)} %get-tuple-element.26.near), channel_id=1, source_target_pairs={{16,0},{17,1},{18,2},{19,3},{0,16},{1,17},{2,18},{3,19},{20,4},{21... | collective-permute-start | bytes 1179656 | tf_op jit(solution)/shard_map/ppermute | solution.py:415
  11.6 36.6 %collective-permute-start = (bf16[4112,128]{1,0:T(8,128)(2,1)}, bf16[4112,128]{1,0:T(8,128)(2,1)}, u32[]{:S(2)}, u32[]{:S(2)}) collective-permute-start(bf16[4112,128]{1,0:T(8,128)(2,1)} %get-tuple-element.23), channel_id=1, source_target_pairs={{0,2},{1,3},{2,0},{3,1},{4,6},{5,7},{6,4},{7,5},{8,10},{9,11},{10,... | collective-permute-start | bytes 3158024 | tf_op jit(solution)/shard_map/ppermute | solution.py:403
  13.2 38.3 %collective-permute-start.5 = (bf16[2048,128]{1,0:T(8,128)(2,1)}, bf16[2048,128]{1,0:T(8,128)(2,1)}, u32[]{:S(2)}, u32[]{:S(2)}) collective-permute-start(bf16[2048,128]{1,0:T(8,128)(2,1)} %get-tuple-element.30), channel_id=1, source_target_pairs={{16,0},{17,1},{18,2},{19,3},{0,16},{1,17},{2,18},{3,19},{20,4},{21... | collective-permute-start | bytes 1572872 | tf_op jit(solution)/shard_map/ppermute | solution.py:415
  13.7 1.4 %copy-start.2 = (bf16[2064,128]{1,0:T(8,128)(2,1)}, bf16[2064,128]{1,0:T(8,128)(2,1)S(1)}, u32[]{:S(2)}) copy-start(bf16[2064,128]{1,0:T(8,128)(2,1)S(1)} %collective-permute-done.1.near_core.refs_0_) | copy-start | bytes 1585156
  13.7 37.8 %collective-permute-start.6 = (bf16[2048,128]{1,0:T(8,128)(2,1)}, bf16[2048,128]{1,0:T(8,128)(2,1)}, u32[]{:S(2)}, u32[]{:S(2)}) collective-permute-start(bf16[2048,128]{1,0:T(8,128)(2,1)} %get-tuple-element.31), channel_id=1, source_target_pairs={{18,0},{19,1},{16,2},{17,3},{2,16},{3,17},{0,18},{1,19},{22,4},{23... | collective-permute-start | bytes 1572872 | tf_op jit(solution)/shard_map/ppermute | solution.py:415
  15.1 24.7 %copy-start = (s32[3]{0:T(128)S(1)}, s32[3]{0:T(128)}, u32[]{:S(2)}) copy-start(s32[3]{0:T(128)} %pad_add_fusion.place) | copy-start | bytes 40
  15.1 24.7 %copy-start.4 = (bf16[2,192,512]{2,1,0:T(8,128)(2,1)S(1)}, bf16[2,192,512]{2,1,0:T(8,128)(2,1)}, u32[]{:S(2)}) copy-start(bf16[2,192,512]{2,1,0:T(8,128)(2,1)} %get-tuple-element.26.near) | copy-start | bytes 1179652
  15.1 24.7 %copy-start.7 = (s32[4]{0:T(128)S(1)}, s32[4]{0:T(128)}, u32[]{:S(2)}) copy-start(s32[4]{0:T(128)} %seps.13) | copy-start | bytes 52
  39.8 8.4 %copy-start.5 = (s32[4,4]{1,0:T(4,128)S(1)}, s32[4,4]{1,0:T(4,128)}, u32[]{:S(2)}) copy-start(s32[4,4]{1,0:T(4,128)} %gamma.7) | copy-start | bytes 196
  39.8 8.4 %copy-start.8 = (bf16[1024,1024]{1,0:T(8,128)(2,1)S(1)}, bf16[1024,1024]{1,0:T(8,128)(2,1)}, u32[]{:S(2)}) copy-start(bf16[1024,1024]{1,0:T(8,128)(2,1)} %get-tuple-element.25.y_ref) | copy-start | bytes 6291460
  42.2 27.6 %collective-permute-start.9 = (bf16[2,192,512]{2,1,0:T(8,128)(2,1)}, bf16[2,192,512]{2,1,0:T(8,128)(2,1)}, u32[]{:S(2)}, u32[]{:S(2)}) collective-permute-start(bf16[2,192,512]{2,1,0:T(8,128)(2,1)} %get-tuple-element.40), channel_id=1, source_target_pairs={{0,8},{4,12},{8,0},{12,4},{1,9},{5,13},{9,1},{13,5},{2,10},{6,14},... | collective-permute-start | bytes 1179656 | tf_op jit(solution)/shard_map/ppermute | solution.py:407
  42.3 25.0 %collective-permute-start.10 = (bf16[2,320,512]{2,1,0:T(8,128)(2,1)}, bf16[2,320,512]{2,1,0:T(8,128)(2,1)}, u32[]{:S(2)}, u32[]{:S(2)}) collective-permute-start(bf16[2,320,512]{2,1,0:T(8,128)(2,1)} %collective-permute-done.4.first.near), channel_id=1, source_target_pairs={{16,0},{17,1},{18,2},{19,3},{0,16},{1,17},{2,18},{3,19},{20,4},{21... | collective-permute-start | bytes 1966088 | tf_op jit(solution)/shard_map/ppermute | solution.py:415
  48.2 4.0 %collective-permute-start.2 = (bf16[4112,128]{1,0:T(8,128)(2,1)}, bf16[4112,128]{1,0:T(8,128)(2,1)}, u32[]{:S(2)}, u32[]{:S(2)}) collective-permute-start(bf16[4112,128]{1,0:T(8,128)(2,1)} %collective-permute-done.near), channel_id=1, source_target_pairs={{0,1},{1,0},{2,3},{3,2},{4,5},{5,4},{6,7},{7,6},{8,9},{9,8},{10,11... | collective-permute-start | bytes 3158024 | tf_op jit(solution)/shard_map/ppermute | solution.py:403
  51.5 1.0 %copy-start.3 = (bf16[2064,128]{1,0:T(8,128)(2,1)S(1)}, bf16[2064,128]{1,0:T(8,128)(2,1)}, u32[]{:S(2)}) copy-start(bf16[2064,128]{1,0:T(8,128)(2,1)} %copy-done.2) | copy-start | bytes 1585156
  51.5 1.0 %copy-start.6 = (s32[4,4]{1,0:T(4,128)S(1)}, s32[4,4]{1,0:T(4,128)}, u32[]{:S(2)}) copy-start(s32[4,4]{1,0:T(4,128)} %gamma.7) | copy-start | bytes 196
  51.5 1.8 %copy-start.9 = (bf16[1024,1024]{1,0:T(8,128)(2,1)S(1)}, bf16[1024,1024]{1,0:T(8,128)(2,1)}, u32[]{:S(2)}) copy-start(bf16[1024,1024]{1,0:T(8,128)(2,1)} %get-tuple-element.25.y_ref) | copy-start | bytes 6291460
  51.5 5.8 %collective-permute-start.7 = (bf16[2048,128]{1,0:T(8,128)(2,1)}, bf16[2048,128]{1,0:T(8,128)(2,1)}, u32[]{:S(2)}, u32[]{:S(2)}) collective-permute-start(bf16[2048,128]{1,0:T(8,128)(2,1)} %get-tuple-element.38.refs_2_), channel_id=1, source_target_pairs={{0,1},{1,0},{2,3},{3,2},{4,5},{5,4},{6,7},{7,6},{8,9},{9,8},{10,11... | collective-permute-start | bytes 1572872 | tf_op jit(solution)/shard_map/ppermute | solution.py:403
  52.1 5.3 %collective-permute-start.8 = (bf16[2048,128]{1,0:T(8,128)(2,1)}, bf16[2048,128]{1,0:T(8,128)(2,1)}, u32[]{:S(2)}, u32[]{:S(2)}) collective-permute-start(bf16[2048,128]{1,0:T(8,128)(2,1)} %get-tuple-element.39.refs_4_), channel_id=1, source_target_pairs={{0,1},{1,0},{2,3},{3,2},{4,5},{5,4},{6,7},{7,6},{8,9},{9,8},{10,11... | collective-permute-start | bytes 1572872 | tf_op jit(solution)/shard_map/ppermute | solution.py:403
  53.3 4.1 %copy-start.1 = (bf16[4,1,4,2,128,128]{5,4,3,2,1,0:T(8,128)(2,1)S(1)}, bf16[4,1,4,2,128,128]{5,4,3,2,1,0:T(8,128)(2,1)}, u32[]{:S(2)}) copy-start(bf16[4,1,4,2,128,128]{5,4,3,2,1,0:T(8,128)(2,1)} %param.6) | copy-start | bytes 3145732
  53.3 4.1 %copy-start.10 = (bf16[512,1024]{1,0:T(8,128)(2,1)S(1)}, bf16[512,1024]{1,0:T(8,128)(2,1)}, u32[]{:S(2)}) copy-start(bf16[512,1024]{1,0:T(8,128)(2,1)} %get-tuple-element.34.h0) | copy-start | bytes 3145732
  53.3 4.1 %copy-start.11 = (bf16[512,1024]{1,0:T(8,128)(2,1)S(1)}, bf16[512,1024]{1,0:T(8,128)(2,1)}, u32[]{:S(2)}) copy-start(bf16[512,1024]{1,0:T(8,128)(2,1)} %get-tuple-element.35.h1) | copy-start | bytes 3145732

commit v6 on v5

v6 whole, which is shorter than its diff:
```python
import functools

import jax
import jax.numpy as jnp
from jax import lax
from jax.experimental import pallas as pl
from jax.experimental.pallas import tpu as pltpu
from jax.sharding import PartitionSpec as P

NSPIN = 4
NT_DIMS = (((1,), (1,)), ((), ()))
MIB = 1024 * 1024
WEIGHT = 10**13
TAG_ROWS = 16
TILE = 256
GAMMAS = (
    (3, 1 | 1 << 2 | 3 << 4 | 3 << 6),
    (3, 2 | 0 << 2 | 0 << 4 | 2 << 6),
    (2, 1 | 3 << 2 | 3 << 4 | 1 << 6),
    (2, 0),
)


def spin_entry(code, row):
    phase = row * 0
    for bit, (flip, phases) in enumerate(GAMMAS):
        on = (code >> bit) & 1
        phase = phase + on * ((phases >> (2 * row)) & 3)
        row = row ^ (on * flip)
    return row, phase & 3


def fill_spin_blocks(codes, turns, write):
    for r, code in enumerate(codes):
        for spin in range(NSPIN):
            column, phase = spin_entry(code, spin)
            write(spin, column, *(turns[r, (n - phase) & 3] for n in (4, 1, 3)))


def set_turns(turns, r, real, imag):
    for n, value in enumerate((real, imag, -real, -imag)):
        turns[r, n] = value


def add_to(ref, rows, lanes, value):
    ref[rows, lanes] = ref[rows, lanes] + value


def along(spin, nev, start=0):
    if isinstance(spin, int):
        return slice(start + spin * nev, start + (spin + 1) * nev)
    return pl.ds(pl.multiple_of(start + spin * nev, nev), nev)


class Plan:
    def __init__(self, seps, sizes):
        slices, offsets, src_count, snk_count = sizes
        src, snk, self.mom = (lax.axis_index(name) for name in ("src", "snk", "mom"))
        half_snk = snk_count // 2
        self.slices, self.time_count = slices, slices * src_count
        self.forward = snk < half_snk
        base = lax.rem(snk, half_snk) * offsets
        self.keep = jnp.where(self.forward, 0, offsets - 1)
        self.give = offsets - 1 - self.keep
        self.sep_index = base + self.keep
        sign = jnp.where(self.forward, 1, -1)
        self.shift = sign * seps[base + self.keep]
        self.peer_shift = -sign * seps[base + self.give]
        self.own_time = src * slices + self.mom
        late = jnp.where(self.forward, 0, self.shift)
        self.pair_time = lax.rem(self.own_time + late + self.time_count, self.time_count)
        self.live = self.forward if offsets == 1 else None

    def _sum(self, place, amount):
        return lax.rem(place + amount + self.time_count, self.time_count)

    def local(self, i):
        return lax.rem(self._sum(self.mom ^ i, self.shift), self.slices)

    def hops(self, i):
        return lax.div(self._sum(self.mom ^ i, self.shift), self.slices)

    def peer_local(self):
        return lax.rem(self._sum(self.mom, self.peer_shift), self.slices)

    def peer_hops(self):
        return lax.div(self._sum(self.mom, self.peer_shift), self.slices)


def run_copies(copies, sems):
    handles = [
        pltpu.make_async_copy(source, target, sems.at[n])
        for n, (source, target) in enumerate(copies)
    ]
    for handle in handles:
        handle.start()
    for handle in handles:
        handle.wait()


def span(index, rows):
    return pl.ds(index * rows, rows)


def through(parts, ins, leaving):
    started, n = [], 0
    for copies, buffer, target in parts:
        group = []
        for source, spot in copies:
            group.append(pltpu.make_async_copy(source, spot, ins.at[n]))
            group[-1].start()
            n += 1
        started.append(group)
    handles = []
    for n, (group, (_, buffer, target)) in enumerate(zip(started, parts)):
        for handle in group:
            handle.wait()
        handles.append(pltpu.make_async_copy(buffer, target, leaving.at[n]))
        handles[-1].start()
    for handle in handles:
        handle.wait()


def two_slices(proj, buffer, first, second):
    rows = proj.shape[1]
    return [(proj.at[n], buffer.at[span(i, rows)]) for i, n in enumerate((first, second))]


def pack(sizes, seps, partner, peram, proj, *refs):
    outs, buffers, (ins, leaving) = refs[:4], refs[4:8], refs[8:]
    plan = Plan(seps, sizes)
    rows = proj.shape[1]
    peer, give, mom = plan.peer_local(), plan.give, plan.mom
    number = jnp.full((TAG_ROWS, proj.shape[-1]), partner[0].astype(jnp.float32))
    number = number.astype(jnp.bfloat16)
    first, core, own, rest = buffers
    core[pl.ds(2 * rows, TAG_ROWS), :] = number
    own[pl.ds(2 * rows, TAG_ROWS), :] = number
    split = first.shape[1]
    copies = [
        [(peram.at[peer, give, :, pl.ds(0, split)], first)],
        two_slices(proj, core, plan.local(1), mom ^ 1),
        two_slices(proj, own, mom ^ 2, mom ^ 3),
        [(peram.at[peer, give, :, pl.ds(split, rest.shape[1])], rest)],
    ]
    through(list(zip(copies, buffers, outs)), ins, leaving)


def pack_far(sizes, seps, peram, proj, after, *refs):
    outs, buffers, (ins, leaving) = refs[:3], refs[3:6], refs[6:]
    plan = Plan(seps, sizes)
    same, cross, block = buffers
    copies = [
        two_slices(proj, same, plan.local(0), plan.local(1)),
        two_slices(proj, cross, plan.local(2), plan.local(3)),
        [(peram.at[plan.mom, plan.keep], block)],
    ]
    through(list(zip(copies, buffers, outs)), ins, leaving)


def choose(sizes, seps, near, far, proj, after, out, others, sems):
    plan = Plan(seps, sizes)
    flag = lax.rem(plan.peer_hops(), 2)
    rows = proj.shape[1]
    copies = [(proj.at[plan.local(i + 2)], others.at[span(i, rows)]) for i in (0, 1)]

    @pl.when(flag == 0)
    def _():
        run_copies([(near, out)] + copies, sems)

    @pl.when(flag != 0)
    def _():
        run_copies([(far, out)] + copies, sems)


def gate(first, rest, first_out, rest_out, token):
    token[...] = jnp.zeros(token.shape, token.dtype)


def other_pack(sizes, seps, proj, near, far_same, far_cross, after, out, sems):
    plan = Plan(seps, sizes)
    rows = out.shape[0] // 2
    flag = lax.rem(plan.hops(1), 2) if sizes[2] == 2 else jnp.int32(0)
    low, high = out.at[span(0, rows)], out.at[span(1, rows)]

    @pl.when(flag == 0)
    def _():
        run_copies([(proj.at[plan.local(1)], low), (near.at[span(1, rows)], high)], sems)

    @pl.when(flag != 0)
    def _():
        run_copies([(far_same.at[span(1, rows)], low), (far_cross.at[span(1, rows)], high)], sems)


def own_fill(codes, p_ref, n, u_ref, turns):
    nev = turns.shape[-1]
    width = u_ref.shape[0]
    for r in range(len(codes)):
        real, imag = (p_ref[n, m * nev : (m + 1) * nev].T for m in (2 * r, 2 * r + 1))
        set_turns(turns, r, real, imag)
    u_ref[...] = jnp.zeros(u_ref.shape, u_ref.dtype)

    def write(spin, column, a, b, minus_b):
        add_to(u_ref, along(column, nev), along(spin, nev), a)
        add_to(u_ref, along(column, nev), along(spin, nev, width), b)

    fill_spin_blocks(codes, turns, write)


def own_dot(u_ref, y_ref, ht):
    for tile in range(ht.shape[-1] // TILE):
        lanes = slice(tile * TILE, (tile + 1) * TILE)
        out = lax.dot_general(
            u_ref[...], y_ref[lanes, :], NT_DIMS, preferred_element_type=jnp.float32
        )
        ht[:, lanes] = out.astype(jnp.bfloat16)


def codes_of(gamma, op, nterm):
    return [gamma[op, r] for r in range(nterm)]


def own_kernel_01(gamma, block, proj, core, y_ref, h_ref, x_ref, p_ref, u0, u1, turns0, turns1, sems):
    mom = lax.axis_index("mom")
    rows = proj.shape[1]
    run_copies(
        [
            (block, x_ref),
            (proj.at[mom], p_ref.at[0]),
            (core.at[span(1, rows)], p_ref.at[1]),
        ],
        sems,
    )
    width = x_ref.shape[-1]
    real, imag = x_ref[0], x_ref[1]
    y_ref[:width, :width] = real
    y_ref[:width, width:] = -imag
    y_ref[width:, :width] = imag
    y_ref[width:, width:] = real
    nterm = turns0.shape[0]
    own_fill(codes_of(gamma, mom, nterm), p_ref, 0, u0, turns0)
    own_dot(u0, y_ref, h_ref.at[0])
    own_fill(codes_of(gamma, mom ^ 1, nterm), p_ref, 1, u1, turns1)
    own_dot(u1, y_ref, h_ref.at[1])


def own_kernel_23(sizes, seps, gamma, partner, core, own, forward, y_ref, h_in, *refs):
    h_ref, label, token, p_ref, u0, u1, turns0, turns1, tags, sems = refs
    rows = p_ref.shape[1]
    spot = pl.ds(core.shape[0] - TAG_ROWS, TAG_ROWS)
    run_copies(
        [(own.at[span(0, rows)], p_ref.at[0]), (forward.at[span(1, rows)], p_ref.at[1])]
        + [(ref.at[spot], tags.at[n]) for n, ref in enumerate((core, own, forward))],
        sems,
    )
    plan = Plan(seps, sizes)
    mom = plan.mom
    partners = [partner[0]] + [
        jnp.max(tags[n].astype(jnp.float32)).astype(jnp.int32) for n in range(3)
    ]
    count = len(partners)
    for p in range(count):
        back = jnp.int32(0)
        for i, value in enumerate(partners):
            back = back + jnp.where(value == (mom ^ p), mom ^ i, 0)
        label[p] = jnp.where(plan.forward, back, mom ^ p)
        label[count + p] = jnp.where(plan.forward, back, partners[p]) ^ mom
    nterm = turns0.shape[0]
    own_fill(codes_of(gamma, mom ^ 2, nterm), p_ref, 0, u0, turns0)
    own_dot(u0, y_ref, h_ref.at[2])
    own_fill(codes_of(gamma, mom ^ 3, nterm), p_ref, 1, u1, turns1)
    own_dot(u1, y_ref, h_ref.at[3])
    token[...] = jnp.zeros(token.shape, token.dtype)


def other_products(pieces, gamma, label, h_ref, refs):
    k_ref, p_ref, va, vb, turns_a, turns_b = refs
    mom = lax.axis_index("mom")
    nterm, nev = turns_a.shape[0], turns_a.shape[-1]
    width = h_ref.shape[1]
    for n, piece in enumerate(pieces):
        v_ref, turns = ((va, turns_a), (vb, turns_b))[n % 2]
        for r in range(nterm):
            real, imag = (p_ref[n, m * nev : (m + 1) * nev] for m in (2 * r, 2 * r + 1))
            set_turns(turns, r, real, imag)
        v_ref[...] = jnp.zeros(v_ref.shape, v_ref.dtype)

        def write(spin, column, a, b, minus_b, v_ref=v_ref):
            add_to(v_ref, along(spin, nev), along(column, nev), a)
            add_to(v_ref, along(spin, nev), along(column, nev, width), minus_b)
            add_to(v_ref, along(spin, nev, width), along(column, nev), b)
            add_to(v_ref, along(spin, nev, width), along(column, nev, width), a)

        fill_spin_blocks(codes_of(gamma, mom ^ piece, nterm), turns, write)
        own = label[4 + piece]
        for tile in range(2 * width // TILE):
            lanes = slice(tile * TILE, (tile + 1) * TILE)
            k_ref[n, :, lanes] = lax.dot_general(
                h_ref[own], v_ref[lanes, :], NT_DIMS, preferred_element_type=jnp.float32
            )


def other_kernel_02(sizes, seps, gamma, label, h_ref, proj, near, far_same, far_cross, *refs):
    k_ref, p_ref, va, vb, turns_a, turns_b, sems = refs
    plan = Plan(seps, sizes)
    rows = p_ref.shape[1]
    low = span(0, rows)
    flag = lax.rem(plan.hops(0), 2) if sizes[2] == 2 else jnp.int32(1)

    @pl.when(flag == 0)
    def _():
        run_copies([(proj.at[plan.local(0)], p_ref.at[0]), (near.at[low], p_ref.at[1])], sems)

    @pl.when(flag != 0)
    def _():
        run_copies([(far_same.at[low], p_ref.at[0]), (far_cross.at[low], p_ref.at[1])], sems)

    out = (k_ref, p_ref, va, vb, turns_a, turns_b)
    other_products((0, 2), gamma, label, h_ref, out)


def other_kernel_13(gamma, label, h_ref, traded, k_ref, p_ref, va, vb, turns_a, turns_b, sems):
    rows = p_ref.shape[1]
    run_copies([(traded.at[span(n, rows)], p_ref.at[n]) for n in range(2)], sems)
    out = (k_ref, p_ref, va, vb, turns_a, turns_b)
    other_products((1, 3), gamma, label, h_ref, out)


def row_sums(k_refs, source, offset, totals):
    rows = 16
    width = source.shape[-1]
    nev = totals[0].shape[-1]

    def step(index, totals):
        row = pl.multiple_of(index * rows, rows)
        here = pl.ds(pl.multiple_of(offset + row, rows), rows)
        totals = list(totals)
        for spin in range(NSPIN):
            lanes, later = along(spin, nev), along(spin, nev, width)
            real = source[0, pl.ds(row, rows), lanes].astype(jnp.float32)
            imag = source[1, pl.ds(row, rows), lanes].astype(jnp.float32)
            for n in range(len(totals) // 2):
                k_ref, p = k_refs[n // 2], n % 2
                kr, ki = k_ref[p, here, lanes], k_ref[p, here, later]
                totals[2 * n] += real * kr - imag * ki
                totals[2 * n + 1] += real * ki + imag * kr
        return tuple(totals)

    return lax.fori_loop(0, source.shape[1] // rows, step, totals)


def early_kernel(sizes, seps, ka, kb, near, far, sums_ref, part_ref, sems):
    plan = Plan(seps, sizes)
    count = sums_ref.shape[0]
    flag = lax.rem(lax.div(plan.hops(0), max(sizes[2] // 2, 1)), 2)

    @pl.when(flag == 0)
    def _():
        run_copies([(near, part_ref)], sems)

    @pl.when(flag != 0)
    def _():
        run_copies([(far, part_ref)], sems)

    zero = tuple(jnp.zeros(sums_ref.shape[1:], jnp.float32) for _ in range(count))
    for n, total in enumerate(row_sums((ka, kb), part_ref, 0, zero)):
        sums_ref[n] = total


def late_kernel(sizes, sep_count, seps, label, ka, kb, rest_ref, sums_ref, out_ref):
    plan = Plan(seps, sizes)
    count = sums_ref.shape[0] // 2
    width = rest_ref.shape[-1]
    start = ka.shape[1] - rest_ref.shape[1]
    totals = row_sums((ka, kb), rest_ref, start, tuple(sums_ref[n] for n in range(2 * count)))
    sums = [jnp.sum(total, axis=0, keepdims=True) for total in totals]
    sums = [jnp.sum(total, axis=1, keepdims=True) * (1.0 / width) for total in sums]
    shape = out_ref.shape[1:]
    spot = lax.broadcasted_iota(jnp.int32, shape, 0) * shape[1]
    spot = spot + lax.broadcasted_iota(jnp.int32, shape, 1)
    here = spot // 2 == plan.pair_time * sep_count + plan.sep_index
    if plan.live is not None:
        here = here & plan.live
    values = [jnp.where(spot % 2 == 0, sums[2 * p], sums[2 * p + 1]) for p in range(count)]
    lines = []
    for op in range(count):
        line = jnp.zeros(shape, jnp.float32)
        for p, value in zip((0, 2, 1, 3), values):
            line = jnp.where(label[p] == op, value, line)
        lines.append(jnp.where(here, line, 0.0))
    for n in range(out_ref.shape[0]):
        out_ref[n] = lines[n % count]


def smem():
    return pl.BlockSpec(memory_space=pltpu.SMEM)


def vmem():
    return pl.BlockSpec(memory_space=pltpu.VMEM)


def anywhere():
    return pl.BlockSpec(memory_space=pl.ANY)


def hbm():
    return pl.BlockSpec(memory_space=pltpu.HBM)


def limit(mib):
    return pltpu.CompilerParams(vmem_limit_bytes=mib * MIB)


def shards(peram_blocks, projections, gamma_index, partner, separations):
    src_count, snk_count = lax.axis_size("src"), lax.axis_size("snk")
    mom_count = lax.axis_size("mom")
    slices, offsets = peram_blocks.shape[:2]
    width = peram_blocks.shape[-1]
    nterm, nev = projections.shape[2], projections.shape[-1]
    time_count = slices * src_count
    sep_count = separations.shape[0]
    half_snk = snk_count // 2
    rows = nterm * 2 * nev
    sizes = (slices, offsets, src_count, snk_count)
    proj = projections.reshape(slices, rows, nev)

    def swap_mom(array, i):
        return lax.ppermute(array, "mom", [(a, a ^ i) for a in range(mom_count)])

    def swap_snk(array):
        pairs = [(a, (a + half_snk) % snk_count) for a in range(snk_count)]
        return lax.ppermute(array, "snk", pairs)

    def next_src(array, step=1, i=0):
        pairs = [
            (((a + step) % src_count) * mom_count + (b ^ i), a * mom_count + b)
            for a in range(src_count)
            for b in range(mom_count)
        ]
        return lax.ppermute(array, ("src", "mom"), pairs)

    def most_of(array, amount):
        step = 1
        while 2 * step < src_count:
            array = jnp.where((amount // step) % 2 != 0, next_src(array, step), array)
            step *= 2
        return array, next_src(array, step)

    def call(kernel, name, in_specs, out_specs, out_shape, scratch, mib, aliases=None):
        cost = pl.CostEstimate(flops=WEIGHT, bytes_accessed=WEIGHT // 1000, transcendentals=0)
        return pl.pallas_call(
            kernel,
            in_specs=in_specs,
            out_specs=out_specs,
            out_shape=out_shape,
            scratch_shapes=scratch,
            input_output_aliases=aliases or {},
            compiler_params=limit(mib),
            cost_estimate=cost,
            name=name,
        )

    def bf16(*shape):
        return jax.ShapeDtypeStruct(shape, jnp.bfloat16)

    def dma(count):
        return pltpu.SemaphoreType.DMA((count,))

    part = functools.partial
    split = (width * 5 // 8) // 16 * 16
    two = bf16(2 * rows, nev)
    tagged = bf16(2 * rows + TAG_ROWS, nev)
    first_shape, rest_shape = bf16(2, split, width), bf16(2, width - split, width)
    token = bf16(16, 128)

    def buffers(shapes):
        return [pltpu.VMEM(shape.shape, shape.dtype) for shape in shapes]

    def alias(kernel, name, in_specs, out_shape, aliases, operands):
        return pl.pallas_call(
            kernel,
            in_specs=in_specs,
            out_specs=[anywhere()] * len(aliases) + [vmem()],
            out_shape=out_shape,
            input_output_aliases=aliases,
            compiler_params=limit(16),
            cost_estimate=pl.CostEstimate(
                flops=WEIGHT, bytes_accessed=WEIGHT // 1000, transcendentals=0
            ),
            name=name,
        )(*operands)

    leaving = [first_shape, tagged, tagged, rest_shape]
    first, core, own, rest = call(
        part(pack, sizes),
        "pack",
        [smem()] * 2 + [hbm()] * 2,
        [hbm()] * len(leaving),
        leaving,
        buffers(leaving) + [dma(6), dma(len(leaving))],
        58,
    )(separations, partner, peram_blocks, proj)

    plan = Plan(separations, sizes)
    first = swap_snk(first)
    core = swap_mom(core, 1)
    own = swap_mom(own, 2)
    rest_near, rest_far = most_of(rest, plan.peer_hops())
    forward = swap_mom(own, 1)
    leaving = [two, two, bf16(2, width, width)]
    far_same, far_cross, block = call(
        part(pack_far, sizes),
        "pack_far",
        [smem()] + [hbm()] * 3,
        [hbm()] * len(leaving),
        leaving,
        buffers(leaving) + [dma(5), dma(len(leaving))],
        58,
    )(separations, peram_blocks, proj, core)
    if src_count == 2:
        far_same, far_cross = next_src(far_same), next_src(far_cross, 1, 2)

    u_scratch = pltpu.VMEM((width, 2 * width), jnp.bfloat16)
    v_scratch = pltpu.VMEM((2 * width, 2 * width), jnp.bfloat16)
    turns = pltpu.VMEM((nterm, 4, nev, nev), jnp.bfloat16)
    products = bf16(mom_count, width, 2 * width)
    y, h = call(
        own_kernel_01,
        "own_products_01",
        [smem()] + [hbm()] * 3,
        [vmem()] * 2,
        [bf16(2 * width, 2 * width), products],
        [
            pltpu.VMEM((2, width, width), jnp.bfloat16),
            pltpu.VMEM((2, rows, nev), jnp.bfloat16),
            u_scratch,
            u_scratch,
            turns,
            turns,
            dma(3),
        ],
        16,
    )(gamma_index, block, proj, core)
    h, label, done_h = call(
        part(own_kernel_23, sizes),
        "own_products_23",
        [smem()] * 3 + [hbm()] * 3 + [vmem()] * 2,
        [vmem(), smem(), vmem()],
        [products, jax.ShapeDtypeStruct((2 * mom_count,), jnp.int32), token],
        [
            pltpu.VMEM((2, rows, nev), jnp.bfloat16),
            u_scratch,
            u_scratch,
            turns,
            turns,
            pltpu.VMEM((3, TAG_ROWS, nev), jnp.bfloat16),
            dma(5),
        ],
        16,
        {7: 0},
    )(separations, gamma_index, partner, core, own, forward, y, h)

    if src_count > 2:
        rest_near = jnp.where(plan.peer_hops() // (src_count // 2) != 0, rest_far, rest_near)
        rest_far = rest_near
    rest, near = call(
        part(choose, sizes),
        "choose",
        [smem()] + [hbm()] * 3 + [vmem()],
        [vmem()] * 2,
        [rest_shape, two],
        [dma(3)],
        16,
    )(separations, rest_near, rest_far, proj, done_h)
    near = swap_mom(near, 2)
    first, rest, opened = alias(
        gate,
        "gate",
        [anywhere()] * 2,
        [first_shape, rest_shape, token],
        {0: 0, 1: 1},
        (first, rest),
    )
    rest = swap_snk(rest)
    first_near, first_far = most_of(first, plan.hops(0))
    other_trade = call(
        part(other_pack, sizes),
        "other_pack",
        [smem()] + [hbm()] * 4 + [vmem()],
        vmem(),
        two,
        [dma(2)],
        16,
    )(separations, proj, near, far_same, far_cross, opened)
    other_got = swap_mom(other_trade, 1)
    if src_count != 2:

        def moved(array):
            if src_count == 1:
                return array
            array, away = most_of(array, plan.hops(0))
            return jnp.where(plan.hops(0) // (src_count // 2) != 0, away, array)

        far_same = moved(lax.dynamic_index_in_dim(proj, plan.local(0), 0, keepdims=False))
        far_cross, other_got = moved(near[:rows]), moved(other_got)

    k_shape = jax.ShapeDtypeStruct((2, width, 2 * width), jnp.float32)
    scratch = [pltpu.VMEM((2, rows, nev), jnp.bfloat16), v_scratch, v_scratch, turns, turns, dma(2)]
    ka = call(
        part(other_kernel_02, sizes),
        "other_products_02",
        [smem()] * 3 + [vmem()] + [hbm()] * 4,
        vmem(),
        k_shape,
        scratch,
        20,
    )(separations, gamma_index, label, h, proj, near, far_same, far_cross)
    kb = call(
        other_kernel_13,
        "other_products_13",
        [smem()] * 2 + [vmem(), hbm()],
        vmem(),
        k_shape,
        scratch,
        20,
    )(gamma_index, label, h, other_got)

    sums = call(
        part(early_kernel, sizes),
        "early_traces",
        [smem()] + [vmem()] * 2 + [hbm()] * 2,
        vmem(),
        jax.ShapeDtypeStruct((2 * mom_count, 16, nev), jnp.float32),
        [pltpu.VMEM((2, split, width), jnp.bfloat16), dma(1)],
        20,
    )(separations, ka, kb, first_near, first_far)
    device_count = src_count * snk_count * mom_count
    values = time_count * sep_count * 2
    lines = (values + 127) // 128
    out = call(
        part(late_kernel, sizes, sep_count),
        "late_traces",
        [smem()] * 2 + [vmem()] * 4,
        vmem(),
        jax.ShapeDtypeStruct((device_count, lines, 128), jnp.float32),
        [],
        20,
    )(separations, label, ka, kb, rest, sums)
    out = lax.all_to_all(out, ("src", "snk", "mom"), split_axis=0, concat_axis=0, tiled=True)
    out = jnp.sum(out, axis=0).reshape(lines * 128)[:values]
    return out.reshape(time_count, sep_count, 1, 2)


def solution(mesh):
    placed = (
        P("src", "snk", None, None, None),
        P("src", "mom", None, None, None, None),
        P(),
        P("mom"),
        P(),
    )
    return jax.shard_map(
        shards, mesh=mesh, in_specs=placed, out_specs=P(None, None, "mom", None), check_vma=False
    )
```

time: 82.7 us -> 85.4 us (1.033)
  waiting for transfers between devices: 22.5 us -> 18 us
  blocking collectives: 9.8 us -> 13.5 us
  Pallas kernels: 34.9 us -> 37.1 us
  local copies, waits for them, and re-layouts: 1.98 us -> 3.95 us
    ppermute x2, waiting for transfers between devices: 17.4 us -> 4.6 us  [swap_snk(): return lax.ppermute(array, 'snk', pairs)]
    ppermute x5, waiting for transfers between devices: 4.18 us -> 13.4 us  [swap_mom(): return lax.ppermute(array, 'mom', [(a, a ^ i) for a in range(mom_count)])]
    all_to_all x1, blocking collectives: 9.8 us -> 13.5 us  [shards(): lax.all_to_all(out, ('src', 'snk', 'mom'), split_axis=0, concat_axis=0, t...]
    pallas_call x9 -> x11, Pallas kernels: 34.9 us -> 37.1 us  [the longest x1 5.89 us: shards(): call(part(other_kernel_02, sizes), 'other_products_02', [smem()] * 3 + [v...]
    unnamed x24 -> x26, local copies, waits for them, and re-layouts: 1.14 us -> 3.11 us
    ppermute x5, starting transfers between devices: 2.71 us -> 4.5 us  [swap_mom(): return lax.ppermute(array, 'mom', [(a, a ^ i) for a in range(mom_count)])]
    ppermute x2, starting transfers between devices: 3.7 us -> 2.69 us  [swap_snk(): return lax.ppermute(array, 'snk', pairs)]
    ppermute x4, waiting for transfers between devices: 0.91 us -> 0.01 us  [next_src(): return lax.ppermute(array, ('src', 'mom'), pairs)]
  transfers between devices with their start and end apart: 11 -> 11, of which waited for: 3 -> 3; matrix products, arithmetic and copies ran while one was open for 0% -> 0% of each run, Pallas kernels for 35% -> 38%
where the time goes in v6:
time: 85.4 us; the launch traced here: 85 us
  Pallas kernels  37.1 us (43%)
  waiting for transfers between devices  18 us (21%)
  blocking collectives  13.5 us (16%)
  starting transfers between devices  11.4 us (13%)
  local copies, waits for them, and re-layouts  3.95 us (5%)
  between operations  0.88 us (1%)
    all_to_all x1, blocking collectives, shards(): lax.all_to_all(out, ('src', 'snk', 'mom'), split_axis=0, concat_axis=0, t...  13.5 us
    ppermute x5, waiting for transfers between devices, swap_mom(): return lax.ppermute(array, 'mom', [(a, a ^ i) for a in range(mom_count)])  13.4 us
    pallas_call x1, Pallas kernels, shards(): call(part(other_kernel_02, sizes), 'other_products_02', [smem()] * 3 + [v...  5.89 us
    pallas_call x1, Pallas kernels, shards(): call(other_kernel_13, 'other_products_13', [smem()] * 2 + [vmem(), hbm()]...  5.69 us
    pallas_call x1, Pallas kernels, shards(): call(part(own_kernel_23, sizes), 'own_products_23', [smem()] * 3 + [hbm()...  5.35 us
    ppermute x2, waiting for transfers between devices, swap_snk(): return lax.ppermute(array, 'snk', pairs)  4.6 us
    ppermute x5, starting transfers between devices, swap_mom(): return lax.ppermute(array, 'mom', [(a, a ^ i) for a in range(mom_count)])  4.5 us
    ppermute x4, starting transfers between devices, next_src(): return lax.ppermute(array, ('src', 'mom'), pairs)  4.21 us
  transfers between devices with their start and end apart: 11, of which 3 were waited for; matrix products, arithmetic and copies ran while one was open for 0% of the time, Pallas kernels for 38%

profile of v6, /device:TPU:0, one launch (start us, length us, event | category | flops | bytes accessed | tf_op | source)
XLA Modules:
  0.0 85.0 jit_solution(5469748248446458316)
XLA Ops:
  0.7 3.2 %pack.1 = (bf16[2,320,512]{2,1,0:T(8,128)(2,1)}, bf16[2064,128]{1,0:T(8,128)(2,1)}, bf16[2064,128]{1,0:T(8,128)(2,1)}, bf16[2,192,512]{2,1,0:T(8,128)(2,1)}) custom-call(s32[4]{0:T(128)} %seps.15, s32[1]{0:T(128)S(6)} %copy.14.partner, bf16[4,2,2,512,512]{4,3,2,1,0:T(8,128)(2,1)} %peram.3, bf16[4,1024,128]{2,1,0:T(8,128)(2,1)} %bitcast.2), custom_call_target="tpu_custom_call" | custom-call | flops 9999999827968 | bytes 10000000000 | tf_op jit(solution)/shard_map/pack/pallas_call | solution.py:495
  3.9 0.8 collective-permute-start
  4.7 2.3 %collective-permute-start.1 = (bf16[2064,128]{1,0:T(8,128)(2,1)}, bf16[2064,128]{1,0:T(8,128)(2,1)}, u32[]{:S(2)}, u32[]{:S(2)}) collective-permute-start(bf16[2064,128]{1,0:T(8,128)(2,1)} %get-tuple-element.23), channel_id=1, source_target_pairs={{0,2},{1,3},{2,0},{3,1},{4,6},{5,7},{6,4},{7,5},{8,10},{9,11},{10,... | collective-permute-start | bytes 1585160 | tf_op jit(solution)/shard_map/ppermute | solution.py:429
  7.0 1.5 %collective-permute-start.3 = (bf16[2,192,512]{2,1,0:T(8,128)(2,1)}, bf16[2,192,512]{2,1,0:T(8,128)(2,1)}, u32[]{:S(2)}, u32[]{:S(2)}) collective-permute-start(bf16[2,192,512]{2,1,0:T(8,128)(2,1)} %get-tuple-element.29.near), channel_id=1, source_target_pairs={{16,0},{17,1},{18,2},{19,3},{0,16},{1,17},{2,18},{3,19},{20,4},{21... | collective-permute-start | bytes 1179656 | tf_op jit(solution)/shard_map/ppermute | solution.py:441
  8.5 2.7 %collective-permute-start.7 = (bf16[2,320,512]{2,1,0:T(8,128)(2,1)}, bf16[2,320,512]{2,1,0:T(8,128)(2,1)}, u32[]{:S(2)}, u32[]{:S(2)}) collective-permute-start(bf16[2,320,512]{2,1,0:T(8,128)(2,1)} %get-tuple-element.34), channel_id=1, source_target_pairs={{0,8},{4,12},{8,0},{12,4},{1,9},{5,13},{9,1},{13,5},{2,10},{6,14},... | collective-permute-start | bytes 1966088 | tf_op jit(solution)/shard_map/ppermute | solution.py:433
  11.2 0.0 collective-permute-done.after.core
  11.2 0.8 copy-done.1
  12.0 3.4 %pack_far.1 = (bf16[2048,128]{1,0:T(8,128)(2,1)}, bf16[2048,128]{1,0:T(8,128)(2,1)}, bf16[2,512,512]{2,1,0:T(8,128)(2,1)}) custom-call(s32[4]{0:T(128)} %seps.15, bf16[4,2,2,512,512]{4,3,2,1,0:T(8,128)(2,1)} %peram.3, bf16[4,1024,128]{2,1,0:T(8,128)(2,1)} %bitcast.3, bf16[2064,128]{1,0:T(8,128)(2,1)} %copy-done.1), custom_call_target="tpu_custom_call" | custom-call | flops 9999999827968 | bytes 10000000000 | tf_op jit(solution)/shard_map/pack_far/pallas_call | solution.py:512
  15.4 0.6 collective-permute-start.5
  16.0 1.5 %collective-permute-start.6 = (bf16[2048,128]{1,0:T(8,128)(2,1)}, bf16[2048,128]{1,0:T(8,128)(2,1)}, u32[]{:S(2)}, u32[]{:S(2)}) collective-permute-start(bf16[2048,128]{1,0:T(8,128)(2,1)} %get-tuple-element.33), channel_id=1, source_target_pairs={{18,0},{19,1},{16,2},{17,3},{2,16},{3,17},{0,18},{1,19},{22,4},{23... | collective-permute-start | bytes 1572872 | tf_op jit(solution)/shard_map/ppermute | solution.py:441
  17.5 2.4 %collective-permute-done.1.own = bf16[2064,128]{1,0:T(8,128)(2,1)} collective-permute-done((bf16[2064,128]{1,0:T(8,128)(2,1)}, bf16[2064,128]{1,0:T(8,128)(2,1)}, u32[]{:S(2)}, u32[]{:S(2)}) %collective-permute-start.1) | collective-permute-done | bytes 528416 | tf_op jit(solution)/shard_map/ppermute | solution.py:429
  19.9 0.0 collective-permute-start.2
  19.9 0.0 copy-done
  19.9 0.0 copy-done.5
  19.9 0.0 copy-start.2
  19.9 1.0 %copy-done.2 = bf16[2064,128]{1,0:T(8,128)(2,1)S(1)} copy-done((bf16[2064,128]{1,0:T(8,128)(2,1)S(1)}, bf16[2064,128]{1,0:T(8,128)(2,1)}, u32[]{:S(2)}) %copy-start.2) | copy-done | bytes 528408
  20.9 1.2 %copy-done.10 = bf16[2,512,512]{2,1,0:T(8,128)(2,1)S(1)} copy-done((bf16[2,512,512]{2,1,0:T(8,128)(2,1)S(1)}, bf16[2,512,512]{2,1,0:T(8,128)(2,1)}, u32[]{:S(2)}) %copy-start.10) | copy-done | bytes 1048600
  22.2 3.9 %own_products_01.1 = (bf16[1024,1024]{1,0:T(8,128)(2,1)S(1)}, bf16[4,512,1024]{2,1,0:T(8,128)(2,1)S(1)}) custom-call(s32[4,4]{1,0:T(4,128)S(1)} %copy-done.5, bf16[2,512,512]{2,1,0:T(8,128)(2,1)S(1)} %copy-done.10, bf16[4,1024,128]{2,1,0:T(8,128)(2,1)S(1)} %bitcast.4, bf16[2064,128]{1,0:T(8,128)(2,1)S(1)} %copy-done.2), custom_call_target="tpu_custom_call" | custom-call | flops 9999999827968 | bytes 10000000000 | tf_op jit(solution)/shard_map/own_products_01/pallas_call | solution.py:528
  26.1 0.0 collective-permute-done.2.forward
  26.1 0.0 copy-done.3
  26.1 0.0 copy-done.6
  26.1 0.0 copy-start.4
  26.1 5.3 %own_products_23.1 = (bf16[4,512,1024]{2,1,0:T(8,128)(2,1)S(1)}, s32[8]{0:T(128)S(1)}, bf16[16,128]{1,0:T(8,128)(2,1)S(1)}) custom-call(s32[4]{0:T(128)S(1)} %copy-done.6, s32[4,4]{1,0:T(4,128)S(1)} %copy-done.5, s32[1]{0:T(128)S(6)} %copy.14.partner, bf16[2064,128]{1,0:T(8,128)(2,1)S(1)} %copy-done.3, ...), custom_call_target="tpu_custom_call", output_to_operand_aliasing={{0}: (7, {})} | custom-call | flops 9999999827968 | bytes 10000000000 | tf_op jit(solution)/shard_map/own_products_23/pallas_call | solution.py:545
  31.5 0.0 copy-start.8
  31.5 0.0 copy-start.11
  31.5 0.0 collective-permute-done.3.far
  31.5 2.9 %choose.1 = (bf16[2,192,512]{2,1,0:T(8,128)(2,1)}, bf16[2048,128]{1,0:T(8,128)(2,1)}) custom-call(s32[4]{0:T(128)S(1)} %copy-done.6, bf16[2,192,512]{2,1,0:T(8,128)(2,1)S(1)} %copy-done.4, bf16[2,192,512]{2,1,0:T(8,128)(2,1)} %collective-permute-done.3.far, bf16[4,1024,128]{2,1,0:T(8,128)(2,1)S(1)} %bitcast.5, bf16[16,128]{1,0:T(8,128)(2,1)S(1)} %get-tuple-element.30.after), custom_call_target="tpu_custom_call" | custom-call | flops 9999999827968 | bytes 10000000000 | tf_op jit(solution)/shard_map/choose/pallas_call | solution.py:567
  34.4 1.2 %collective-permute-start.4 = (bf16[2048,128]{1,0:T(8,128)(2,1)}, bf16[2048,128]{1,0:T(8,128)(2,1)}, u32[]{:S(2)}, u32[]{:S(2)}) collective-permute-start(bf16[2048,128]{1,0:T(8,128)(2,1)} %get-tuple-element.31), channel_id=1, source_target_pairs={{0,2},{1,3},{2,0},{3,1},{4,6},{5,7},{6,4},{7,5},{8,10},{9,11},{10,... | collective-permute-start | bytes 1572872 | tf_op jit(solution)/shard_map/ppermute | solution.py:429
  35.6 4.6 %collective-permute-done.7.first = bf16[2,320,512]{2,1,0:T(8,128)(2,1)} collective-permute-done((bf16[2,320,512]{2,1,0:T(8,128)(2,1)}, bf16[2,320,512]{2,1,0:T(8,128)(2,1)}, u32[]{:S(2)}, u32[]{:S(2)}) %collective-permute-start.7) | collective-permute-done | bytes 655392 | tf_op jit(solution)/shard_map/ppermute | solution.py:433
  40.2 0.0 collective-permute-start.9
  40.2 0.6 collective-permute-start.10
  40.8 0.0 collective-permute-done.5.far_same
  40.8 0.0 collective-permute-done.6.far_cross
  40.8 11.0 %collective-permute-done.4.near = bf16[2048,128]{1,0:T(8,128)(2,1)} collective-permute-done((bf16[2048,128]{1,0:T(8,128)(2,1)}, bf16[2048,128]{1,0:T(8,128)(2,1)}, u32[]{:S(2)}, u32[]{:S(2)}) %collective-permute-start.4) | collective-permute-done | bytes 524320 | tf_op jit(solution)/shard_map/ppermute | solution.py:429
  51.9 2.6 %other_pack.1 = bf16[2048,128]{1,0:T(8,128)(2,1)} custom-call(s32[4]{0:T(128)S(1)} %copy-done.7, bf16[4,1024,128]{2,1,0:T(8,128)(2,1)S(1)} %bitcast.6, bf16[2048,128]{1,0:T(8,128)(2,1)} %collective-permute-done.4.near, bf16[2048,128]{1,0:T(8,128)(2,1)} %collective-permute-done.5.far_same, bf16[2048,128]{1,0:T(8,128)(2,1)} %collective-permute-done.6.far_cross, ...), custom_call_target="tpu_custom_call" | custom-call | flops 9999999827968 | bytes 10000000000 | tf_op jit(solution)/shard_map/other_pack/pallas_call | solution.py:587
  54.5 0.1 collective-permute-start.8
  54.7 5.9 %other_products_02.1.ka = f32[2,512,1024]{2,1,0:T(8,128)S(1)} custom-call(s32[4]{0:T(128)S(1)} %copy-done.7, s32[4,4]{1,0:T(4,128)S(1)} %copy-done.5, s32[8]{0:T(128)S(1)} %get-tuple-element.27.label, bf16[4,512,1024]{2,1,0:T(8,128)(2,1)S(1)} %copy-done.9, bf16[4,1024,128]{2,1,0:T(8,128)(2,1)S(1)} %bitcast.7, bf16[2048,128]{1,0:T(8,128)(2,1)} %collective-permute-done.4.near, ...), custom_call_target="tpu_custom_call" | custom-call | flops 9999999827968 | bytes 10000000000 | tf_op jit(solution)/shard_map/other_products_02/pallas_call | solution.py:610
  60.6 0.0 collective-permute-done.8.traded
  60.6 5.7 %other_products_13.1.kb = f32[2,512,1024]{2,1,0:T(8,128)S(1)} custom-call(s32[4,4]{1,0:T(4,128)S(1)} %copy-done.5, s32[8]{0:T(128)S(1)} %get-tuple-element.27.label, bf16[4,512,1024]{2,1,0:T(8,128)(2,1)S(1)} %copy-done.9, bf16[2048,128]{1,0:T(8,128)(2,1)} %collective-permute-done.8.traded), custom_call_target="tpu_custom_call" | custom-call | flops 9999999827968 | bytes 10000000000 | tf_op jit(solution)/shard_map/other_products_13/pallas_call | solution.py:619
  66.3 0.0 collective-permute-done.10.far
  66.3 0.0 copy-start.12
  66.3 2.5 %early_traces.1.sums_ref = f32[8,16,128]{2,1,0:T(8,128)S(1)} custom-call(s32[4]{0:T(128)S(1)} %copy-done.7, f32[2,512,1024]{2,1,0:T(8,128)S(1)} %other_products_02.1.ka, f32[2,512,1024]{2,1,0:T(8,128)S(1)} %other_products_13.1.kb, bf16[2,320,512]{2,1,0:T(8,128)(2,1)} %get-tuple-element.38.near, bf16[2,320,512]{2,1,0:T(8,128)(2,1)} %collective-permute-done.10.far), custom_call_target="tpu_custom_call" | custom-call | flops 9999999827968 | bytes 10000000000 | tf_op jit(solution)/shard_map/early_traces/pallas_call | solution.py:629
  68.8 0.0 collective-permute-done.9.rest_ref
  68.9 1.6 %late_traces.1 = f32[32,1,128]{2,1,0:T(1,128)S(1)} custom-call(s32[4]{0:T(128)S(1)} %copy-done.7, s32[8]{0:T(128)S(1)} %copy-done.12, f32[2,512,1024]{2,1,0:T(8,128)S(1)} %other_products_02.1.ka, f32[2,512,1024]{2,1,0:T(8,128)S(1)} %other_products_13.1.kb, bf16[2,192,512]{2,1,0:T(8,128)(2,1)} %collective-permute-done.9.rest_ref, ...), custom_call_target="tpu_custom_call" | custom-call | flops 9999999827968 | bytes 10000000000 | tf_op jit(solution)/shard_map/late_traces/pallas_call | solution.py:641
  70.5 13.5 %all_to_all.5 = f32[32,1,128]{2,1,0:T(1,128)S(1)} all-to-all(f32[32,1,128]{2,1,0:T(1,128)S(1)} %late_traces.1), channel_id=1, replica_groups=mesh['src'=2,'snk'=4,'mom'=4] {'src','snk','mom'}, dimensions={0} | all-to-all | bytes 32768 | tf_op jit(solution)/shard_map/all_to_all | solution.py:650
  84.1 0.1 reduce_sum.11
  84.1 0.1 reshape.11
  84.2 0.7 copy.10
  (16 shorter events, 0.0 us)
Async XLA Ops:
  3.9 7.3 %collective-permute-start = (bf16[2064,128]{1,0:T(8,128)(2,1)}, bf16[2064,128]{1,0:T(8,128)(2,1)S(1)}, u32[]{:S(2)}, u32[]{:S(2)}) collective-permute-start(bf16[2064,128]{1,0:T(8,128)(2,1)} %get-tuple-element.22), channel_id=1, source_target_pairs={{0,1},{1,0},{2,3},{3,2},{4,5},{5,4},{6,7},{7,6},{8,9},{9,8},{10,11... | collective-permute-start | bytes 1585160 | tf_op jit(solution)/shard_map/ppermute | solution.py:429
  4.7 15.2 %collective-permute-start.1 = (bf16[2064,128]{1,0:T(8,128)(2,1)}, bf16[2064,128]{1,0:T(8,128)(2,1)}, u32[]{:S(2)}, u32[]{:S(2)}) collective-permute-start(bf16[2064,128]{1,0:T(8,128)(2,1)} %get-tuple-element.23), channel_id=1, source_target_pairs={{0,2},{1,3},{2,0},{3,1},{4,6},{5,7},{6,4},{7,5},{8,10},{9,11},{10,... | collective-permute-start | bytes 1585160 | tf_op jit(solution)/shard_map/ppermute | solution.py:429
  7.0 24.5 %collective-permute-start.3 = (bf16[2,192,512]{2,1,0:T(8,128)(2,1)}, bf16[2,192,512]{2,1,0:T(8,128)(2,1)}, u32[]{:S(2)}, u32[]{:S(2)}) collective-permute-start(bf16[2,192,512]{2,1,0:T(8,128)(2,1)} %get-tuple-element.29.near), channel_id=1, source_target_pairs={{16,0},{17,1},{18,2},{19,3},{0,16},{1,17},{2,18},{3,19},{20,4},{21... | collective-permute-start | bytes 1179656 | tf_op jit(solution)/shard_map/ppermute | solution.py:441
  8.5 31.8 %collective-permute-start.7 = (bf16[2,320,512]{2,1,0:T(8,128)(2,1)}, bf16[2,320,512]{2,1,0:T(8,128)(2,1)}, u32[]{:S(2)}, u32[]{:S(2)}) collective-permute-start(bf16[2,320,512]{2,1,0:T(8,128)(2,1)} %get-tuple-element.34), channel_id=1, source_target_pairs={{0,8},{4,12},{8,0},{12,4},{1,9},{5,13},{9,1},{13,5},{2,10},{6,14},... | collective-permute-start | bytes 1966088 | tf_op jit(solution)/shard_map/ppermute | solution.py:433
  11.2 0.8 copy-start.1
  12.0 7.9 %copy-start = (bf16[4,1,4,2,128,128]{5,4,3,2,1,0:T(8,128)(2,1)S(1)}, bf16[4,1,4,2,128,128]{5,4,3,2,1,0:T(8,128)(2,1)}, u32[]{:S(2)}) copy-start(bf16[4,1,4,2,128,128]{5,4,3,2,1,0:T(8,128)(2,1)} %param.6) | copy-start | bytes 3145732
  12.0 7.9 %copy-start.5 = (s32[4,4]{1,0:T(4,128)S(1)}, s32[4,4]{1,0:T(4,128)}, u32[]{:S(2)}) copy-start(s32[4,4]{1,0:T(4,128)} %gamma.7) | copy-start | bytes 196
  15.4 25.4 %collective-permute-start.5 = (bf16[2048,128]{1,0:T(8,128)(2,1)}, bf16[2048,128]{1,0:T(8,128)(2,1)}, u32[]{:S(2)}, u32[]{:S(2)}) collective-permute-start(bf16[2048,128]{1,0:T(8,128)(2,1)} %get-tuple-element.32), channel_id=1, source_target_pairs={{16,0},{17,1},{18,2},{19,3},{0,16},{1,17},{2,18},{3,19},{20,4},{21... | collective-permute-start | bytes 1572872 | tf_op jit(solution)/shard_map/ppermute | solution.py:441
  16.0 24.8 %collective-permute-start.6 = (bf16[2048,128]{1,0:T(8,128)(2,1)}, bf16[2048,128]{1,0:T(8,128)(2,1)}, u32[]{:S(2)}, u32[]{:S(2)}) collective-permute-start(bf16[2048,128]{1,0:T(8,128)(2,1)} %get-tuple-element.33), channel_id=1, source_target_pairs={{18,0},{19,1},{16,2},{17,3},{2,16},{3,17},{0,18},{1,19},{22,4},{23... | collective-permute-start | bytes 1572872 | tf_op jit(solution)/shard_map/ppermute | solution.py:441
  19.9 6.2 %collective-permute-start.2 = (bf16[2064,128]{1,0:T(8,128)(2,1)}, bf16[2064,128]{1,0:T(8,128)(2,1)}, u32[]{:S(2)}, u32[]{:S(2)}) collective-permute-start(bf16[2064,128]{1,0:T(8,128)(2,1)} %collective-permute-done.1.own), channel_id=1, source_target_pairs={{0,1},{1,0},{2,3},{3,2},{4,5},{5,4},{6,7},{7,6},{8,9},{9,8},{10,11... | collective-permute-start | bytes 1585160 | tf_op jit(solution)/shard_map/ppermute | solution.py:429
  19.9 1.0 %copy-start.2 = (bf16[2064,128]{1,0:T(8,128)(2,1)S(1)}, bf16[2064,128]{1,0:T(8,128)(2,1)}, u32[]{:S(2)}) copy-start(bf16[2064,128]{1,0:T(8,128)(2,1)} %copy-done.1) | copy-start | bytes 1585156
  20.9 1.2 %copy-start.10 = (bf16[2,512,512]{2,1,0:T(8,128)(2,1)S(1)}, bf16[2,512,512]{2,1,0:T(8,128)(2,1)}, u32[]{:S(2)}) copy-start(bf16[2,512,512]{2,1,0:T(8,128)(2,1)} %get-tuple-element.24.block) | copy-start | bytes 3145732
  22.2 3.9 %copy-start.3 = (bf16[2064,128]{1,0:T(8,128)(2,1)S(1)}, bf16[2064,128]{1,0:T(8,128)(2,1)}, u32[]{:S(2)}) copy-start(bf16[2064,128]{1,0:T(8,128)(2,1)} %copy-done.1) | copy-start | bytes 1585156
  22.2 3.9 %copy-start.6 = (s32[4]{0:T(128)S(1)}, s32[4]{0:T(128)}, u32[]{:S(2)}) copy-start(s32[4]{0:T(128)} %seps.15) | copy-start | bytes 52
  26.1 5.4 %copy-start.4 = (bf16[2,192,512]{2,1,0:T(8,128)(2,1)S(1)}, bf16[2,192,512]{2,1,0:T(8,128)(2,1)}, u32[]{:S(2)}) copy-start(bf16[2,192,512]{2,1,0:T(8,128)(2,1)} %get-tuple-element.29.near) | copy-start | bytes 1179652
  31.5 2.9 %copy-start.8 = (bf16[4,512,1024]{2,1,0:T(8,128)(2,1)}, bf16[4,512,1024]{2,1,0:T(8,128)(2,1)S(1)}, u32[]{:S(2)}) copy-start(bf16[4,512,1024]{2,1,0:T(8,128)(2,1)S(1)} %get-tuple-element.28.h_ref) | copy-start | bytes 12582916
  31.5 29.1 %copy-start.11 = (s32[8]{0:T(128)}, s32[8]{0:T(128)S(1)}, u32[]{:S(2)}) copy-start(s32[8]{0:T(128)S(1)} %get-tuple-element.27.label) | copy-start | bytes 100
  34.4 17.5 %collective-permute-start.4 = (bf16[2048,128]{1,0:T(8,128)(2,1)}, bf16[2048,128]{1,0:T(8,128)(2,1)}, u32[]{:S(2)}, u32[]{:S(2)}) collective-permute-start(bf16[2048,128]{1,0:T(8,128)(2,1)} %get-tuple-element.31), channel_id=1, source_target_pairs={{0,2},{1,3},{2,0},{3,1},{4,6},{5,7},{6,4},{7,5},{8,10},{9,11},{10,... | collective-permute-start | bytes 1572872 | tf_op jit(solution)/shard_map/ppermute | solution.py:429
  40.2 11.6 %copy-start.7 = (s32[4]{0:T(128)S(1)}, s32[4]{0:T(128)}, u32[]{:S(2)}) copy-start(s32[4]{0:T(128)} %seps.15) | copy-start | bytes 52
  40.2 28.6 %collective-permute-start.9 = (bf16[2,192,512]{2,1,0:T(8,128)(2,1)}, bf16[2,192,512]{2,1,0:T(8,128)(2,1)}, u32[]{:S(2)}, u32[]{:S(2)}) collective-permute-start(bf16[2,192,512]{2,1,0:T(8,128)(2,1)} %get-tuple-element.37), channel_id=1, source_target_pairs={{0,8},{4,12},{8,0},{12,4},{1,9},{5,13},{9,1},{13,5},{2,10},{6,14},... | collective-permute-start | bytes 1179656 | tf_op jit(solution)/shard_map/ppermute | solution.py:433
  40.2 26.1 %collective-permute-start.10 = (bf16[2,320,512]{2,1,0:T(8,128)(2,1)}, bf16[2,320,512]{2,1,0:T(8,128)(2,1)}, u32[]{:S(2)}, u32[]{:S(2)}) collective-permute-start(bf16[2,320,512]{2,1,0:T(8,128)(2,1)} %get-tuple-element.38.near), channel_id=1, source_target_pairs={{16,0},{17,1},{18,2},{19,3},{0,16},{1,17},{2,18},{3,19},{20,4},{21... | collective-permute-start | bytes 1966088 | tf_op jit(solution)/shard_map/ppermute | solution.py:441
  51.9 2.8 %copy-start.9 = (bf16[4,512,1024]{2,1,0:T(8,128)(2,1)S(1)}, bf16[4,512,1024]{2,1,0:T(8,128)(2,1)}, u32[]{:S(2)}) copy-start(bf16[4,512,1024]{2,1,0:T(8,128)(2,1)} %copy-done.8) | copy-start | bytes 12582916
  54.5 6.0 %collective-permute-start.8 = (bf16[2048,128]{1,0:T(8,128)(2,1)}, bf16[2048,128]{1,0:T(8,128)(2,1)}, u32[]{:S(2)}, u32[]{:S(2)}) collective-permute-start(bf16[2048,128]{1,0:T(8,128)(2,1)} %other_pack.1), channel_id=1, source_target_pairs={{0,1},{1,0},{2,3},{3,2},{4,5},{5,4},{6,7},{7,6},{8,9},{9,8},{10,11... | collective-permute-start | bytes 1572872 | tf_op jit(solution)/shard_map/ppermute | solution.py:429
  66.3 2.5 %copy-start.12 = (s32[8]{0:T(128)S(1)}, s32[8]{0:T(128)}, u32[]{:S(2)}) copy-start(s32[8]{0:T(128)} %copy-done.11) | copy-start | bytes 100

commit v7 on v6

--- a/solution.py
+++ b/solution.py
@@ -34,7 +34,7 @@
     for r, code in enumerate(codes):
         for spin in range(NSPIN):
             column, phase = spin_entry(code, spin)
-            write(spin, column, *(turns[r, (n - phase) & 3] for n in (4, 1, 3)))
+            write(spin, column, *(turns[r, (n - phase) & 3] for n in (4, 1)))
 
 
 def set_turns(turns, r, real, imag):
@@ -126,54 +126,68 @@
     return [(proj.at[n], buffer.at[span(i, rows)]) for i, n in enumerate((first, second))]
 
 
-def pack(sizes, seps, partner, peram, proj, *refs):
-    outs, buffers, (ins, leaving) = refs[:4], refs[4:8], refs[8:]
+def tag_of(partner, lanes):
+    number = jnp.full((TAG_ROWS, lanes), partner[0].astype(jnp.float32))
+    return number.astype(jnp.bfloat16)
+
+
+def pack_first(sizes, seps, peram, out, token, buffer, ins, leaving):
+    plan = Plan(seps, sizes)
+    source = peram.at[plan.peer_local(), plan.give, :, pl.ds(0, out.shape[1])]
+    through([([(source, buffer)], buffer, out)], ins, leaving)
+    token[...] = jnp.zeros(token.shape, token.dtype)
+
+
+def pack(sizes, seps, partner, peram, proj, after, *refs):
+    outs, buffers, (ins, leaving) = refs[:5], refs[5:10], refs[10:]
     plan = Plan(seps, sizes)
     rows = proj.shape[1]
-    peer, give, mom = plan.peer_local(), plan.give, plan.mom
-    number = jnp.full((TAG_ROWS, proj.shape[-1]), partner[0].astype(jnp.float32))
-    number = number.astype(jnp.bfloat16)
-    first, core, own, rest = buffers
-    core[pl.ds(2 * rows, TAG_ROWS), :] = number
-    own[pl.ds(2 * rows, TAG_ROWS), :] = number
-    split = first.shape[1]
+    mom = plan.mom
+    own, rest, same, cross, block = buffers
+    own[pl.ds(2 * rows, TAG_ROWS), :] = tag_of(partner, proj.shape[-1])
+    start = peram.shape[-2] - rest.shape[1]
+    source = peram.at[plan.peer_local(), plan.give, :, pl.ds(start, rest.shape[1])]
     copies = [
-        [(peram.at[peer, give, :, pl.ds(0, split)], first)],
-        two_slices(proj, core, plan.local(1), mom ^ 1),
         two_slices(proj, own, mom ^ 2, mom ^ 3),
-        [(peram.at[peer, give, :, pl.ds(split, rest.shape[1])], rest)],
+        [(source, rest)],
+        two_slices(proj, same, plan.local(0), plan.local(1)),
+        two_slices(proj, cross, plan.local(2), plan.local(3)),
+        [(peram.at[mom, plan.keep], block)],
     ]
     through(list(zip(copies, buffers, outs)), ins, leaving)
 
 
-def pack_far(sizes, seps, peram, proj, after, *refs):
-    outs, buffers, (ins, leaving) = refs[:3], refs[3:6], refs[6:]
+def pack_later(sizes, seps, partner, proj, own, after, *refs):
+    outs, buffers, (ins, leaving) = refs[:2], refs[2:4], refs[4:]
     plan = Plan(seps, sizes)
-    same, cross, block = buffers
+    rows = proj.shape[1]
+    trade, near = buffers
+    trade[pl.ds(2 * rows, TAG_ROWS), :] = tag_of(partner, proj.shape[-1])
+    spot = pl.ds(2 * rows, TAG_ROWS)
     copies = [
-        two_slices(proj, same, plan.local(0), plan.local(1)),
-        two_slices(proj, cross, plan.local(2), plan.local(3)),
-        [(peram.at[plan.mom, plan.keep], block)],
+        [
+            (proj.at[plan.mom ^ 1], trade.at[span(0, rows)]),
+            (own.at[span(1, rows)], trade.at[span(1, rows)]),
+            (own.at[spot], trade.at[pl.ds(2 * rows + TAG_ROWS, TAG_ROWS)]),
+        ],
+        two_slices(proj, near, plan.local(2), plan.local(3)),
     ]
     through(list(zip(copies, buffers, outs)), ins, leaving)
 
 
-def choose(sizes, seps, near, far, proj, after, out, others, sems):
-    plan = Plan(seps, sizes)
-    flag = lax.rem(plan.peer_hops(), 2)
-    rows = proj.shape[1]
-    copies = [(proj.at[plan.local(i + 2)], others.at[span(i, rows)]) for i in (0, 1)]
+def choose(sizes, seps, near, far, after, out, sems):
+    flag = lax.rem(Plan(seps, sizes).peer_hops(), 2)
 
     @pl.when(flag == 0)
     def _():
-        run_copies([(near, out)] + copies, sems)
+        run_copies([(near, out)], sems)
 
     @pl.when(flag != 0)
     def _():
-        run_copies([(far, out)] + copies, sems)
-
-
-def gate(first, rest, first_out, rest_out, token):
+        run_copies([(far, out)], sems)
+
+
+def gate(first, rest, after, first_out, rest_out, token):
     token[...] = jnp.zeros(token.shape, token.dtype)
 
 
@@ -200,7 +214,7 @@
         set_turns(turns, r, real, imag)
     u_ref[...] = jnp.zeros(u_ref.shape, u_ref.dtype)
 
-    def write(spin, column, a, b, minus_b):
+    def write(spin, column, a, b):
         add_to(u_ref, along(column, nev), along(spin, nev), a)
         add_to(u_ref, along(column, nev), along(spin, nev, width), b)
 
@@ -208,49 +222,57 @@
 
 
 def own_dot(u_ref, y_ref, ht):
-    for tile in range(ht.shape[-1] // TILE):
-        lanes = slice(tile * TILE, (tile + 1) * TILE)
+    width = u_ref.shape[0]
+    for tile in range(2 * width // TILE):
+        start = tile * TILE
         out = lax.dot_general(
-            u_ref[...], y_ref[lanes, :], NT_DIMS, preferred_element_type=jnp.float32
-        )
-        ht[:, lanes] = out.astype(jnp.bfloat16)
+            u_ref[...], y_ref[start : start + TILE, :], NT_DIMS, preferred_element_type=jnp.float32
+        ).astype(jnp.bfloat16)
+        if start < width:
+            ht[:, width + start : width + start + TILE] = out
+        else:
+            ht[:, start - width : start - width + TILE] = out
+            ht[:, width + start : width + start + TILE] = -out
 
 
 def codes_of(gamma, op, nterm):
     return [gamma[op, r] for r in range(nterm)]
 
 
-def own_kernel_01(gamma, block, proj, core, y_ref, h_ref, x_ref, p_ref, u0, u1, turns0, turns1, sems):
+def own_kernel_0(gamma, block, proj, y_ref, h_ref, token, x_ref, p_ref, u_ref, turns, sems):
     mom = lax.axis_index("mom")
-    rows = proj.shape[1]
-    run_copies(
-        [
-            (block, x_ref),
-            (proj.at[mom], p_ref.at[0]),
-            (core.at[span(1, rows)], p_ref.at[1]),
-        ],
-        sems,
-    )
+    run_copies([(block, x_ref), (proj.at[mom], p_ref.at[0])], sems)
     width = x_ref.shape[-1]
     real, imag = x_ref[0], x_ref[1]
     y_ref[:width, :width] = real
     y_ref[:width, width:] = -imag
     y_ref[width:, :width] = imag
     y_ref[width:, width:] = real
-    nterm = turns0.shape[0]
-    own_fill(codes_of(gamma, mom, nterm), p_ref, 0, u0, turns0)
-    own_dot(u0, y_ref, h_ref.at[0])
-    own_fill(codes_of(gamma, mom ^ 1, nterm), p_ref, 1, u1, turns1)
-    own_dot(u1, y_ref, h_ref.at[1])
-
-
-def own_kernel_23(sizes, seps, gamma, partner, core, own, forward, y_ref, h_in, *refs):
+    own_fill(codes_of(gamma, mom, turns.shape[0]), p_ref, 0, u_ref, turns)
+    own_dot(u_ref, y_ref, h_ref.at[0])
+    token[...] = jnp.zeros(token.shape, token.dtype)
+
+
+def own_kernel_2(gamma, own, y_ref, h_in, h_ref, token, p_ref, u_ref, turns, sems):
+    run_copies([(own.at[span(0, p_ref.shape[1])], p_ref.at[0])], sems)
+    codes = codes_of(gamma, lax.axis_index("mom") ^ 2, turns.shape[0])
+    own_fill(codes, p_ref, 0, u_ref, turns)
+    own_dot(u_ref, y_ref, h_ref.at[2])
+    token[...] = jnp.zeros(token.shape, token.dtype)
+
+
+def own_kernel_13(sizes, seps, gamma, partner, own, traded, y_ref, h_in, after, *refs):
     h_ref, label, token, p_ref, u0, u1, turns0, turns1, tags, sems = refs
     rows = p_ref.shape[1]
-    spot = pl.ds(core.shape[0] - TAG_ROWS, TAG_ROWS)
+    spots = [pl.ds(2 * rows, TAG_ROWS), pl.ds(2 * rows + TAG_ROWS, TAG_ROWS)]
     run_copies(
-        [(own.at[span(0, rows)], p_ref.at[0]), (forward.at[span(1, rows)], p_ref.at[1])]
-        + [(ref.at[spot], tags.at[n]) for n, ref in enumerate((core, own, forward))],
+        [
+            (traded.at[span(0, rows)], p_ref.at[0]),
+            (traded.at[span(1, rows)], p_ref.at[1]),
+            (traded.at[spots[0]], tags.at[0]),
+            (own.at[spots[0]], tags.at[1]),
+            (traded.at[spots[1]], tags.at[2]),
+        ],
         sems,
     )
     plan = Plan(seps, sizes)
@@ -266,42 +288,44 @@
         label[p] = jnp.where(plan.forward, back, mom ^ p)
         label[count + p] = jnp.where(plan.forward, back, partners[p]) ^ mom
     nterm = turns0.shape[0]
-    own_fill(codes_of(gamma, mom ^ 2, nterm), p_ref, 0, u0, turns0)
-    own_dot(u0, y_ref, h_ref.at[2])
+    own_fill(codes_of(gamma, mom ^ 1, nterm), p_ref, 0, u0, turns0)
+    own_dot(u0, y_ref, h_ref.at[1])
     own_fill(codes_of(gamma, mom ^ 3, nterm), p_ref, 1, u1, turns1)
     own_dot(u1, y_ref, h_ref.at[3])
     token[...] = jnp.zeros(token.shape, token.dtype)
 
 
 def other_products(pieces, gamma, label, h_ref, refs):
-    k_ref, p_ref, va, vb, turns_a, turns_b = refs
+    k_ref, p_ref, wa, wb, turns_a, turns_b = refs
     mom = lax.axis_index("mom")
     nterm, nev = turns_a.shape[0], turns_a.shape[-1]
-    width = h_ref.shape[1]
+    width = wa.shape[0]
     for n, piece in enumerate(pieces):
-        v_ref, turns = ((va, turns_a), (vb, turns_b))[n % 2]
+        w_ref, turns = ((wa, turns_a), (wb, turns_b))[n % 2]
         for r in range(nterm):
             real, imag = (p_ref[n, m * nev : (m + 1) * nev] for m in (2 * r, 2 * r + 1))
             set_turns(turns, r, real, imag)
-        v_ref[...] = jnp.zeros(v_ref.shape, v_ref.dtype)
-
-        def write(spin, column, a, b, minus_b, v_ref=v_ref):
-            add_to(v_ref, along(spin, nev), along(column, nev), a)
-            add_to(v_ref, along(spin, nev), along(column, nev, width), minus_b)
-            add_to(v_ref, along(spin, nev, width), along(column, nev), b)
-            add_to(v_ref, along(spin, nev, width), along(column, nev, width), a)
+        w_ref[...] = jnp.zeros(w_ref.shape, w_ref.dtype)
+
+        def write(spin, column, a, b, w_ref=w_ref):
+            add_to(w_ref, along(spin, nev), along(column, nev), a)
+            add_to(w_ref, along(spin, nev), along(column, nev, width), b)
 
         fill_spin_blocks(codes_of(gamma, mom ^ piece, nterm), turns, write)
         own = label[4 + piece]
-        for tile in range(2 * width // TILE):
+        for tile in range(width // TILE):
             lanes = slice(tile * TILE, (tile + 1) * TILE)
-            k_ref[n, :, lanes] = lax.dot_general(
-                h_ref[own], v_ref[lanes, :], NT_DIMS, preferred_element_type=jnp.float32
+            weights = w_ref[lanes, :]
+            k_ref[n, :width, lanes] = lax.dot_general(
+                h_ref[own, :, width:], weights, NT_DIMS, preferred_element_type=jnp.float32
             )
+            k_ref[n, width:, lanes] = lax.dot_general(
+                h_ref[own, :, : 2 * width], weights, NT_DIMS, preferred_element_type=jnp.float32
+            )
 
 
 def other_kernel_02(sizes, seps, gamma, label, h_ref, proj, near, far_same, far_cross, *refs):
-    k_ref, p_ref, va, vb, turns_a, turns_b, sems = refs
+    k_ref, p_ref, wa, wb, turns_a, turns_b, sems = refs
     plan = Plan(seps, sizes)
     rows = p_ref.shape[1]
     low = span(0, rows)
@@ -315,14 +339,14 @@
     def _():
         run_copies([(far_same.at[low], p_ref.at[0]), (far_cross.at[low], p_ref.at[1])], sems)
 
-    out = (k_ref, p_ref, va, vb, turns_a, turns_b)
+    out = (k_ref, p_ref, wa, wb, turns_a, turns_b)
     other_products((0, 2), gamma, label, h_ref, out)
 
 
-def other_kernel_13(gamma, label, h_ref, traded, k_ref, p_ref, va, vb, turns_a, turns_b, sems):
+def other_kernel_13(gamma, label, h_ref, traded, k_ref, p_ref, wa, wb, turns_a, turns_b, sems):
     rows = p_ref.shape[1]
     run_copies([(traded.at[span(n, rows)], p_ref.at[n]) for n in range(2)], sems)
-    out = (k_ref, p_ref, va, vb, turns_a, turns_b)
+    out = (k_ref, p_ref, wa, wb, turns_a, turns_b)
     other_products((1, 3), gamma, label, h_ref, out)
 
 
@@ -334,14 +358,15 @@
     def step(index, totals):
         row = pl.multiple_of(index * rows, rows)
         here = pl.ds(pl.multiple_of(offset + row, rows), rows)
+        later = pl.ds(pl.multiple_of(width + offset + row, rows), rows)
         totals = list(totals)
         for spin in range(NSPIN):
-            lanes, later = along(spin, nev), along(spin, nev, width)
+            lanes = along(spin, nev)
             real = source[0, pl.ds(row, rows), lanes].astype(jnp.float32)
             imag = source[1, pl.ds(row, rows), lanes].astype(jnp.float32)
             for n in range(len(totals) // 2):
                 k_ref, p = k_refs[n // 2], n % 2
-                kr, ki = k_ref[p, here, lanes], k_ref[p, here, later]
+                kr, ki = k_ref[p, here, lanes], k_ref[p, later, lanes]
                 totals[2 * n] += real * kr - imag * ki
                 totals[2 * n + 1] += real * ki + imag * kr
         return tuple(totals)
@@ -349,30 +374,27 @@
     return lax.fori_loop(0, source.shape[1] // rows, step, totals)
 
 
-def early_kernel(sizes, seps, ka, kb, near, far, sums_ref, part_ref, sems):
+def trace_kernel(sizes, sep_count, seps, label, ka, kb, near, far, rest, out_ref, first_buf, rest_buf, sems):
     plan = Plan(seps, sizes)
-    count = sums_ref.shape[0]
+    count = 2 * ka.shape[0]
+    width = rest_buf.shape[-1]
+    nev = width // NSPIN
     flag = lax.rem(lax.div(plan.hops(0), max(sizes[2] // 2, 1)), 2)
+    later = pltpu.make_async_copy(rest, rest_buf, sems.at[1])
+    later.start()
 
     @pl.when(flag == 0)
     def _():
-        run_copies([(near, part_ref)], sems)
+        run_copies([(near, first_buf)], sems)
 
     @pl.when(flag != 0)
     def _():
-        run_copies([(far, part_ref)], sems)
-
-    zero = tuple(jnp.zeros(sums_ref.shape[1:], jnp.float32) for _ in range(count))
-    for n, total in enumerate(row_sums((ka, kb), part_ref, 0, zero)):
-        sums_ref[n] = total
-
-
-def late_kernel(sizes, sep_count, seps, label, ka, kb, rest_ref, sums_ref, out_ref):
-    plan = Plan(seps, sizes)
-    count = sums_ref.shape[0] // 2
-    width = rest_ref.shape[-1]
-    start = ka.shape[1] - rest_ref.shape[1]
-    totals = row_sums((ka, kb), rest_ref, start, tuple(sums_ref[n] for n in range(2 * count)))
+        run_copies([(far, first_buf)], sems)
+
+    totals = tuple(jnp.zeros((16, nev), jnp.float32) for _ in range(2 * count))
+    totals = row_sums((ka, kb), first_buf, 0, totals)
+    later.wait()
+    totals = row_sums((ka, kb), rest_buf, first_buf.shape[1], totals)
     sums = [jnp.sum(total, axis=0, keepdims=True) for total in totals]
     sums = [jnp.sum(total, axis=1, keepdims=True) * (1.0 / width) for total in sums]
     shape = out_ref.shape[1:]
@@ -491,99 +513,103 @@
             name=name,
         )(*operands)
 
-    leaving = [first_shape, tagged, tagged, rest_shape]
-    first, core, own, rest = call(
+    first, tick = call(
+        part(pack_first, sizes),
+        "pack_first",
+        [smem(), hbm()],
+        [hbm(), vmem()],
+        [first_shape, token],
+        buffers([first_shape]) + [dma(1), dma(1)],
+        58,
+    )(separations, peram_blocks)
+    leaving = [tagged, rest_shape, two, two, bf16(2, width, width)]
+    own, rest, far_same, far_cross, block = call(
         part(pack, sizes),
         "pack",
-        [smem()] * 2 + [hbm()] * 2,
+        [smem()] * 2 + [hbm()] * 2 + [vmem()],
         [hbm()] * len(leaving),
         leaving,
-        buffers(leaving) + [dma(6), dma(len(leaving))],
+        buffers(leaving) + [dma(8), dma(len(leaving))],
         58,
-    )(separations, partner, peram_blocks, proj)
+    )(separations, partner, peram_blocks, proj, swap_mom(tick, 1))
 
     plan = Plan(separations, sizes)
     first = swap_snk(first)
-    core = swap_mom(core, 1)
     own = swap_mom(own, 2)
     rest_near, rest_far = most_of(rest, plan.peer_hops())
-    forward = swap_mom(own, 1)
-    leaving = [two, two, bf16(2, width, width)]
-    far_same, far_cross, block = call(
-        part(pack_far, sizes),
-        "pack_far",
-        [smem()] + [hbm()] * 3,
+    if src_count == 2:
+        far_same, far_cross = next_src(far_same), next_src(far_cross, 1, 2)
+    u_scratch = pltpu.VMEM((width, 2 * width), jnp.bfloat16)
+    turns = pltpu.VMEM((nterm, 4, nev, nev), jnp.bfloat16)
+    piece = pltpu.VMEM((1, rows, nev), jnp.bfloat16)
+    pieces = pltpu.VMEM((2, rows, nev), jnp.bfloat16)
+    products = bf16(mom_count, width, 3 * width)
+    y, h, done_0 = call(
+        own_kernel_0,
+        "own_products_0",
+        [smem()] + [hbm()] * 2,
+        [vmem()] * 3,
+        [bf16(2 * width, 2 * width), products, token],
+        [pltpu.VMEM((2, width, width), jnp.bfloat16), piece, u_scratch, turns, dma(2)],
+        16,
+    )(gamma_index, block, proj)
+    leaving = [bf16(2 * (rows + TAG_ROWS), nev), two]
+    traded, near = call(
+        part(pack_later, sizes),
+        "pack_later",
+        [smem()] * 2 + [hbm()] * 2 + [vmem()],
         [hbm()] * len(leaving),
         leaving,
         buffers(leaving) + [dma(5), dma(len(leaving))],
-        58,
-    )(separations, peram_blocks, proj, core)
-    if src_count == 2:
-        far_same, far_cross = next_src(far_same), next_src(far_cross, 1, 2)
-
-    u_scratch = pltpu.VMEM((width, 2 * width), jnp.bfloat16)
-    v_scratch = pltpu.VMEM((2 * width, 2 * width), jnp.bfloat16)
-    turns = pltpu.VMEM((nterm, 4, nev, nev), jnp.bfloat16)
-    products = bf16(mom_count, width, 2 * width)
-    y, h = call(
-        own_kernel_01,
-        "own_products_01",
-        [smem()] + [hbm()] * 3,
+        16,
+    )(separations, partner, proj, own, done_0)
+    traded = swap_mom(traded, 1)
+    near = swap_mom(near, 2)
+    h, done_2 = call(
+        own_kernel_2,
+        "own_products_2",
+        [smem(), hbm()] + [vmem()] * 2,
         [vmem()] * 2,
-        [bf16(2 * width, 2 * width), products],
-        [
-            pltpu.VMEM((2, width, width), jnp.bfloat16),
-            pltpu.VMEM((2, rows, nev), jnp.bfloat16),
-            u_scratch,
-            u_scratch,
-            turns,
-            turns,
-            dma(3),
-        ],
+        [products, token],
+        [piece, u_scratch, turns, dma(1)],
         16,
-    )(gamma_index, block, proj, core)
-    h, label, done_h = call(
-        part(own_kernel_23, sizes),
-        "own_products_23",
-        [smem()] * 3 + [hbm()] * 3 + [vmem()] * 2,
-        [vmem(), smem(), vmem()],
-        [products, jax.ShapeDtypeStruct((2 * mom_count,), jnp.int32), token],
-        [
-            pltpu.VMEM((2, rows, nev), jnp.bfloat16),
-            u_scratch,
-            u_scratch,
-            turns,
-            turns,
-            pltpu.VMEM((3, TAG_ROWS, nev), jnp.bfloat16),
-            dma(5),
-        ],
-        16,
-        {7: 0},
-    )(separations, gamma_index, partner, core, own, forward, y, h)
+        {3: 0},
+    )(gamma_index, own, y, h)
 
     if src_count > 2:
         rest_near = jnp.where(plan.peer_hops() // (src_count // 2) != 0, rest_far, rest_near)
         rest_far = rest_near
-    rest, near = call(
+    rest = call(
         part(choose, sizes),
         "choose",
-        [smem()] + [hbm()] * 3 + [vmem()],
-        [vmem()] * 2,
-        [rest_shape, two],
-        [dma(3)],
+        [smem()] + [hbm()] * 2 + [vmem()],
+        vmem(),
+        rest_shape,
+        [dma(1)],
         16,
-    )(separations, rest_near, rest_far, proj, done_h)
-    near = swap_mom(near, 2)
+    )(separations, rest_near, rest_far, done_0)
     first, rest, opened = alias(
         gate,
         "gate",
-        [anywhere()] * 2,
+        [anywhere()] * 2 + [vmem()],
         [first_shape, rest_shape, token],
         {0: 0, 1: 1},
-        (first, rest),
+        (first, rest, done_2),
     )
     rest = swap_snk(rest)
     first_near, first_far = most_of(first, plan.hops(0))
+    h, label, done_h = call(
+        part(own_kernel_13, sizes),
+        "own_products_13",
+        [smem()] * 3 + [hbm()] * 2 + [vmem()] * 3,
+        [vmem(), smem(), vmem()],
+        [products, jax.ShapeDtypeStruct((2 * mom_count,), jnp.int32), token],
+        [pieces, u_scratch, u_scratch, turns, turns]
+        + [pltpu.VMEM((3, TAG_ROWS, nev), jnp.bfloat16), dma(5)],
+        16,
+        {6: 0},
+    )(separations, gamma_index, partner, own, traded, y, h, opened)
+
     other_trade = call(
         part(other_pack, sizes),
         "other_pack",
@@ -592,7 +618,7 @@
         two,
         [dma(2)],
         16,
-    )(separations, proj, near, far_same, far_cross, opened)
+    )(separations, proj, near, far_same, far_cross, done_h)
     other_got = swap_mom(other_trade, 1)
     if src_count != 2:
 
@@ -605,8 +631,8 @@
         far_same = moved(lax.dynamic_index_in_dim(proj, plan.local(0), 0, keepdims=False))
         far_cross, other_got = moved(near[:rows]), moved(other_got)
 
-    k_shape = jax.ShapeDtypeStruct((2, width, 2 * width), jnp.float32)
-    scratch = [pltpu.VMEM((2, rows, nev), jnp.bfloat16), v_scratch, v_scratch, turns, turns, dma(2)]
+    k_shape = jax.ShapeDtypeStruct((2, 2 * width, width), jnp.float32)
+    scratch = [pieces, u_scratch, u_scratch, turns, turns, dma(2)]
     ka = call(
         part(other_kernel_02, sizes),
         "other_products_02",
@@ -626,27 +652,18 @@
         20,
     )(gamma_index, label, h, other_got)
 
-    sums = call(
-        part(early_kernel, sizes),
-        "early_traces",
-        [smem()] + [vmem()] * 2 + [hbm()] * 2,
-        vmem(),
-        jax.ShapeDtypeStruct((2 * mom_count, 16, nev), jnp.float32),
-        [pltpu.VMEM((2, split, width), jnp.bfloat16), dma(1)],
-        20,
-    )(separations, ka, kb, first_near, first_far)
     device_count = src_count * snk_count * mom_count
     values = time_count * sep_count * 2
     lines = (values + 127) // 128
     out = call(
-        part(late_kernel, sizes, sep_count),
-        "late_traces",
-        [smem()] * 2 + [vmem()] * 4,
+        part(trace_kernel, sizes, sep_count),
+        "traces",
+        [smem()] * 2 + [vmem()] * 2 + [hbm()] * 3,
         vmem(),
         jax.ShapeDtypeStruct((device_count, lines, 128), jnp.float32),
-        [],
+        buffers([first_shape, rest_shape]) + [dma(2)],
         20,
-    )(separations, label, ka, kb, rest, sums)
+    )(separations, label, ka, kb, first_near, first_far, rest)
     out = lax.all_to_all(out, ("src", "snk", "mom"), split_axis=0, concat_axis=0, tiled=True)
     out = jnp.sum(out, axis=0).reshape(lines * 128)[:values]
     return out.reshape(time_count, sep_count, 1, 2)

time: 85.4 us -> 87.5 us (1.025)
  blocking collectives: 13.5 us -> 10.8 us
  waiting for transfers between devices: 18 us -> 20.2 us
  local copies, waits for them, and re-layouts: 3.95 us -> 5.45 us
  Pallas kernels: 37.1 us -> 38.2 us
    ppermute x4, waiting for transfers between devices: 0.01 us -> 10.3 us  [next_src(): return lax.ppermute(array, ('src', 'mom'), pairs)]
    ppermute x5, waiting for transfers between devices: 13.4 us -> 7.6 us  [swap_mom(): return lax.ppermute(array, 'mom', [(a, a ^ i) for a in range(mom_count)])]
    pallas_call x7 -> x8, Pallas kernels: 22.9 us -> 25.9 us  [the longest x1 5.35 us: shards(): call(part(own_kernel_13, sizes), 'own_products_13', [smem()] * 3 + [hbm()...]
    all_to_all x1, blocking collectives: 13.5 us -> 10.8 us  [shards(): lax.all_to_all(out, ('src', 'snk', 'mom'), split_axis=0, concat_axis=0, t...]
    ppermute x2, waiting for transfers between devices: 4.6 us -> 2.29 us  [swap_snk(): return lax.ppermute(array, 'snk', pairs)]
    ppermute x5, starting transfers between devices: 4.5 us -> 2.81 us  [swap_mom(): return lax.ppermute(array, 'mom', [(a, a ^ i) for a in range(mom_count)])]
    unnamed x26 -> x18, local copies, waits for them, and re-layouts: 3.11 us -> 4.61 us
    ppermute x2, starting transfers between devices: 2.69 us -> 3.66 us  [swap_snk(): return lax.ppermute(array, 'snk', pairs)]
  transfers between devices with their start and end apart: 11 -> 11, of which waited for: 3 -> 4; matrix products, arithmetic and copies ran while one was open for 0% -> 0% of each run, Pallas kernels for 38% -> 36%
where the time goes in v7:
time: 87.5 us; the launch traced here: 87.1 us
  Pallas kernels  38.2 us (44%)
  waiting for transfers between devices  20.2 us (23%)
  starting transfers between devices  11.5 us (13%)
  blocking collectives  10.8 us (12%)
  local copies, waits for them, and re-layouts  5.45 us (6%)
    all_to_all x1, blocking collectives, shards(): lax.all_to_all(out, ('src', 'snk', 'mom'), split_axis=0, concat_axis=0, t...  10.8 us
    ppermute x4, waiting for transfers between devices, next_src(): return lax.ppermute(array, ('src', 'mom'), pairs)  10.3 us
    ppermute x5, waiting for transfers between devices, swap_mom(): return lax.ppermute(array, 'mom', [(a, a ^ i) for a in range(mom_count)])  7.6 us
    pallas_call x1, Pallas kernels, shards(): call(part(own_kernel_13, sizes), 'own_products_13', [smem()] * 3 + [hbm()...  5.35 us
    ppermute x4, starting transfers between devices, next_src(): return lax.ppermute(array, ('src', 'mom'), pairs)  5.07 us
    pallas_call x1, Pallas kernels, shards(): call(part(other_kernel_02, sizes), 'other_products_02', [smem()] * 3 + [v...  4.97 us
    pallas_call x1, Pallas kernels, shards(): call(other_kernel_13, 'other_products_13', [smem()] * 2 + [vmem(), hbm()]...  4.94 us
    unnamed x18, local copies, waits for them, and re-layouts  4.61 us
  transfers between devices with their start and end apart: 11, of which 4 were waited for; matrix products, arithmetic and copies ran while one was open for 0% of the time, Pallas kernels for 36%

profile of v7, /device:TPU:0, one launch (start us, length us, event | category | flops | bytes accessed | tf_op | source)
XLA Modules:
  0.0 87.1 jit_solution(12946865948268345199)
XLA Ops:
  0.0 3.3 %pack_first.1 = (bf16[2,320,512]{2,1,0:T(8,128)(2,1)}, bf16[16,128]{1,0:T(8,128)(2,1)}) custom-call(s32[4]{0:T(128)} %seps.15, bf16[4,2,2,512,512]{4,3,2,1,0:T(8,128)(2,1)} %peram.3), custom_call_target="tpu_custom_call" | custom-call | flops 9999999827968 | bytes 10000000000 | tf_op jit(solution)/shard_map/pack_first/pallas_call | solution.py:516
  3.3 0.5 collective-permute-start
  3.8 3.7 %collective-permute-start.3 = (bf16[2,320,512]{2,1,0:T(8,128)(2,1)}, bf16[2,320,512]{2,1,0:T(8,128)(2,1)}, u32[]{:S(2)}, u32[]{:S(2)}) collective-permute-start(bf16[2,320,512]{2,1,0:T(8,128)(2,1)} %get-tuple-element.33), channel_id=1, source_target_pairs={{0,8},{4,12},{8,0},{12,4},{1,9},{5,13},{9,1},{13,5},{2,10},{6,14},... | collective-permute-start | bytes 1966088 | tf_op jit(solution)/shard_map/ppermute | solution.py:455
  8.1 0.0 collective-permute-done.after
  8.1 0.0 copy-start.8
  8.1 0.6 copy-done.8
  8.7 4.2 %pack.1 = (bf16[2064,128]{1,0:T(8,128)(2,1)}, bf16[2,192,512]{2,1,0:T(8,128)(2,1)}, bf16[2048,128]{1,0:T(8,128)(2,1)}, bf16[2048,128]{1,0:T(8,128)(2,1)}, bf16[2,512,512]{2,1,0:T(8,128)(2,1)}) custom-call(s32[4]{0:T(128)} %seps.15, s32[1]{0:T(128)S(6)} %copy.16.partner, bf16[4,2,2,512,512]{4,3,2,1,0:T(8,128)(2,1)} %peram.3, bf16[4,1024,128]{2,1,0:T(8,128)(2,1)} %bitcast.2, ...), custom_call_target="tpu_custom_call" | custom-call | flops 9999999827968 | bytes 10000000000 | tf_op jit(solution)/shard_map/pack/pallas_call | solution.py:526
  12.9 1.5 %collective-permute-start.1 = (bf16[2064,128]{1,0:T(8,128)(2,1)}, bf16[2064,128]{1,0:T(8,128)(2,1)}, u32[]{:S(2)}, u32[]{:S(2)}) collective-permute-start(bf16[2064,128]{1,0:T(8,128)(2,1)} %get-tuple-element.26), channel_id=1, source_target_pairs={{0,2},{1,3},{2,0},{3,1},{4,6},{5,7},{6,4},{7,5},{8,10},{9,11},{10,... | collective-permute-start | bytes 1585160 | tf_op jit(solution)/shard_map/ppermute | solution.py:451
  14.5 1.5 %collective-permute-start.4 = (bf16[2,192,512]{2,1,0:T(8,128)(2,1)}, bf16[2,192,512]{2,1,0:T(8,128)(2,1)}, u32[]{:S(2)}, u32[]{:S(2)}) collective-permute-start(bf16[2,192,512]{2,1,0:T(8,128)(2,1)} %get-tuple-element.34.near), channel_id=1, source_target_pairs={{16,0},{17,1},{18,2},{19,3},{0,16},{1,17},{2,18},{3,19},{20,4},{21... | collective-permute-start | bytes 1179656 | tf_op jit(solution)/shard_map/ppermute | solution.py:463
  15.9 0.5 collective-permute-start.6
  16.5 1.5 %collective-permute-start.7 = (bf16[2048,128]{1,0:T(8,128)(2,1)}, bf16[2048,128]{1,0:T(8,128)(2,1)}, u32[]{:S(2)}, u32[]{:S(2)}) collective-permute-start(bf16[2048,128]{1,0:T(8,128)(2,1)} %get-tuple-element.41), channel_id=1, source_target_pairs={{18,0},{19,1},{16,2},{17,3},{2,16},{3,17},{0,18},{1,19},{22,4},{23... | collective-permute-start | bytes 1572872 | tf_op jit(solution)/shard_map/ppermute | solution.py:463
  18.0 0.0 copy-done
  18.0 0.0 copy-done.2
  18.0 1.2 %copy-done.7 = bf16[2,512,512]{2,1,0:T(8,128)(2,1)S(1)} copy-done((bf16[2,512,512]{2,1,0:T(8,128)(2,1)S(1)}, bf16[2,512,512]{2,1,0:T(8,128)(2,1)}, u32[]{:S(2)}) %copy-start.7) | copy-done | bytes 1048600
  19.2 2.5 %own_products_0.1 = (bf16[1024,1024]{1,0:T(8,128)(2,1)S(1)}, bf16[4,512,1536]{2,1,0:T(8,128)(2,1)S(1)}, bf16[16,128]{1,0:T(8,128)(2,1)S(1)}) custom-call(s32[4,4]{1,0:T(4,128)S(1)} %copy-done.2, bf16[2,512,512]{2,1,0:T(8,128)(2,1)S(1)} %copy-done.7, bf16[4,1024,128]{2,1,0:T(8,128)(2,1)S(1)} %bitcast.3), custom_call_target="tpu_custom_call" | custom-call | flops 9999999827968 | bytes 10000000000 | tf_op jit(solution)/shard_map/own_products_0/pallas_call | solution.py:547
  21.7 5.1 %collective-permute-done.4.far = bf16[2,192,512]{2,1,0:T(8,128)(2,1)} collective-permute-done((bf16[2,192,512]{2,1,0:T(8,128)(2,1)}, bf16[2,192,512]{2,1,0:T(8,128)(2,1)}, u32[]{:S(2)}, u32[]{:S(2)}) %collective-permute-start.4) | collective-permute-done | bytes 393248 | tf_op jit(solution)/shard_map/ppermute | solution.py:463
  26.8 0.0 copy-done.1
  26.8 0.0 copy-done.3
  26.8 1.5 %choose.1.rest = bf16[2,192,512]{2,1,0:T(8,128)(2,1)} custom-call(s32[4]{0:T(128)S(1)} %copy-done.3, bf16[2,192,512]{2,1,0:T(8,128)(2,1)S(1)} %copy-done.1, bf16[2,192,512]{2,1,0:T(8,128)(2,1)} %collective-permute-done.4.far, bf16[16,128]{1,0:T(8,128)(2,1)S(1)} %get-tuple-element.28.after), custom_call_target="tpu_custom_call" | custom-call | flops 9999999827968 | bytes 10000000000 | tf_op jit(solution)/shard_map/choose/pallas_call | solution.py:582
  28.3 0.0 collective-permute-done.1.own
  28.3 2.6 %pack_later.1 = (bf16[2080,128]{1,0:T(8,128)(2,1)}, bf16[2048,128]{1,0:T(8,128)(2,1)}) custom-call(s32[4]{0:T(128)S(1)} %copy-done.3, s32[1]{0:T(128)S(6)} %copy.16.partner, bf16[4,1024,128]{2,1,0:T(8,128)(2,1)S(1)} %bitcast.4, bf16[2064,128]{1,0:T(8,128)(2,1)} %collective-permute-done.1.own, bf16[16,128]{1,0:T(8,128)(2,1)S(1)} %get-tuple-element.28.after), custom_call_target="tpu_custom_call" | custom-call | flops 9999999827968 | bytes 10000000000 | tf_op jit(solution)/shard_map/pack_later/pallas_call | solution.py:557
  30.9 0.1 collective-permute-start.2
  31.0 0.6 collective-permute-start.5
  31.6 3.2 %own_products_2.1 = (bf16[4,512,1536]{2,1,0:T(8,128)(2,1)S(1)}, bf16[16,128]{1,0:T(8,128)(2,1)S(1)}) custom-call(s32[4,4]{1,0:T(4,128)S(1)} %copy-done.2, bf16[2064,128]{1,0:T(8,128)(2,1)} %collective-permute-done.1.own, bf16[1024,1024]{1,0:T(8,128)(2,1)S(1)} %get-tuple-element.30.y_ref, ...), custom_call_target="tpu_custom_call", output_to_operand_aliasing={{0}: (3, {})} | custom-call | flops 9999999827968 | bytes 10000000000 | tf_op jit(solution)/shard_map/own_products_2/pallas_call | solution.py:568
  34.8 2.3 %collective-permute-done.3.first = bf16[2,320,512]{2,1,0:T(8,128)(2,1)} collective-permute-done((bf16[2,320,512]{2,1,0:T(8,128)(2,1)}, bf16[2,320,512]{2,1,0:T(8,128)(2,1)}, u32[]{:S(2)}, u32[]{:S(2)}) %collective-permute-start.3) | collective-permute-done | bytes 655392 | tf_op jit(solution)/shard_map/ppermute | solution.py:455
  37.1 1.6 %collective-permute-start.9 = (bf16[2,320,512]{2,1,0:T(8,128)(2,1)}, bf16[2,320,512]{2,1,0:T(8,128)(2,1)}, u32[]{:S(2)}, u32[]{:S(2)}) collective-permute-start(bf16[2,320,512]{2,1,0:T(8,128)(2,1)} %get-tuple-element.43.near), channel_id=1, source_target_pairs={{16,0},{17,1},{18,2},{19,3},{0,16},{1,17},{2,18},{3,19},{20,4},{21... | collective-permute-start | bytes 1966088 | tf_op jit(solution)/shard_map/ppermute | solution.py:463
  38.7 0.0 collective-permute-done.2.traded
  38.7 0.0 collective-permute-start.10
  38.7 5.4 %own_products_13.1 = (bf16[4,512,1536]{2,1,0:T(8,128)(2,1)S(1)}, s32[8]{0:T(128)S(1)}, bf16[16,128]{1,0:T(8,128)(2,1)S(1)}) custom-call(s32[4]{0:T(128)S(1)} %copy-done.3, s32[4,4]{1,0:T(4,128)S(1)} %copy-done.2, s32[1]{0:T(128)S(6)} %copy.16.partner, bf16[2064,128]{1,0:T(8,128)(2,1)} %collective-permute-done.1.own, ...), custom_call_target="tpu_custom_call", output_to_operand_aliasing={{0}: (6, {})} | custom-call | flops 9999999827968 | bytes 10000000000 | tf_op jit(solution)/shard_map/own_products_13/pallas_call | solution.py:601
  44.1 0.0 copy-start.5
  44.1 0.0 collective-permute-done.6.far_same
  44.1 5.2 %collective-permute-done.7.far_cross = bf16[2048,128]{1,0:T(8,128)(2,1)} collective-permute-done((bf16[2048,128]{1,0:T(8,128)(2,1)}, bf16[2048,128]{1,0:T(8,128)(2,1)}, u32[]{:S(2)}, u32[]{:S(2)}) %collective-permute-start.7) | collective-permute-done | bytes 524320 | tf_op jit(solution)/shard_map/ppermute | solution.py:463
  49.3 7.6 %collective-permute-done.5.near = bf16[2048,128]{1,0:T(8,128)(2,1)} collective-permute-done((bf16[2048,128]{1,0:T(8,128)(2,1)}, bf16[2048,128]{1,0:T(8,128)(2,1)}, u32[]{:S(2)}, u32[]{:S(2)}) %collective-permute-start.5) | collective-permute-done | bytes 524320 | tf_op jit(solution)/shard_map/ppermute | solution.py:451
  56.9 2.4 %other_pack.1 = bf16[2048,128]{1,0:T(8,128)(2,1)} custom-call(s32[4]{0:T(128)S(1)} %copy-done.3, bf16[4,1024,128]{2,1,0:T(8,128)(2,1)S(1)} %bitcast.5, bf16[2048,128]{1,0:T(8,128)(2,1)} %collective-permute-done.5.near, bf16[2048,128]{1,0:T(8,128)(2,1)} %collective-permute-done.6.far_same, bf16[2048,128]{1,0:T(8,128)(2,1)} %collective-permute-done.7.far_cross, ...), custom_call_target="tpu_custom_call" | custom-call | flops 9999999827968 | bytes 10000000000 | tf_op jit(solution)/shard_map/other_pack/pallas_call | solution.py:613
  59.3 0.0 copy-done.5
  59.3 0.1 collective-permute-start.8
  59.4 0.0 copy-done.4
  59.4 2.8 %copy-done.6 = bf16[4,512,1536]{2,1,0:T(8,128)(2,1)S(1)} copy-done((bf16[4,512,1536]{2,1,0:T(8,128)(2,1)S(1)}, bf16[4,512,1536]{2,1,0:T(8,128)(2,1)}, u32[]{:S(2)}) %copy-start.6) | copy-done | bytes 6291480
  62.2 5.0 %other_products_02.1.ka = f32[2,1024,512]{2,1,0:T(8,128)S(1)} custom-call(s32[4]{0:T(128)S(1)} %copy-done.4, s32[4,4]{1,0:T(4,128)S(1)} %copy-done.2, s32[8]{0:T(128)S(1)} %get-tuple-element.37.label, bf16[4,512,1536]{2,1,0:T(8,128)(2,1)S(1)} %copy-done.6, bf16[4,1024,128]{2,1,0:T(8,128)(2,1)S(1)} %bitcast.6, bf16[2048,128]{1,0:T(8,128)(2,1)} %collective-permute-done.5.near, ...), custom_call_target="tpu_custom_call" | custom-call | flops 9999999827968 | bytes 10000000000 | tf_op jit(solution)/shard_map/other_products_02/pallas_call | solution.py:636
  67.2 0.0 collective-permute-done.8.traded
  67.2 4.9 %other_products_13.1.kb = f32[2,1024,512]{2,1,0:T(8,128)S(1)} custom-call(s32[4,4]{1,0:T(4,128)S(1)} %copy-done.2, s32[8]{0:T(128)S(1)} %get-tuple-element.37.label, bf16[4,512,1536]{2,1,0:T(8,128)(2,1)S(1)} %copy-done.6, bf16[2048,128]{1,0:T(8,128)(2,1)} %collective-permute-done.8.traded), custom_call_target="tpu_custom_call" | custom-call | flops 9999999827968 | bytes 10000000000 | tf_op jit(solution)/shard_map/other_products_13/pallas_call | solution.py:645
  72.1 0.0 collective-permute-done.10.rest
  72.2 0.0 collective-permute-done.9.far
  72.2 3.3 %traces.1 = f32[32,1,128]{2,1,0:T(1,128)S(1)} custom-call(s32[4]{0:T(128)S(1)} %copy-done.4, s32[8]{0:T(128)S(1)} %get-tuple-element.37.label, f32[2,1024,512]{2,1,0:T(8,128)S(1)} %other_products_02.1.ka, f32[2,1024,512]{2,1,0:T(8,128)S(1)} %other_products_13.1.kb, bf16[2,320,512]{2,1,0:T(8,128)(2,1)} %get-tuple-element.43.near, ...), custom_call_target="tpu_custom_call" | custom-call | flops 9999999827968 | bytes 10000000000 | tf_op jit(solution)/shard_map/traces/pallas_call | solution.py:658
  75.4 10.8 %all_to_all.5 = f32[32,1,128]{2,1,0:T(1,128)S(1)} all-to-all(f32[32,1,128]{2,1,0:T(1,128)S(1)} %traces.1), channel_id=1, replica_groups=mesh['src'=2,'snk'=4,'mom'=4] {'src','snk','mom'}, dimensions={0} | all-to-all | bytes 32768 | tf_op jit(solution)/shard_map/all_to_all | solution.py:667
  86.2 0.1 reduce_sum.11
  86.3 0.1 reshape.11
  86.4 0.7 copy.11
  (9 shorter events, 0.0 us)
Async XLA Ops:
  3.3 4.8 %collective-permute-start = (bf16[16,128]{1,0:T(8,128)(2,1)}, bf16[16,128]{1,0:T(8,128)(2,1)S(1)}, u32[]{:S(2)}, u32[]{:S(2)}) collective-permute-start(bf16[16,128]{1,0:T(8,128)(2,1)} %get-tuple-element.25), channel_id=1, source_target_pairs={{0,1},{1,0},{2,3},{3,2},{4,5},{5,4},{6,7},{7,6},{8,9},{9,8},{10,11... | collective-permute-start | bytes 12296 | tf_op jit(solution)/shard_map/ppermute | solution.py:451
  3.8 33.3 %collective-permute-start.3 = (bf16[2,320,512]{2,1,0:T(8,128)(2,1)}, bf16[2,320,512]{2,1,0:T(8,128)(2,1)}, u32[]{:S(2)}, u32[]{:S(2)}) collective-permute-start(bf16[2,320,512]{2,1,0:T(8,128)(2,1)} %get-tuple-element.33), channel_id=1, source_target_pairs={{0,8},{4,12},{8,0},{12,4},{1,9},{5,13},{9,1},{13,5},{2,10},{6,14},... | collective-permute-start | bytes 1966088 | tf_op jit(solution)/shard_map/ppermute | solution.py:455
  8.1 0.6 copy-start.8
  8.7 9.3 %copy-start = (bf16[4,1,4,2,128,128]{5,4,3,2,1,0:T(8,128)(2,1)S(1)}, bf16[4,1,4,2,128,128]{5,4,3,2,1,0:T(8,128)(2,1)}, u32[]{:S(2)}) copy-start(bf16[4,1,4,2,128,128]{5,4,3,2,1,0:T(8,128)(2,1)} %param.6) | copy-start | bytes 3145732
  8.7 9.3 %copy-start.2 = (s32[4,4]{1,0:T(4,128)S(1)}, s32[4,4]{1,0:T(4,128)}, u32[]{:S(2)}) copy-start(s32[4,4]{1,0:T(4,128)} %gamma.9) | copy-start | bytes 196
  12.9 15.4 %collective-permute-start.1 = (bf16[2064,128]{1,0:T(8,128)(2,1)}, bf16[2064,128]{1,0:T(8,128)(2,1)}, u32[]{:S(2)}, u32[]{:S(2)}) collective-permute-start(bf16[2064,128]{1,0:T(8,128)(2,1)} %get-tuple-element.26), channel_id=1, source_target_pairs={{0,2},{1,3},{2,0},{3,1},{4,6},{5,7},{6,4},{7,5},{8,10},{9,11},{10,... | collective-permute-start | bytes 1585160 | tf_op jit(solution)/shard_map/ppermute | solution.py:451
  14.5 12.3 %collective-permute-start.4 = (bf16[2,192,512]{2,1,0:T(8,128)(2,1)}, bf16[2,192,512]{2,1,0:T(8,128)(2,1)}, u32[]{:S(2)}, u32[]{:S(2)}) collective-permute-start(bf16[2,192,512]{2,1,0:T(8,128)(2,1)} %get-tuple-element.34.near), channel_id=1, source_target_pairs={{16,0},{17,1},{18,2},{19,3},{0,16},{1,17},{2,18},{3,19},{20,4},{21... | collective-permute-start | bytes 1179656 | tf_op jit(solution)/shard_map/ppermute | solution.py:463
  15.9 28.1 %collective-permute-start.6 = (bf16[2048,128]{1,0:T(8,128)(2,1)}, bf16[2048,128]{1,0:T(8,128)(2,1)}, u32[]{:S(2)}, u32[]{:S(2)}) collective-permute-start(bf16[2048,128]{1,0:T(8,128)(2,1)} %get-tuple-element.40), channel_id=1, source_target_pairs={{16,0},{17,1},{18,2},{19,3},{0,16},{1,17},{2,18},{3,19},{20,4},{21... | collective-permute-start | bytes 1572872 | tf_op jit(solution)/shard_map/ppermute | solution.py:463
  16.5 32.8 %collective-permute-start.7 = (bf16[2048,128]{1,0:T(8,128)(2,1)}, bf16[2048,128]{1,0:T(8,128)(2,1)}, u32[]{:S(2)}, u32[]{:S(2)}) collective-permute-start(bf16[2048,128]{1,0:T(8,128)(2,1)} %get-tuple-element.41), channel_id=1, source_target_pairs={{18,0},{19,1},{16,2},{17,3},{2,16},{3,17},{0,18},{1,19},{22,4},{23... | collective-permute-start | bytes 1572872 | tf_op jit(solution)/shard_map/ppermute | solution.py:463
  18.0 1.2 %copy-start.7 = (bf16[2,512,512]{2,1,0:T(8,128)(2,1)S(1)}, bf16[2,512,512]{2,1,0:T(8,128)(2,1)}, u32[]{:S(2)}) copy-start(bf16[2,512,512]{2,1,0:T(8,128)(2,1)} %get-tuple-element.27.block) | copy-start | bytes 3145732
  19.2 7.6 %copy-start.1 = (bf16[2,192,512]{2,1,0:T(8,128)(2,1)S(1)}, bf16[2,192,512]{2,1,0:T(8,128)(2,1)}, u32[]{:S(2)}) copy-start(bf16[2,192,512]{2,1,0:T(8,128)(2,1)} %get-tuple-element.34.near) | copy-start | bytes 1179652
  19.2 7.6 %copy-start.3 = (s32[4]{0:T(128)S(1)}, s32[4]{0:T(128)}, u32[]{:S(2)}) copy-start(s32[4]{0:T(128)} %seps.15) | copy-start | bytes 52
  30.9 7.8 %collective-permute-start.2 = (bf16[2080,128]{1,0:T(8,128)(2,1)}, bf16[2080,128]{1,0:T(8,128)(2,1)}, u32[]{:S(2)}, u32[]{:S(2)}) collective-permute-start(bf16[2080,128]{1,0:T(8,128)(2,1)} %get-tuple-element.29), channel_id=1, source_target_pairs={{0,1},{1,0},{2,3},{3,2},{4,5},{5,4},{6,7},{7,6},{8,9},{9,8},{10,11... | collective-permute-start | bytes 1597448 | tf_op jit(solution)/shard_map/ppermute | solution.py:451
  31.0 25.9 %collective-permute-start.5 = (bf16[2048,128]{1,0:T(8,128)(2,1)}, bf16[2048,128]{1,0:T(8,128)(2,1)}, u32[]{:S(2)}, u32[]{:S(2)}) collective-permute-start(bf16[2048,128]{1,0:T(8,128)(2,1)} %get-tuple-element.39), channel_id=1, source_target_pairs={{0,2},{1,3},{2,0},{3,1},{4,6},{5,7},{6,4},{7,5},{8,10},{9,11},{10,... | collective-permute-start | bytes 1572872 | tf_op jit(solution)/shard_map/ppermute | solution.py:451
  37.1 35.0 %collective-permute-start.9 = (bf16[2,320,512]{2,1,0:T(8,128)(2,1)}, bf16[2,320,512]{2,1,0:T(8,128)(2,1)}, u32[]{:S(2)}, u32[]{:S(2)}) collective-permute-start(bf16[2,320,512]{2,1,0:T(8,128)(2,1)} %get-tuple-element.43.near), channel_id=1, source_target_pairs={{16,0},{17,1},{18,2},{19,3},{0,16},{1,17},{2,18},{3,19},{20,4},{21... | collective-permute-start | bytes 1966088 | tf_op jit(solution)/shard_map/ppermute | solution.py:463
  38.7 33.5 %collective-permute-start.10 = (bf16[2,192,512]{2,1,0:T(8,128)(2,1)}, bf16[2,192,512]{2,1,0:T(8,128)(2,1)}, u32[]{:S(2)}, u32[]{:S(2)}) collective-permute-start(bf16[2,192,512]{2,1,0:T(8,128)(2,1)} %get-tuple-element.44), channel_id=1, source_target_pairs={{0,8},{4,12},{8,0},{12,4},{1,9},{5,13},{9,1},{13,5},{2,10},{6,14},... | collective-permute-start | bytes 1179656 | tf_op jit(solution)/shard_map/ppermute | solution.py:455
  44.1 15.3 %copy-start.5 = (bf16[4,512,1536]{2,1,0:T(8,128)(2,1)}, bf16[4,512,1536]{2,1,0:T(8,128)(2,1)S(1)}, u32[]{:S(2)}) copy-start(bf16[4,512,1536]{2,1,0:T(8,128)(2,1)S(1)} %get-tuple-element.38.h_ref) | copy-start | bytes 18874372
  56.9 2.5 %copy-start.4 = (s32[4]{0:T(128)S(1)}, s32[4]{0:T(128)}, u32[]{:S(2)}) copy-start(s32[4]{0:T(128)} %seps.15) | copy-start | bytes 52
  59.3 7.9 %collective-permute-start.8 = (bf16[2048,128]{1,0:T(8,128)(2,1)}, bf16[2048,128]{1,0:T(8,128)(2,1)}, u32[]{:S(2)}, u32[]{:S(2)}) collective-permute-start(bf16[2048,128]{1,0:T(8,128)(2,1)} %other_pack.1), channel_id=1, source_target_pairs={{0,1},{1,0},{2,3},{3,2},{4,5},{5,4},{6,7},{7,6},{8,9},{9,8},{10,11... | collective-permute-start | bytes 1572872 | tf_op jit(solution)/shard_map/ppermute | solution.py:451
  59.4 2.8 %copy-start.6 = (bf16[4,512,1536]{2,1,0:T(8,128)(2,1)S(1)}, bf16[4,512,1536]{2,1,0:T(8,128)(2,1)}, u32[]{:S(2)}) copy-start(bf16[4,512,1536]{2,1,0:T(8,128)(2,1)} %copy-done.5) | copy-start | bytes 18874372

commit v8 on v7

--- a/solution.py
+++ b/solution.py
@@ -139,11 +139,11 @@
 
 
 def pack(sizes, seps, partner, peram, proj, after, *refs):
-    outs, buffers, (ins, leaving) = refs[:5], refs[5:10], refs[10:]
+    outs, buffers, (ins, leaving) = refs[:6], refs[6:12], refs[12:]
     plan = Plan(seps, sizes)
     rows = proj.shape[1]
     mom = plan.mom
-    own, rest, same, cross, block = buffers
+    own, rest, same, cross, block, near = buffers
     own[pl.ds(2 * rows, TAG_ROWS), :] = tag_of(partner, proj.shape[-1])
     start = peram.shape[-2] - rest.shape[1]
     source = peram.at[plan.peer_local(), plan.give, :, pl.ds(start, rest.shape[1])]
@@ -153,28 +153,27 @@
         two_slices(proj, same, plan.local(0), plan.local(1)),
         two_slices(proj, cross, plan.local(2), plan.local(3)),
         [(peram.at[mom, plan.keep], block)],
-    ]
-    through(list(zip(copies, buffers, outs)), ins, leaving)
-
-
-def pack_later(sizes, seps, partner, proj, own, after, *refs):
-    outs, buffers, (ins, leaving) = refs[:2], refs[2:4], refs[4:]
-    plan = Plan(seps, sizes)
-    rows = proj.shape[1]
-    trade, near = buffers
-    trade[pl.ds(2 * rows, TAG_ROWS), :] = tag_of(partner, proj.shape[-1])
-    spot = pl.ds(2 * rows, TAG_ROWS)
-    copies = [
-        [
-            (proj.at[plan.mom ^ 1], trade.at[span(0, rows)]),
-            (own.at[span(1, rows)], trade.at[span(1, rows)]),
-            (own.at[spot], trade.at[pl.ds(2 * rows + TAG_ROWS, TAG_ROWS)]),
-        ],
         two_slices(proj, near, plan.local(2), plan.local(3)),
     ]
     through(list(zip(copies, buffers, outs)), ins, leaving)
 
 
+def pack_later(sizes, seps, partner, proj, own, after, out, buffer, ins, leaving):
+    rows = proj.shape[1]
+    plan = Plan(seps, sizes)
+    buffer[pl.ds(3 * rows, TAG_ROWS), :] = tag_of(partner, proj.shape[-1])
+    copies = [
+        (proj.at[plan.mom ^ 1], buffer.at[span(0, rows)]),
+        (own.at[span(1, rows)], buffer.at[span(1, rows)]),
+        (proj.at[plan.local(1)], buffer.at[span(2, rows)]),
+        (
+            own.at[pl.ds(2 * rows, TAG_ROWS)],
+            buffer.at[pl.ds(3 * rows + TAG_ROWS, TAG_ROWS)],
+        ),
+    ]
+    through([(copies, buffer, out)], ins, leaving)
+
+
 def choose(sizes, seps, near, far, after, out, sems):
     flag = lax.rem(Plan(seps, sizes).peer_hops(), 2)
 
@@ -191,19 +190,8 @@
     token[...] = jnp.zeros(token.shape, token.dtype)
 
 
-def other_pack(sizes, seps, proj, near, far_same, far_cross, after, out, sems):
-    plan = Plan(seps, sizes)
-    rows = out.shape[0] // 2
-    flag = lax.rem(plan.hops(1), 2) if sizes[2] == 2 else jnp.int32(0)
-    low, high = out.at[span(0, rows)], out.at[span(1, rows)]
-
-    @pl.when(flag == 0)
-    def _():
-        run_copies([(proj.at[plan.local(1)], low), (near.at[span(1, rows)], high)], sems)
-
-    @pl.when(flag != 0)
-    def _():
-        run_copies([(far_same.at[span(1, rows)], low), (far_cross.at[span(1, rows)], high)], sems)
+def gate_far(near, same, cross, h, near_out, same_out, cross_out, h_out):
+    h_out[0, :16, :128] = h[0, :16, :128]
 
 
 def own_fill(codes, p_ref, n, u_ref, turns):
@@ -262,16 +250,16 @@
 
 
 def own_kernel_13(sizes, seps, gamma, partner, own, traded, y_ref, h_in, after, *refs):
-    h_ref, label, token, p_ref, u0, u1, turns0, turns1, tags, sems = refs
+    h_ref, label, p_ref, u0, u1, turns0, turns1, tags, sems = refs
     rows = p_ref.shape[1]
-    spots = [pl.ds(2 * rows, TAG_ROWS), pl.ds(2 * rows + TAG_ROWS, TAG_ROWS)]
+    spots = [pl.ds(n * rows + m * TAG_ROWS, TAG_ROWS) for n, m in ((3, 0), (2, 0), (3, 1))]
     run_copies(
         [
             (traded.at[span(0, rows)], p_ref.at[0]),
             (traded.at[span(1, rows)], p_ref.at[1]),
             (traded.at[spots[0]], tags.at[0]),
-            (own.at[spots[0]], tags.at[1]),
-            (traded.at[spots[1]], tags.at[2]),
+            (own.at[spots[1]], tags.at[1]),
+            (traded.at[spots[2]], tags.at[2]),
         ],
         sems,
     )
@@ -292,14 +280,23 @@
     own_dot(u0, y_ref, h_ref.at[1])
     own_fill(codes_of(gamma, mom ^ 3, nterm), p_ref, 1, u1, turns1)
     own_dot(u1, y_ref, h_ref.at[3])
-    token[...] = jnp.zeros(token.shape, token.dtype)
-
-
-def other_products(pieces, gamma, label, h_ref, refs):
-    k_ref, p_ref, wa, wb, turns_a, turns_b = refs
+
+
+def other_products(pieces, gamma, label, h_ref, sources, refs):
+    k_ref, p_ref, wa, wb, turns_a, turns_b, sems = refs
     mom = lax.axis_index("mom")
     nterm, nev = turns_a.shape[0], turns_a.shape[-1]
     width = wa.shape[0]
+    (here, away), flag = sources
+
+    @pl.when(flag == 0)
+    def _():
+        run_copies([(ref, p_ref.at[n]) for n, ref in enumerate(here)], sems)
+
+    @pl.when(flag != 0)
+    def _():
+        run_copies([(ref, p_ref.at[n]) for n, ref in enumerate(away)], sems)
+
     for n, piece in enumerate(pieces):
         w_ref, turns = ((wa, turns_a), (wb, turns_b))[n % 2]
         for r in range(nterm):
@@ -324,30 +321,25 @@
             )
 
 
-def other_kernel_02(sizes, seps, gamma, label, h_ref, proj, near, far_same, far_cross, *refs):
-    k_ref, p_ref, wa, wb, turns_a, turns_b, sems = refs
+def other_flag(plan, sizes):
+    return lax.rem(plan.hops(0), 2) if sizes[2] == 2 else jnp.int32(1)
+
+
+def other_kernel_02(sizes, seps, gamma, label, h_ref, proj, near, same, cross, *refs):
     plan = Plan(seps, sizes)
-    rows = p_ref.shape[1]
-    low = span(0, rows)
-    flag = lax.rem(plan.hops(0), 2) if sizes[2] == 2 else jnp.int32(1)
-
-    @pl.when(flag == 0)
-    def _():
-        run_copies([(proj.at[plan.local(0)], p_ref.at[0]), (near.at[low], p_ref.at[1])], sems)
-
-    @pl.when(flag != 0)
-    def _():
-        run_copies([(far_same.at[low], p_ref.at[0]), (far_cross.at[low], p_ref.at[1])], sems)
-
-    out = (k_ref, p_ref, wa, wb, turns_a, turns_b)
-    other_products((0, 2), gamma, label, h_ref, out)
-
-
-def other_kernel_13(gamma, label, h_ref, traded, k_ref, p_ref, wa, wb, turns_a, turns_b, sems):
-    rows = p_ref.shape[1]
-    run_copies([(traded.at[span(n, rows)], p_ref.at[n]) for n in range(2)], sems)
-    out = (k_ref, p_ref, wa, wb, turns_a, turns_b)
-    other_products((1, 3), gamma, label, h_ref, out)
+    low = span(0, proj.shape[1])
+    here, away = (proj.at[plan.local(0)], near.at[low]), (same.at[low], cross.at[low])
+    sources = ((here, away), other_flag(plan, sizes))
+    other_products((0, 2), gamma, label, h_ref, sources, refs)
+
+
+def other_kernel_13(sizes, seps, gamma, label, h_ref, traded, near, same, cross, *refs):
+    plan = Plan(seps, sizes)
+    rows = refs[1].shape[1]
+    at = span(1 if sizes[2] == 2 else 0, rows)
+    here = (traded.at[span(2, rows)], near.at[span(1, rows)])
+    sources = ((here, (same.at[at], cross.at[at])), other_flag(plan, sizes))
+    other_products((1, 3), gamma, label, h_ref, sources, refs)
 
 
 def row_sums(k_refs, source, offset, totals):
@@ -506,7 +498,7 @@
             out_specs=[anywhere()] * len(aliases) + [vmem()],
             out_shape=out_shape,
             input_output_aliases=aliases,
-            compiler_params=limit(16),
+            compiler_params=limit(20),
             cost_estimate=pl.CostEstimate(
                 flops=WEIGHT, bytes_accessed=WEIGHT // 1000, transcendentals=0
             ),
@@ -522,14 +514,14 @@
         buffers([first_shape]) + [dma(1), dma(1)],
         58,
     )(separations, peram_blocks)
-    leaving = [tagged, rest_shape, two, two, bf16(2, width, width)]
-    own, rest, far_same, far_cross, block = call(
+    leaving = [tagged, rest_shape, two, two, bf16(2, width, width), two]
+    own, rest, far_same, far_cross, block, near = call(
         part(pack, sizes),
         "pack",
         [smem()] * 2 + [hbm()] * 2 + [vmem()],
         [hbm()] * len(leaving),
         leaving,
-        buffers(leaving) + [dma(8), dma(len(leaving))],
+        buffers(leaving) + [dma(10), dma(len(leaving))],
         58,
     )(separations, partner, peram_blocks, proj, swap_mom(tick, 1))
 
@@ -551,17 +543,17 @@
         [vmem()] * 3,
         [bf16(2 * width, 2 * width), products, token],
         [pltpu.VMEM((2, width, width), jnp.bfloat16), piece, u_scratch, turns, dma(2)],
-        16,
+        20,
     )(gamma_index, block, proj)
-    leaving = [bf16(2 * (rows + TAG_ROWS), nev), two]
-    traded, near = call(
+    trade = bf16(3 * rows + 2 * TAG_ROWS, nev)
+    traded = call(
         part(pack_later, sizes),
         "pack_later",
         [smem()] * 2 + [hbm()] * 2 + [vmem()],
-        [hbm()] * len(leaving),
-        leaving,
-        buffers(leaving) + [dma(5), dma(len(leaving))],
-        16,
+        hbm(),
+        trade,
+        buffers([trade]) + [dma(4), dma(1)],
+        20,
     )(separations, partner, proj, own, done_0)
     traded = swap_mom(traded, 1)
     near = swap_mom(near, 2)
@@ -572,7 +564,7 @@
         [vmem()] * 2,
         [products, token],
         [piece, u_scratch, turns, dma(1)],
-        16,
+        20,
         {3: 0},
     )(gamma_index, own, y, h)
 
@@ -586,7 +578,7 @@
         vmem(),
         rest_shape,
         [dma(1)],
-        16,
+        20,
     )(separations, rest_near, rest_far, done_0)
     first, rest, opened = alias(
         gate,
@@ -598,29 +590,34 @@
     )
     rest = swap_snk(rest)
     first_near, first_far = most_of(first, plan.hops(0))
-    h, label, done_h = call(
+    h, label = call(
         part(own_kernel_13, sizes),
         "own_products_13",
         [smem()] * 3 + [hbm()] * 2 + [vmem()] * 3,
-        [vmem(), smem(), vmem()],
-        [products, jax.ShapeDtypeStruct((2 * mom_count,), jnp.int32), token],
+        [vmem(), smem()],
+        [products, jax.ShapeDtypeStruct((2 * mom_count,), jnp.int32)],
         [pieces, u_scratch, u_scratch, turns, turns]
         + [pltpu.VMEM((3, TAG_ROWS, nev), jnp.bfloat16), dma(5)],
-        16,
+        20,
         {6: 0},
     )(separations, gamma_index, partner, own, traded, y, h, opened)
 
-    other_trade = call(
-        part(other_pack, sizes),
-        "other_pack",
-        [smem()] + [hbm()] * 4 + [vmem()],
-        vmem(),
-        two,
-        [dma(2)],
-        16,
-    )(separations, proj, near, far_same, far_cross, done_h)
-    other_got = swap_mom(other_trade, 1)
-    if src_count != 2:
+    near, far_same, far_cross, h = pl.pallas_call(
+        gate_far,
+        in_specs=[anywhere()] * 3 + [vmem()],
+        out_specs=[anywhere()] * 3 + [vmem()],
+        out_shape=[two, two, two, products],
+        input_output_aliases={n: n for n in range(4)},
+        compiler_params=limit(20),
+        cost_estimate=pl.CostEstimate(
+            flops=WEIGHT, bytes_accessed=WEIGHT // 1000, transcendentals=0
+        ),
+        name="gate_far",
+    )(near, far_same, far_cross, h)
+    near_core = swap_mom(near, 1)
+    if src_count == 2:
+        far = [far_same, far_cross, swap_mom(far_same, 1), swap_mom(far_cross, 1)]
+    else:
 
         def moved(array):
             if src_count == 1:
@@ -628,8 +625,9 @@
             array, away = most_of(array, plan.hops(0))
             return jnp.where(plan.hops(0) // (src_count // 2) != 0, away, array)
 
-        far_same = moved(lax.dynamic_index_in_dim(proj, plan.local(0), 0, keepdims=False))
-        far_cross, other_got = moved(near[:rows]), moved(other_got)
+        here = lax.dynamic_index_in_dim(proj, plan.local(0), 0, keepdims=False)
+        here = (here, near[:rows], traded[2 * rows : 3 * rows], near_core[rows:])
+        far = [moved(array) for array in here]
 
     k_shape = jax.ShapeDtypeStruct((2, 2 * width, width), jnp.float32)
     scratch = [pieces, u_scratch, u_scratch, turns, turns, dma(2)]
@@ -641,16 +639,16 @@
         k_shape,
         scratch,
         20,
-    )(separations, gamma_index, label, h, proj, near, far_same, far_cross)
+    )(separations, gamma_index, label, h, proj, near, far[0], far[1])
     kb = call(
-        other_kernel_13,
+        part(other_kernel_13, sizes),
         "other_products_13",
-        [smem()] * 2 + [vmem(), hbm()],
+        [smem()] * 3 + [vmem()] + [hbm()] * 4,
         vmem(),
         k_shape,
         scratch,
         20,
-    )(gamma_index, label, h, other_got)
+    )(separations, gamma_index, label, h, traded, near_core, far[2], far[3])
 
     device_count = src_count * snk_count * mom_count
     values = time_count * sep_count * 2

time: 87.5 us -> 79.1 us (0.904)
  waiting for transfers between devices: 20.2 us -> 11.2 us
  local copies, waits for them, and re-layouts: 5.45 us -> 8.23 us
  Pallas kernels: 38.2 us -> 35.9 us
    ppermute x5 -> x7, waiting for transfers between devices: 7.6 us -> 3.57 us  [swap_mom(): return lax.ppermute(array, 'mom', [(a, a ^ i) for a in range(mom_count)])]
    ppermute x4, waiting for transfers between devices: 10.3 us -> 6.36 us  [next_src(): return lax.ppermute(array, ('src', 'mom'), pairs)]
    unnamed x18, local copies, waits for them, and re-layouts: 4.61 us -> 7.39 us
    pallas_call x2, Pallas kernels: 7.39 us -> 4.95 us  [the longest x1 4.94 us: shards(): call(part(other_kernel_13, sizes), 'other_products_13', [smem()] * 3 + [v...]
    ppermute x2, waiting for transfers between devices: 2.29 us -> 1.23 us  [swap_snk(): return lax.ppermute(array, 'snk', pairs)]
    ppermute x5 -> x7, starting transfers between devices: 2.81 us -> 3.19 us  [swap_mom(): return lax.ppermute(array, 'mom', [(a, a ^ i) for a in range(mom_count)])]
  transfers between devices with their start and end apart: 11 -> 13, of which waited for: 4 -> 3; matrix products, arithmetic and copies ran while one was open for 0% -> 0% of each run, Pallas kernels for 36% -> 37%
where the time goes in v8:
time: 79.1 us; the launch traced here: 78.7 us
  Pallas kernels  35.9 us (45%)
  starting transfers between devices  11.6 us (15%)
  waiting for transfers between devices  11.2 us (14%)
  blocking collectives  10.9 us (14%)
  local copies, waits for them, and re-layouts  8.23 us (10%)
  between operations  0.84 us (1%)
    all_to_all x1, blocking collectives, shards(): lax.all_to_all(out, ('src', 'snk', 'mom'), split_axis=0, concat_axis=0, t...  10.9 us
    unnamed x18, local copies, waits for them, and re-layouts  7.39 us
    ppermute x4, waiting for transfers between devices, next_src(): return lax.ppermute(array, ('src', 'mom'), pairs)  6.36 us
    pallas_call x1, Pallas kernels, shards(): call(part(own_kernel_13, sizes), 'own_products_13', [smem()] * 3 + [hbm()...  5.35 us
    pallas_call x1, Pallas kernels, shards(): call(part(other_kernel_13, sizes), 'other_products_13', [smem()] * 3 + [v...  4.94 us
    pallas_call x1, Pallas kernels, shards(): call(part(other_kernel_02, sizes), 'other_products_02', [smem()] * 3 + [v...  4.93 us
    ppermute x4, starting transfers between devices, next_src(): return lax.ppermute(array, ('src', 'mom'), pairs)  4.73 us
    pallas_call x1, Pallas kernels, shards(): call(part(pack, sizes), 'pack', [smem()] * 2 + [hbm()] * 2 + [vmem()], [h...  4.53 us
  transfers between devices with their start and end apart: 13, of which 3 were waited for; matrix products, arithmetic and copies ran while one was open for 0% of the time, Pallas kernels for 37%

profile of v8, /device:TPU:0, one launch (start us, length us, event | category | flops | bytes accessed | tf_op | source)
XLA Modules:
  0.0 78.7 jit_solution(6307870531343150549)
XLA Ops:
  0.0 3.2 %pack_first.1 = (bf16[2,320,512]{2,1,0:T(8,128)(2,1)}, bf16[16,128]{1,0:T(8,128)(2,1)}) custom-call(s32[4]{0:T(128)} %seps.15, bf16[4,2,2,512,512]{4,3,2,1,0:T(8,128)(2,1)} %peram.3), custom_call_target="tpu_custom_call" | custom-call | flops 9999999827968 | bytes 10000000000 | tf_op jit(solution)/shard_map/pack_first/pallas_call | solution.py:508
  3.2 0.5 collective-permute-start
  3.7 3.7 %collective-permute-start.3 = (bf16[2,320,512]{2,1,0:T(8,128)(2,1)}, bf16[2,320,512]{2,1,0:T(8,128)(2,1)}, u32[]{:S(2)}, u32[]{:S(2)}) collective-permute-start(bf16[2,320,512]{2,1,0:T(8,128)(2,1)} %get-tuple-element.34), channel_id=1, source_target_pairs={{0,8},{4,12},{8,0},{12,4},{1,9},{5,13},{9,1},{13,5},{2,10},{6,14},... | collective-permute-start | bytes 1966088 | tf_op jit(solution)/shard_map/ppermute | solution.py:447
  8.1 0.0 collective-permute-done.after
  8.1 0.0 copy-start.8
  8.1 0.6 copy-done.8
  8.7 4.5 %pack.1 = (bf16[2064,128]{1,0:T(8,128)(2,1)}, bf16[2,192,512]{2,1,0:T(8,128)(2,1)}, bf16[2048,128]{1,0:T(8,128)(2,1)}, bf16[2048,128]{1,0:T(8,128)(2,1)}, bf16[2...) custom-call(s32[4]{0:T(128)} %seps.15, s32[1]{0:T(128)S(6)} %copy.24.partner, bf16[4,2,2,512,512]{4,3,2,1,0:T(8,128)(2,1)} %peram.3, ...), custom_call_target="tpu_custom_call" | custom-call | flops 9999999827968 | bytes 10000000000 | tf_op jit(solution)/shard_map/pack/pallas_call | solution.py:518
  13.2 1.8 %collective-permute-start.1 = (bf16[2064,128]{1,0:T(8,128)(2,1)}, bf16[2064,128]{1,0:T(8,128)(2,1)}, u32[]{:S(2)}, u32[]{:S(2)}) collective-permute-start(bf16[2064,128]{1,0:T(8,128)(2,1)} %get-tuple-element.28), channel_id=1, source_target_pairs={{0,2},{1,3},{2,0},{3,1},{4,6},{5,7},{6,4},{7,5},{8,10},{9,11},{10,... | collective-permute-start | bytes 1585160 | tf_op jit(solution)/shard_map/ppermute | solution.py:443
  15.0 1.5 %collective-permute-start.4 = (bf16[2,192,512]{2,1,0:T(8,128)(2,1)}, bf16[2,192,512]{2,1,0:T(8,128)(2,1)}, u32[]{:S(2)}, u32[]{:S(2)}) collective-permute-start(bf16[2,192,512]{2,1,0:T(8,128)(2,1)} %get-tuple-element.35.near), channel_id=1, source_target_pairs={{16,0},{17,1},{18,2},{19,3},{0,16},{1,17},{2,18},{3,19},{20,4},{21... | collective-permute-start | bytes 1179656 | tf_op jit(solution)/shard_map/ppermute | solution.py:455
  16.5 0.3 collective-permute-start.5
  16.8 0.5 collective-permute-start.6
  17.3 0.0 copy-done
  17.3 1.2 %copy-done.7 = bf16[2,512,512]{2,1,0:T(8,128)(2,1)S(1)} copy-done((bf16[2,512,512]{2,1,0:T(8,128)(2,1)S(1)}, bf16[2,512,512]{2,1,0:T(8,128)(2,1)}, u32[]{:S(2)}) %copy-start.7) | copy-done | bytes 1048600
  18.6 2.5 %own_products_0.1 = (bf16[1024,1024]{1,0:T(8,128)(2,1)S(1)}, bf16[4,512,1536]{2,1,0:T(8,128)(2,1)S(1)}, bf16[16,128]{1,0:T(8,128)(2,1)S(1)}) custom-call(s32[4,4]{1,0:T(4,128)S(1)} %copy-done.2, bf16[2,512,512]{2,1,0:T(8,128)(2,1)S(1)} %copy-done.7, bf16[4,1024,128]{2,1,0:T(8,128)(2,1)S(1)} %bitcast.3), custom_call_target="tpu_custom_call" | custom-call | flops 9999999827968 | bytes 10000000000 | tf_op jit(solution)/shard_map/own_products_0/pallas_call | solution.py:539
  21.0 6.4 %collective-permute-done.4.far = bf16[2,192,512]{2,1,0:T(8,128)(2,1)} collective-permute-done((bf16[2,192,512]{2,1,0:T(8,128)(2,1)}, bf16[2,192,512]{2,1,0:T(8,128)(2,1)}, u32[]{:S(2)}, u32[]{:S(2)}) %collective-permute-start.4) | collective-permute-done | bytes 393248 | tf_op jit(solution)/shard_map/ppermute | solution.py:455
  27.4 1.1 %collective-permute-start.7 = (bf16[2048,128]{1,0:T(8,128)(2,1)}, bf16[2048,128]{1,0:T(8,128)(2,1)}, u32[]{:S(2)}, u32[]{:S(2)}) collective-permute-start(bf16[2048,128]{1,0:T(8,128)(2,1)} %get-tuple-element.41), channel_id=1, source_target_pairs={{18,0},{19,1},{16,2},{17,3},{2,16},{3,17},{0,18},{1,19},{22,4},{23... | collective-permute-start | bytes 1572872 | tf_op jit(solution)/shard_map/ppermute | solution.py:455
  28.5 0.0 copy-done.1
  28.5 1.5 %choose.1.rest = bf16[2,192,512]{2,1,0:T(8,128)(2,1)} custom-call(s32[4]{0:T(128)S(1)} %copy-done.3, bf16[2,192,512]{2,1,0:T(8,128)(2,1)S(1)} %copy-done.1, bf16[2,192,512]{2,1,0:T(8,128)(2,1)} %collective-permute-done.4.far, bf16[16,128]{1,0:T(8,128)(2,1)S(1)} %get-tuple-element.30.after), custom_call_target="tpu_custom_call" | custom-call | flops 9999999827968 | bytes 10000000000 | tf_op jit(solution)/shard_map/choose/pallas_call | solution.py:574
  30.1 0.0 collective-permute-done.1.own
  30.1 2.5 %pack_later.1 = bf16[3104,128]{1,0:T(8,128)(2,1)} custom-call(s32[4]{0:T(128)S(1)} %copy-done.3, s32[1]{0:T(128)S(6)} %copy.24.partner, bf16[4,1024,128]{2,1,0:T(8,128)(2,1)S(1)} %bitcast.4, bf16[2064,128]{1,0:T(8,128)(2,1)} %collective-permute-done.1.own, bf16[16,128]{1,0:T(8,128)(2,1)S(1)} %get-tuple-element.30.after), custom_call_target="tpu_custom_call" | custom-call | flops 9999999827968 | bytes 10000000000 | tf_op jit(solution)/shard_map/pack_later/pallas_call | solution.py:549
  32.5 0.1 collective-permute-start.2
  32.6 3.2 %own_products_2.1 = (bf16[4,512,1536]{2,1,0:T(8,128)(2,1)S(1)}, bf16[16,128]{1,0:T(8,128)(2,1)S(1)}) custom-call(s32[4,4]{1,0:T(4,128)S(1)} %copy-done.2, bf16[2064,128]{1,0:T(8,128)(2,1)} %collective-permute-done.1.own, bf16[1024,1024]{1,0:T(8,128)(2,1)S(1)} %get-tuple-element.31.y_ref, ...), custom_call_target="tpu_custom_call", output_to_operand_aliasing={{0}: (3, {})} | custom-call | flops 9999999827968 | bytes 10000000000 | tf_op jit(solution)/shard_map/own_products_2/pallas_call | solution.py:560
  35.9 1.2 %collective-permute-done.3.first = bf16[2,320,512]{2,1,0:T(8,128)(2,1)} collective-permute-done((bf16[2,320,512]{2,1,0:T(8,128)(2,1)}, bf16[2,320,512]{2,1,0:T(8,128)(2,1)}, u32[]{:S(2)}, u32[]{:S(2)}) %collective-permute-start.3) | collective-permute-done | bytes 655392 | tf_op jit(solution)/shard_map/ppermute | solution.py:447
  37.1 1.6 %collective-permute-start.11 = (bf16[2,320,512]{2,1,0:T(8,128)(2,1)}, bf16[2,320,512]{2,1,0:T(8,128)(2,1)}, u32[]{:S(2)}, u32[]{:S(2)}) collective-permute-start(bf16[2,320,512]{2,1,0:T(8,128)(2,1)} %get-tuple-element.47.near), channel_id=1, source_target_pairs={{16,0},{17,1},{18,2},{19,3},{0,16},{1,17},{2,18},{3,19},{20,4},{21... | collective-permute-start | bytes 1966088 | tf_op jit(solution)/shard_map/ppermute | solution.py:455
  38.7 0.0 collective-permute-done.2.traded
  38.7 0.0 collective-permute-start.12
  38.7 5.4 %own_products_13.1 = (bf16[4,512,1536]{2,1,0:T(8,128)(2,1)S(1)}, s32[8]{0:T(128)S(1)}) custom-call(s32[4]{0:T(128)S(1)} %copy-done.3, s32[4,4]{1,0:T(4,128)S(1)} %copy-done.2, s32[1]{0:T(128)S(6)} %copy.24.partner, bf16[2064,128]{1,0:T(8,128)(2,1)} %collective-permute-done.1.own, ...), custom_call_target="tpu_custom_call", output_to_operand_aliasing={{0}: (6, {})} | custom-call | flops 9999999827968 | bytes 10000000000 | tf_op jit(solution)/shard_map/own_products_13/pallas_call | solution.py:593
  44.0 2.6 %copy-done.5 = bf16[4,512,1536]{2,1,0:T(8,128)(2,1)} copy-done((bf16[4,512,1536]{2,1,0:T(8,128)(2,1)}, bf16[4,512,1536]{2,1,0:T(8,128)(2,1)S(1)}, u32[]{:S(2)}) %copy-start.5) | copy-done | bytes 6291480
  46.7 3.6 %collective-permute-done.5.near = bf16[2048,128]{1,0:T(8,128)(2,1)} collective-permute-done((bf16[2048,128]{1,0:T(8,128)(2,1)}, bf16[2048,128]{1,0:T(8,128)(2,1)}, u32[]{:S(2)}, u32[]{:S(2)}) %collective-permute-start.5) | collective-permute-done | bytes 524320 | tf_op jit(solution)/shard_map/ppermute | solution.py:443
  50.2 0.0 collective-permute-done.6.same
  50.2 0.0 collective-permute-done.7.cross
  50.2 2.8 %copy-done.6 = bf16[4,512,1536]{2,1,0:T(8,128)(2,1)S(1)} copy-done((bf16[4,512,1536]{2,1,0:T(8,128)(2,1)S(1)}, bf16[4,512,1536]{2,1,0:T(8,128)(2,1)}, u32[]{:S(2)}) %copy-start.6) | copy-done | bytes 6291480
  53.0 0.0 collective-permute-start.10
  53.0 0.5 collective-permute-start.8
  53.5 0.0 collective-permute-start.9
  53.5 0.1 copy-done.4
  53.7 4.9 %other_products_02.1.ka = f32[2,1024,512]{2,1,0:T(8,128)S(1)} custom-call(s32[4]{0:T(128)S(1)} %copy-done.4, s32[4,4]{1,0:T(4,128)S(1)} %copy-done.2, s32[8]{0:T(128)S(1)} %get-tuple-element.38.label, bf16[4,512,1536]{2,1,0:T(8,128)(2,1)S(1)} %get-tuple-element.43.h_ref, bf16[4,1024,128]{2,1,0:T(8,128)(2,1)S(1)} %bitcast.5, ...), custom_call_target="tpu_custom_call" | custom-call | flops 9999999827968 | bytes 10000000000 | tf_op jit(solution)/shard_map/other_products_02/pallas_call | solution.py:634
  58.6 0.0 collective-permute-done.10.cross
  58.6 0.0 collective-permute-done.8.near
  58.6 0.0 collective-permute-done.9.same
  58.7 4.9 %other_products_13.1.kb = f32[2,1024,512]{2,1,0:T(8,128)S(1)} custom-call(s32[4]{0:T(128)S(1)} %copy-done.4, s32[4,4]{1,0:T(4,128)S(1)} %copy-done.2, s32[8]{0:T(128)S(1)} %get-tuple-element.38.label, bf16[4,512,1536]{2,1,0:T(8,128)(2,1)S(1)} %get-tuple-element.43.h_ref, bf16[3104,128]{1,0:T(8,128)(2,1)} %collective-permute-done.2.traded, ...), custom_call_target="tpu_custom_call" | custom-call | flops 9999999827968 | bytes 10000000000 | tf_op jit(solution)/shard_map/other_products_13/pallas_call | solution.py:643
  63.6 0.0 collective-permute-done.12.rest
  63.6 0.0 collective-permute-done.11.far
  63.6 3.3 %traces.1 = f32[32,1,128]{2,1,0:T(1,128)S(1)} custom-call(s32[4]{0:T(128)S(1)} %copy-done.4, s32[8]{0:T(128)S(1)} %get-tuple-element.38.label, f32[2,1024,512]{2,1,0:T(8,128)S(1)} %other_products_02.1.ka, f32[2,1024,512]{2,1,0:T(8,128)S(1)} %other_products_13.1.kb, bf16[2,320,512]{2,1,0:T(8,128)(2,1)} %get-tuple-element.47.near, ...), custom_call_target="tpu_custom_call" | custom-call | flops 9999999827968 | bytes 10000000000 | tf_op jit(solution)/shard_map/traces/pallas_call | solution.py:656
  66.9 10.9 %all_to_all.5 = f32[32,1,128]{2,1,0:T(1,128)S(1)} all-to-all(f32[32,1,128]{2,1,0:T(1,128)S(1)} %traces.1), channel_id=1, replica_groups=mesh['src'=2,'snk'=4,'mom'=4] {'src','snk','mom'}, dimensions={0} | all-to-all | bytes 32768 | tf_op jit(solution)/shard_map/all_to_all | solution.py:665
  77.8 0.1 reduce_sum.11
  77.8 0.1 reshape.11
  77.9 0.7 copy.15
  (13 shorter events, 0.0 us)
Async XLA Ops:
  3.2 4.8 %collective-permute-start = (bf16[16,128]{1,0:T(8,128)(2,1)}, bf16[16,128]{1,0:T(8,128)(2,1)S(1)}, u32[]{:S(2)}, u32[]{:S(2)}) collective-permute-start(bf16[16,128]{1,0:T(8,128)(2,1)} %get-tuple-element.27), channel_id=1, source_target_pairs={{0,1},{1,0},{2,3},{3,2},{4,5},{5,4},{6,7},{7,6},{8,9},{9,8},{10,11... | collective-permute-start | bytes 12296 | tf_op jit(solution)/shard_map/ppermute | solution.py:443
  3.7 33.3 %collective-permute-start.3 = (bf16[2,320,512]{2,1,0:T(8,128)(2,1)}, bf16[2,320,512]{2,1,0:T(8,128)(2,1)}, u32[]{:S(2)}, u32[]{:S(2)}) collective-permute-start(bf16[2,320,512]{2,1,0:T(8,128)(2,1)} %get-tuple-element.34), channel_id=1, source_target_pairs={{0,8},{4,12},{8,0},{12,4},{1,9},{5,13},{9,1},{13,5},{2,10},{6,14},... | collective-permute-start | bytes 1966088 | tf_op jit(solution)/shard_map/ppermute | solution.py:447
  8.1 0.6 copy-start.8
  8.7 8.7 %copy-start = (bf16[4,1,4,2,128,128]{5,4,3,2,1,0:T(8,128)(2,1)S(1)}, bf16[4,1,4,2,128,128]{5,4,3,2,1,0:T(8,128)(2,1)}, u32[]{:S(2)}) copy-start(bf16[4,1,4,2,128,128]{5,4,3,2,1,0:T(8,128)(2,1)} %param.6) | copy-start | bytes 3145732
  8.7 8.7 %copy-start.2 = (s32[4,4]{1,0:T(4,128)S(1)}, s32[4,4]{1,0:T(4,128)}, u32[]{:S(2)}) copy-start(s32[4,4]{1,0:T(4,128)} %gamma.9) | copy-start | bytes 196
  13.2 16.8 %collective-permute-start.1 = (bf16[2064,128]{1,0:T(8,128)(2,1)}, bf16[2064,128]{1,0:T(8,128)(2,1)}, u32[]{:S(2)}, u32[]{:S(2)}) collective-permute-start(bf16[2064,128]{1,0:T(8,128)(2,1)} %get-tuple-element.28), channel_id=1, source_target_pairs={{0,2},{1,3},{2,0},{3,1},{4,6},{5,7},{6,4},{7,5},{8,10},{9,11},{10,... | collective-permute-start | bytes 1585160 | tf_op jit(solution)/shard_map/ppermute | solution.py:443
  15.0 12.3 %collective-permute-start.4 = (bf16[2,192,512]{2,1,0:T(8,128)(2,1)}, bf16[2,192,512]{2,1,0:T(8,128)(2,1)}, u32[]{:S(2)}, u32[]{:S(2)}) collective-permute-start(bf16[2,192,512]{2,1,0:T(8,128)(2,1)} %get-tuple-element.35.near), channel_id=1, source_target_pairs={{16,0},{17,1},{18,2},{19,3},{0,16},{1,17},{2,18},{3,19},{20,4},{21... | collective-permute-start | bytes 1179656 | tf_op jit(solution)/shard_map/ppermute | solution.py:455
  16.5 33.7 %collective-permute-start.5 = (bf16[2048,128]{1,0:T(8,128)(2,1)}, bf16[2048,128]{1,0:T(8,128)(2,1)}, u32[]{:S(2)}, u32[]{:S(2)}) collective-permute-start(bf16[2048,128]{1,0:T(8,128)(2,1)} %get-tuple-element.39), channel_id=1, source_target_pairs={{0,2},{1,3},{2,0},{3,1},{4,6},{5,7},{6,4},{7,5},{8,10},{9,11},{10,... | collective-permute-start | bytes 1572872 | tf_op jit(solution)/shard_map/ppermute | solution.py:443
  16.8 33.4 %collective-permute-start.6 = (bf16[2048,128]{1,0:T(8,128)(2,1)}, bf16[2048,128]{1,0:T(8,128)(2,1)}, u32[]{:S(2)}, u32[]{:S(2)}) collective-permute-start(bf16[2048,128]{1,0:T(8,128)(2,1)} %get-tuple-element.40), channel_id=1, source_target_pairs={{16,0},{17,1},{18,2},{19,3},{0,16},{1,17},{2,18},{3,19},{20,4},{21... | collective-permute-start | bytes 1572872 | tf_op jit(solution)/shard_map/ppermute | solution.py:455
  17.3 1.2 %copy-start.7 = (bf16[2,512,512]{2,1,0:T(8,128)(2,1)S(1)}, bf16[2,512,512]{2,1,0:T(8,128)(2,1)}, u32[]{:S(2)}) copy-start(bf16[2,512,512]{2,1,0:T(8,128)(2,1)} %get-tuple-element.29.block) | copy-start | bytes 3145732
  18.6 10.0 %copy-start.1 = (bf16[2,192,512]{2,1,0:T(8,128)(2,1)S(1)}, bf16[2,192,512]{2,1,0:T(8,128)(2,1)}, u32[]{:S(2)}) copy-start(bf16[2,192,512]{2,1,0:T(8,128)(2,1)} %get-tuple-element.35.near) | copy-start | bytes 1179652
  18.6 10.0 %copy-start.3 = (s32[4]{0:T(128)S(1)}, s32[4]{0:T(128)}, u32[]{:S(2)}) copy-start(s32[4]{0:T(128)} %seps.15) | copy-start | bytes 52
  27.4 22.9 %collective-permute-start.7 = (bf16[2048,128]{1,0:T(8,128)(2,1)}, bf16[2048,128]{1,0:T(8,128)(2,1)}, u32[]{:S(2)}, u32[]{:S(2)}) collective-permute-start(bf16[2048,128]{1,0:T(8,128)(2,1)} %get-tuple-element.41), channel_id=1, source_target_pairs={{18,0},{19,1},{16,2},{17,3},{2,16},{3,17},{0,18},{1,19},{22,4},{23... | collective-permute-start | bytes 1572872 | tf_op jit(solution)/shard_map/ppermute | solution.py:455
  32.5 6.1 %collective-permute-start.2 = (bf16[3104,128]{1,0:T(8,128)(2,1)}, bf16[3104,128]{1,0:T(8,128)(2,1)}, u32[]{:S(2)}, u32[]{:S(2)}) collective-permute-start(bf16[3104,128]{1,0:T(8,128)(2,1)} %pack_later.1), channel_id=1, source_target_pairs={{0,1},{1,0},{2,3},{3,2},{4,5},{5,4},{6,7},{7,6},{8,9},{9,8},{10,11... | collective-permute-start | bytes 2383880 | tf_op jit(solution)/shard_map/ppermute | solution.py:443
  37.1 26.5 %collective-permute-start.11 = (bf16[2,320,512]{2,1,0:T(8,128)(2,1)}, bf16[2,320,512]{2,1,0:T(8,128)(2,1)}, u32[]{:S(2)}, u32[]{:S(2)}) collective-permute-start(bf16[2,320,512]{2,1,0:T(8,128)(2,1)} %get-tuple-element.47.near), channel_id=1, source_target_pairs={{16,0},{17,1},{18,2},{19,3},{0,16},{1,17},{2,18},{3,19},{20,4},{21... | collective-permute-start | bytes 1966088 | tf_op jit(solution)/shard_map/ppermute | solution.py:455
  38.7 24.9 %collective-permute-start.12 = (bf16[2,192,512]{2,1,0:T(8,128)(2,1)}, bf16[2,192,512]{2,1,0:T(8,128)(2,1)}, u32[]{:S(2)}, u32[]{:S(2)}) collective-permute-start(bf16[2,192,512]{2,1,0:T(8,128)(2,1)} %get-tuple-element.48), channel_id=1, source_target_pairs={{0,8},{4,12},{8,0},{12,4},{1,9},{5,13},{9,1},{13,5},{2,10},{6,14},... | collective-permute-start | bytes 1179656 | tf_op jit(solution)/shard_map/ppermute | solution.py:447
  44.0 2.7 %copy-start.5 = (bf16[4,512,1536]{2,1,0:T(8,128)(2,1)}, bf16[4,512,1536]{2,1,0:T(8,128)(2,1)S(1)}, u32[]{:S(2)}) copy-start(bf16[4,512,1536]{2,1,0:T(8,128)(2,1)S(1)} %get-tuple-element.42.h) | copy-start | bytes 18874372
  50.2 2.8 %copy-start.6 = (bf16[4,512,1536]{2,1,0:T(8,128)(2,1)S(1)}, bf16[4,512,1536]{2,1,0:T(8,128)(2,1)}, u32[]{:S(2)}) copy-start(bf16[4,512,1536]{2,1,0:T(8,128)(2,1)} %copy-done.5) | copy-start | bytes 18874372
  53.0 0.7 copy-start.4
  53.0 5.6 %collective-permute-start.10 = (bf16[2048,128]{1,0:T(8,128)(2,1)}, bf16[2048,128]{1,0:T(8,128)(2,1)}, u32[]{:S(2)}, u32[]{:S(2)}) collective-permute-start(bf16[2048,128]{1,0:T(8,128)(2,1)} %get-tuple-element.46.cross), channel_id=1, source_target_pairs={{0,1},{1,0},{2,3},{3,2},{4,5},{5,4},{6,7},{7,6},{8,9},{9,8},{10,11... | collective-permute-start | bytes 1572872 | tf_op jit(solution)/shard_map/ppermute | solution.py:443
  53.0 5.6 %collective-permute-start.8 = (bf16[2048,128]{1,0:T(8,128)(2,1)}, bf16[2048,128]{1,0:T(8,128)(2,1)}, u32[]{:S(2)}, u32[]{:S(2)}) collective-permute-start(bf16[2048,128]{1,0:T(8,128)(2,1)} %get-tuple-element.44.near), channel_id=1, source_target_pairs={{0,1},{1,0},{2,3},{3,2},{4,5},{5,4},{6,7},{7,6},{8,9},{9,8},{10,11... | collective-permute-start | bytes 1572872 | tf_op jit(solution)/shard_map/ppermute | solution.py:443
  53.5 5.1 %collective-permute-start.9 = (bf16[2048,128]{1,0:T(8,128)(2,1)}, bf16[2048,128]{1,0:T(8,128)(2,1)}, u32[]{:S(2)}, u32[]{:S(2)}) collective-permute-start(bf16[2048,128]{1,0:T(8,128)(2,1)} %get-tuple-element.45.same), channel_id=1, source_target_pairs={{0,1},{1,0},{2,3},{3,2},{4,5},{5,4},{6,7},{7,6},{8,9},{9,8},{10,11... | collective-permute-start | bytes 1572872 | tf_op jit(solution)/shard_map/ppermute | solution.py:443

commit v9 on v8

--- a/solution.py
+++ b/solution.py
@@ -131,47 +131,31 @@
     return number.astype(jnp.bfloat16)
 
 
-def pack_first(sizes, seps, peram, out, token, buffer, ins, leaving):
+def pack_first(sizes, seps, partner, peram, *refs):
+    outs, token, buffers, (ins, leaving) = refs[:2], refs[2], refs[3:5], refs[5:]
     plan = Plan(seps, sizes)
-    source = peram.at[plan.peer_local(), plan.give, :, pl.ds(0, out.shape[1])]
-    through([([(source, buffer)], buffer, out)], ins, leaving)
-    token[...] = jnp.zeros(token.shape, token.dtype)
-
-
-def pack(sizes, seps, partner, peram, proj, after, *refs):
-    outs, buffers, (ins, leaving) = refs[:6], refs[6:12], refs[12:]
+    start, copies = 0, []
+    for buffer in buffers:
+        rows = buffer.shape[1]
+        source = peram.at[plan.peer_local(), plan.give, :, pl.ds(start, rows)]
+        copies.append([(source, buffer)])
+        start += rows
+    token[...] = tag_of(partner, token.shape[-1])
+    through(list(zip(copies, buffers, outs)), ins, leaving)
+
+
+def pack(sizes, seps, partner, proj, tick, after, *refs):
+    outs, buffers, (ins, leaving) = refs[:2], refs[2:4], refs[4:]
     plan = Plan(seps, sizes)
     rows = proj.shape[1]
-    mom = plan.mom
-    own, rest, same, cross, block, near = buffers
-    own[pl.ds(2 * rows, TAG_ROWS), :] = tag_of(partner, proj.shape[-1])
-    start = peram.shape[-2] - rest.shape[1]
-    source = peram.at[plan.peer_local(), plan.give, :, pl.ds(start, rest.shape[1])]
+    same, cross = buffers
+    cross[pl.ds(2 * rows, TAG_ROWS), :] = tag_of(partner, cross.shape[-1])
+    cross[pl.ds(2 * rows + TAG_ROWS, TAG_ROWS), :] = tick[...]
     copies = [
-        two_slices(proj, own, mom ^ 2, mom ^ 3),
-        [(source, rest)],
         two_slices(proj, same, plan.local(0), plan.local(1)),
         two_slices(proj, cross, plan.local(2), plan.local(3)),
-        [(peram.at[mom, plan.keep], block)],
-        two_slices(proj, near, plan.local(2), plan.local(3)),
     ]
     through(list(zip(copies, buffers, outs)), ins, leaving)
-
-
-def pack_later(sizes, seps, partner, proj, own, after, out, buffer, ins, leaving):
-    rows = proj.shape[1]
-    plan = Plan(seps, sizes)
-    buffer[pl.ds(3 * rows, TAG_ROWS), :] = tag_of(partner, proj.shape[-1])
-    copies = [
-        (proj.at[plan.mom ^ 1], buffer.at[span(0, rows)]),
-        (own.at[span(1, rows)], buffer.at[span(1, rows)]),
-        (proj.at[plan.local(1)], buffer.at[span(2, rows)]),
-        (
-            own.at[pl.ds(2 * rows, TAG_ROWS)],
-            buffer.at[pl.ds(3 * rows + TAG_ROWS, TAG_ROWS)],
-        ),
-    ]
-    through([(copies, buffer, out)], ins, leaving)
 
 
 def choose(sizes, seps, near, far, after, out, sems):
@@ -190,8 +174,12 @@
     token[...] = jnp.zeros(token.shape, token.dtype)
 
 
-def gate_far(near, same, cross, h, near_out, same_out, cross_out, h_out):
-    h_out[0, :16, :128] = h[0, :16, :128]
+def gate_one(after, array, array_out, token):
+    token[...] = after[...]
+
+
+def gate_far(after, same, cross, same_out, cross_out, token):
+    token[...] = after[...]
 
 
 def own_fill(codes, p_ref, n, u_ref, turns):
@@ -227,9 +215,10 @@
     return [gamma[op, r] for r in range(nterm)]
 
 
-def own_kernel_0(gamma, block, proj, y_ref, h_ref, token, x_ref, p_ref, u_ref, turns, sems):
-    mom = lax.axis_index("mom")
-    run_copies([(block, x_ref), (proj.at[mom], p_ref.at[0])], sems)
+def own_kernel_0(sizes, seps, gamma, peram, proj, y_ref, ht, token, x_ref, p_ref, u_ref, turns, sems):
+    plan = Plan(seps, sizes)
+    mom = plan.mom
+    run_copies([(peram.at[mom, plan.keep], x_ref), (proj.at[mom], p_ref.at[0])], sems)
     width = x_ref.shape[-1]
     real, imag = x_ref[0], x_ref[1]
     y_ref[:width, :width] = real
@@ -237,37 +226,25 @@
     y_ref[width:, :width] = imag
     y_ref[width:, width:] = real
     own_fill(codes_of(gamma, mom, turns.shape[0]), p_ref, 0, u_ref, turns)
-    own_dot(u_ref, y_ref, h_ref.at[0])
+    own_dot(u_ref, y_ref, ht)
     token[...] = jnp.zeros(token.shape, token.dtype)
 
 
-def own_kernel_2(gamma, own, y_ref, h_in, h_ref, token, p_ref, u_ref, turns, sems):
-    run_copies([(own.at[span(0, p_ref.shape[1])], p_ref.at[0])], sems)
-    codes = codes_of(gamma, lax.axis_index("mom") ^ 2, turns.shape[0])
-    own_fill(codes, p_ref, 0, u_ref, turns)
-    own_dot(u_ref, y_ref, h_ref.at[2])
+def own_kernel(piece, gamma, source, y_ref, after, ht, token, p_ref, u_ref, turns, sems):
+    mom = lax.axis_index("mom")
+    run_copies([(source.at[mom], p_ref.at[0])], sems)
+    own_fill(codes_of(gamma, mom ^ piece, turns.shape[0]), p_ref, 0, u_ref, turns)
+    own_dot(u_ref, y_ref, ht)
     token[...] = jnp.zeros(token.shape, token.dtype)
 
 
-def own_kernel_13(sizes, seps, gamma, partner, own, traded, y_ref, h_in, after, *refs):
-    h_ref, label, p_ref, u0, u1, turns0, turns1, tags, sems = refs
-    rows = p_ref.shape[1]
-    spots = [pl.ds(n * rows + m * TAG_ROWS, TAG_ROWS) for n, m in ((3, 0), (2, 0), (3, 1))]
-    run_copies(
-        [
-            (traded.at[span(0, rows)], p_ref.at[0]),
-            (traded.at[span(1, rows)], p_ref.at[1]),
-            (traded.at[spots[0]], tags.at[0]),
-            (own.at[spots[1]], tags.at[1]),
-            (traded.at[spots[2]], tags.at[2]),
-        ],
-        sems,
-    )
-    plan = Plan(seps, sizes)
+def find_labels(plan, partner, tick, tags, label):
     mom = plan.mom
-    partners = [partner[0]] + [
-        jnp.max(tags[n].astype(jnp.float32)).astype(jnp.int32) for n in range(3)
-    ]
+
+    def number(tag):
+        return jnp.max(tag.astype(jnp.float32)).astype(jnp.int32)
+
+    partners = [partner[0], number(tick[...]), number(tags[:TAG_ROWS]), number(tags[TAG_ROWS:])]
     count = len(partners)
     for p in range(count):
         back = jnp.int32(0)
@@ -275,30 +252,33 @@
             back = back + jnp.where(value == (mom ^ p), mom ^ i, 0)
         label[p] = jnp.where(plan.forward, back, mom ^ p)
         label[count + p] = jnp.where(plan.forward, back, partners[p]) ^ mom
-    nterm = turns0.shape[0]
-    own_fill(codes_of(gamma, mom ^ 1, nterm), p_ref, 0, u0, turns0)
-    own_dot(u0, y_ref, h_ref.at[1])
-    own_fill(codes_of(gamma, mom ^ 3, nterm), p_ref, 1, u1, turns1)
-    own_dot(u1, y_ref, h_ref.at[3])
-
-
-def other_products(pieces, gamma, label, h_ref, sources, refs):
-    k_ref, p_ref, wa, wb, turns_a, turns_b, sems = refs
+
+
+def other_products(pieces, gamma, label, products, sources, refs, before=None):
+    k_ref, p_ref, hs, wa, wb, turns_a, turns_b, sems = refs
     mom = lax.axis_index("mom")
     nterm, nev = turns_a.shape[0], turns_a.shape[-1]
     width = wa.shape[0]
     (here, away), flag = sources
-
-    @pl.when(flag == 0)
-    def _():
-        run_copies([(ref, p_ref.at[n]) for n, ref in enumerate(here)], sems)
-
-    @pl.when(flag != 0)
-    def _():
-        run_copies([(ref, p_ref.at[n]) for n, ref in enumerate(away)], sems)
+    for n in range(2):
+        for wanted, refs_now in ((0, here), (1, away)):
+
+            @pl.when(flag == wanted)
+            def _():
+                pltpu.make_async_copy(refs_now[n], p_ref.at[n], sems.at[n]).start()
+
+    if before is not None:
+        before()
+    for n, piece in enumerate(pieces):
+        for own, source in enumerate(products):
+
+            @pl.when(label[4 + piece] == own)
+            def _():
+                pltpu.make_async_copy(source, hs.at[n], sems.at[2 + n]).start()
 
     for n, piece in enumerate(pieces):
         w_ref, turns = ((wa, turns_a), (wb, turns_b))[n % 2]
+        pltpu.make_async_copy(away[n], p_ref.at[n], sems.at[n]).wait()
         for r in range(nterm):
             real, imag = (p_ref[n, m * nev : (m + 1) * nev] for m in (2 * r, 2 * r + 1))
             set_turns(turns, r, real, imag)
@@ -309,15 +289,15 @@
             add_to(w_ref, along(spin, nev), along(column, nev, width), b)
 
         fill_spin_blocks(codes_of(gamma, mom ^ piece, nterm), turns, write)
-        own = label[4 + piece]
+        pltpu.make_async_copy(products[0], hs.at[n], sems.at[2 + n]).wait()
         for tile in range(width // TILE):
             lanes = slice(tile * TILE, (tile + 1) * TILE)
             weights = w_ref[lanes, :]
             k_ref[n, :width, lanes] = lax.dot_general(
-                h_ref[own, :, width:], weights, NT_DIMS, preferred_element_type=jnp.float32
+                hs[n, :, width:], weights, NT_DIMS, preferred_element_type=jnp.float32
             )
             k_ref[n, width:, lanes] = lax.dot_general(
-                h_ref[own, :, : 2 * width], weights, NT_DIMS, preferred_element_type=jnp.float32
+                hs[n, :, : 2 * width], weights, NT_DIMS, preferred_element_type=jnp.float32
             )
 
 
@@ -325,21 +305,26 @@
     return lax.rem(plan.hops(0), 2) if sizes[2] == 2 else jnp.int32(1)
 
 
-def other_kernel_02(sizes, seps, gamma, label, h_ref, proj, near, same, cross, *refs):
+def other_kernel_02(sizes, seps, gamma, partner, tick, h0, h1, h2, h3, proj, near, same, cross, *refs):
+    k_ref, label, tags, sems, refs = refs[0], refs[1], refs[2], refs[3], (refs[0],) + refs[4:]
     plan = Plan(seps, sizes)
-    low = span(0, proj.shape[1])
-    here, away = (proj.at[plan.local(0)], near.at[low]), (same.at[low], cross.at[low])
-    sources = ((here, away), other_flag(plan, sizes))
-    other_products((0, 2), gamma, label, h_ref, sources, refs)
-
-
-def other_kernel_13(sizes, seps, gamma, label, h_ref, traded, near, same, cross, *refs):
+    rows = proj.shape[1]
+    low, at = span(0, rows), plan.local(0)
+    sources = (((proj.at[at], near.at[at]), (same.at[low], cross.at[low])), other_flag(plan, sizes))
+
+    def before():
+        run_copies([(cross.at[pl.ds(2 * rows, 2 * TAG_ROWS)], tags)], sems)
+        find_labels(plan, partner, tick, tags, label)
+
+    other_products((0, 2), gamma, label, (h0, h1, h2, h3), sources, refs, before)
+
+
+def other_kernel_13(sizes, seps, gamma, label, h0, h1, h2, h3, core, near, same, cross, *refs):
     plan = Plan(seps, sizes)
-    rows = refs[1].shape[1]
-    at = span(1 if sizes[2] == 2 else 0, rows)
-    here = (traded.at[span(2, rows)], near.at[span(1, rows)])
-    sources = ((here, (same.at[at], cross.at[at])), other_flag(plan, sizes))
-    other_products((1, 3), gamma, label, h_ref, sources, refs)
+    rows = core.shape[1]
+    away, at = span(1 if sizes[2] == 2 else 0, rows), plan.local(0)
+    sources = (((core.at[at], near.at[at]), (same.at[away], cross.at[away])), other_flag(plan, sizes))
+    other_products((1, 3), gamma, label, (h0, h1, h2, h3), sources, refs)
 
 
 def row_sums(k_refs, source, offset, totals):
@@ -505,68 +490,72 @@
             name=name,
         )(*operands)
 
-    first, tick = call(
+    leaving = [first_shape, rest_shape]
+    first, rest, tick = call(
         part(pack_first, sizes),
         "pack_first",
-        [smem(), hbm()],
-        [hbm(), vmem()],
-        [first_shape, token],
-        buffers([first_shape]) + [dma(1), dma(1)],
+        [smem()] * 2 + [hbm()],
+        [hbm()] * 2 + [vmem()],
+        leaving + [token],
+        buffers(leaving) + [dma(2), dma(2)],
         58,
-    )(separations, peram_blocks)
-    leaving = [tagged, rest_shape, two, two, bf16(2, width, width), two]
-    own, rest, far_same, far_cross, block, near = call(
-        part(pack, sizes),
-        "pack",
-        [smem()] * 2 + [hbm()] * 2 + [vmem()],
-        [hbm()] * len(leaving),
-        leaving,
-        buffers(leaving) + [dma(10), dma(len(leaving))],
-        58,
-    )(separations, partner, peram_blocks, proj, swap_mom(tick, 1))
+    )(separations, partner, peram_blocks)
 
     plan = Plan(separations, sizes)
+    near = swap_mom(proj, 2)
+    core = swap_mom(proj, 1)
     first = swap_snk(first)
-    own = swap_mom(own, 2)
     rest_near, rest_far = most_of(rest, plan.peer_hops())
-    if src_count == 2:
-        far_same, far_cross = next_src(far_same), next_src(far_cross, 1, 2)
+    tick = swap_mom(tick, 1)
     u_scratch = pltpu.VMEM((width, 2 * width), jnp.bfloat16)
     turns = pltpu.VMEM((nterm, 4, nev, nev), jnp.bfloat16)
     piece = pltpu.VMEM((1, rows, nev), jnp.bfloat16)
     pieces = pltpu.VMEM((2, rows, nev), jnp.bfloat16)
-    products = bf16(mom_count, width, 3 * width)
-    y, h, done_0 = call(
-        own_kernel_0,
+    product = bf16(width, 3 * width)
+    y, h0, done_0 = call(
+        part(own_kernel_0, sizes),
         "own_products_0",
-        [smem()] + [hbm()] * 2,
+        [smem()] * 2 + [hbm()] * 2,
         [vmem()] * 3,
-        [bf16(2 * width, 2 * width), products, token],
+        [bf16(2 * width, 2 * width), product, token],
         [pltpu.VMEM((2, width, width), jnp.bfloat16), piece, u_scratch, turns, dma(2)],
-        20,
-    )(gamma_index, block, proj)
-    trade = bf16(3 * rows + 2 * TAG_ROWS, nev)
-    traded = call(
-        part(pack_later, sizes),
-        "pack_later",
-        [smem()] * 2 + [hbm()] * 2 + [vmem()],
-        hbm(),
-        trade,
-        buffers([trade]) + [dma(4), dma(1)],
-        20,
-    )(separations, partner, proj, own, done_0)
-    traded = swap_mom(traded, 1)
-    near = swap_mom(near, 2)
-    h, done_2 = call(
-        own_kernel_2,
-        "own_products_2",
-        [smem(), hbm()] + [vmem()] * 2,
-        [vmem()] * 2,
-        [products, token],
-        [piece, u_scratch, turns, dma(1)],
-        20,
-        {3: 0},
-    )(gamma_index, own, y, h)
+        58,
+    )(separations, gamma_index, peram_blocks, proj)
+    leaving = [two, bf16(2 * (rows + TAG_ROWS), nev)]
+    far_same, far_cross = call(
+        part(pack, sizes),
+        "pack",
+        [smem()] * 2 + [hbm(), vmem(), vmem()],
+        [hbm()] * 2,
+        leaving,
+        buffers(leaving) + [dma(4), dma(2)],
+        58,
+    )(separations, partner, proj, tick, done_0)
+    if src_count == 2:
+        far_same, far_cross = next_src(far_same), next_src(far_cross, 1, 2)
+    else:
+        far_cross = swap_mom(far_cross, 2)
+    def own_one(number, source, after):
+        return call(
+            part(own_kernel, number),
+            "own_products_%d" % number,
+            [smem(), hbm(), vmem(), vmem()],
+            [vmem()] * 2,
+            [product, token],
+            [piece, u_scratch, turns, dma(1)],
+            20,
+        )(gamma_index, source, y, after)
+
+    h1, done_1 = own_one(1, core, done_0)
+    near, _ = alias(
+        gate_one,
+        "gate_near",
+        [vmem(), anywhere()],
+        [bf16(*proj.shape), token],
+        {1: 0},
+        (done_1, near),
+    )
+    near_core = swap_mom(near, 1)
 
     if src_count > 2:
         rest_near = jnp.where(plan.peer_hops() // (src_count // 2) != 0, rest_far, rest_near)
@@ -579,7 +568,8 @@
         rest_shape,
         [dma(1)],
         20,
-    )(separations, rest_near, rest_far, done_0)
+    )(separations, rest_near, rest_far, done_1)
+    h2, done_2 = own_one(2, near, done_1)
     first, rest, opened = alias(
         gate,
         "gate",
@@ -590,65 +580,52 @@
     )
     rest = swap_snk(rest)
     first_near, first_far = most_of(first, plan.hops(0))
-    h, label = call(
-        part(own_kernel_13, sizes),
-        "own_products_13",
-        [smem()] * 3 + [hbm()] * 2 + [vmem()] * 3,
-        [vmem(), smem()],
-        [products, jax.ShapeDtypeStruct((2 * mom_count,), jnp.int32)],
-        [pieces, u_scratch, u_scratch, turns, turns]
-        + [pltpu.VMEM((3, TAG_ROWS, nev), jnp.bfloat16), dma(5)],
-        20,
-        {6: 0},
-    )(separations, gamma_index, partner, own, traded, y, h, opened)
-
-    near, far_same, far_cross, h = pl.pallas_call(
+    h3, done_3 = own_one(3, near_core, opened)
+    far_same, far_cross, _ = alias(
         gate_far,
-        in_specs=[anywhere()] * 3 + [vmem()],
-        out_specs=[anywhere()] * 3 + [vmem()],
-        out_shape=[two, two, two, products],
-        input_output_aliases={n: n for n in range(4)},
-        compiler_params=limit(20),
-        cost_estimate=pl.CostEstimate(
-            flops=WEIGHT, bytes_accessed=WEIGHT // 1000, transcendentals=0
-        ),
-        name="gate_far",
-    )(near, far_same, far_cross, h)
-    near_core = swap_mom(near, 1)
+        "gate_far",
+        [vmem()] + [anywhere()] * 2,
+        [two, bf16(2 * (rows + TAG_ROWS), nev), token],
+        {1: 0, 2: 1},
+        (done_3, far_same, far_cross),
+    )
     if src_count == 2:
         far = [far_same, far_cross, swap_mom(far_same, 1), swap_mom(far_cross, 1)]
     else:
 
         def moved(array):
+            array = lax.dynamic_index_in_dim(array, plan.local(0), 0, keepdims=False)
             if src_count == 1:
                 return array
             array, away = most_of(array, plan.hops(0))
             return jnp.where(plan.hops(0) // (src_count // 2) != 0, away, array)
 
-        here = lax.dynamic_index_in_dim(proj, plan.local(0), 0, keepdims=False)
-        here = (here, near[:rows], traded[2 * rows : 3 * rows], near_core[rows:])
-        far = [moved(array) for array in here]
+        far = [moved(array) for array in (proj, near, core, near_core)]
+        far[1] = jnp.concatenate([far[1], far[1], far_cross[2 * rows :]])
 
     k_shape = jax.ShapeDtypeStruct((2, 2 * width, width), jnp.float32)
-    scratch = [pieces, u_scratch, u_scratch, turns, turns, dma(2)]
-    ka = call(
+    scratch = [pieces, pltpu.VMEM((2, width, 3 * width), jnp.bfloat16)]
+    scratch += [u_scratch, u_scratch, turns, turns, dma(4)]
+    ka, label = call(
         part(other_kernel_02, sizes),
         "other_products_02",
-        [smem()] * 3 + [vmem()] + [hbm()] * 4,
+        [smem()] * 3 + [vmem()] + [hbm()] * 8,
+        [vmem(), smem()],
+        [k_shape, jax.ShapeDtypeStruct((2 * mom_count,), jnp.int32)],
+        [pltpu.VMEM((2 * TAG_ROWS, nev), jnp.bfloat16), dma(1)] + scratch,
+        20,
+    )(
+        separations, gamma_index, partner, tick, h0, h1, h2, h3, proj, near, far[0], far[1],
+    )
+    kb = call(
+        part(other_kernel_13, sizes),
+        "other_products_13",
+        [smem()] * 3 + [hbm()] * 8,
         vmem(),
         k_shape,
         scratch,
         20,
-    )(separations, gamma_index, label, h, proj, near, far[0], far[1])
-    kb = call(
-        part(other_kernel_13, sizes),
-        "other_products_13",
-        [smem()] * 3 + [vmem()] + [hbm()] * 4,
-        vmem(),
-        k_shape,
-        scratch,
-        20,
-    )(separations, gamma_index, label, h, traded, near_core, far[2], far[3])
+    )(separations, gamma_index, label, h0, h1, h2, h3, core, near_core, far[2], far[3])
 
     device_count = src_count * snk_count * mom_count
     values = time_count * sep_count * 2

time: 79.1 us -> 74.3 us (0.939)
  local copies, waits for them, and re-layouts: 8.23 us -> 1.5 us
  Pallas kernels: 35.9 us -> 38.7 us
  blocking collectives: 10.9 us -> 8.84 us
  waiting for transfers between devices: 11.2 us -> 12.5 us
    ppermute x2, waiting for transfers between devices: 1.23 us -> 8.35 us  [swap_snk(): return lax.ppermute(array, 'snk', pairs)]
    unnamed x18 -> x16, local copies, waits for them, and re-layouts: 7.39 us -> 0.67 us
    ppermute x4, waiting for transfers between devices: 6.36 us -> 1.66 us  [next_src(): return lax.ppermute(array, ('src', 'mom'), pairs)]
    all_to_all x1, blocking collectives: 10.9 us -> 8.84 us  [shards(): lax.all_to_all(out, ('src', 'snk', 'mom'), split_axis=0, concat_axis=0, t...]
    pallas_call x1 -> x3, Pallas kernels: 0.01 us -> 1.19 us  [alias(): pl.pallas_call(kernel, in_specs=in_specs, out_specs=[anywhere()] * len(al...]
    ppermute x7 -> x6, waiting for transfers between devices: 3.57 us -> 2.48 us  [swap_mom(): return lax.ppermute(array, 'mom', [(a, a ^ i) for a in range(mom_count)])]
    ppermute x2, starting transfers between devices: 3.66 us -> 2.59 us  [swap_snk(): return lax.ppermute(array, 'snk', pairs)]
    pallas_call x1, Pallas kernels: 1.51 us -> 2.32 us  [shards(): call(part(choose, sizes), 'choose', [smem()] + [hbm()] * 2 + [vmem()], vm...]
  transfers between devices with their start and end apart: 13 -> 12, of which waited for: 3 -> 4; matrix products, arithmetic and copies ran while one was open for 0% -> 0% of each run, Pallas kernels for 37% -> 48%
where the time goes in v9:
time: 74.3 us; the launch traced here: 73.8 us
  Pallas kernels  38.7 us (52%)
  waiting for transfers between devices  12.5 us (17%)
  starting transfers between devices  11.4 us (15%)
  blocking collectives  8.84 us (12%)
  local copies, waits for them, and re-layouts  1.5 us (2%)
  between operations  0.84 us (1%)
    pallas_call x3, Pallas kernels, own_one(): call(part(own_kernel, number), 'own_products_%d' % number, [smem(), hbm()...  9.75 us
    all_to_all x1, blocking collectives, shards(): lax.all_to_all(out, ('src', 'snk', 'mom'), split_axis=0, concat_axis=0, t...  8.84 us
    ppermute x2, waiting for transfers between devices, swap_snk(): return lax.ppermute(array, 'snk', pairs)  8.35 us
    pallas_call x1, Pallas kernels, shards(): call(part(other_kernel_02, sizes), 'other_products_02', [smem()] * 3 + [v...  5.64 us
    pallas_call x1, Pallas kernels, shards(): call(part(other_kernel_13, sizes), 'other_products_13', [smem()] * 3 + [h...  5.22 us
    ppermute x4, starting transfers between devices, next_src(): return lax.ppermute(array, ('src', 'mom'), pairs)  5.01 us
    pallas_call x1, Pallas kernels, shards(): call(part(own_kernel_0, sizes), 'own_products_0', [smem()] * 2 + [hbm()]...  4.91 us
    ppermute x6, starting transfers between devices, swap_mom(): return lax.ppermute(array, 'mom', [(a, a ^ i) for a in range(mom_count)])  3.84 us
  transfers between devices with their start and end apart: 12, of which 4 were waited for; matrix products, arithmetic and copies ran while one was open for 0% of the time, Pallas kernels for 48%

profile of v9, /device:TPU:0, one launch (start us, length us, event | category | flops | bytes accessed | tf_op | source)
XLA Modules:
  0.0 73.8 jit_solution(1882368865378701582)
XLA Ops:
  0.0 0.5 collective-permute-start.1
  0.5 2.5 %collective-permute-start.2 = (bf16[4,1024,128]{2,1,0:T(8,128)(2,1)}, bf16[4,1024,128]{2,1,0:T(8,128)(2,1)}, u32[]{:S(2)}, u32[]{:S(2)}) collective-permute-start(bf16[4,1024,128]{2,1,0:T(8,128)(2,1)} %bitcast.3), channel_id=1, source_target_pairs={{0,2},{1,3},{2,0},{3,1},{4,6},{5,7},{6,4},{7,5},{8,10},{9,11},{10,... | collective-permute-start | bytes 3145736 | tf_op jit(solution)/shard_map/ppermute | solution.py:428
  3.6 3.4 %pack_first.1 = (bf16[2,320,512]{2,1,0:T(8,128)(2,1)}, bf16[2,192,512]{2,1,0:T(8,128)(2,1)}, bf16[16,128]{1,0:T(8,128)(2,1)}) custom-call(s32[4]{0:T(128)} %seps.13, s32[1]{0:T(128)S(6)} %copy.18.partner, bf16[4,2,2,512,512]{4,3,2,1,0:T(8,128)(2,1)} %peram.3), custom_call_target="tpu_custom_call" | custom-call | flops 9999999827968 | bytes 10000000000 | tf_op jit(solution)/shard_map/pack_first/pallas_call | solution.py:494
  7.0 0.3 collective-permute-start
  7.3 2.6 %collective-permute-start.4 = (bf16[2,320,512]{2,1,0:T(8,128)(2,1)}, bf16[2,320,512]{2,1,0:T(8,128)(2,1)}, u32[]{:S(2)}, u32[]{:S(2)}) collective-permute-start(bf16[2,320,512]{2,1,0:T(8,128)(2,1)} %get-tuple-element.35), channel_id=1, source_target_pairs={{0,8},{4,12},{8,0},{12,4},{1,9},{5,13},{9,1},{13,5},{2,10},{6,14},... | collective-permute-start | bytes 1966088 | tf_op jit(solution)/shard_map/ppermute | solution.py:432
  9.9 1.5 %collective-permute-start.5 = (bf16[2,192,512]{2,1,0:T(8,128)(2,1)}, bf16[2,192,512]{2,1,0:T(8,128)(2,1)}, u32[]{:S(2)}, u32[]{:S(2)}) collective-permute-start(bf16[2,192,512]{2,1,0:T(8,128)(2,1)} %get-tuple-element.36.near), channel_id=1, source_target_pairs={{16,0},{17,1},{18,2},{19,3},{0,16},{1,17},{2,18},{3,19},{20,4},{21... | collective-permute-start | bytes 1179656 | tf_op jit(solution)/shard_map/ppermute | solution.py:440
  11.4 4.9 %own_products_0.1 = (bf16[1024,1024]{1,0:T(8,128)(2,1)}, bf16[512,1536]{1,0:T(8,128)(2,1)}, bf16[16,128]{1,0:T(8,128)(2,1)}) custom-call(s32[4]{0:T(128)} %seps.13, s32[4,4]{1,0:T(4,128)} %gamma.11, bf16[4,2,2,512,512]{4,3,2,1,0:T(8,128)(2,1)} %peram.3, bf16[4,1024,128]{2,1,0:T(8,128)(2,1)} %bitcast.4), custom_call_target="tpu_custom_call" | custom-call | flops 9999999827968 | bytes 10000000000 | tf_op jit(solution)/shard_map/own_products_0/pallas_call | solution.py:515
  16.3 0.0 collective-permute-done.tick
  16.3 0.0 copy-start.2
  16.3 0.0 copy-start.5
  16.3 0.0 copy-start.7
  16.3 3.0 %pack.1 = (bf16[2048,128]{1,0:T(8,128)(2,1)}, bf16[2080,128]{1,0:T(8,128)(2,1)}) custom-call(s32[4]{0:T(128)} %seps.13, s32[1]{0:T(128)S(6)} %copy.18.partner, bf16[4,1024,128]{2,1,0:T(8,128)(2,1)} %bitcast.5, bf16[16,128]{1,0:T(8,128)(2,1)} %collective-permute-done.tick, bf16[16,128]{1,0:T(8,128)(2,1)} %get-tuple-element.30.after), custom_call_target="tpu_custom_call" | custom-call | flops 9999999827968 | bytes 10000000000 | tf_op jit(solution)/shard_map/pack/pallas_call | solution.py:525
  19.3 0.6 collective-permute-start.6
  19.9 0.0 collective-permute-done.1.source.core
  19.9 1.4 %collective-permute-start.7 = (bf16[2080,128]{1,0:T(8,128)(2,1)}, bf16[2080,128]{1,0:T(8,128)(2,1)}, u32[]{:S(2)}, u32[]{:S(2)}) collective-permute-start(bf16[2080,128]{1,0:T(8,128)(2,1)} %get-tuple-element.42), channel_id=1, source_target_pairs={{18,0},{19,1},{16,2},{17,3},{2,16},{3,17},{0,18},{1,19},{22,4},{23... | collective-permute-start | bytes 1597448 | tf_op jit(solution)/shard_map/ppermute | solution.py:440
  21.4 0.0 copy-done.2
  21.4 0.0 copy-done.5
  21.4 0.0 copy-done.7
  21.4 3.3 %own_products_1.1 = (bf16[512,1536]{1,0:T(8,128)(2,1)S(1)}, bf16[16,128]{1,0:T(8,128)(2,1)S(1)}) custom-call(s32[4,4]{1,0:T(4,128)S(1)} %copy-done.2, bf16[4,1024,128]{2,1,0:T(8,128)(2,1)} %collective-permute-done.1.source.core, bf16[1024,1024]{1,0:T(8,128)(2,1)S(1)} %copy-done.5, bf16[16,128]{1,0:T(8,128)(2,1)S(1)} %copy-done.7), custom_call_target="tpu_custom_call" | custom-call | flops 9999999827968 | bytes 10000000000 | tf_op jit(solution)/shard_map/own_products_1/pallas_call | solution.py:539
  24.6 2.5 %collective-permute-done.2.array = bf16[4,1024,128]{2,1,0:T(8,128)(2,1)} collective-permute-done((bf16[4,1024,128]{2,1,0:T(8,128)(2,1)}, bf16[4,1024,128]{2,1,0:T(8,128)(2,1)}, u32[]{:S(2)}, u32[]{:S(2)}) %collective-permute-start.2) | collective-permute-done | bytes 1048608 | tf_op jit(solution)/shard_map/ppermute | solution.py:428
  27.1 0.6 gate_near.1
  27.7 3.2 %own_products_2.1 = (bf16[512,1536]{1,0:T(8,128)(2,1)S(1)}, bf16[16,128]{1,0:T(8,128)(2,1)S(1)}) custom-call(s32[4,4]{1,0:T(4,128)S(1)} %copy-done.2, bf16[4,1024,128]{2,1,0:T(8,128)(2,1)} %get-tuple-element.33.source.near, bf16[1024,1024]{1,0:T(8,128)(2,1)S(1)} %copy-done.5, bf16[16,128]{1,0:T(8,128)(2,1)S(1)} %get-tuple-element.32.after), custom_call_target="tpu_custom_call" | custom-call | flops 9999999827968 | bytes 10000000000 | tf_op jit(solution)/shard_map/own_products_2/pallas_call | solution.py:539
  31.0 0.1 collective-permute-start.3
  31.0 0.0 collective-permute-done.5.far
  31.1 2.3 %choose.1.rest = bf16[2,192,512]{2,1,0:T(8,128)(2,1)} custom-call(s32[4]{0:T(128)S(1)} %copy-done.3, bf16[2,192,512]{2,1,0:T(8,128)(2,1)S(1)} %copy-done.1, bf16[2,192,512]{2,1,0:T(8,128)(2,1)} %collective-permute-done.5.far, bf16[16,128]{1,0:T(8,128)(2,1)S(1)} %get-tuple-element.32.after), custom_call_target="tpu_custom_call" | custom-call | flops 9999999827968 | bytes 10000000000 | tf_op jit(solution)/shard_map/choose/pallas_call | solution.py:563
  33.4 6.1 %collective-permute-done.4.first = bf16[2,320,512]{2,1,0:T(8,128)(2,1)} collective-permute-done((bf16[2,320,512]{2,1,0:T(8,128)(2,1)}, bf16[2,320,512]{2,1,0:T(8,128)(2,1)}, u32[]{:S(2)}, u32[]{:S(2)}) %collective-permute-start.4) | collective-permute-done | bytes 655392 | tf_op jit(solution)/shard_map/ppermute | solution.py:432
  39.5 1.5 %collective-permute-start.10 = (bf16[2,320,512]{2,1,0:T(8,128)(2,1)}, bf16[2,320,512]{2,1,0:T(8,128)(2,1)}, u32[]{:S(2)}, u32[]{:S(2)}) collective-permute-start(bf16[2,320,512]{2,1,0:T(8,128)(2,1)} %get-tuple-element.47.near), channel_id=1, source_target_pairs={{16,0},{17,1},{18,2},{19,3},{0,16},{1,17},{2,18},{3,19},{20,4},{21... | collective-permute-start | bytes 1966088 | tf_op jit(solution)/shard_map/ppermute | solution.py:440
  41.0 0.0 collective-permute-start.11
  41.0 0.0 collective-permute-done.3.source.near
  41.0 3.3 %own_products_3.1 = (bf16[512,1536]{1,0:T(8,128)(2,1)S(1)}, bf16[16,128]{1,0:T(8,128)(2,1)S(1)}) custom-call(s32[4,4]{1,0:T(4,128)S(1)} %copy-done.2, bf16[4,1024,128]{2,1,0:T(8,128)(2,1)} %collective-permute-done.3.source.near, bf16[1024,1024]{1,0:T(8,128)(2,1)S(1)} %copy-done.5, bf16[16,128]{1,0:T(8,128)(2,1)S(1)} %get-tuple-element.38.after), custom_call_target="tpu_custom_call" | custom-call | flops 9999999827968 | bytes 10000000000 | tf_op jit(solution)/shard_map/own_products_3/pallas_call | solution.py:539
  44.2 0.0 collective-permute-done.6.same
  44.3 1.7 %collective-permute-done.7.cross = bf16[2080,128]{1,0:T(8,128)(2,1)} collective-permute-done((bf16[2080,128]{1,0:T(8,128)(2,1)}, bf16[2080,128]{1,0:T(8,128)(2,1)}, u32[]{:S(2)}, u32[]{:S(2)}) %collective-permute-start.7) | collective-permute-done | bytes 532512 | tf_op jit(solution)/shard_map/ppermute | solution.py:440
  45.9 0.6 gate_far.1
  46.5 0.0 collective-permute-start.8
  46.5 0.5 collective-permute-start.9
  47.0 0.1 copy-done
  47.1 0.5 copy-done.6
  47.7 5.6 %other_products_02.1 = (f32[2,1024,512]{2,1,0:T(8,128)S(1)}, s32[8]{0:T(128)S(1)}) custom-call(s32[4]{0:T(128)S(1)} %copy-done.4, s32[4,4]{1,0:T(4,128)S(1)} %copy-done.2, s32[1]{0:T(128)S(6)} %copy.18.partner, bf16[16,128]{1,0:T(8,128)(2,1)} %collective-permute-done.tick, bf16[512,1536]{1,0:T(8,128)(2,1)S(1)} %copy-done.6, ...), custom_call_target="tpu_custom_call" | custom-call | flops 9999999827968 | bytes 10000000000 | tf_op jit(solution)/shard_map/other_products_02/pallas_call | solution.py:609
  53.3 0.0 collective-permute-done.8.same
  53.3 0.0 collective-permute-done.9.cross
  53.3 5.2 %other_products_13.1.kb = f32[2,1024,512]{2,1,0:T(8,128)S(1)} custom-call(s32[4]{0:T(128)S(1)} %copy-done.4, s32[4,4]{1,0:T(4,128)S(1)} %copy-done.2, s32[8]{0:T(128)S(1)} %get-tuple-element.45.label, bf16[512,1536]{1,0:T(8,128)(2,1)S(1)} %copy-done.6, bf16[512,1536]{1,0:T(8,128)(2,1)S(1)} %get-tuple-element.31.h1, ...), custom_call_target="tpu_custom_call" | custom-call | flops 9999999827968 | bytes 10000000000 | tf_op jit(solution)/shard_map/other_products_13/pallas_call | solution.py:620
  58.6 2.3 %collective-permute-done.11.rest = bf16[2,192,512]{2,1,0:T(8,128)(2,1)} collective-permute-done((bf16[2,192,512]{2,1,0:T(8,128)(2,1)}, bf16[2,192,512]{2,1,0:T(8,128)(2,1)}, u32[]{:S(2)}, u32[]{:S(2)}) %collective-permute-start.11) | collective-permute-done | bytes 393248 | tf_op jit(solution)/shard_map/ppermute | solution.py:432
  60.8 0.0 collective-permute-done.10.far
  60.8 3.2 %traces.1 = f32[32,1,128]{2,1,0:T(1,128)S(1)} custom-call(s32[4]{0:T(128)S(1)} %copy-done.4, s32[8]{0:T(128)S(1)} %get-tuple-element.45.label, f32[2,1024,512]{2,1,0:T(8,128)S(1)} %get-tuple-element.46.ka, f32[2,1024,512]{2,1,0:T(8,128)S(1)} %other_products_13.1.kb, bf16[2,320,512]{2,1,0:T(8,128)(2,1)} %get-tuple-element.47.near, ...), custom_call_target="tpu_custom_call" | custom-call | flops 9999999827968 | bytes 10000000000 | tf_op jit(solution)/shard_map/traces/pallas_call | solution.py:633
  64.1 8.8 %all_to_all.5 = f32[32,1,128]{2,1,0:T(1,128)S(1)} all-to-all(f32[32,1,128]{2,1,0:T(1,128)S(1)} %traces.1), channel_id=1, replica_groups=mesh['src'=2,'snk'=4,'mom'=4] {'src','snk','mom'}, dimensions={0} | all-to-all | bytes 32768 | tf_op jit(solution)/shard_map/all_to_all | solution.py:642
  72.9 0.1 reduce_sum.11
  73.0 0.1 reshape.11
  73.1 0.7 copy.12
  (10 shorter events, 0.0 us)
Async XLA Ops:
  0.0 19.9 %collective-permute-start.1 = (bf16[4,1024,128]{2,1,0:T(8,128)(2,1)}, bf16[4,1024,128]{2,1,0:T(8,128)(2,1)}, u32[]{:S(2)}, u32[]{:S(2)}) collective-permute-start(bf16[4,1024,128]{2,1,0:T(8,128)(2,1)} %bitcast.2), channel_id=1, source_target_pairs={{0,1},{1,0},{2,3},{3,2},{4,5},{5,4},{6,7},{7,6},{8,9},{9,8},{10,11... | collective-permute-start | bytes 3145736 | tf_op jit(solution)/shard_map/ppermute | solution.py:428
  0.5 26.7 %collective-permute-start.2 = (bf16[4,1024,128]{2,1,0:T(8,128)(2,1)}, bf16[4,1024,128]{2,1,0:T(8,128)(2,1)}, u32[]{:S(2)}, u32[]{:S(2)}) collective-permute-start(bf16[4,1024,128]{2,1,0:T(8,128)(2,1)} %bitcast.3), channel_id=1, source_target_pairs={{0,2},{1,3},{2,0},{3,1},{4,6},{5,7},{6,4},{7,5},{8,10},{9,11},{10,... | collective-permute-start | bytes 3145736 | tf_op jit(solution)/shard_map/ppermute | solution.py:428
  7.0 9.3 %collective-permute-start = (bf16[16,128]{1,0:T(8,128)(2,1)}, bf16[16,128]{1,0:T(8,128)(2,1)}, u32[]{:S(2)}, u32[]{:S(2)}) collective-permute-start(bf16[16,128]{1,0:T(8,128)(2,1)} %get-tuple-element.27), channel_id=1, source_target_pairs={{0,1},{1,0},{2,3},{3,2},{4,5},{5,4},{6,7},{7,6},{8,9},{9,8},{10,11... | collective-permute-start | bytes 12296 | tf_op jit(solution)/shard_map/ppermute | solution.py:428
  7.3 32.2 %collective-permute-start.4 = (bf16[2,320,512]{2,1,0:T(8,128)(2,1)}, bf16[2,320,512]{2,1,0:T(8,128)(2,1)}, u32[]{:S(2)}, u32[]{:S(2)}) collective-permute-start(bf16[2,320,512]{2,1,0:T(8,128)(2,1)} %get-tuple-element.35), channel_id=1, source_target_pairs={{0,8},{4,12},{8,0},{12,4},{1,9},{5,13},{9,1},{13,5},{2,10},{6,14},... | collective-permute-start | bytes 1966088 | tf_op jit(solution)/shard_map/ppermute | solution.py:432
  9.9 21.2 %collective-permute-start.5 = (bf16[2,192,512]{2,1,0:T(8,128)(2,1)}, bf16[2,192,512]{2,1,0:T(8,128)(2,1)}, u32[]{:S(2)}, u32[]{:S(2)}) collective-permute-start(bf16[2,192,512]{2,1,0:T(8,128)(2,1)} %get-tuple-element.36.near), channel_id=1, source_target_pairs={{16,0},{17,1},{18,2},{19,3},{0,16},{1,17},{2,18},{3,19},{20,4},{21... | collective-permute-start | bytes 1179656 | tf_op jit(solution)/shard_map/ppermute | solution.py:440
  16.3 5.1 %copy-start.2 = (s32[4,4]{1,0:T(4,128)S(1)}, s32[4,4]{1,0:T(4,128)}, u32[]{:S(2)}) copy-start(s32[4,4]{1,0:T(4,128)} %gamma.11) | copy-start | bytes 196
  16.3 5.1 %copy-start.5 = (bf16[1024,1024]{1,0:T(8,128)(2,1)S(1)}, bf16[1024,1024]{1,0:T(8,128)(2,1)}, u32[]{:S(2)}) copy-start(bf16[1024,1024]{1,0:T(8,128)(2,1)} %get-tuple-element.29.y_ref) | copy-start | bytes 6291460
  16.3 5.1 %copy-start.7 = (bf16[16,128]{1,0:T(8,128)(2,1)S(1)}, bf16[16,128]{1,0:T(8,128)(2,1)}, u32[]{:S(2)}) copy-start(bf16[16,128]{1,0:T(8,128)(2,1)} %get-tuple-element.30.after) | copy-start | bytes 12292
  19.3 24.9 %collective-permute-start.6 = (bf16[2048,128]{1,0:T(8,128)(2,1)}, bf16[2048,128]{1,0:T(8,128)(2,1)}, u32[]{:S(2)}, u32[]{:S(2)}) collective-permute-start(bf16[2048,128]{1,0:T(8,128)(2,1)} %get-tuple-element.41), channel_id=1, source_target_pairs={{16,0},{17,1},{18,2},{19,3},{0,16},{1,17},{2,18},{3,19},{20,4},{21... | collective-permute-start | bytes 1572872 | tf_op jit(solution)/shard_map/ppermute | solution.py:440
  19.9 26.0 %collective-permute-start.7 = (bf16[2080,128]{1,0:T(8,128)(2,1)}, bf16[2080,128]{1,0:T(8,128)(2,1)}, u32[]{:S(2)}, u32[]{:S(2)}) collective-permute-start(bf16[2080,128]{1,0:T(8,128)(2,1)} %get-tuple-element.42), channel_id=1, source_target_pairs={{18,0},{19,1},{16,2},{17,3},{2,16},{3,17},{0,18},{1,19},{22,4},{23... | collective-permute-start | bytes 1597448 | tf_op jit(solution)/shard_map/ppermute | solution.py:440
  27.7 3.4 %copy-start.1 = (bf16[2,192,512]{2,1,0:T(8,128)(2,1)S(1)}, bf16[2,192,512]{2,1,0:T(8,128)(2,1)}, u32[]{:S(2)}) copy-start(bf16[2,192,512]{2,1,0:T(8,128)(2,1)} %get-tuple-element.36.near) | copy-start | bytes 1179652
  27.7 3.4 %copy-start.3 = (s32[4]{0:T(128)S(1)}, s32[4]{0:T(128)}, u32[]{:S(2)}) copy-start(s32[4]{0:T(128)} %seps.13) | copy-start | bytes 52
  31.0 10.0 %collective-permute-start.3 = (bf16[4,1024,128]{2,1,0:T(8,128)(2,1)}, bf16[4,1024,128]{2,1,0:T(8,128)(2,1)}, u32[]{:S(2)}, u32[]{:S(2)}) collective-permute-start(bf16[4,1024,128]{2,1,0:T(8,128)(2,1)} %get-tuple-element.33.source.near), channel_id=1, source_target_pairs={{0,1},{1,0},{2,3},{3,2},{4,5},{5,4},{6,7},{7,6},{8,9},{9,8},{10,11... | collective-permute-start | bytes 3145736 | tf_op jit(solution)/shard_map/ppermute | solution.py:428
  39.5 21.3 %collective-permute-start.10 = (bf16[2,320,512]{2,1,0:T(8,128)(2,1)}, bf16[2,320,512]{2,1,0:T(8,128)(2,1)}, u32[]{:S(2)}, u32[]{:S(2)}) collective-permute-start(bf16[2,320,512]{2,1,0:T(8,128)(2,1)} %get-tuple-element.47.near), channel_id=1, source_target_pairs={{16,0},{17,1},{18,2},{19,3},{0,16},{1,17},{2,18},{3,19},{20,4},{21... | collective-permute-start | bytes 1966088 | tf_op jit(solution)/shard_map/ppermute | solution.py:440
  41.0 19.8 %collective-permute-start.11 = (bf16[2,192,512]{2,1,0:T(8,128)(2,1)}, bf16[2,192,512]{2,1,0:T(8,128)(2,1)}, u32[]{:S(2)}, u32[]{:S(2)}) collective-permute-start(bf16[2,192,512]{2,1,0:T(8,128)(2,1)} %get-tuple-element.48), channel_id=1, source_target_pairs={{0,8},{4,12},{8,0},{12,4},{1,9},{5,13},{9,1},{13,5},{2,10},{6,14},... | collective-permute-start | bytes 1179656 | tf_op jit(solution)/shard_map/ppermute | solution.py:432
  45.9 1.2 %copy-start = (bf16[4,1,4,2,128,128]{5,4,3,2,1,0:T(8,128)(2,1)S(1)}, bf16[4,1,4,2,128,128]{5,4,3,2,1,0:T(8,128)(2,1)}, u32[]{:S(2)}) copy-start(bf16[4,1,4,2,128,128]{5,4,3,2,1,0:T(8,128)(2,1)} %param.6) | copy-start | bytes 3145732
  45.9 1.2 %copy-start.4 = (s32[4]{0:T(128)S(1)}, s32[4]{0:T(128)}, u32[]{:S(2)}) copy-start(s32[4]{0:T(128)} %seps.13) | copy-start | bytes 52
  45.9 1.7 %copy-start.6 = (bf16[512,1536]{1,0:T(8,128)(2,1)S(1)}, bf16[512,1536]{1,0:T(8,128)(2,1)}, u32[]{:S(2)}) copy-start(bf16[512,1536]{1,0:T(8,128)(2,1)} %get-tuple-element.28.h0) | copy-start | bytes 4718596
  46.5 6.8 %collective-permute-start.8 = (bf16[2048,128]{1,0:T(8,128)(2,1)}, bf16[2048,128]{1,0:T(8,128)(2,1)}, u32[]{:S(2)}, u32[]{:S(2)}) collective-permute-start(bf16[2048,128]{1,0:T(8,128)(2,1)} %get-tuple-element.43.same), channel_id=1, source_target_pairs={{0,1},{1,0},{2,3},{3,2},{4,5},{5,4},{6,7},{7,6},{8,9},{9,8},{10,11... | collective-permute-start | bytes 1572872 | tf_op jit(solution)/shard_map/ppermute | solution.py:428
  46.5 6.8 %collective-permute-start.9 = (bf16[2080,128]{1,0:T(8,128)(2,1)}, bf16[2080,128]{1,0:T(8,128)(2,1)}, u32[]{:S(2)}, u32[]{:S(2)}) collective-permute-start(bf16[2080,128]{1,0:T(8,128)(2,1)} %get-tuple-element.44.cross), channel_id=1, source_target_pairs={{0,1},{1,0},{2,3},{3,2},{4,5},{5,4},{6,7},{7,6},{8,9},{9,8},{10,11... | collective-permute-start | bytes 1597448 | tf_op jit(solution)/shard_map/ppermute | solution.py:428

commit v10 on v9

--- a/solution.py
+++ b/solution.py
@@ -31,10 +31,14 @@
 
 
 def fill_spin_blocks(codes, turns, write):
-    for r, code in enumerate(codes):
-        for spin in range(NSPIN):
-            column, phase = spin_entry(code, spin)
-            write(spin, column, *(turns[r, (n - phase) & 3] for n in (4, 1)))
+    for r in range(len(codes)):
+        fill_term(codes, turns, write, r)
+
+
+def fill_term(codes, turns, write, r):
+    for spin in range(NSPIN):
+        column, phase = spin_entry(codes[r], spin)
+        write(spin, column, *(turns[r, (n - phase) & 3] for n in (4, 1)))
 
 
 def set_turns(turns, r, real, imag):
@@ -276,29 +280,51 @@
             def _():
                 pltpu.make_async_copy(source, hs.at[n], sems.at[2 + n]).start()
 
-    for n, piece in enumerate(pieces):
-        w_ref, turns = ((wa, turns_a), (wb, turns_b))[n % 2]
-        pltpu.make_async_copy(away[n], p_ref.at[n], sems.at[n]).wait()
-        for r in range(nterm):
+    pairs = ((wa, turns_a), (wb, turns_b))
+
+    def fill(n):
+        w_ref, turns = pairs[n]
+        codes = codes_of(gamma, mom ^ pieces[n], nterm)
+
+        def write(spin, column, a, b):
+            add_to(w_ref, along(spin, nev), along(column, nev), a)
+            add_to(w_ref, along(spin, nev), along(column, nev, width), b)
+
+        def step(r):
+            rows = slice(r * nev, (r + 1) * nev)
+            w_ref[rows, :] = jnp.zeros((nev, w_ref.shape[1]), w_ref.dtype)
             real, imag = (p_ref[n, m * nev : (m + 1) * nev] for m in (2 * r, 2 * r + 1))
             set_turns(turns, r, real, imag)
-        w_ref[...] = jnp.zeros(w_ref.shape, w_ref.dtype)
-
-        def write(spin, column, a, b, w_ref=w_ref):
-            add_to(w_ref, along(spin, nev), along(column, nev), a)
-            add_to(w_ref, along(spin, nev), along(column, nev, width), b)
-
-        fill_spin_blocks(codes_of(gamma, mom ^ piece, nterm), turns, write)
+
+        def term(r):
+            fill_term(codes, turns, write, r)
+
+        return [functools.partial(f, r) for f in (step, term) for r in range(nterm)]
+
+    def dots(n):
+        def dot(start, half):
+            lanes = slice(start, start + TILE)
+            left = slice(width, 3 * width) if half == 0 else slice(0, 2 * width)
+            rows = slice(half * width, (half + 1) * width)
+            k_ref[n, rows, lanes] = lax.dot_general(
+                hs[n, :, left], pairs[n][0][lanes, :], NT_DIMS, preferred_element_type=jnp.float32
+            )
+
+        return [functools.partial(dot, tile, half) for tile in range(0, width, TILE) for half in (0, 1)]
+
+    for n in range(2):
+        pltpu.make_async_copy(away[n], p_ref.at[n], sems.at[n]).wait()
+    for step in fill(0):
+        step()
+    for n in range(2):
         pltpu.make_async_copy(products[0], hs.at[n], sems.at[2 + n]).wait()
-        for tile in range(width // TILE):
-            lanes = slice(tile * TILE, (tile + 1) * TILE)
-            weights = w_ref[lanes, :]
-            k_ref[n, :width, lanes] = lax.dot_general(
-                hs[n, :, width:], weights, NT_DIMS, preferred_element_type=jnp.float32
-            )
-            k_ref[n, width:, lanes] = lax.dot_general(
-                hs[n, :, : 2 * width], weights, NT_DIMS, preferred_element_type=jnp.float32
-            )
+    ahead = fill(1)
+    for n, dot in enumerate(dots(0)):
+        for step in ahead[2 * n : 2 * n + 2]:
+            step()
+        dot()
+    for dot in dots(1):
+        dot()
 
 
 def other_flag(plan, sizes):
@@ -358,18 +384,22 @@
     nev = width // NSPIN
     flag = lax.rem(lax.div(plan.hops(0), max(sizes[2] // 2, 1)), 2)
     later = pltpu.make_async_copy(rest, rest_buf, sems.at[1])
+    chunk = first_buf.shape[1] // 2
+    parts = [pl.ds(n * chunk, chunk) for n in range(2)]
+    for wanted, source in ((0, near), (1, far)):
+
+        @pl.when(flag == wanted)
+        def _():
+            for n, rows in enumerate(parts):
+                pltpu.make_async_copy(
+                    source.at[:, rows], first_buf.at[:, rows], sems.at[2 * n]
+                ).start()
+
     later.start()
-
-    @pl.when(flag == 0)
-    def _():
-        run_copies([(near, first_buf)], sems)
-
-    @pl.when(flag != 0)
-    def _():
-        run_copies([(far, first_buf)], sems)
-
     totals = tuple(jnp.zeros((16, nev), jnp.float32) for _ in range(2 * count))
-    totals = row_sums((ka, kb), first_buf, 0, totals)
+    for n, rows in enumerate(parts):
+        pltpu.make_async_copy(far.at[:, rows], first_buf.at[:, rows], sems.at[2 * n]).wait()
+        totals = row_sums((ka, kb), first_buf.at[:, rows], n * chunk, totals)
     later.wait()
     totals = row_sums((ka, kb), rest_buf, first_buf.shape[1], totals)
     sums = [jnp.sum(total, axis=0, keepdims=True) for total in totals]
@@ -636,7 +666,7 @@
         [smem()] * 2 + [vmem()] * 2 + [hbm()] * 3,
         vmem(),
         jax.ShapeDtypeStruct((device_count, lines, 128), jnp.float32),
-        buffers([first_shape, rest_shape]) + [dma(2)],
+        buffers([first_shape, rest_shape]) + [dma(3)],
         20,
     )(separations, label, ka, kb, first_near, first_far, rest)
     out = lax.all_to_all(out, ("src", "snk", "mom"), split_axis=0, concat_axis=0, tiled=True)

time: 74.3 us -> 74.1 us (level)
  Pallas kernels: 38.7 us -> 37.1 us
  waiting for transfers between devices: 12.5 us -> 13.9 us
    ppermute x2, waiting for transfers between devices: 8.35 us -> 9.75 us  [swap_snk(): return lax.ppermute(array, 'snk', pairs)]
    pallas_call x1, Pallas kernels: 2.32 us -> 1.51 us  [shards(): call(part(choose, sizes), 'choose', [smem()] + [hbm()] * 2 + [vmem()], vm...]
  transfers between devices with their start and end apart: 12 -> 12, of which waited for: 4 -> 4; matrix products, arithmetic and copies ran while one was open for 0% -> 0% of each run, Pallas kernels for 48% -> 46%
where the time goes in v10:
time: 74.1 us; the launch traced here: 73.6 us
  Pallas kernels  37.1 us (50%)
  waiting for transfers between devices  13.9 us (19%)
  starting transfers between devices  11.4 us (15%)
  blocking collectives  8.84 us (12%)
  local copies, waits for them, and re-layouts  1.5 us (2%)
  between operations  0.84 us (1%)
    ppermute x2, waiting for transfers between devices, swap_snk(): return lax.ppermute(array, 'snk', pairs)  9.75 us
    pallas_call x3, Pallas kernels, own_one(): call(part(own_kernel, number), 'own_products_%d' % number, [smem(), hbm()...  9.75 us
    all_to_all x1, blocking collectives, shards(): lax.all_to_all(out, ('src', 'snk', 'mom'), split_axis=0, concat_axis=0, t...  8.84 us
    pallas_call x1, Pallas kernels, shards(): call(part(other_kernel_02, sizes), 'other_products_02', [smem()] * 3 + [v...  5.33 us
    ppermute x4, starting transfers between devices, next_src(): return lax.ppermute(array, ('src', 'mom'), pairs)  5.01 us
    pallas_call x1, Pallas kernels, shards(): call(part(other_kernel_13, sizes), 'other_products_13', [smem()] * 3 + [h...  4.94 us
    pallas_call x1, Pallas kernels, shards(): call(part(own_kernel_0, sizes), 'own_products_0', [smem()] * 2 + [hbm()]...  4.91 us
    ppermute x6, starting transfers between devices, swap_mom(): return lax.ppermute(array, 'mom', [(a, a ^ i) for a in range(mom_count)])  3.84 us
  transfers between devices with their start and end apart: 12, of which 4 were waited for; matrix products, arithmetic and copies ran while one was open for 0% of the time, Pallas kernels for 46%

profile of v10, /device:TPU:0, one launch (start us, length us, event | category | flops | bytes accessed | tf_op | source)
XLA Modules:
  0.0 73.6 jit_solution(8681468367322646903)
XLA Ops:
  0.0 0.5 collective-permute-start.1
  0.5 2.5 %collective-permute-start.2 = (bf16[4,1024,128]{2,1,0:T(8,128)(2,1)}, bf16[4,1024,128]{2,1,0:T(8,128)(2,1)}, u32[]{:S(2)}, u32[]{:S(2)}) collective-permute-start(bf16[4,1024,128]{2,1,0:T(8,128)(2,1)} %bitcast.3), channel_id=1, source_target_pairs={{0,2},{1,3},{2,0},{3,1},{4,6},{5,7},{6,4},{7,5},{8,10},{9,11},{10,... | collective-permute-start | bytes 3145736 | tf_op jit(solution)/shard_map/ppermute | solution.py:458
  3.6 3.4 %pack_first.1 = (bf16[2,320,512]{2,1,0:T(8,128)(2,1)}, bf16[2,192,512]{2,1,0:T(8,128)(2,1)}, bf16[16,128]{1,0:T(8,128)(2,1)}) custom-call(s32[4]{0:T(128)} %seps.13, s32[1]{0:T(128)S(6)} %copy.18.partner, bf16[4,2,2,512,512]{4,3,2,1,0:T(8,128)(2,1)} %peram.3), custom_call_target="tpu_custom_call" | custom-call | flops 9999999827968 | bytes 10000000000 | tf_op jit(solution)/shard_map/pack_first/pallas_call | solution.py:524
  7.0 0.3 collective-permute-start
  7.3 2.6 %collective-permute-start.4 = (bf16[2,320,512]{2,1,0:T(8,128)(2,1)}, bf16[2,320,512]{2,1,0:T(8,128)(2,1)}, u32[]{:S(2)}, u32[]{:S(2)}) collective-permute-start(bf16[2,320,512]{2,1,0:T(8,128)(2,1)} %get-tuple-element.35), channel_id=1, source_target_pairs={{0,8},{4,12},{8,0},{12,4},{1,9},{5,13},{9,1},{13,5},{2,10},{6,14},... | collective-permute-start | bytes 1966088 | tf_op jit(solution)/shard_map/ppermute | solution.py:462
  9.9 1.5 %collective-permute-start.5 = (bf16[2,192,512]{2,1,0:T(8,128)(2,1)}, bf16[2,192,512]{2,1,0:T(8,128)(2,1)}, u32[]{:S(2)}, u32[]{:S(2)}) collective-permute-start(bf16[2,192,512]{2,1,0:T(8,128)(2,1)} %get-tuple-element.36.near), channel_id=1, source_target_pairs={{16,0},{17,1},{18,2},{19,3},{0,16},{1,17},{2,18},{3,19},{20,4},{21... | collective-permute-start | bytes 1179656 | tf_op jit(solution)/shard_map/ppermute | solution.py:470
  11.4 4.9 %own_products_0.1 = (bf16[1024,1024]{1,0:T(8,128)(2,1)}, bf16[512,1536]{1,0:T(8,128)(2,1)}, bf16[16,128]{1,0:T(8,128)(2,1)}) custom-call(s32[4]{0:T(128)} %seps.13, s32[4,4]{1,0:T(4,128)} %gamma.11, bf16[4,2,2,512,512]{4,3,2,1,0:T(8,128)(2,1)} %peram.3, bf16[4,1024,128]{2,1,0:T(8,128)(2,1)} %bitcast.4), custom_call_target="tpu_custom_call" | custom-call | flops 9999999827968 | bytes 10000000000 | tf_op jit(solution)/shard_map/own_products_0/pallas_call | solution.py:545
  16.3 0.0 collective-permute-done.tick
  16.3 0.0 copy-start.2
  16.3 0.0 copy-start.5
  16.3 0.0 copy-start.7
  16.3 3.0 %pack.1 = (bf16[2048,128]{1,0:T(8,128)(2,1)}, bf16[2080,128]{1,0:T(8,128)(2,1)}) custom-call(s32[4]{0:T(128)} %seps.13, s32[1]{0:T(128)S(6)} %copy.18.partner, bf16[4,1024,128]{2,1,0:T(8,128)(2,1)} %bitcast.5, bf16[16,128]{1,0:T(8,128)(2,1)} %collective-permute-done.tick, bf16[16,128]{1,0:T(8,128)(2,1)} %get-tuple-element.30.after), custom_call_target="tpu_custom_call" | custom-call | flops 9999999827968 | bytes 10000000000 | tf_op jit(solution)/shard_map/pack/pallas_call | solution.py:555
  19.3 0.6 collective-permute-start.6
  19.9 0.0 collective-permute-done.1.source.core
  19.9 1.4 %collective-permute-start.7 = (bf16[2080,128]{1,0:T(8,128)(2,1)}, bf16[2080,128]{1,0:T(8,128)(2,1)}, u32[]{:S(2)}, u32[]{:S(2)}) collective-permute-start(bf16[2080,128]{1,0:T(8,128)(2,1)} %get-tuple-element.42), channel_id=1, source_target_pairs={{18,0},{19,1},{16,2},{17,3},{2,16},{3,17},{0,18},{1,19},{22,4},{23... | collective-permute-start | bytes 1597448 | tf_op jit(solution)/shard_map/ppermute | solution.py:470
  21.4 0.0 copy-done.2
  21.4 0.0 copy-done.5
  21.4 0.0 copy-done.7
  21.4 3.3 %own_products_1.1 = (bf16[512,1536]{1,0:T(8,128)(2,1)S(1)}, bf16[16,128]{1,0:T(8,128)(2,1)S(1)}) custom-call(s32[4,4]{1,0:T(4,128)S(1)} %copy-done.2, bf16[4,1024,128]{2,1,0:T(8,128)(2,1)} %collective-permute-done.1.source.core, bf16[1024,1024]{1,0:T(8,128)(2,1)S(1)} %copy-done.5, bf16[16,128]{1,0:T(8,128)(2,1)S(1)} %copy-done.7), custom_call_target="tpu_custom_call" | custom-call | flops 9999999827968 | bytes 10000000000 | tf_op jit(solution)/shard_map/own_products_1/pallas_call | solution.py:569
  24.6 2.5 %collective-permute-done.2.array = bf16[4,1024,128]{2,1,0:T(8,128)(2,1)} collective-permute-done((bf16[4,1024,128]{2,1,0:T(8,128)(2,1)}, bf16[4,1024,128]{2,1,0:T(8,128)(2,1)}, u32[]{:S(2)}, u32[]{:S(2)}) %collective-permute-start.2) | collective-permute-done | bytes 1048608 | tf_op jit(solution)/shard_map/ppermute | solution.py:458
  27.1 0.6 gate_near.1
  27.7 3.2 %own_products_2.1 = (bf16[512,1536]{1,0:T(8,128)(2,1)S(1)}, bf16[16,128]{1,0:T(8,128)(2,1)S(1)}) custom-call(s32[4,4]{1,0:T(4,128)S(1)} %copy-done.2, bf16[4,1024,128]{2,1,0:T(8,128)(2,1)} %get-tuple-element.33.source.near, bf16[1024,1024]{1,0:T(8,128)(2,1)S(1)} %copy-done.5, bf16[16,128]{1,0:T(8,128)(2,1)S(1)} %get-tuple-element.32.after), custom_call_target="tpu_custom_call" | custom-call | flops 9999999827968 | bytes 10000000000 | tf_op jit(solution)/shard_map/own_products_2/pallas_call | solution.py:569
  31.0 0.1 collective-permute-start.3
  31.0 0.0 collective-permute-done.5.far
  31.1 1.5 %choose.1.rest = bf16[2,192,512]{2,1,0:T(8,128)(2,1)} custom-call(s32[4]{0:T(128)S(1)} %copy-done.3, bf16[2,192,512]{2,1,0:T(8,128)(2,1)S(1)} %copy-done.1, bf16[2,192,512]{2,1,0:T(8,128)(2,1)} %collective-permute-done.5.far, bf16[16,128]{1,0:T(8,128)(2,1)S(1)} %get-tuple-element.32.after), custom_call_target="tpu_custom_call" | custom-call | flops 9999999827968 | bytes 10000000000 | tf_op jit(solution)/shard_map/choose/pallas_call | solution.py:593
  32.6 6.9 %collective-permute-done.4.first = bf16[2,320,512]{2,1,0:T(8,128)(2,1)} collective-permute-done((bf16[2,320,512]{2,1,0:T(8,128)(2,1)}, bf16[2,320,512]{2,1,0:T(8,128)(2,1)}, u32[]{:S(2)}, u32[]{:S(2)}) %collective-permute-start.4) | collective-permute-done | bytes 655392 | tf_op jit(solution)/shard_map/ppermute | solution.py:462
  39.5 1.5 %collective-permute-start.10 = (bf16[2,320,512]{2,1,0:T(8,128)(2,1)}, bf16[2,320,512]{2,1,0:T(8,128)(2,1)}, u32[]{:S(2)}, u32[]{:S(2)}) collective-permute-start(bf16[2,320,512]{2,1,0:T(8,128)(2,1)} %get-tuple-element.47.near), channel_id=1, source_target_pairs={{16,0},{17,1},{18,2},{19,3},{0,16},{1,17},{2,18},{3,19},{20,4},{21... | collective-permute-start | bytes 1966088 | tf_op jit(solution)/shard_map/ppermute | solution.py:470
  41.0 0.0 collective-permute-start.11
  41.0 0.0 collective-permute-done.3.source.near
  41.0 3.3 %own_products_3.1 = (bf16[512,1536]{1,0:T(8,128)(2,1)S(1)}, bf16[16,128]{1,0:T(8,128)(2,1)S(1)}) custom-call(s32[4,4]{1,0:T(4,128)S(1)} %copy-done.2, bf16[4,1024,128]{2,1,0:T(8,128)(2,1)} %collective-permute-done.3.source.near, bf16[1024,1024]{1,0:T(8,128)(2,1)S(1)} %copy-done.5, bf16[16,128]{1,0:T(8,128)(2,1)S(1)} %get-tuple-element.38.after), custom_call_target="tpu_custom_call" | custom-call | flops 9999999827968 | bytes 10000000000 | tf_op jit(solution)/shard_map/own_products_3/pallas_call | solution.py:569
  44.2 0.0 collective-permute-done.6.same
  44.3 1.7 %collective-permute-done.7.cross = bf16[2080,128]{1,0:T(8,128)(2,1)} collective-permute-done((bf16[2080,128]{1,0:T(8,128)(2,1)}, bf16[2080,128]{1,0:T(8,128)(2,1)}, u32[]{:S(2)}, u32[]{:S(2)}) %collective-permute-start.7) | collective-permute-done | bytes 532512 | tf_op jit(solution)/shard_map/ppermute | solution.py:470
  45.9 0.6 gate_far.1
  46.5 0.0 collective-permute-start.8
  46.5 0.5 collective-permute-start.9
  47.0 0.1 copy-done
  47.1 0.5 copy-done.6
  47.7 5.3 %other_products_02.1 = (f32[2,1024,512]{2,1,0:T(8,128)S(1)}, s32[8]{0:T(128)S(1)}) custom-call(s32[4]{0:T(128)S(1)} %copy-done.4, s32[4,4]{1,0:T(4,128)S(1)} %copy-done.2, s32[1]{0:T(128)S(6)} %copy.18.partner, bf16[16,128]{1,0:T(8,128)(2,1)} %collective-permute-done.tick, bf16[512,1536]{1,0:T(8,128)(2,1)S(1)} %copy-done.6, ...), custom_call_target="tpu_custom_call" | custom-call | flops 9999999827968 | bytes 10000000000 | tf_op jit(solution)/shard_map/other_products_02/pallas_call | solution.py:639
  53.0 0.0 collective-permute-done.8.same
  53.0 0.0 collective-permute-done.9.cross
  53.0 4.9 %other_products_13.1.kb = f32[2,1024,512]{2,1,0:T(8,128)S(1)} custom-call(s32[4]{0:T(128)S(1)} %copy-done.4, s32[4,4]{1,0:T(4,128)S(1)} %copy-done.2, s32[8]{0:T(128)S(1)} %get-tuple-element.45.label, bf16[512,1536]{1,0:T(8,128)(2,1)S(1)} %copy-done.6, bf16[512,1536]{1,0:T(8,128)(2,1)S(1)} %get-tuple-element.31.h1, ...), custom_call_target="tpu_custom_call" | custom-call | flops 9999999827968 | bytes 10000000000 | tf_op jit(solution)/shard_map/other_products_13/pallas_call | solution.py:650
  58.0 2.9 %collective-permute-done.11.rest = bf16[2,192,512]{2,1,0:T(8,128)(2,1)} collective-permute-done((bf16[2,192,512]{2,1,0:T(8,128)(2,1)}, bf16[2,192,512]{2,1,0:T(8,128)(2,1)}, u32[]{:S(2)}, u32[]{:S(2)}) %collective-permute-start.11) | collective-permute-done | bytes 393248 | tf_op jit(solution)/shard_map/ppermute | solution.py:462
  60.8 0.0 collective-permute-done.10.far
  60.8 3.1 %traces.1 = f32[32,1,128]{2,1,0:T(1,128)S(1)} custom-call(s32[4]{0:T(128)S(1)} %copy-done.4, s32[8]{0:T(128)S(1)} %get-tuple-element.45.label, f32[2,1024,512]{2,1,0:T(8,128)S(1)} %get-tuple-element.46.ka, f32[2,1024,512]{2,1,0:T(8,128)S(1)} %other_products_13.1.kb, bf16[2,320,512]{2,1,0:T(8,128)(2,1)} %get-tuple-element.47.near, ...), custom_call_target="tpu_custom_call" | custom-call | flops 9999999827968 | bytes 10000000000 | tf_op jit(solution)/shard_map/traces/pallas_call | solution.py:663
  63.9 8.8 %all_to_all.5 = f32[32,1,128]{2,1,0:T(1,128)S(1)} all-to-all(f32[32,1,128]{2,1,0:T(1,128)S(1)} %traces.1), channel_id=1, replica_groups=mesh['src'=2,'snk'=4,'mom'=4] {'src','snk','mom'}, dimensions={0} | all-to-all | bytes 32768 | tf_op jit(solution)/shard_map/all_to_all | solution.py:672
  72.7 0.1 reduce_sum.11
  72.8 0.1 reshape.11
  72.9 0.7 copy.12
  (10 shorter events, 0.0 us)
Async XLA Ops:
  0.0 19.9 %collective-permute-start.1 = (bf16[4,1024,128]{2,1,0:T(8,128)(2,1)}, bf16[4,1024,128]{2,1,0:T(8,128)(2,1)}, u32[]{:S(2)}, u32[]{:S(2)}) collective-permute-start(bf16[4,1024,128]{2,1,0:T(8,128)(2,1)} %bitcast.2), channel_id=1, source_target_pairs={{0,1},{1,0},{2,3},{3,2},{4,5},{5,4},{6,7},{7,6},{8,9},{9,8},{10,11... | collective-permute-start | bytes 3145736 | tf_op jit(solution)/shard_map/ppermute | solution.py:458
  0.5 26.7 %collective-permute-start.2 = (bf16[4,1024,128]{2,1,0:T(8,128)(2,1)}, bf16[4,1024,128]{2,1,0:T(8,128)(2,1)}, u32[]{:S(2)}, u32[]{:S(2)}) collective-permute-start(bf16[4,1024,128]{2,1,0:T(8,128)(2,1)} %bitcast.3), channel_id=1, source_target_pairs={{0,2},{1,3},{2,0},{3,1},{4,6},{5,7},{6,4},{7,5},{8,10},{9,11},{10,... | collective-permute-start | bytes 3145736 | tf_op jit(solution)/shard_map/ppermute | solution.py:458
  7.0 9.3 %collective-permute-start = (bf16[16,128]{1,0:T(8,128)(2,1)}, bf16[16,128]{1,0:T(8,128)(2,1)}, u32[]{:S(2)}, u32[]{:S(2)}) collective-permute-start(bf16[16,128]{1,0:T(8,128)(2,1)} %get-tuple-element.27), channel_id=1, source_target_pairs={{0,1},{1,0},{2,3},{3,2},{4,5},{5,4},{6,7},{7,6},{8,9},{9,8},{10,11... | collective-permute-start | bytes 12296 | tf_op jit(solution)/shard_map/ppermute | solution.py:458
  7.3 32.2 %collective-permute-start.4 = (bf16[2,320,512]{2,1,0:T(8,128)(2,1)}, bf16[2,320,512]{2,1,0:T(8,128)(2,1)}, u32[]{:S(2)}, u32[]{:S(2)}) collective-permute-start(bf16[2,320,512]{2,1,0:T(8,128)(2,1)} %get-tuple-element.35), channel_id=1, source_target_pairs={{0,8},{4,12},{8,0},{12,4},{1,9},{5,13},{9,1},{13,5},{2,10},{6,14},... | collective-permute-start | bytes 1966088 | tf_op jit(solution)/shard_map/ppermute | solution.py:462
  9.9 21.2 %collective-permute-start.5 = (bf16[2,192,512]{2,1,0:T(8,128)(2,1)}, bf16[2,192,512]{2,1,0:T(8,128)(2,1)}, u32[]{:S(2)}, u32[]{:S(2)}) collective-permute-start(bf16[2,192,512]{2,1,0:T(8,128)(2,1)} %get-tuple-element.36.near), channel_id=1, source_target_pairs={{16,0},{17,1},{18,2},{19,3},{0,16},{1,17},{2,18},{3,19},{20,4},{21... | collective-permute-start | bytes 1179656 | tf_op jit(solution)/shard_map/ppermute | solution.py:470
  16.3 5.1 %copy-start.2 = (s32[4,4]{1,0:T(4,128)S(1)}, s32[4,4]{1,0:T(4,128)}, u32[]{:S(2)}) copy-start(s32[4,4]{1,0:T(4,128)} %gamma.11) | copy-start | bytes 196
  16.3 5.1 %copy-start.5 = (bf16[1024,1024]{1,0:T(8,128)(2,1)S(1)}, bf16[1024,1024]{1,0:T(8,128)(2,1)}, u32[]{:S(2)}) copy-start(bf16[1024,1024]{1,0:T(8,128)(2,1)} %get-tuple-element.29.y_ref) | copy-start | bytes 6291460
  16.3 5.1 %copy-start.7 = (bf16[16,128]{1,0:T(8,128)(2,1)S(1)}, bf16[16,128]{1,0:T(8,128)(2,1)}, u32[]{:S(2)}) copy-start(bf16[16,128]{1,0:T(8,128)(2,1)} %get-tuple-element.30.after) | copy-start | bytes 12292
  19.3 24.9 %collective-permute-start.6 = (bf16[2048,128]{1,0:T(8,128)(2,1)}, bf16[2048,128]{1,0:T(8,128)(2,1)}, u32[]{:S(2)}, u32[]{:S(2)}) collective-permute-start(bf16[2048,128]{1,0:T(8,128)(2,1)} %get-tuple-element.41), channel_id=1, source_target_pairs={{16,0},{17,1},{18,2},{19,3},{0,16},{1,17},{2,18},{3,19},{20,4},{21... | collective-permute-start | bytes 1572872 | tf_op jit(solution)/shard_map/ppermute | solution.py:470
  19.9 26.0 %collective-permute-start.7 = (bf16[2080,128]{1,0:T(8,128)(2,1)}, bf16[2080,128]{1,0:T(8,128)(2,1)}, u32[]{:S(2)}, u32[]{:S(2)}) collective-permute-start(bf16[2080,128]{1,0:T(8,128)(2,1)} %get-tuple-element.42), channel_id=1, source_target_pairs={{18,0},{19,1},{16,2},{17,3},{2,16},{3,17},{0,18},{1,19},{22,4},{23... | collective-permute-start | bytes 1597448 | tf_op jit(solution)/shard_map/ppermute | solution.py:470
  27.7 3.4 %copy-start.1 = (bf16[2,192,512]{2,1,0:T(8,128)(2,1)S(1)}, bf16[2,192,512]{2,1,0:T(8,128)(2,1)}, u32[]{:S(2)}) copy-start(bf16[2,192,512]{2,1,0:T(8,128)(2,1)} %get-tuple-element.36.near) | copy-start | bytes 1179652
  27.7 3.4 %copy-start.3 = (s32[4]{0:T(128)S(1)}, s32[4]{0:T(128)}, u32[]{:S(2)}) copy-start(s32[4]{0:T(128)} %seps.13) | copy-start | bytes 52
  31.0 10.0 %collective-permute-start.3 = (bf16[4,1024,128]{2,1,0:T(8,128)(2,1)}, bf16[4,1024,128]{2,1,0:T(8,128)(2,1)}, u32[]{:S(2)}, u32[]{:S(2)}) collective-permute-start(bf16[4,1024,128]{2,1,0:T(8,128)(2,1)} %get-tuple-element.33.source.near), channel_id=1, source_target_pairs={{0,1},{1,0},{2,3},{3,2},{4,5},{5,4},{6,7},{7,6},{8,9},{9,8},{10,11... | collective-permute-start | bytes 3145736 | tf_op jit(solution)/shard_map/ppermute | solution.py:458
  39.5 21.3 %collective-permute-start.10 = (bf16[2,320,512]{2,1,0:T(8,128)(2,1)}, bf16[2,320,512]{2,1,0:T(8,128)(2,1)}, u32[]{:S(2)}, u32[]{:S(2)}) collective-permute-start(bf16[2,320,512]{2,1,0:T(8,128)(2,1)} %get-tuple-element.47.near), channel_id=1, source_target_pairs={{16,0},{17,1},{18,2},{19,3},{0,16},{1,17},{2,18},{3,19},{20,4},{21... | collective-permute-start | bytes 1966088 | tf_op jit(solution)/shard_map/ppermute | solution.py:470
  41.0 19.8 %collective-permute-start.11 = (bf16[2,192,512]{2,1,0:T(8,128)(2,1)}, bf16[2,192,512]{2,1,0:T(8,128)(2,1)}, u32[]{:S(2)}, u32[]{:S(2)}) collective-permute-start(bf16[2,192,512]{2,1,0:T(8,128)(2,1)} %get-tuple-element.48), channel_id=1, source_target_pairs={{0,8},{4,12},{8,0},{12,4},{1,9},{5,13},{9,1},{13,5},{2,10},{6,14},... | collective-permute-start | bytes 1179656 | tf_op jit(solution)/shard_map/ppermute | solution.py:462
  45.9 1.2 %copy-start = (bf16[4,1,4,2,128,128]{5,4,3,2,1,0:T(8,128)(2,1)S(1)}, bf16[4,1,4,2,128,128]{5,4,3,2,1,0:T(8,128)(2,1)}, u32[]{:S(2)}) copy-start(bf16[4,1,4,2,128,128]{5,4,3,2,1,0:T(8,128)(2,1)} %param.6) | copy-start | bytes 3145732
  45.9 1.2 %copy-start.4 = (s32[4]{0:T(128)S(1)}, s32[4]{0:T(128)}, u32[]{:S(2)}) copy-start(s32[4]{0:T(128)} %seps.13) | copy-start | bytes 52
  45.9 1.7 %copy-start.6 = (bf16[512,1536]{1,0:T(8,128)(2,1)S(1)}, bf16[512,1536]{1,0:T(8,128)(2,1)}, u32[]{:S(2)}) copy-start(bf16[512,1536]{1,0:T(8,128)(2,1)} %get-tuple-element.28.h0) | copy-start | bytes 4718596
  46.5 6.5 %collective-permute-start.8 = (bf16[2048,128]{1,0:T(8,128)(2,1)}, bf16[2048,128]{1,0:T(8,128)(2,1)}, u32[]{:S(2)}, u32[]{:S(2)}) collective-permute-start(bf16[2048,128]{1,0:T(8,128)(2,1)} %get-tuple-element.43.same), channel_id=1, source_target_pairs={{0,1},{1,0},{2,3},{3,2},{4,5},{5,4},{6,7},{7,6},{8,9},{9,8},{10,11... | collective-permute-start | bytes 1572872 | tf_op jit(solution)/shard_map/ppermute | solution.py:458
  46.5 6.5 %collective-permute-start.9 = (bf16[2080,128]{1,0:T(8,128)(2,1)}, bf16[2080,128]{1,0:T(8,128)(2,1)}, u32[]{:S(2)}, u32[]{:S(2)}) collective-permute-start(bf16[2080,128]{1,0:T(8,128)(2,1)} %get-tuple-element.44.cross), channel_id=1, source_target_pairs={{0,1},{1,0},{2,3},{3,2},{4,5},{5,4},{6,7},{7,6},{8,9},{9,8},{10,11... | collective-permute-start | bytes 1597448 | tf_op jit(solution)/shard_map/ppermute | solution.py:458

commit v11 on v10

--- a/solution.py
+++ b/solution.py
@@ -138,14 +138,18 @@
 def pack_first(sizes, seps, partner, peram, *refs):
     outs, token, buffers, (ins, leaving) = refs[:2], refs[2], refs[3:5], refs[5:]
     plan = Plan(seps, sizes)
-    start, copies = 0, []
-    for buffer in buffers:
-        rows = buffer.shape[1]
-        source = peram.at[plan.peer_local(), plan.give, :, pl.ds(start, rows)]
-        copies.append([(source, buffer)])
-        start += rows
+    start, parts = 0, []
+    for out, buffer in zip(outs, buffers):
+        chunk = buffer.shape[1] // 2
+        for plane in range(2):
+            for n in range(2):
+                rows = pl.ds(n * chunk, chunk)
+                source = peram.at[plan.peer_local(), plan.give, plane, pl.ds(start + n * chunk, chunk)]
+                spot = buffer.at[plane, rows]
+                parts.append(([(source, spot)], spot, out.at[plane, rows]))
+        start += buffer.shape[1]
     token[...] = tag_of(partner, token.shape[-1])
-    through(list(zip(copies, buffers, outs)), ins, leaving)
+    through(parts, ins, leaving)
 
 
 def pack(sizes, seps, partner, proj, tick, after, *refs):
@@ -316,13 +320,13 @@
         pltpu.make_async_copy(away[n], p_ref.at[n], sems.at[n]).wait()
     for step in fill(0):
         step()
-    for n in range(2):
-        pltpu.make_async_copy(products[0], hs.at[n], sems.at[2 + n]).wait()
+    pltpu.make_async_copy(products[0], hs.at[0], sems.at[2]).wait()
     ahead = fill(1)
     for n, dot in enumerate(dots(0)):
         for step in ahead[2 * n : 2 * n + 2]:
             step()
         dot()
+    pltpu.make_async_copy(products[0], hs.at[1], sems.at[3]).wait()
     for dot in dots(1):
         dot()
 
@@ -527,7 +531,7 @@
         [smem()] * 2 + [hbm()],
         [hbm()] * 2 + [vmem()],
         leaving + [token],
-        buffers(leaving) + [dma(2), dma(2)],
+        buffers(leaving) + [dma(8), dma(8)],
         58,
     )(separations, partner, peram_blocks)
 

time: 74.1 us -> 74.1 us (level)
  no operation moved by 1% of the time
where the time goes in v11:
time: 74.1 us; the launch traced here: 73.6 us
  Pallas kernels  37.2 us (50%)
  waiting for transfers between devices  13.8 us (19%)
  starting transfers between devices  11.4 us (15%)
  blocking collectives  8.84 us (12%)
  local copies, waits for them, and re-layouts  1.5 us (2%)
  between operations  0.84 us (1%)
    pallas_call x3, Pallas kernels, own_one(): call(part(own_kernel, number), 'own_products_%d' % number, [smem(), hbm()...  9.75 us
    ppermute x2, waiting for transfers between devices, swap_snk(): return lax.ppermute(array, 'snk', pairs)  9.63 us
    all_to_all x1, blocking collectives, shards(): lax.all_to_all(out, ('src', 'snk', 'mom'), split_axis=0, concat_axis=0, t...  8.84 us
    pallas_call x1, Pallas kernels, shards(): call(part(other_kernel_02, sizes), 'other_products_02', [smem()] * 3 + [v...  5.37 us
    pallas_call x1, Pallas kernels, shards(): call(part(other_kernel_13, sizes), 'other_products_13', [smem()] * 3 + [h...  5.02 us
    ppermute x4, starting transfers between devices, next_src(): return lax.ppermute(array, ('src', 'mom'), pairs)  5.01 us
    pallas_call x1, Pallas kernels, shards(): call(part(own_kernel_0, sizes), 'own_products_0', [smem()] * 2 + [hbm()]...  4.9 us
    ppermute x6, starting transfers between devices, swap_mom(): return lax.ppermute(array, 'mom', [(a, a ^ i) for a in range(mom_count)])  3.84 us
  transfers between devices with their start and end apart: 12, of which 4 were waited for; matrix products, arithmetic and copies ran while one was open for 0% of the time, Pallas kernels for 46%

profile of v11, /device:TPU:0, one launch (start us, length us, event | category | flops | bytes accessed | tf_op | source)
XLA Modules:
  0.0 73.6 jit_solution(5699164411571116877)
XLA Ops:
  0.0 0.5 collective-permute-start.1
  0.5 2.5 %collective-permute-start.2 = (bf16[4,1024,128]{2,1,0:T(8,128)(2,1)}, bf16[4,1024,128]{2,1,0:T(8,128)(2,1)}, u32[]{:S(2)}, u32[]{:S(2)}) collective-permute-start(bf16[4,1024,128]{2,1,0:T(8,128)(2,1)} %bitcast.3), channel_id=1, source_target_pairs={{0,2},{1,3},{2,0},{3,1},{4,6},{5,7},{6,4},{7,5},{8,10},{9,11},{10,... | collective-permute-start | bytes 3145736 | tf_op jit(solution)/shard_map/ppermute | solution.py:462
  3.6 3.4 %pack_first.1 = (bf16[2,320,512]{2,1,0:T(8,128)(2,1)}, bf16[2,192,512]{2,1,0:T(8,128)(2,1)}, bf16[16,128]{1,0:T(8,128)(2,1)}) custom-call(s32[4]{0:T(128)} %seps.13, s32[1]{0:T(128)S(6)} %copy.18.partner, bf16[4,2,2,512,512]{4,3,2,1,0:T(8,128)(2,1)} %peram.3), custom_call_target="tpu_custom_call" | custom-call | flops 9999999827968 | bytes 10000000000 | tf_op jit(solution)/shard_map/pack_first/pallas_call | solution.py:528
  7.0 0.3 collective-permute-start
  7.3 2.6 %collective-permute-start.4 = (bf16[2,320,512]{2,1,0:T(8,128)(2,1)}, bf16[2,320,512]{2,1,0:T(8,128)(2,1)}, u32[]{:S(2)}, u32[]{:S(2)}) collective-permute-start(bf16[2,320,512]{2,1,0:T(8,128)(2,1)} %get-tuple-element.35), channel_id=1, source_target_pairs={{0,8},{4,12},{8,0},{12,4},{1,9},{5,13},{9,1},{13,5},{2,10},{6,14},... | collective-permute-start | bytes 1966088 | tf_op jit(solution)/shard_map/ppermute | solution.py:466
  9.9 1.5 %collective-permute-start.5 = (bf16[2,192,512]{2,1,0:T(8,128)(2,1)}, bf16[2,192,512]{2,1,0:T(8,128)(2,1)}, u32[]{:S(2)}, u32[]{:S(2)}) collective-permute-start(bf16[2,192,512]{2,1,0:T(8,128)(2,1)} %get-tuple-element.36.near), channel_id=1, source_target_pairs={{16,0},{17,1},{18,2},{19,3},{0,16},{1,17},{2,18},{3,19},{20,4},{21... | collective-permute-start | bytes 1179656 | tf_op jit(solution)/shard_map/ppermute | solution.py:474
  11.4 4.9 %own_products_0.1 = (bf16[1024,1024]{1,0:T(8,128)(2,1)}, bf16[512,1536]{1,0:T(8,128)(2,1)}, bf16[16,128]{1,0:T(8,128)(2,1)}) custom-call(s32[4]{0:T(128)} %seps.13, s32[4,4]{1,0:T(4,128)} %gamma.11, bf16[4,2,2,512,512]{4,3,2,1,0:T(8,128)(2,1)} %peram.3, bf16[4,1024,128]{2,1,0:T(8,128)(2,1)} %bitcast.4), custom_call_target="tpu_custom_call" | custom-call | flops 9999999827968 | bytes 10000000000 | tf_op jit(solution)/shard_map/own_products_0/pallas_call | solution.py:549
  16.3 0.0 collective-permute-done.tick
  16.3 0.0 copy-start.2
  16.3 0.0 copy-start.5
  16.3 0.0 copy-start.7
  16.3 3.0 %pack.1 = (bf16[2048,128]{1,0:T(8,128)(2,1)}, bf16[2080,128]{1,0:T(8,128)(2,1)}) custom-call(s32[4]{0:T(128)} %seps.13, s32[1]{0:T(128)S(6)} %copy.18.partner, bf16[4,1024,128]{2,1,0:T(8,128)(2,1)} %bitcast.5, bf16[16,128]{1,0:T(8,128)(2,1)} %collective-permute-done.tick, bf16[16,128]{1,0:T(8,128)(2,1)} %get-tuple-element.30.after), custom_call_target="tpu_custom_call" | custom-call | flops 9999999827968 | bytes 10000000000 | tf_op jit(solution)/shard_map/pack/pallas_call | solution.py:559
  19.3 0.6 collective-permute-start.6
  19.9 0.0 collective-permute-done.1.source.core
  19.9 1.4 %collective-permute-start.7 = (bf16[2080,128]{1,0:T(8,128)(2,1)}, bf16[2080,128]{1,0:T(8,128)(2,1)}, u32[]{:S(2)}, u32[]{:S(2)}) collective-permute-start(bf16[2080,128]{1,0:T(8,128)(2,1)} %get-tuple-element.42), channel_id=1, source_target_pairs={{18,0},{19,1},{16,2},{17,3},{2,16},{3,17},{0,18},{1,19},{22,4},{23... | collective-permute-start | bytes 1597448 | tf_op jit(solution)/shard_map/ppermute | solution.py:474
  21.4 0.0 copy-done.2
  21.4 0.0 copy-done.5
  21.4 0.0 copy-done.7
  21.4 3.3 %own_products_1.1 = (bf16[512,1536]{1,0:T(8,128)(2,1)S(1)}, bf16[16,128]{1,0:T(8,128)(2,1)S(1)}) custom-call(s32[4,4]{1,0:T(4,128)S(1)} %copy-done.2, bf16[4,1024,128]{2,1,0:T(8,128)(2,1)} %collective-permute-done.1.source.core, bf16[1024,1024]{1,0:T(8,128)(2,1)S(1)} %copy-done.5, bf16[16,128]{1,0:T(8,128)(2,1)S(1)} %copy-done.7), custom_call_target="tpu_custom_call" | custom-call | flops 9999999827968 | bytes 10000000000 | tf_op jit(solution)/shard_map/own_products_1/pallas_call | solution.py:573
  24.6 2.5 %collective-permute-done.2.array = bf16[4,1024,128]{2,1,0:T(8,128)(2,1)} collective-permute-done((bf16[4,1024,128]{2,1,0:T(8,128)(2,1)}, bf16[4,1024,128]{2,1,0:T(8,128)(2,1)}, u32[]{:S(2)}, u32[]{:S(2)}) %collective-permute-start.2) | collective-permute-done | bytes 1048608 | tf_op jit(solution)/shard_map/ppermute | solution.py:462
  27.1 0.6 gate_near.1
  27.7 3.2 %own_products_2.1 = (bf16[512,1536]{1,0:T(8,128)(2,1)S(1)}, bf16[16,128]{1,0:T(8,128)(2,1)S(1)}) custom-call(s32[4,4]{1,0:T(4,128)S(1)} %copy-done.2, bf16[4,1024,128]{2,1,0:T(8,128)(2,1)} %get-tuple-element.33.source.near, bf16[1024,1024]{1,0:T(8,128)(2,1)S(1)} %copy-done.5, bf16[16,128]{1,0:T(8,128)(2,1)S(1)} %get-tuple-element.32.after), custom_call_target="tpu_custom_call" | custom-call | flops 9999999827968 | bytes 10000000000 | tf_op jit(solution)/shard_map/own_products_2/pallas_call | solution.py:573
  31.0 0.1 collective-permute-start.3
  31.0 0.0 collective-permute-done.5.far
  31.1 1.5 %choose.1.rest = bf16[2,192,512]{2,1,0:T(8,128)(2,1)} custom-call(s32[4]{0:T(128)S(1)} %copy-done.3, bf16[2,192,512]{2,1,0:T(8,128)(2,1)S(1)} %copy-done.1, bf16[2,192,512]{2,1,0:T(8,128)(2,1)} %collective-permute-done.5.far, bf16[16,128]{1,0:T(8,128)(2,1)S(1)} %get-tuple-element.32.after), custom_call_target="tpu_custom_call" | custom-call | flops 9999999827968 | bytes 10000000000 | tf_op jit(solution)/shard_map/choose/pallas_call | solution.py:597
  32.6 6.9 %collective-permute-done.4.first = bf16[2,320,512]{2,1,0:T(8,128)(2,1)} collective-permute-done((bf16[2,320,512]{2,1,0:T(8,128)(2,1)}, bf16[2,320,512]{2,1,0:T(8,128)(2,1)}, u32[]{:S(2)}, u32[]{:S(2)}) %collective-permute-start.4) | collective-permute-done | bytes 655392 | tf_op jit(solution)/shard_map/ppermute | solution.py:466
  39.5 1.5 %collective-permute-start.10 = (bf16[2,320,512]{2,1,0:T(8,128)(2,1)}, bf16[2,320,512]{2,1,0:T(8,128)(2,1)}, u32[]{:S(2)}, u32[]{:S(2)}) collective-permute-start(bf16[2,320,512]{2,1,0:T(8,128)(2,1)} %get-tuple-element.47.near), channel_id=1, source_target_pairs={{16,0},{17,1},{18,2},{19,3},{0,16},{1,17},{2,18},{3,19},{20,4},{21... | collective-permute-start | bytes 1966088 | tf_op jit(solution)/shard_map/ppermute | solution.py:474
  41.0 0.0 collective-permute-start.11
  41.0 0.0 collective-permute-done.3.source.near
  41.0 3.2 %own_products_3.1 = (bf16[512,1536]{1,0:T(8,128)(2,1)S(1)}, bf16[16,128]{1,0:T(8,128)(2,1)S(1)}) custom-call(s32[4,4]{1,0:T(4,128)S(1)} %copy-done.2, bf16[4,1024,128]{2,1,0:T(8,128)(2,1)} %collective-permute-done.3.source.near, bf16[1024,1024]{1,0:T(8,128)(2,1)S(1)} %copy-done.5, bf16[16,128]{1,0:T(8,128)(2,1)S(1)} %get-tuple-element.38.after), custom_call_target="tpu_custom_call" | custom-call | flops 9999999827968 | bytes 10000000000 | tf_op jit(solution)/shard_map/own_products_3/pallas_call | solution.py:573
  44.2 0.0 collective-permute-done.6.same
  44.3 1.7 %collective-permute-done.7.cross = bf16[2080,128]{1,0:T(8,128)(2,1)} collective-permute-done((bf16[2080,128]{1,0:T(8,128)(2,1)}, bf16[2080,128]{1,0:T(8,128)(2,1)}, u32[]{:S(2)}, u32[]{:S(2)}) %collective-permute-start.7) | collective-permute-done | bytes 532512 | tf_op jit(solution)/shard_map/ppermute | solution.py:474
  45.9 0.6 gate_far.1
  46.5 0.0 collective-permute-start.8
  46.5 0.5 collective-permute-start.9
  47.0 0.1 copy-done
  47.1 0.5 copy-done.6
  47.7 5.4 %other_products_02.1 = (f32[2,1024,512]{2,1,0:T(8,128)S(1)}, s32[8]{0:T(128)S(1)}) custom-call(s32[4]{0:T(128)S(1)} %copy-done.4, s32[4,4]{1,0:T(4,128)S(1)} %copy-done.2, s32[1]{0:T(128)S(6)} %copy.18.partner, bf16[16,128]{1,0:T(8,128)(2,1)} %collective-permute-done.tick, bf16[512,1536]{1,0:T(8,128)(2,1)S(1)} %copy-done.6, ...), custom_call_target="tpu_custom_call" | custom-call | flops 9999999827968 | bytes 10000000000 | tf_op jit(solution)/shard_map/other_products_02/pallas_call | solution.py:643
  53.0 0.0 collective-permute-done.8.same
  53.0 0.0 collective-permute-done.9.cross
  53.1 5.0 %other_products_13.1.kb = f32[2,1024,512]{2,1,0:T(8,128)S(1)} custom-call(s32[4]{0:T(128)S(1)} %copy-done.4, s32[4,4]{1,0:T(4,128)S(1)} %copy-done.2, s32[8]{0:T(128)S(1)} %get-tuple-element.45.label, bf16[512,1536]{1,0:T(8,128)(2,1)S(1)} %copy-done.6, bf16[512,1536]{1,0:T(8,128)(2,1)S(1)} %get-tuple-element.31.h1, ...), custom_call_target="tpu_custom_call" | custom-call | flops 9999999827968 | bytes 10000000000 | tf_op jit(solution)/shard_map/other_products_13/pallas_call | solution.py:654
  58.1 2.7 %collective-permute-done.11.rest = bf16[2,192,512]{2,1,0:T(8,128)(2,1)} collective-permute-done((bf16[2,192,512]{2,1,0:T(8,128)(2,1)}, bf16[2,192,512]{2,1,0:T(8,128)(2,1)}, u32[]{:S(2)}, u32[]{:S(2)}) %collective-permute-start.11) | collective-permute-done | bytes 393248 | tf_op jit(solution)/shard_map/ppermute | solution.py:466
  60.8 0.0 collective-permute-done.10.far
  60.8 3.1 %traces.1 = f32[32,1,128]{2,1,0:T(1,128)S(1)} custom-call(s32[4]{0:T(128)S(1)} %copy-done.4, s32[8]{0:T(128)S(1)} %get-tuple-element.45.label, f32[2,1024,512]{2,1,0:T(8,128)S(1)} %get-tuple-element.46.ka, f32[2,1024,512]{2,1,0:T(8,128)S(1)} %other_products_13.1.kb, bf16[2,320,512]{2,1,0:T(8,128)(2,1)} %get-tuple-element.47.near, ...), custom_call_target="tpu_custom_call" | custom-call | flops 9999999827968 | bytes 10000000000 | tf_op jit(solution)/shard_map/traces/pallas_call | solution.py:667
  63.9 8.8 %all_to_all.5 = f32[32,1,128]{2,1,0:T(1,128)S(1)} all-to-all(f32[32,1,128]{2,1,0:T(1,128)S(1)} %traces.1), channel_id=1, replica_groups=mesh['src'=2,'snk'=4,'mom'=4] {'src','snk','mom'}, dimensions={0} | all-to-all | bytes 32768 | tf_op jit(solution)/shard_map/all_to_all | solution.py:676
  72.7 0.1 reduce_sum.11
  72.8 0.1 reshape.11
  72.9 0.7 copy.12
  (10 shorter events, 0.0 us)
Async XLA Ops:
  0.0 19.9 %collective-permute-start.1 = (bf16[4,1024,128]{2,1,0:T(8,128)(2,1)}, bf16[4,1024,128]{2,1,0:T(8,128)(2,1)}, u32[]{:S(2)}, u32[]{:S(2)}) collective-permute-start(bf16[4,1024,128]{2,1,0:T(8,128)(2,1)} %bitcast.2), channel_id=1, source_target_pairs={{0,1},{1,0},{2,3},{3,2},{4,5},{5,4},{6,7},{7,6},{8,9},{9,8},{10,11... | collective-permute-start | bytes 3145736 | tf_op jit(solution)/shard_map/ppermute | solution.py:462
  0.5 26.7 %collective-permute-start.2 = (bf16[4,1024,128]{2,1,0:T(8,128)(2,1)}, bf16[4,1024,128]{2,1,0:T(8,128)(2,1)}, u32[]{:S(2)}, u32[]{:S(2)}) collective-permute-start(bf16[4,1024,128]{2,1,0:T(8,128)(2,1)} %bitcast.3), channel_id=1, source_target_pairs={{0,2},{1,3},{2,0},{3,1},{4,6},{5,7},{6,4},{7,5},{8,10},{9,11},{10,... | collective-permute-start | bytes 3145736 | tf_op jit(solution)/shard_map/ppermute | solution.py:462
  7.0 9.3 %collective-permute-start = (bf16[16,128]{1,0:T(8,128)(2,1)}, bf16[16,128]{1,0:T(8,128)(2,1)}, u32[]{:S(2)}, u32[]{:S(2)}) collective-permute-start(bf16[16,128]{1,0:T(8,128)(2,1)} %get-tuple-element.27), channel_id=1, source_target_pairs={{0,1},{1,0},{2,3},{3,2},{4,5},{5,4},{6,7},{7,6},{8,9},{9,8},{10,11... | collective-permute-start | bytes 12296 | tf_op jit(solution)/shard_map/ppermute | solution.py:462
  7.3 32.2 %collective-permute-start.4 = (bf16[2,320,512]{2,1,0:T(8,128)(2,1)}, bf16[2,320,512]{2,1,0:T(8,128)(2,1)}, u32[]{:S(2)}, u32[]{:S(2)}) collective-permute-start(bf16[2,320,512]{2,1,0:T(8,128)(2,1)} %get-tuple-element.35), channel_id=1, source_target_pairs={{0,8},{4,12},{8,0},{12,4},{1,9},{5,13},{9,1},{13,5},{2,10},{6,14},... | collective-permute-start | bytes 1966088 | tf_op jit(solution)/shard_map/ppermute | solution.py:466
  9.9 21.2 %collective-permute-start.5 = (bf16[2,192,512]{2,1,0:T(8,128)(2,1)}, bf16[2,192,512]{2,1,0:T(8,128)(2,1)}, u32[]{:S(2)}, u32[]{:S(2)}) collective-permute-start(bf16[2,192,512]{2,1,0:T(8,128)(2,1)} %get-tuple-element.36.near), channel_id=1, source_target_pairs={{16,0},{17,1},{18,2},{19,3},{0,16},{1,17},{2,18},{3,19},{20,4},{21... | collective-permute-start | bytes 1179656 | tf_op jit(solution)/shard_map/ppermute | solution.py:474
  16.3 5.1 %copy-start.2 = (s32[4,4]{1,0:T(4,128)S(1)}, s32[4,4]{1,0:T(4,128)}, u32[]{:S(2)}) copy-start(s32[4,4]{1,0:T(4,128)} %gamma.11) | copy-start | bytes 196
  16.3 5.1 %copy-start.5 = (bf16[1024,1024]{1,0:T(8,128)(2,1)S(1)}, bf16[1024,1024]{1,0:T(8,128)(2,1)}, u32[]{:S(2)}) copy-start(bf16[1024,1024]{1,0:T(8,128)(2,1)} %get-tuple-element.29.y_ref) | copy-start | bytes 6291460
  16.3 5.1 %copy-start.7 = (bf16[16,128]{1,0:T(8,128)(2,1)S(1)}, bf16[16,128]{1,0:T(8,128)(2,1)}, u32[]{:S(2)}) copy-start(bf16[16,128]{1,0:T(8,128)(2,1)} %get-tuple-element.30.after) | copy-start | bytes 12292
  19.3 24.9 %collective-permute-start.6 = (bf16[2048,128]{1,0:T(8,128)(2,1)}, bf16[2048,128]{1,0:T(8,128)(2,1)}, u32[]{:S(2)}, u32[]{:S(2)}) collective-permute-start(bf16[2048,128]{1,0:T(8,128)(2,1)} %get-tuple-element.41), channel_id=1, source_target_pairs={{16,0},{17,1},{18,2},{19,3},{0,16},{1,17},{2,18},{3,19},{20,4},{21... | collective-permute-start | bytes 1572872 | tf_op jit(solution)/shard_map/ppermute | solution.py:474
  19.9 26.0 %collective-permute-start.7 = (bf16[2080,128]{1,0:T(8,128)(2,1)}, bf16[2080,128]{1,0:T(8,128)(2,1)}, u32[]{:S(2)}, u32[]{:S(2)}) collective-permute-start(bf16[2080,128]{1,0:T(8,128)(2,1)} %get-tuple-element.42), channel_id=1, source_target_pairs={{18,0},{19,1},{16,2},{17,3},{2,16},{3,17},{0,18},{1,19},{22,4},{23... | collective-permute-start | bytes 1597448 | tf_op jit(solution)/shard_map/ppermute | solution.py:474
  27.7 3.4 %copy-start.1 = (bf16[2,192,512]{2,1,0:T(8,128)(2,1)S(1)}, bf16[2,192,512]{2,1,0:T(8,128)(2,1)}, u32[]{:S(2)}) copy-start(bf16[2,192,512]{2,1,0:T(8,128)(2,1)} %get-tuple-element.36.near) | copy-start | bytes 1179652
  27.7 3.4 %copy-start.3 = (s32[4]{0:T(128)S(1)}, s32[4]{0:T(128)}, u32[]{:S(2)}) copy-start(s32[4]{0:T(128)} %seps.13) | copy-start | bytes 52
  31.0 10.0 %collective-permute-start.3 = (bf16[4,1024,128]{2,1,0:T(8,128)(2,1)}, bf16[4,1024,128]{2,1,0:T(8,128)(2,1)}, u32[]{:S(2)}, u32[]{:S(2)}) collective-permute-start(bf16[4,1024,128]{2,1,0:T(8,128)(2,1)} %get-tuple-element.33.source.near), channel_id=1, source_target_pairs={{0,1},{1,0},{2,3},{3,2},{4,5},{5,4},{6,7},{7,6},{8,9},{9,8},{10,11... | collective-permute-start | bytes 3145736 | tf_op jit(solution)/shard_map/ppermute | solution.py:462
  39.5 21.3 %collective-permute-start.10 = (bf16[2,320,512]{2,1,0:T(8,128)(2,1)}, bf16[2,320,512]{2,1,0:T(8,128)(2,1)}, u32[]{:S(2)}, u32[]{:S(2)}) collective-permute-start(bf16[2,320,512]{2,1,0:T(8,128)(2,1)} %get-tuple-element.47.near), channel_id=1, source_target_pairs={{16,0},{17,1},{18,2},{19,3},{0,16},{1,17},{2,18},{3,19},{20,4},{21... | collective-permute-start | bytes 1966088 | tf_op jit(solution)/shard_map/ppermute | solution.py:474
  41.0 19.8 %collective-permute-start.11 = (bf16[2,192,512]{2,1,0:T(8,128)(2,1)}, bf16[2,192,512]{2,1,0:T(8,128)(2,1)}, u32[]{:S(2)}, u32[]{:S(2)}) collective-permute-start(bf16[2,192,512]{2,1,0:T(8,128)(2,1)} %get-tuple-element.48), channel_id=1, source_target_pairs={{0,8},{4,12},{8,0},{12,4},{1,9},{5,13},{9,1},{13,5},{2,10},{6,14},... | collective-permute-start | bytes 1179656 | tf_op jit(solution)/shard_map/ppermute | solution.py:466
  45.9 1.2 %copy-start = (bf16[4,1,4,2,128,128]{5,4,3,2,1,0:T(8,128)(2,1)S(1)}, bf16[4,1,4,2,128,128]{5,4,3,2,1,0:T(8,128)(2,1)}, u32[]{:S(2)}) copy-start(bf16[4,1,4,2,128,128]{5,4,3,2,1,0:T(8,128)(2,1)} %param.6) | copy-start | bytes 3145732
  45.9 1.2 %copy-start.4 = (s32[4]{0:T(128)S(1)}, s32[4]{0:T(128)}, u32[]{:S(2)}) copy-start(s32[4]{0:T(128)} %seps.13) | copy-start | bytes 52
  45.9 1.7 %copy-start.6 = (bf16[512,1536]{1,0:T(8,128)(2,1)S(1)}, bf16[512,1536]{1,0:T(8,128)(2,1)}, u32[]{:S(2)}) copy-start(bf16[512,1536]{1,0:T(8,128)(2,1)} %get-tuple-element.28.h0) | copy-start | bytes 4718596
  46.5 6.5 %collective-permute-start.8 = (bf16[2048,128]{1,0:T(8,128)(2,1)}, bf16[2048,128]{1,0:T(8,128)(2,1)}, u32[]{:S(2)}, u32[]{:S(2)}) collective-permute-start(bf16[2048,128]{1,0:T(8,128)(2,1)} %get-tuple-element.43.same), channel_id=1, source_target_pairs={{0,1},{1,0},{2,3},{3,2},{4,5},{5,4},{6,7},{7,6},{8,9},{9,8},{10,11... | collective-permute-start | bytes 1572872 | tf_op jit(solution)/shard_map/ppermute | solution.py:462
  46.5 6.5 %collective-permute-start.9 = (bf16[2080,128]{1,0:T(8,128)(2,1)}, bf16[2080,128]{1,0:T(8,128)(2,1)}, u32[]{:S(2)}, u32[]{:S(2)}) collective-permute-start(bf16[2080,128]{1,0:T(8,128)(2,1)} %get-tuple-element.44.cross), channel_id=1, source_target_pairs={{0,1},{1,0},{2,3},{3,2},{4,5},{5,4},{6,7},{7,6},{8,9},{9,8},{10,11... | collective-permute-start | bytes 1597448 | tf_op jit(solution)/shard_map/ppermute | solution.py:462

commit v12 on v10

--- a/solution.py
+++ b/solution.py
@@ -377,7 +377,7 @@
     return lax.fori_loop(0, source.shape[1] // rows, step, totals)
 
 
-def trace_kernel(sizes, sep_count, seps, label, ka, kb, near, far, rest, out_ref, first_buf, rest_buf, sems):
+def trace_kernel(sizes, sep_count, rest, seps, label, ka, kb, near, far, out_ref, first_buf, rest_buf, sems):
     plan = Plan(seps, sizes)
     count = 2 * ka.shape[0]
     width = rest_buf.shape[-1]
@@ -663,12 +663,12 @@
     out = call(
         part(trace_kernel, sizes, sep_count),
         "traces",
-        [smem()] * 2 + [vmem()] * 2 + [hbm()] * 3,
+        [hbm()] + [smem()] * 2 + [vmem()] * 2 + [hbm()] * 2,
         vmem(),
         jax.ShapeDtypeStruct((device_count, lines, 128), jnp.float32),
         buffers([first_shape, rest_shape]) + [dma(3)],
         20,
-    )(separations, label, ka, kb, first_near, first_far, rest)
+    )(rest, separations, label, ka, kb, first_near, first_far)
     out = lax.all_to_all(out, ("src", "snk", "mom"), split_axis=0, concat_axis=0, tiled=True)
     out = jnp.sum(out, axis=0).reshape(lines * 128)[:values]
     return out.reshape(time_count, sep_count, 1, 2)

time: 74.1 us -> 73.2 us (0.988)
  waiting for transfers between devices: 13.9 us -> 11.9 us
    ppermute x2, waiting for transfers between devices: 9.75 us -> 7.51 us  [swap_snk(): return lax.ppermute(array, 'snk', pairs)]
    pallas_call x1, Pallas kernels: 1.51 us -> 2.32 us  [shards(): call(part(choose, sizes), 'choose', [smem()] + [hbm()] * 2 + [vmem()], vm...]
  transfers between devices with their start and end apart: 12 -> 12, of which waited for: 4 -> 4; matrix products, arithmetic and copies ran while one was open for 0% -> 0% of each run, Pallas kernels for 46% -> 48%
where the time goes in v12:
time: 73.2 us; the launch traced here: 72.7 us
  Pallas kernels  37.8 us (52%)
  waiting for transfers between devices  11.9 us (16%)
  starting transfers between devices  11.2 us (15%)
  blocking collectives  9.41 us (13%)
  local copies, waits for them, and re-layouts  1.5 us (2%)
  between operations  0.84 us (1%)
    pallas_call x3, Pallas kernels, own_one(): call(part(own_kernel, number), 'own_products_%d' % number, [smem(), hbm()...  9.75 us
    all_to_all x1, blocking collectives, shards(): lax.all_to_all(out, ('src', 'snk', 'mom'), split_axis=0, concat_axis=0, t...  9.41 us
    ppermute x2, waiting for transfers between devices, swap_snk(): return lax.ppermute(array, 'snk', pairs)  7.51 us
    pallas_call x1, Pallas kernels, shards(): call(part(other_kernel_02, sizes), 'other_products_02', [smem()] * 3 + [v...  5.26 us
    ppermute x4, starting transfers between devices, next_src(): return lax.ppermute(array, ('src', 'mom'), pairs)  5.02 us
    pallas_call x1, Pallas kernels, shards(): call(part(other_kernel_13, sizes), 'other_products_13', [smem()] * 3 + [h...  4.94 us
    pallas_call x1, Pallas kernels, shards(): call(part(own_kernel_0, sizes), 'own_products_0', [smem()] * 2 + [hbm()]...  4.9 us
    ppermute x6, starting transfers between devices, swap_mom(): return lax.ppermute(array, 'mom', [(a, a ^ i) for a in range(mom_count)])  3.55 us
  transfers between devices with their start and end apart: 12, of which 4 were waited for; matrix products, arithmetic and copies ran while one was open for 0% of the time, Pallas kernels for 48%

profile of v12, /device:TPU:0, one launch (start us, length us, event | category | flops | bytes accessed | tf_op | source)
XLA Modules:
  0.0 72.7 jit_solution(9777239703939591489)
XLA Ops:
  0.0 0.5 collective-permute-start.2
  0.5 2.5 %collective-permute-start.3 = (bf16[4,1024,128]{2,1,0:T(8,128)(2,1)}, bf16[4,1024,128]{2,1,0:T(8,128)(2,1)}, u32[]{:S(2)}, u32[]{:S(2)}) collective-permute-start(bf16[4,1024,128]{2,1,0:T(8,128)(2,1)} %bitcast.3), channel_id=1, source_target_pairs={{0,2},{1,3},{2,0},{3,1},{4,6},{5,7},{6,4},{7,5},{8,10},{9,11},{10,... | collective-permute-start | bytes 3145736 | tf_op jit(solution)/shard_map/ppermute | solution.py:458
  3.6 3.4 %pack_first.1 = (bf16[2,320,512]{2,1,0:T(8,128)(2,1)}, bf16[2,192,512]{2,1,0:T(8,128)(2,1)}, bf16[16,128]{1,0:T(8,128)(2,1)}) custom-call(s32[4]{0:T(128)} %seps.13, s32[1]{0:T(128)S(6)} %copy.18.partner, bf16[4,2,2,512,512]{4,3,2,1,0:T(8,128)(2,1)} %peram.3), custom_call_target="tpu_custom_call" | custom-call | flops 9999999827968 | bytes 10000000000 | tf_op jit(solution)/shard_map/pack_first/pallas_call | solution.py:524
  7.0 2.7 %collective-permute-start = (bf16[2,320,512]{2,1,0:T(8,128)(2,1)}, bf16[2,320,512]{2,1,0:T(8,128)(2,1)}, u32[]{:S(2)}, u32[]{:S(2)}) collective-permute-start(bf16[2,320,512]{2,1,0:T(8,128)(2,1)} %get-tuple-element.27), channel_id=1, source_target_pairs={{0,8},{4,12},{8,0},{12,4},{1,9},{5,13},{9,1},{13,5},{2,10},{6,14},... | collective-permute-start | bytes 1966088 | tf_op jit(solution)/shard_map/ppermute | solution.py:462
  9.7 1.5 %collective-permute-start.1 = (bf16[2,192,512]{2,1,0:T(8,128)(2,1)}, bf16[2,192,512]{2,1,0:T(8,128)(2,1)}, u32[]{:S(2)}, u32[]{:S(2)}) collective-permute-start(bf16[2,192,512]{2,1,0:T(8,128)(2,1)} %get-tuple-element.28.near), channel_id=1, source_target_pairs={{16,0},{17,1},{18,2},{19,3},{0,16},{1,17},{2,18},{3,19},{20,4},{21... | collective-permute-start | bytes 1179656 | tf_op jit(solution)/shard_map/ppermute | solution.py:470
  11.2 0.0 collective-permute-start.5
  11.2 4.9 %own_products_0.1 = (bf16[1024,1024]{1,0:T(8,128)(2,1)}, bf16[512,1536]{1,0:T(8,128)(2,1)}, bf16[16,128]{1,0:T(8,128)(2,1)}) custom-call(s32[4]{0:T(128)} %seps.13, s32[4,4]{1,0:T(4,128)} %gamma.11, bf16[4,2,2,512,512]{4,3,2,1,0:T(8,128)(2,1)} %peram.3, bf16[4,1024,128]{2,1,0:T(8,128)(2,1)} %bitcast.4), custom_call_target="tpu_custom_call" | custom-call | flops 9999999827968 | bytes 10000000000 | tf_op jit(solution)/shard_map/own_products_0/pallas_call | solution.py:545
  16.1 0.0 collective-permute-done.5.tick
  16.1 0.0 copy-start.2
  16.1 0.0 copy-start.5
  16.1 0.0 copy-start.7
  16.1 3.0 %pack.1 = (bf16[2048,128]{1,0:T(8,128)(2,1)}, bf16[2080,128]{1,0:T(8,128)(2,1)}) custom-call(s32[4]{0:T(128)} %seps.13, s32[1]{0:T(128)S(6)} %copy.18.partner, bf16[4,1024,128]{2,1,0:T(8,128)(2,1)} %bitcast.5, bf16[16,128]{1,0:T(8,128)(2,1)} %collective-permute-done.5.tick, bf16[16,128]{1,0:T(8,128)(2,1)} %get-tuple-element.30.after), custom_call_target="tpu_custom_call" | custom-call | flops 9999999827968 | bytes 10000000000 | tf_op jit(solution)/shard_map/pack/pallas_call | solution.py:555
  19.1 0.6 collective-permute-start.7
  19.7 0.0 collective-permute-done.2.source.core
  19.7 1.4 %collective-permute-start.8 = (bf16[2080,128]{1,0:T(8,128)(2,1)}, bf16[2080,128]{1,0:T(8,128)(2,1)}, u32[]{:S(2)}, u32[]{:S(2)}) collective-permute-start(bf16[2080,128]{1,0:T(8,128)(2,1)} %get-tuple-element.43), channel_id=1, source_target_pairs={{18,0},{19,1},{16,2},{17,3},{2,16},{3,17},{0,18},{1,19},{22,4},{23... | collective-permute-start | bytes 1597448 | tf_op jit(solution)/shard_map/ppermute | solution.py:470
  21.2 0.0 copy-done.2
  21.2 0.0 copy-done.5
  21.2 3.3 %own_products_1.1 = (bf16[512,1536]{1,0:T(8,128)(2,1)S(1)}, bf16[16,128]{1,0:T(8,128)(2,1)S(1)}) custom-call(s32[4,4]{1,0:T(4,128)S(1)} %copy-done.2, bf16[4,1024,128]{2,1,0:T(8,128)(2,1)} %collective-permute-done.2.source.core, bf16[1024,1024]{1,0:T(8,128)(2,1)S(1)} %copy-done.5, bf16[16,128]{1,0:T(8,128)(2,1)S(1)} %copy-done.7), custom_call_target="tpu_custom_call" | custom-call | flops 9999999827968 | bytes 10000000000 | tf_op jit(solution)/shard_map/own_products_1/pallas_call | solution.py:569
  24.4 2.7 %collective-permute-done.3.array = bf16[4,1024,128]{2,1,0:T(8,128)(2,1)} collective-permute-done((bf16[4,1024,128]{2,1,0:T(8,128)(2,1)}, bf16[4,1024,128]{2,1,0:T(8,128)(2,1)}, u32[]{:S(2)}, u32[]{:S(2)}) %collective-permute-start.3) | collective-permute-done | bytes 1048608 | tf_op jit(solution)/shard_map/ppermute | solution.py:458
  27.1 0.6 gate_near.1
  27.7 3.2 %own_products_2.1 = (bf16[512,1536]{1,0:T(8,128)(2,1)S(1)}, bf16[16,128]{1,0:T(8,128)(2,1)S(1)}) custom-call(s32[4,4]{1,0:T(4,128)S(1)} %copy-done.2, bf16[4,1024,128]{2,1,0:T(8,128)(2,1)} %get-tuple-element.32.source.near, bf16[1024,1024]{1,0:T(8,128)(2,1)S(1)} %copy-done.5, bf16[16,128]{1,0:T(8,128)(2,1)S(1)} %get-tuple-element.31.after), custom_call_target="tpu_custom_call" | custom-call | flops 9999999827968 | bytes 10000000000 | tf_op jit(solution)/shard_map/own_products_2/pallas_call | solution.py:569
  31.0 0.1 collective-permute-start.6
  31.0 0.0 collective-permute-done.1.far
  31.1 2.3 %choose.1.rest = bf16[2,192,512]{2,1,0:T(8,128)(2,1)} custom-call(s32[4]{0:T(128)S(1)} %copy-done.3, bf16[2,192,512]{2,1,0:T(8,128)(2,1)S(1)} %copy-done.1, bf16[2,192,512]{2,1,0:T(8,128)(2,1)} %collective-permute-done.1.far, bf16[16,128]{1,0:T(8,128)(2,1)S(1)} %get-tuple-element.31.after), custom_call_target="tpu_custom_call" | custom-call | flops 9999999827968 | bytes 10000000000 | tf_op jit(solution)/shard_map/choose/pallas_call | solution.py:593
  33.4 5.8 %collective-permute-done.first = bf16[2,320,512]{2,1,0:T(8,128)(2,1)} collective-permute-done((bf16[2,320,512]{2,1,0:T(8,128)(2,1)}, bf16[2,320,512]{2,1,0:T(8,128)(2,1)}, u32[]{:S(2)}, u32[]{:S(2)}) %collective-permute-start) | collective-permute-done | bytes 655392 | tf_op jit(solution)/shard_map/ppermute | solution.py:462
  39.2 0.0 collective-permute-start.4
  39.2 1.5 %collective-permute-start.11 = (bf16[2,320,512]{2,1,0:T(8,128)(2,1)}, bf16[2,320,512]{2,1,0:T(8,128)(2,1)}, u32[]{:S(2)}, u32[]{:S(2)}) collective-permute-start(bf16[2,320,512]{2,1,0:T(8,128)(2,1)} %get-tuple-element.48.near), channel_id=1, source_target_pairs={{16,0},{17,1},{18,2},{19,3},{0,16},{1,17},{2,18},{3,19},{20,4},{21... | collective-permute-start | bytes 1966088 | tf_op jit(solution)/shard_map/ppermute | solution.py:470
  40.7 0.0 collective-permute-done.6.source.near
  40.7 3.3 %own_products_3.1 = (bf16[512,1536]{1,0:T(8,128)(2,1)S(1)}, bf16[16,128]{1,0:T(8,128)(2,1)S(1)}) custom-call(s32[4,4]{1,0:T(4,128)S(1)} %copy-done.2, bf16[4,1024,128]{2,1,0:T(8,128)(2,1)} %collective-permute-done.6.source.near, bf16[1024,1024]{1,0:T(8,128)(2,1)S(1)} %copy-done.5, bf16[16,128]{1,0:T(8,128)(2,1)S(1)} %get-tuple-element.39.after), custom_call_target="tpu_custom_call" | custom-call | flops 9999999827968 | bytes 10000000000 | tf_op jit(solution)/shard_map/own_products_3/pallas_call | solution.py:569
  44.0 0.0 collective-permute-done.7.same
  44.0 1.6 %collective-permute-done.8.cross = bf16[2080,128]{1,0:T(8,128)(2,1)} collective-permute-done((bf16[2080,128]{1,0:T(8,128)(2,1)}, bf16[2080,128]{1,0:T(8,128)(2,1)}, u32[]{:S(2)}, u32[]{:S(2)}) %collective-permute-start.8) | collective-permute-done | bytes 532512 | tf_op jit(solution)/shard_map/ppermute | solution.py:470
  45.6 0.6 gate_far.1
  46.2 0.0 collective-permute-start.9
  46.2 0.5 collective-permute-start.10
  46.7 0.1 copy-done
  46.8 0.0 copy-done.4
  46.8 0.5 copy-done.6
  47.3 5.3 %other_products_02.1 = (f32[2,1024,512]{2,1,0:T(8,128)S(1)}, s32[8]{0:T(128)S(1)}) custom-call(s32[4]{0:T(128)S(1)} %copy-done.4, s32[4,4]{1,0:T(4,128)S(1)} %copy-done.2, s32[1]{0:T(128)S(6)} %copy.18.partner, bf16[16,128]{1,0:T(8,128)(2,1)} %collective-permute-done.5.tick, bf16[512,1536]{1,0:T(8,128)(2,1)S(1)} %copy-done.6, ...), custom_call_target="tpu_custom_call" | custom-call | flops 9999999827968 | bytes 10000000000 | tf_op jit(solution)/shard_map/other_products_02/pallas_call | solution.py:639
  52.6 0.0 collective-permute-done.9.same
  52.6 0.0 collective-permute-done.10.cross
  52.6 4.9 %other_products_13.1.kb = f32[2,1024,512]{2,1,0:T(8,128)S(1)} custom-call(s32[4]{0:T(128)S(1)} %copy-done.4, s32[4,4]{1,0:T(4,128)S(1)} %copy-done.2, s32[8]{0:T(128)S(1)} %get-tuple-element.46.label, bf16[512,1536]{1,0:T(8,128)(2,1)S(1)} %copy-done.6, bf16[512,1536]{1,0:T(8,128)(2,1)S(1)} %get-tuple-element.37.h1, ...), custom_call_target="tpu_custom_call" | custom-call | flops 9999999827968 | bytes 10000000000 | tf_op jit(solution)/shard_map/other_products_13/pallas_call | solution.py:650
  57.6 1.7 %collective-permute-done.4.rest = bf16[2,192,512]{2,1,0:T(8,128)(2,1)} collective-permute-done((bf16[2,192,512]{2,1,0:T(8,128)(2,1)}, bf16[2,192,512]{2,1,0:T(8,128)(2,1)}, u32[]{:S(2)}, u32[]{:S(2)}) %collective-permute-start.4) | collective-permute-done | bytes 393248 | tf_op jit(solution)/shard_map/ppermute | solution.py:462
  59.3 0.0 collective-permute-done.11.far
  59.3 3.1 %traces.1 = f32[32,1,128]{2,1,0:T(1,128)S(1)} custom-call(bf16[2,192,512]{2,1,0:T(8,128)(2,1)} %collective-permute-done.4.rest, s32[4]{0:T(128)S(1)} %copy-done.4, s32[8]{0:T(128)S(1)} %get-tuple-element.46.label, f32[2,1024,512]{2,1,0:T(8,128)S(1)} %get-tuple-element.47.ka, f32[2,1024,512]{2,1,0:T(8,128)S(1)} %other_products_13.1.kb, ...), custom_call_target="tpu_custom_call" | custom-call | flops 9999999827968 | bytes 10000000000 | tf_op jit(solution)/shard_map/traces/pallas_call | solution.py:663
  62.4 9.4 %all_to_all.5 = f32[32,1,128]{2,1,0:T(1,128)S(1)} all-to-all(f32[32,1,128]{2,1,0:T(1,128)S(1)} %traces.1), channel_id=1, replica_groups=mesh['src'=2,'snk'=4,'mom'=4] {'src','snk','mom'}, dimensions={0} | all-to-all | bytes 32768 | tf_op jit(solution)/shard_map/all_to_all | solution.py:672
  71.8 0.1 reduce_sum.11
  71.8 0.1 reshape.11
  72.0 0.7 copy.12
  (10 shorter events, 0.0 us)
Async XLA Ops:
  0.0 19.7 %collective-permute-start.2 = (bf16[4,1024,128]{2,1,0:T(8,128)(2,1)}, bf16[4,1024,128]{2,1,0:T(8,128)(2,1)}, u32[]{:S(2)}, u32[]{:S(2)}) collective-permute-start(bf16[4,1024,128]{2,1,0:T(8,128)(2,1)} %bitcast.2), channel_id=1, source_target_pairs={{0,1},{1,0},{2,3},{3,2},{4,5},{5,4},{6,7},{7,6},{8,9},{9,8},{10,11... | collective-permute-start | bytes 3145736 | tf_op jit(solution)/shard_map/ppermute | solution.py:458
  0.5 26.7 %collective-permute-start.3 = (bf16[4,1024,128]{2,1,0:T(8,128)(2,1)}, bf16[4,1024,128]{2,1,0:T(8,128)(2,1)}, u32[]{:S(2)}, u32[]{:S(2)}) collective-permute-start(bf16[4,1024,128]{2,1,0:T(8,128)(2,1)} %bitcast.3), channel_id=1, source_target_pairs={{0,2},{1,3},{2,0},{3,1},{4,6},{5,7},{6,4},{7,5},{8,10},{9,11},{10,... | collective-permute-start | bytes 3145736 | tf_op jit(solution)/shard_map/ppermute | solution.py:458
  7.0 32.2 %collective-permute-start = (bf16[2,320,512]{2,1,0:T(8,128)(2,1)}, bf16[2,320,512]{2,1,0:T(8,128)(2,1)}, u32[]{:S(2)}, u32[]{:S(2)}) collective-permute-start(bf16[2,320,512]{2,1,0:T(8,128)(2,1)} %get-tuple-element.27), channel_id=1, source_target_pairs={{0,8},{4,12},{8,0},{12,4},{1,9},{5,13},{9,1},{13,5},{2,10},{6,14},... | collective-permute-start | bytes 1966088 | tf_op jit(solution)/shard_map/ppermute | solution.py:462
  9.7 21.4 %collective-permute-start.1 = (bf16[2,192,512]{2,1,0:T(8,128)(2,1)}, bf16[2,192,512]{2,1,0:T(8,128)(2,1)}, u32[]{:S(2)}, u32[]{:S(2)}) collective-permute-start(bf16[2,192,512]{2,1,0:T(8,128)(2,1)} %get-tuple-element.28.near), channel_id=1, source_target_pairs={{16,0},{17,1},{18,2},{19,3},{0,16},{1,17},{2,18},{3,19},{20,4},{21... | collective-permute-start | bytes 1179656 | tf_op jit(solution)/shard_map/ppermute | solution.py:470
  11.2 4.9 %collective-permute-start.5 = (bf16[16,128]{1,0:T(8,128)(2,1)}, bf16[16,128]{1,0:T(8,128)(2,1)}, u32[]{:S(2)}, u32[]{:S(2)}) collective-permute-start(bf16[16,128]{1,0:T(8,128)(2,1)} %get-tuple-element.35), channel_id=1, source_target_pairs={{0,1},{1,0},{2,3},{3,2},{4,5},{5,4},{6,7},{7,6},{8,9},{9,8},{10,11... | collective-permute-start | bytes 12296 | tf_op jit(solution)/shard_map/ppermute | solution.py:458
  16.1 5.1 %copy-start.2 = (s32[4,4]{1,0:T(4,128)S(1)}, s32[4,4]{1,0:T(4,128)}, u32[]{:S(2)}) copy-start(s32[4,4]{1,0:T(4,128)} %gamma.11) | copy-start | bytes 196
  16.1 5.1 %copy-start.5 = (bf16[1024,1024]{1,0:T(8,128)(2,1)S(1)}, bf16[1024,1024]{1,0:T(8,128)(2,1)}, u32[]{:S(2)}) copy-start(bf16[1024,1024]{1,0:T(8,128)(2,1)} %get-tuple-element.29.y_ref) | copy-start | bytes 6291460
  16.1 5.1 %copy-start.7 = (bf16[16,128]{1,0:T(8,128)(2,1)S(1)}, bf16[16,128]{1,0:T(8,128)(2,1)}, u32[]{:S(2)}) copy-start(bf16[16,128]{1,0:T(8,128)(2,1)} %get-tuple-element.30.after) | copy-start | bytes 12292
  19.1 24.8 %collective-permute-start.7 = (bf16[2048,128]{1,0:T(8,128)(2,1)}, bf16[2048,128]{1,0:T(8,128)(2,1)}, u32[]{:S(2)}, u32[]{:S(2)}) collective-permute-start(bf16[2048,128]{1,0:T(8,128)(2,1)} %get-tuple-element.42), channel_id=1, source_target_pairs={{16,0},{17,1},{18,2},{19,3},{0,16},{1,17},{2,18},{3,19},{20,4},{21... | collective-permute-start | bytes 1572872 | tf_op jit(solution)/shard_map/ppermute | solution.py:470
  19.7 25.9 %collective-permute-start.8 = (bf16[2080,128]{1,0:T(8,128)(2,1)}, bf16[2080,128]{1,0:T(8,128)(2,1)}, u32[]{:S(2)}, u32[]{:S(2)}) collective-permute-start(bf16[2080,128]{1,0:T(8,128)(2,1)} %get-tuple-element.43), channel_id=1, source_target_pairs={{18,0},{19,1},{16,2},{17,3},{2,16},{3,17},{0,18},{1,19},{22,4},{23... | collective-permute-start | bytes 1597448 | tf_op jit(solution)/shard_map/ppermute | solution.py:470
  27.7 3.4 %copy-start.1 = (bf16[2,192,512]{2,1,0:T(8,128)(2,1)S(1)}, bf16[2,192,512]{2,1,0:T(8,128)(2,1)}, u32[]{:S(2)}) copy-start(bf16[2,192,512]{2,1,0:T(8,128)(2,1)} %get-tuple-element.28.near) | copy-start | bytes 1179652
  27.7 3.4 %copy-start.3 = (s32[4]{0:T(128)S(1)}, s32[4]{0:T(128)}, u32[]{:S(2)}) copy-start(s32[4]{0:T(128)} %seps.13) | copy-start | bytes 52
  31.0 9.7 %collective-permute-start.6 = (bf16[4,1024,128]{2,1,0:T(8,128)(2,1)}, bf16[4,1024,128]{2,1,0:T(8,128)(2,1)}, u32[]{:S(2)}, u32[]{:S(2)}) collective-permute-start(bf16[4,1024,128]{2,1,0:T(8,128)(2,1)} %get-tuple-element.32.source.near), channel_id=1, source_target_pairs={{0,1},{1,0},{2,3},{3,2},{4,5},{5,4},{6,7},{7,6},{8,9},{9,8},{10,11... | collective-permute-start | bytes 3145736 | tf_op jit(solution)/shard_map/ppermute | solution.py:458
  39.2 20.1 %collective-permute-start.4 = (bf16[2,192,512]{2,1,0:T(8,128)(2,1)}, bf16[2,192,512]{2,1,0:T(8,128)(2,1)}, u32[]{:S(2)}, u32[]{:S(2)}) collective-permute-start(bf16[2,192,512]{2,1,0:T(8,128)(2,1)} %get-tuple-element.34), channel_id=1, source_target_pairs={{0,8},{4,12},{8,0},{12,4},{1,9},{5,13},{9,1},{13,5},{2,10},{6,14},... | collective-permute-start | bytes 1179656 | tf_op jit(solution)/shard_map/ppermute | solution.py:462
  39.2 20.1 %collective-permute-start.11 = (bf16[2,320,512]{2,1,0:T(8,128)(2,1)}, bf16[2,320,512]{2,1,0:T(8,128)(2,1)}, u32[]{:S(2)}, u32[]{:S(2)}) collective-permute-start(bf16[2,320,512]{2,1,0:T(8,128)(2,1)} %get-tuple-element.48.near), channel_id=1, source_target_pairs={{16,0},{17,1},{18,2},{19,3},{0,16},{1,17},{2,18},{3,19},{20,4},{21... | collective-permute-start | bytes 1966088 | tf_op jit(solution)/shard_map/ppermute | solution.py:470
  45.6 1.2 %copy-start = (bf16[4,1,4,2,128,128]{5,4,3,2,1,0:T(8,128)(2,1)S(1)}, bf16[4,1,4,2,128,128]{5,4,3,2,1,0:T(8,128)(2,1)}, u32[]{:S(2)}) copy-start(bf16[4,1,4,2,128,128]{5,4,3,2,1,0:T(8,128)(2,1)} %param.6) | copy-start | bytes 3145732
  45.6 1.2 %copy-start.4 = (s32[4]{0:T(128)S(1)}, s32[4]{0:T(128)}, u32[]{:S(2)}) copy-start(s32[4]{0:T(128)} %seps.13) | copy-start | bytes 52
  45.6 1.7 %copy-start.6 = (bf16[512,1536]{1,0:T(8,128)(2,1)S(1)}, bf16[512,1536]{1,0:T(8,128)(2,1)}, u32[]{:S(2)}) copy-start(bf16[512,1536]{1,0:T(8,128)(2,1)} %get-tuple-element.36.h0) | copy-start | bytes 4718596
  46.2 6.4 %collective-permute-start.9 = (bf16[2048,128]{1,0:T(8,128)(2,1)}, bf16[2048,128]{1,0:T(8,128)(2,1)}, u32[]{:S(2)}, u32[]{:S(2)}) collective-permute-start(bf16[2048,128]{1,0:T(8,128)(2,1)} %get-tuple-element.44.same), channel_id=1, source_target_pairs={{0,1},{1,0},{2,3},{3,2},{4,5},{5,4},{6,7},{7,6},{8,9},{9,8},{10,11... | collective-permute-start | bytes 1572872 | tf_op jit(solution)/shard_map/ppermute | solution.py:458
  46.2 6.4 %collective-permute-start.10 = (bf16[2080,128]{1,0:T(8,128)(2,1)}, bf16[2080,128]{1,0:T(8,128)(2,1)}, u32[]{:S(2)}, u32[]{:S(2)}) collective-permute-start(bf16[2080,128]{1,0:T(8,128)(2,1)} %get-tuple-element.45.cross), channel_id=1, source_target_pairs={{0,1},{1,0},{2,3},{3,2},{4,5},{5,4},{6,7},{7,6},{8,9},{9,8},{10,11... | collective-permute-start | bytes 1597448 | tf_op jit(solution)/shard_map/ppermute | solution.py:458

commit v13 on v12

--- a/solution.py
+++ b/solution.py
@@ -377,7 +377,7 @@
     return lax.fori_loop(0, source.shape[1] // rows, step, totals)
 
 
-def trace_kernel(sizes, sep_count, rest, seps, label, ka, kb, near, far, out_ref, first_buf, rest_buf, sems):
+def trace_kernel(sizes, rest, seps, label, ka, kb, near, far, out_ref, first_buf, rest_buf, sems):
     plan = Plan(seps, sizes)
     count = 2 * ka.shape[0]
     width = rest_buf.shape[-1]
@@ -407,10 +407,11 @@
     shape = out_ref.shape[1:]
     spot = lax.broadcasted_iota(jnp.int32, shape, 0) * shape[1]
     spot = spot + lax.broadcasted_iota(jnp.int32, shape, 1)
-    here = spot // 2 == plan.pair_time * sep_count + plan.sep_index
+    row = lax.div(spot, plan.time_count)
+    here = (row // 2 == plan.sep_index) & (lax.rem(spot, plan.time_count) == plan.pair_time)
     if plan.live is not None:
         here = here & plan.live
-    values = [jnp.where(spot % 2 == 0, sums[2 * p], sums[2 * p + 1]) for p in range(count)]
+    values = [jnp.where(row % 2 == 0, sums[2 * p], sums[2 * p + 1]) for p in range(count)]
     lines = []
     for op in range(count):
         line = jnp.zeros(shape, jnp.float32)
@@ -661,7 +662,7 @@
     values = time_count * sep_count * 2
     lines = (values + 127) // 128
     out = call(
-        part(trace_kernel, sizes, sep_count),
+        part(trace_kernel, sizes),
         "traces",
         [hbm()] + [smem()] * 2 + [vmem()] * 2 + [hbm()] * 2,
         vmem(),
@@ -671,7 +672,7 @@
     )(rest, separations, label, ka, kb, first_near, first_far)
     out = lax.all_to_all(out, ("src", "snk", "mom"), split_axis=0, concat_axis=0, tiled=True)
     out = jnp.sum(out, axis=0).reshape(lines * 128)[:values]
-    return out.reshape(time_count, sep_count, 1, 2)
+    return out.reshape(sep_count, 1, 2, time_count).transpose(3, 0, 1, 2)
 
 
 def solution(mesh):

time: 73.2 us -> 73 us (level)
  waiting for transfers between devices: 11.9 us -> 12.7 us
  Pallas kernels: 37.8 us -> 37 us
    ppermute x2, waiting for transfers between devices: 7.51 us -> 8.32 us  [swap_snk(): return lax.ppermute(array, 'snk', pairs)]
    pallas_call x1, Pallas kernels: 2.32 us -> 1.51 us  [shards(): call(part(choose, sizes), 'choose', [smem()] + [hbm()] * 2 + [vmem()], vm...]
  transfers between devices with their start and end apart: 12 -> 12, of which waited for: 4 -> 4; matrix products, arithmetic and copies ran while one was open for 0% -> 0% of each run, Pallas kernels for 48% -> 47%
where the time goes in v13:
time: 73 us; the launch traced here: 72.5 us
  Pallas kernels  37 us (51%)
  waiting for transfers between devices  12.7 us (17%)
  starting transfers between devices  11.2 us (15%)
  blocking collectives  9.41 us (13%)
  local copies, waits for them, and re-layouts  1.37 us (2%)
  between operations  0.84 us (1%)
    pallas_call x3, Pallas kernels, own_one(): call(part(own_kernel, number), 'own_products_%d' % number, [smem(), hbm()...  9.75 us
    all_to_all x1, blocking collectives, shards(): lax.all_to_all(out, ('src', 'snk', 'mom'), split_axis=0, concat_axis=0, t...  9.41 us
    ppermute x2, waiting for transfers between devices, swap_snk(): return lax.ppermute(array, 'snk', pairs)  8.32 us
    pallas_call x1, Pallas kernels, shards(): call(part(other_kernel_02, sizes), 'other_products_02', [smem()] * 3 + [v...  5.26 us
    ppermute x4, starting transfers between devices, next_src(): return lax.ppermute(array, ('src', 'mom'), pairs)  5.02 us
    pallas_call x1, Pallas kernels, shards(): call(part(other_kernel_13, sizes), 'other_products_13', [smem()] * 3 + [h...  4.93 us
    pallas_call x1, Pallas kernels, shards(): call(part(own_kernel_0, sizes), 'own_products_0', [smem()] * 2 + [hbm()]...  4.9 us
    ppermute x6, starting transfers between devices, swap_mom(): return lax.ppermute(array, 'mom', [(a, a ^ i) for a in range(mom_count)])  3.55 us
  transfers between devices with their start and end apart: 12, of which 4 were waited for; matrix products, arithmetic and copies ran while one was open for 0% of the time, Pallas kernels for 47%

profile of v13, /device:TPU:0, one launch (start us, length us, event | category | flops | bytes accessed | tf_op | source)
XLA Modules:
  0.0 72.5 jit_solution(10962982768329215206)
XLA Ops:
  0.0 0.5 collective-permute-start.2
  0.5 2.5 %collective-permute-start.3 = (bf16[4,1024,128]{2,1,0:T(8,128)(2,1)}, bf16[4,1024,128]{2,1,0:T(8,128)(2,1)}, u32[]{:S(2)}, u32[]{:S(2)}) collective-permute-start(bf16[4,1024,128]{2,1,0:T(8,128)(2,1)} %bitcast.6), channel_id=1, source_target_pairs={{0,2},{1,3},{2,0},{3,1},{4,6},{5,7},{6,4},{7,5},{8,10},{9,11},{10,... | collective-permute-start | bytes 3145736 | tf_op jit(solution)/shard_map/ppermute | solution.py:459
  3.6 3.4 %pack_first.1 = (bf16[2,320,512]{2,1,0:T(8,128)(2,1)}, bf16[2,192,512]{2,1,0:T(8,128)(2,1)}, bf16[16,128]{1,0:T(8,128)(2,1)}) custom-call(s32[4]{0:T(128)} %seps.13, s32[1]{0:T(128)S(6)} %copy.17.partner, bf16[4,2,2,512,512]{4,3,2,1,0:T(8,128)(2,1)} %peram.3), custom_call_target="tpu_custom_call" | custom-call | flops 9999999827968 | bytes 10000000000 | tf_op jit(solution)/shard_map/pack_first/pallas_call | solution.py:525
  7.0 2.7 %collective-permute-start = (bf16[2,320,512]{2,1,0:T(8,128)(2,1)}, bf16[2,320,512]{2,1,0:T(8,128)(2,1)}, u32[]{:S(2)}, u32[]{:S(2)}) collective-permute-start(bf16[2,320,512]{2,1,0:T(8,128)(2,1)} %get-tuple-element.27), channel_id=1, source_target_pairs={{0,8},{4,12},{8,0},{12,4},{1,9},{5,13},{9,1},{13,5},{2,10},{6,14},... | collective-permute-start | bytes 1966088 | tf_op jit(solution)/shard_map/ppermute | solution.py:463
  9.7 1.5 %collective-permute-start.1 = (bf16[2,192,512]{2,1,0:T(8,128)(2,1)}, bf16[2,192,512]{2,1,0:T(8,128)(2,1)}, u32[]{:S(2)}, u32[]{:S(2)}) collective-permute-start(bf16[2,192,512]{2,1,0:T(8,128)(2,1)} %get-tuple-element.28.near), channel_id=1, source_target_pairs={{16,0},{17,1},{18,2},{19,3},{0,16},{1,17},{2,18},{3,19},{20,4},{21... | collective-permute-start | bytes 1179656 | tf_op jit(solution)/shard_map/ppermute | solution.py:471
  11.2 0.0 collective-permute-start.5
  11.2 4.9 %own_products_0.1 = (bf16[1024,1024]{1,0:T(8,128)(2,1)}, bf16[512,1536]{1,0:T(8,128)(2,1)}, bf16[16,128]{1,0:T(8,128)(2,1)}) custom-call(s32[4]{0:T(128)} %seps.13, s32[4,4]{1,0:T(4,128)} %gamma.11, bf16[4,2,2,512,512]{4,3,2,1,0:T(8,128)(2,1)} %peram.3, bf16[4,1024,128]{2,1,0:T(8,128)(2,1)} %bitcast.7), custom_call_target="tpu_custom_call" | custom-call | flops 9999999827968 | bytes 10000000000 | tf_op jit(solution)/shard_map/own_products_0/pallas_call | solution.py:546
  16.1 0.0 collective-permute-done.5.tick
  16.1 0.0 copy-start.2
  16.1 0.0 copy-start.5
  16.1 0.0 copy-start.7
  16.1 3.0 %pack.1 = (bf16[2048,128]{1,0:T(8,128)(2,1)}, bf16[2080,128]{1,0:T(8,128)(2,1)}) custom-call(s32[4]{0:T(128)} %seps.13, s32[1]{0:T(128)S(6)} %copy.17.partner, bf16[4,1024,128]{2,1,0:T(8,128)(2,1)} %bitcast.8, bf16[16,128]{1,0:T(8,128)(2,1)} %collective-permute-done.5.tick, bf16[16,128]{1,0:T(8,128)(2,1)} %get-tuple-element.30.after), custom_call_target="tpu_custom_call" | custom-call | flops 9999999827968 | bytes 10000000000 | tf_op jit(solution)/shard_map/pack/pallas_call | solution.py:556
  19.1 0.6 collective-permute-start.7
  19.7 0.0 collective-permute-done.2.source.core
  19.7 1.4 %collective-permute-start.8 = (bf16[2080,128]{1,0:T(8,128)(2,1)}, bf16[2080,128]{1,0:T(8,128)(2,1)}, u32[]{:S(2)}, u32[]{:S(2)}) collective-permute-start(bf16[2080,128]{1,0:T(8,128)(2,1)} %get-tuple-element.43), channel_id=1, source_target_pairs={{18,0},{19,1},{16,2},{17,3},{2,16},{3,17},{0,18},{1,19},{22,4},{23... | collective-permute-start | bytes 1597448 | tf_op jit(solution)/shard_map/ppermute | solution.py:471
  21.2 0.0 copy-done.2
  21.2 0.0 copy-done.5
  21.2 0.0 copy-done.7
  21.2 3.3 %own_products_1.1 = (bf16[512,1536]{1,0:T(8,128)(2,1)S(1)}, bf16[16,128]{1,0:T(8,128)(2,1)S(1)}) custom-call(s32[4,4]{1,0:T(4,128)S(1)} %copy-done.2, bf16[4,1024,128]{2,1,0:T(8,128)(2,1)} %collective-permute-done.2.source.core, bf16[1024,1024]{1,0:T(8,128)(2,1)S(1)} %copy-done.5, bf16[16,128]{1,0:T(8,128)(2,1)S(1)} %copy-done.7), custom_call_target="tpu_custom_call" | custom-call | flops 9999999827968 | bytes 10000000000 | tf_op jit(solution)/shard_map/own_products_1/pallas_call | solution.py:570
  24.4 2.7 %collective-permute-done.3.array = bf16[4,1024,128]{2,1,0:T(8,128)(2,1)} collective-permute-done((bf16[4,1024,128]{2,1,0:T(8,128)(2,1)}, bf16[4,1024,128]{2,1,0:T(8,128)(2,1)}, u32[]{:S(2)}, u32[]{:S(2)}) %collective-permute-start.3) | collective-permute-done | bytes 1048608 | tf_op jit(solution)/shard_map/ppermute | solution.py:459
  27.1 0.6 gate_near.1
  27.7 3.2 %own_products_2.1 = (bf16[512,1536]{1,0:T(8,128)(2,1)S(1)}, bf16[16,128]{1,0:T(8,128)(2,1)S(1)}) custom-call(s32[4,4]{1,0:T(4,128)S(1)} %copy-done.2, bf16[4,1024,128]{2,1,0:T(8,128)(2,1)} %get-tuple-element.32.source.near, bf16[1024,1024]{1,0:T(8,128)(2,1)S(1)} %copy-done.5, bf16[16,128]{1,0:T(8,128)(2,1)S(1)} %get-tuple-element.31.after), custom_call_target="tpu_custom_call" | custom-call | flops 9999999827968 | bytes 10000000000 | tf_op jit(solution)/shard_map/own_products_2/pallas_call | solution.py:570
  31.0 0.1 collective-permute-start.6
  31.0 0.0 collective-permute-done.1.far
  31.1 1.5 %choose.1.rest = bf16[2,192,512]{2,1,0:T(8,128)(2,1)} custom-call(s32[4]{0:T(128)S(1)} %copy-done.3, bf16[2,192,512]{2,1,0:T(8,128)(2,1)S(1)} %copy-done.1, bf16[2,192,512]{2,1,0:T(8,128)(2,1)} %collective-permute-done.1.far, bf16[16,128]{1,0:T(8,128)(2,1)S(1)} %get-tuple-element.31.after), custom_call_target="tpu_custom_call" | custom-call | flops 9999999827968 | bytes 10000000000 | tf_op jit(solution)/shard_map/choose/pallas_call | solution.py:594
  32.6 6.6 %collective-permute-done.first = bf16[2,320,512]{2,1,0:T(8,128)(2,1)} collective-permute-done((bf16[2,320,512]{2,1,0:T(8,128)(2,1)}, bf16[2,320,512]{2,1,0:T(8,128)(2,1)}, u32[]{:S(2)}, u32[]{:S(2)}) %collective-permute-start) | collective-permute-done | bytes 655392 | tf_op jit(solution)/shard_map/ppermute | solution.py:463
  39.2 0.0 collective-permute-start.4
  39.2 1.5 %collective-permute-start.11 = (bf16[2,320,512]{2,1,0:T(8,128)(2,1)}, bf16[2,320,512]{2,1,0:T(8,128)(2,1)}, u32[]{:S(2)}, u32[]{:S(2)}) collective-permute-start(bf16[2,320,512]{2,1,0:T(8,128)(2,1)} %get-tuple-element.48.near), channel_id=1, source_target_pairs={{16,0},{17,1},{18,2},{19,3},{0,16},{1,17},{2,18},{3,19},{20,4},{21... | collective-permute-start | bytes 1966088 | tf_op jit(solution)/shard_map/ppermute | solution.py:471
  40.7 0.0 collective-permute-done.6.source.near
  40.7 3.3 %own_products_3.1 = (bf16[512,1536]{1,0:T(8,128)(2,1)S(1)}, bf16[16,128]{1,0:T(8,128)(2,1)S(1)}) custom-call(s32[4,4]{1,0:T(4,128)S(1)} %copy-done.2, bf16[4,1024,128]{2,1,0:T(8,128)(2,1)} %collective-permute-done.6.source.near, bf16[1024,1024]{1,0:T(8,128)(2,1)S(1)} %copy-done.5, bf16[16,128]{1,0:T(8,128)(2,1)S(1)} %get-tuple-element.39.after), custom_call_target="tpu_custom_call" | custom-call | flops 9999999827968 | bytes 10000000000 | tf_op jit(solution)/shard_map/own_products_3/pallas_call | solution.py:570
  44.0 0.0 collective-permute-done.7.same
  44.0 1.6 %collective-permute-done.8.cross = bf16[2080,128]{1,0:T(8,128)(2,1)} collective-permute-done((bf16[2080,128]{1,0:T(8,128)(2,1)}, bf16[2080,128]{1,0:T(8,128)(2,1)}, u32[]{:S(2)}, u32[]{:S(2)}) %collective-permute-start.8) | collective-permute-done | bytes 532512 | tf_op jit(solution)/shard_map/ppermute | solution.py:471
  45.6 0.6 gate_far.1
  46.2 0.0 collective-permute-start.9
  46.2 0.5 collective-permute-start.10
  46.7 0.1 copy-done
  46.8 0.0 copy-done.4
  46.8 0.5 copy-done.6
  47.3 5.3 %other_products_02.1 = (f32[2,1024,512]{2,1,0:T(8,128)S(1)}, s32[8]{0:T(128)S(1)}) custom-call(s32[4]{0:T(128)S(1)} %copy-done.4, s32[4,4]{1,0:T(4,128)S(1)} %copy-done.2, s32[1]{0:T(128)S(6)} %copy.17.partner, bf16[16,128]{1,0:T(8,128)(2,1)} %collective-permute-done.5.tick, bf16[512,1536]{1,0:T(8,128)(2,1)S(1)} %copy-done.6, ...), custom_call_target="tpu_custom_call" | custom-call | flops 9999999827968 | bytes 10000000000 | tf_op jit(solution)/shard_map/other_products_02/pallas_call | solution.py:640
  52.6 0.0 collective-permute-done.9.same
  52.6 0.0 collective-permute-done.10.cross
  52.6 4.9 %other_products_13.1.kb = f32[2,1024,512]{2,1,0:T(8,128)S(1)} custom-call(s32[4]{0:T(128)S(1)} %copy-done.4, s32[4,4]{1,0:T(4,128)S(1)} %copy-done.2, s32[8]{0:T(128)S(1)} %get-tuple-element.46.label, bf16[512,1536]{1,0:T(8,128)(2,1)S(1)} %copy-done.6, bf16[512,1536]{1,0:T(8,128)(2,1)S(1)} %get-tuple-element.37.h1, ...), custom_call_target="tpu_custom_call" | custom-call | flops 9999999827968 | bytes 10000000000 | tf_op jit(solution)/shard_map/other_products_13/pallas_call | solution.py:651
  57.6 1.7 %collective-permute-done.4.rest = bf16[2,192,512]{2,1,0:T(8,128)(2,1)} collective-permute-done((bf16[2,192,512]{2,1,0:T(8,128)(2,1)}, bf16[2,192,512]{2,1,0:T(8,128)(2,1)}, u32[]{:S(2)}, u32[]{:S(2)}) %collective-permute-start.4) | collective-permute-done | bytes 393248 | tf_op jit(solution)/shard_map/ppermute | solution.py:463
  59.3 0.0 collective-permute-done.11.far
  59.3 3.1 %traces.1 = f32[32,1,128]{2,1,0:T(1,128)S(1)} custom-call(bf16[2,192,512]{2,1,0:T(8,128)(2,1)} %collective-permute-done.4.rest, s32[4]{0:T(128)S(1)} %copy-done.4, s32[8]{0:T(128)S(1)} %get-tuple-element.46.label, f32[2,1024,512]{2,1,0:T(8,128)S(1)} %get-tuple-element.47.ka, f32[2,1024,512]{2,1,0:T(8,128)S(1)} %other_products_13.1.kb, ...), custom_call_target="tpu_custom_call" | custom-call | flops 9999999827968 | bytes 10000000000 | tf_op jit(solution)/shard_map/traces/pallas_call | solution.py:664
  62.4 9.4 %all_to_all.5 = f32[32,1,128]{2,1,0:T(1,128)S(1)} all-to-all(f32[32,1,128]{2,1,0:T(1,128)S(1)} %traces.1), channel_id=1, replica_groups=mesh['src'=2,'snk'=4,'mom'=4] {'src','snk','mom'}, dimensions={0} | all-to-all | bytes 32768 | tf_op jit(solution)/shard_map/all_to_all | solution.py:673
  71.8 0.1 reduce_sum.11
  71.8 0.7 reshape.11
  (9 shorter events, 0.0 us)
Async XLA Ops:
  0.0 19.7 %collective-permute-start.2 = (bf16[4,1024,128]{2,1,0:T(8,128)(2,1)}, bf16[4,1024,128]{2,1,0:T(8,128)(2,1)}, u32[]{:S(2)}, u32[]{:S(2)}) collective-permute-start(bf16[4,1024,128]{2,1,0:T(8,128)(2,1)} %bitcast.5), channel_id=1, source_target_pairs={{0,1},{1,0},{2,3},{3,2},{4,5},{5,4},{6,7},{7,6},{8,9},{9,8},{10,11... | collective-permute-start | bytes 3145736 | tf_op jit(solution)/shard_map/ppermute | solution.py:459
  0.5 26.7 %collective-permute-start.3 = (bf16[4,1024,128]{2,1,0:T(8,128)(2,1)}, bf16[4,1024,128]{2,1,0:T(8,128)(2,1)}, u32[]{:S(2)}, u32[]{:S(2)}) collective-permute-start(bf16[4,1024,128]{2,1,0:T(8,128)(2,1)} %bitcast.6), channel_id=1, source_target_pairs={{0,2},{1,3},{2,0},{3,1},{4,6},{5,7},{6,4},{7,5},{8,10},{9,11},{10,... | collective-permute-start | bytes 3145736 | tf_op jit(solution)/shard_map/ppermute | solution.py:459
  7.0 32.2 %collective-permute-start = (bf16[2,320,512]{2,1,0:T(8,128)(2,1)}, bf16[2,320,512]{2,1,0:T(8,128)(2,1)}, u32[]{:S(2)}, u32[]{:S(2)}) collective-permute-start(bf16[2,320,512]{2,1,0:T(8,128)(2,1)} %get-tuple-element.27), channel_id=1, source_target_pairs={{0,8},{4,12},{8,0},{12,4},{1,9},{5,13},{9,1},{13,5},{2,10},{6,14},... | collective-permute-start | bytes 1966088 | tf_op jit(solution)/shard_map/ppermute | solution.py:463
  9.7 21.4 %collective-permute-start.1 = (bf16[2,192,512]{2,1,0:T(8,128)(2,1)}, bf16[2,192,512]{2,1,0:T(8,128)(2,1)}, u32[]{:S(2)}, u32[]{:S(2)}) collective-permute-start(bf16[2,192,512]{2,1,0:T(8,128)(2,1)} %get-tuple-element.28.near), channel_id=1, source_target_pairs={{16,0},{17,1},{18,2},{19,3},{0,16},{1,17},{2,18},{3,19},{20,4},{21... | collective-permute-start | bytes 1179656 | tf_op jit(solution)/shard_map/ppermute | solution.py:471
  11.2 4.9 %collective-permute-start.5 = (bf16[16,128]{1,0:T(8,128)(2,1)}, bf16[16,128]{1,0:T(8,128)(2,1)}, u32[]{:S(2)}, u32[]{:S(2)}) collective-permute-start(bf16[16,128]{1,0:T(8,128)(2,1)} %get-tuple-element.35), channel_id=1, source_target_pairs={{0,1},{1,0},{2,3},{3,2},{4,5},{5,4},{6,7},{7,6},{8,9},{9,8},{10,11... | collective-permute-start | bytes 12296 | tf_op jit(solution)/shard_map/ppermute | solution.py:459
  16.1 5.1 %copy-start.2 = (s32[4,4]{1,0:T(4,128)S(1)}, s32[4,4]{1,0:T(4,128)}, u32[]{:S(2)}) copy-start(s32[4,4]{1,0:T(4,128)} %gamma.11) | copy-start | bytes 196
  16.1 5.1 %copy-start.5 = (bf16[1024,1024]{1,0:T(8,128)(2,1)S(1)}, bf16[1024,1024]{1,0:T(8,128)(2,1)}, u32[]{:S(2)}) copy-start(bf16[1024,1024]{1,0:T(8,128)(2,1)} %get-tuple-element.29.y_ref) | copy-start | bytes 6291460
  16.1 5.1 %copy-start.7 = (bf16[16,128]{1,0:T(8,128)(2,1)S(1)}, bf16[16,128]{1,0:T(8,128)(2,1)}, u32[]{:S(2)}) copy-start(bf16[16,128]{1,0:T(8,128)(2,1)} %get-tuple-element.30.after) | copy-start | bytes 12292
  19.1 24.8 %collective-permute-start.7 = (bf16[2048,128]{1,0:T(8,128)(2,1)}, bf16[2048,128]{1,0:T(8,128)(2,1)}, u32[]{:S(2)}, u32[]{:S(2)}) collective-permute-start(bf16[2048,128]{1,0:T(8,128)(2,1)} %get-tuple-element.42), channel_id=1, source_target_pairs={{16,0},{17,1},{18,2},{19,3},{0,16},{1,17},{2,18},{3,19},{20,4},{21... | collective-permute-start | bytes 1572872 | tf_op jit(solution)/shard_map/ppermute | solution.py:471
  19.7 25.9 %collective-permute-start.8 = (bf16[2080,128]{1,0:T(8,128)(2,1)}, bf16[2080,128]{1,0:T(8,128)(2,1)}, u32[]{:S(2)}, u32[]{:S(2)}) collective-permute-start(bf16[2080,128]{1,0:T(8,128)(2,1)} %get-tuple-element.43), channel_id=1, source_target_pairs={{18,0},{19,1},{16,2},{17,3},{2,16},{3,17},{0,18},{1,19},{22,4},{23... | collective-permute-start | bytes 1597448 | tf_op jit(solution)/shard_map/ppermute | solution.py:471
  27.7 3.4 %copy-start.1 = (bf16[2,192,512]{2,1,0:T(8,128)(2,1)S(1)}, bf16[2,192,512]{2,1,0:T(8,128)(2,1)}, u32[]{:S(2)}) copy-start(bf16[2,192,512]{2,1,0:T(8,128)(2,1)} %get-tuple-element.28.near) | copy-start | bytes 1179652
  27.7 3.4 %copy-start.3 = (s32[4]{0:T(128)S(1)}, s32[4]{0:T(128)}, u32[]{:S(2)}) copy-start(s32[4]{0:T(128)} %seps.13) | copy-start | bytes 52
  31.0 9.7 %collective-permute-start.6 = (bf16[4,1024,128]{2,1,0:T(8,128)(2,1)}, bf16[4,1024,128]{2,1,0:T(8,128)(2,1)}, u32[]{:S(2)}, u32[]{:S(2)}) collective-permute-start(bf16[4,1024,128]{2,1,0:T(8,128)(2,1)} %get-tuple-element.32.source.near), channel_id=1, source_target_pairs={{0,1},{1,0},{2,3},{3,2},{4,5},{5,4},{6,7},{7,6},{8,9},{9,8},{10,11... | collective-permute-start | bytes 3145736 | tf_op jit(solution)/shard_map/ppermute | solution.py:459
  39.2 20.1 %collective-permute-start.4 = (bf16[2,192,512]{2,1,0:T(8,128)(2,1)}, bf16[2,192,512]{2,1,0:T(8,128)(2,1)}, u32[]{:S(2)}, u32[]{:S(2)}) collective-permute-start(bf16[2,192,512]{2,1,0:T(8,128)(2,1)} %get-tuple-element.34), channel_id=1, source_target_pairs={{0,8},{4,12},{8,0},{12,4},{1,9},{5,13},{9,1},{13,5},{2,10},{6,14},... | collective-permute-start | bytes 1179656 | tf_op jit(solution)/shard_map/ppermute | solution.py:463
  39.2 20.1 %collective-permute-start.11 = (bf16[2,320,512]{2,1,0:T(8,128)(2,1)}, bf16[2,320,512]{2,1,0:T(8,128)(2,1)}, u32[]{:S(2)}, u32[]{:S(2)}) collective-permute-start(bf16[2,320,512]{2,1,0:T(8,128)(2,1)} %get-tuple-element.48.near), channel_id=1, source_target_pairs={{16,0},{17,1},{18,2},{19,3},{0,16},{1,17},{2,18},{3,19},{20,4},{21... | collective-permute-start | bytes 1966088 | tf_op jit(solution)/shard_map/ppermute | solution.py:471
  45.6 1.2 %copy-start = (bf16[4,1,4,2,128,128]{5,4,3,2,1,0:T(8,128)(2,1)S(1)}, bf16[4,1,4,2,128,128]{5,4,3,2,1,0:T(8,128)(2,1)}, u32[]{:S(2)}) copy-start(bf16[4,1,4,2,128,128]{5,4,3,2,1,0:T(8,128)(2,1)} %param.6) | copy-start | bytes 3145732
  45.6 1.2 %copy-start.4 = (s32[4]{0:T(128)S(1)}, s32[4]{0:T(128)}, u32[]{:S(2)}) copy-start(s32[4]{0:T(128)} %seps.13) | copy-start | bytes 52
  45.6 1.7 %copy-start.6 = (bf16[512,1536]{1,0:T(8,128)(2,1)S(1)}, bf16[512,1536]{1,0:T(8,128)(2,1)}, u32[]{:S(2)}) copy-start(bf16[512,1536]{1,0:T(8,128)(2,1)} %get-tuple-element.36.h0) | copy-start | bytes 4718596
  46.2 6.4 %collective-permute-start.9 = (bf16[2048,128]{1,0:T(8,128)(2,1)}, bf16[2048,128]{1,0:T(8,128)(2,1)}, u32[]{:S(2)}, u32[]{:S(2)}) collective-permute-start(bf16[2048,128]{1,0:T(8,128)(2,1)} %get-tuple-element.44.same), channel_id=1, source_target_pairs={{0,1},{1,0},{2,3},{3,2},{4,5},{5,4},{6,7},{7,6},{8,9},{9,8},{10,11... | collective-permute-start | bytes 1572872 | tf_op jit(solution)/shard_map/ppermute | solution.py:459
  46.2 6.4 %collective-permute-start.10 = (bf16[2080,128]{1,0:T(8,128)(2,1)}, bf16[2080,128]{1,0:T(8,128)(2,1)}, u32[]{:S(2)}, u32[]{:S(2)}) collective-permute-start(bf16[2080,128]{1,0:T(8,128)(2,1)} %get-tuple-element.45.cross), channel_id=1, source_target_pairs={{0,1},{1,0},{2,3},{3,2},{4,5},{5,4},{6,7},{7,6},{8,9},{9,8},{10,11... | collective-permute-start | bytes 1597448 | tf_op jit(solution)/shard_map/ppermute | solution.py:459

commit v14 on v13

--- a/solution.py
+++ b/solution.py
@@ -374,7 +374,7 @@
                 totals[2 * n + 1] += real * ki + imag * kr
         return tuple(totals)
 
-    return lax.fori_loop(0, source.shape[1] // rows, step, totals)
+    return lax.fori_loop(0, source.shape[1] // rows, step, totals, unroll=2)
 
 
 def trace_kernel(sizes, rest, seps, label, ka, kb, near, far, out_ref, first_buf, rest_buf, sems):

time: 73 us -> 72.9 us (level)
  waiting for transfers between devices: 12.7 us -> 11.8 us
    ppermute x2, waiting for transfers between devices: 8.32 us -> 7.5 us  [swap_snk(): return lax.ppermute(array, 'snk', pairs)]
    pallas_call x1, Pallas kernels: 1.51 us -> 2.32 us  [shards(): call(part(choose, sizes), 'choose', [smem()] + [hbm()] * 2 + [vmem()], vm...]
  transfers between devices with their start and end apart: 12 -> 12, of which waited for: 4 -> 4; matrix products, arithmetic and copies ran while one was open for 0% -> 0% of each run, Pallas kernels for 47% -> 48%
where the time goes in v14:
time: 72.9 us; the launch traced here: 72.4 us
  Pallas kernels  37.7 us (52%)
  waiting for transfers between devices  11.8 us (16%)
  starting transfers between devices  11.2 us (15%)
  blocking collectives  9.43 us (13%)
  local copies, waits for them, and re-layouts  1.37 us (2%)
  between operations  0.84 us (1%)
    pallas_call x3, Pallas kernels, own_one(): call(part(own_kernel, number), 'own_products_%d' % number, [smem(), hbm()...  9.75 us
    all_to_all x1, blocking collectives, shards(): lax.all_to_all(out, ('src', 'snk', 'mom'), split_axis=0, concat_axis=0, t...  9.43 us
    ppermute x2, waiting for transfers between devices, swap_snk(): return lax.ppermute(array, 'snk', pairs)  7.5 us
    pallas_call x1, Pallas kernels, shards(): call(part(other_kernel_02, sizes), 'other_products_02', [smem()] * 3 + [v...  5.26 us
    ppermute x4, starting transfers between devices, next_src(): return lax.ppermute(array, ('src', 'mom'), pairs)  5.02 us
    pallas_call x1, Pallas kernels, shards(): call(part(other_kernel_13, sizes), 'other_products_13', [smem()] * 3 + [h...  4.94 us
    pallas_call x1, Pallas kernels, shards(): call(part(own_kernel_0, sizes), 'own_products_0', [smem()] * 2 + [hbm()]...  4.9 us
    ppermute x6, starting transfers between devices, swap_mom(): return lax.ppermute(array, 'mom', [(a, a ^ i) for a in range(mom_count)])  3.55 us
  transfers between devices with their start and end apart: 12, of which 4 were waited for; matrix products, arithmetic and copies ran while one was open for 0% of the time, Pallas kernels for 48%

profile of v14, /device:TPU:0, one launch (start us, length us, event | category | flops | bytes accessed | tf_op | source)
XLA Modules:
  0.0 72.4 jit_solution(17324617215906006292)
XLA Ops:
  0.0 0.5 collective-permute-start.2
  0.5 2.5 %collective-permute-start.3 = (bf16[4,1024,128]{2,1,0:T(8,128)(2,1)}, bf16[4,1024,128]{2,1,0:T(8,128)(2,1)}, u32[]{:S(2)}, u32[]{:S(2)}) collective-permute-start(bf16[4,1024,128]{2,1,0:T(8,128)(2,1)} %bitcast.6), channel_id=1, source_target_pairs={{0,2},{1,3},{2,0},{3,1},{4,6},{5,7},{6,4},{7,5},{8,10},{9,11},{10,... | collective-permute-start | bytes 3145736 | tf_op jit(solution)/shard_map/ppermute | solution.py:459
  3.6 3.4 %pack_first.1 = (bf16[2,320,512]{2,1,0:T(8,128)(2,1)}, bf16[2,192,512]{2,1,0:T(8,128)(2,1)}, bf16[16,128]{1,0:T(8,128)(2,1)}) custom-call(s32[4]{0:T(128)} %seps.13, s32[1]{0:T(128)S(6)} %copy.17.partner, bf16[4,2,2,512,512]{4,3,2,1,0:T(8,128)(2,1)} %peram.3), custom_call_target="tpu_custom_call" | custom-call | flops 9999999827968 | bytes 10000000000 | tf_op jit(solution)/shard_map/pack_first/pallas_call | solution.py:525
  7.0 2.7 %collective-permute-start = (bf16[2,320,512]{2,1,0:T(8,128)(2,1)}, bf16[2,320,512]{2,1,0:T(8,128)(2,1)}, u32[]{:S(2)}, u32[]{:S(2)}) collective-permute-start(bf16[2,320,512]{2,1,0:T(8,128)(2,1)} %get-tuple-element.27), channel_id=1, source_target_pairs={{0,8},{4,12},{8,0},{12,4},{1,9},{5,13},{9,1},{13,5},{2,10},{6,14},... | collective-permute-start | bytes 1966088 | tf_op jit(solution)/shard_map/ppermute | solution.py:463
  9.7 1.5 %collective-permute-start.1 = (bf16[2,192,512]{2,1,0:T(8,128)(2,1)}, bf16[2,192,512]{2,1,0:T(8,128)(2,1)}, u32[]{:S(2)}, u32[]{:S(2)}) collective-permute-start(bf16[2,192,512]{2,1,0:T(8,128)(2,1)} %get-tuple-element.28.near), channel_id=1, source_target_pairs={{16,0},{17,1},{18,2},{19,3},{0,16},{1,17},{2,18},{3,19},{20,4},{21... | collective-permute-start | bytes 1179656 | tf_op jit(solution)/shard_map/ppermute | solution.py:471
  11.2 0.0 collective-permute-start.5
  11.2 4.9 %own_products_0.1 = (bf16[1024,1024]{1,0:T(8,128)(2,1)}, bf16[512,1536]{1,0:T(8,128)(2,1)}, bf16[16,128]{1,0:T(8,128)(2,1)}) custom-call(s32[4]{0:T(128)} %seps.13, s32[4,4]{1,0:T(4,128)} %gamma.11, bf16[4,2,2,512,512]{4,3,2,1,0:T(8,128)(2,1)} %peram.3, bf16[4,1024,128]{2,1,0:T(8,128)(2,1)} %bitcast.7), custom_call_target="tpu_custom_call" | custom-call | flops 9999999827968 | bytes 10000000000 | tf_op jit(solution)/shard_map/own_products_0/pallas_call | solution.py:546
  16.1 0.0 collective-permute-done.5.tick
  16.1 0.0 copy-start.2
  16.1 0.0 copy-start.5
  16.1 0.0 copy-start.7
  16.1 3.0 %pack.1 = (bf16[2048,128]{1,0:T(8,128)(2,1)}, bf16[2080,128]{1,0:T(8,128)(2,1)}) custom-call(s32[4]{0:T(128)} %seps.13, s32[1]{0:T(128)S(6)} %copy.17.partner, bf16[4,1024,128]{2,1,0:T(8,128)(2,1)} %bitcast.8, bf16[16,128]{1,0:T(8,128)(2,1)} %collective-permute-done.5.tick, bf16[16,128]{1,0:T(8,128)(2,1)} %get-tuple-element.30.after), custom_call_target="tpu_custom_call" | custom-call | flops 9999999827968 | bytes 10000000000 | tf_op jit(solution)/shard_map/pack/pallas_call | solution.py:556
  19.1 0.6 collective-permute-start.7
  19.7 0.0 collective-permute-done.2.source.core
  19.7 1.4 %collective-permute-start.8 = (bf16[2080,128]{1,0:T(8,128)(2,1)}, bf16[2080,128]{1,0:T(8,128)(2,1)}, u32[]{:S(2)}, u32[]{:S(2)}) collective-permute-start(bf16[2080,128]{1,0:T(8,128)(2,1)} %get-tuple-element.43), channel_id=1, source_target_pairs={{18,0},{19,1},{16,2},{17,3},{2,16},{3,17},{0,18},{1,19},{22,4},{23... | collective-permute-start | bytes 1597448 | tf_op jit(solution)/shard_map/ppermute | solution.py:471
  21.2 0.0 copy-done.2
  21.2 0.0 copy-done.5
  21.2 0.0 copy-done.7
  21.2 3.3 %own_products_1.1 = (bf16[512,1536]{1,0:T(8,128)(2,1)S(1)}, bf16[16,128]{1,0:T(8,128)(2,1)S(1)}) custom-call(s32[4,4]{1,0:T(4,128)S(1)} %copy-done.2, bf16[4,1024,128]{2,1,0:T(8,128)(2,1)} %collective-permute-done.2.source.core, bf16[1024,1024]{1,0:T(8,128)(2,1)S(1)} %copy-done.5, bf16[16,128]{1,0:T(8,128)(2,1)S(1)} %copy-done.7), custom_call_target="tpu_custom_call" | custom-call | flops 9999999827968 | bytes 10000000000 | tf_op jit(solution)/shard_map/own_products_1/pallas_call | solution.py:570
  24.4 2.7 %collective-permute-done.3.array = bf16[4,1024,128]{2,1,0:T(8,128)(2,1)} collective-permute-done((bf16[4,1024,128]{2,1,0:T(8,128)(2,1)}, bf16[4,1024,128]{2,1,0:T(8,128)(2,1)}, u32[]{:S(2)}, u32[]{:S(2)}) %collective-permute-start.3) | collective-permute-done | bytes 1048608 | tf_op jit(solution)/shard_map/ppermute | solution.py:459
  27.1 0.6 gate_near.1
  27.7 3.2 %own_products_2.1 = (bf16[512,1536]{1,0:T(8,128)(2,1)S(1)}, bf16[16,128]{1,0:T(8,128)(2,1)S(1)}) custom-call(s32[4,4]{1,0:T(4,128)S(1)} %copy-done.2, bf16[4,1024,128]{2,1,0:T(8,128)(2,1)} %get-tuple-element.32.source.near, bf16[1024,1024]{1,0:T(8,128)(2,1)S(1)} %copy-done.5, bf16[16,128]{1,0:T(8,128)(2,1)S(1)} %get-tuple-element.31.after), custom_call_target="tpu_custom_call" | custom-call | flops 9999999827968 | bytes 10000000000 | tf_op jit(solution)/shard_map/own_products_2/pallas_call | solution.py:570
  31.0 0.1 collective-permute-start.6
  31.0 0.0 collective-permute-done.1.far
  31.1 2.3 %choose.1.rest = bf16[2,192,512]{2,1,0:T(8,128)(2,1)} custom-call(s32[4]{0:T(128)S(1)} %copy-done.3, bf16[2,192,512]{2,1,0:T(8,128)(2,1)S(1)} %copy-done.1, bf16[2,192,512]{2,1,0:T(8,128)(2,1)} %collective-permute-done.1.far, bf16[16,128]{1,0:T(8,128)(2,1)S(1)} %get-tuple-element.31.after), custom_call_target="tpu_custom_call" | custom-call | flops 9999999827968 | bytes 10000000000 | tf_op jit(solution)/shard_map/choose/pallas_call | solution.py:594
  33.4 5.8 %collective-permute-done.first = bf16[2,320,512]{2,1,0:T(8,128)(2,1)} collective-permute-done((bf16[2,320,512]{2,1,0:T(8,128)(2,1)}, bf16[2,320,512]{2,1,0:T(8,128)(2,1)}, u32[]{:S(2)}, u32[]{:S(2)}) %collective-permute-start) | collective-permute-done | bytes 655392 | tf_op jit(solution)/shard_map/ppermute | solution.py:463
  39.2 0.0 collective-permute-start.4
  39.2 1.5 %collective-permute-start.11 = (bf16[2,320,512]{2,1,0:T(8,128)(2,1)}, bf16[2,320,512]{2,1,0:T(8,128)(2,1)}, u32[]{:S(2)}, u32[]{:S(2)}) collective-permute-start(bf16[2,320,512]{2,1,0:T(8,128)(2,1)} %get-tuple-element.48.near), channel_id=1, source_target_pairs={{16,0},{17,1},{18,2},{19,3},{0,16},{1,17},{2,18},{3,19},{20,4},{21... | collective-permute-start | bytes 1966088 | tf_op jit(solution)/shard_map/ppermute | solution.py:471
  40.7 0.0 collective-permute-done.6.source.near
  40.7 3.3 %own_products_3.1 = (bf16[512,1536]{1,0:T(8,128)(2,1)S(1)}, bf16[16,128]{1,0:T(8,128)(2,1)S(1)}) custom-call(s32[4,4]{1,0:T(4,128)S(1)} %copy-done.2, bf16[4,1024,128]{2,1,0:T(8,128)(2,1)} %collective-permute-done.6.source.near, bf16[1024,1024]{1,0:T(8,128)(2,1)S(1)} %copy-done.5, bf16[16,128]{1,0:T(8,128)(2,1)S(1)} %get-tuple-element.39.after), custom_call_target="tpu_custom_call" | custom-call | flops 9999999827968 | bytes 10000000000 | tf_op jit(solution)/shard_map/own_products_3/pallas_call | solution.py:570
  44.0 0.0 collective-permute-done.7.same
  44.0 1.6 %collective-permute-done.8.cross = bf16[2080,128]{1,0:T(8,128)(2,1)} collective-permute-done((bf16[2080,128]{1,0:T(8,128)(2,1)}, bf16[2080,128]{1,0:T(8,128)(2,1)}, u32[]{:S(2)}, u32[]{:S(2)}) %collective-permute-start.8) | collective-permute-done | bytes 532512 | tf_op jit(solution)/shard_map/ppermute | solution.py:471
  45.6 0.6 gate_far.1
  46.2 0.0 collective-permute-start.9
  46.2 0.5 collective-permute-start.10
  46.7 0.1 copy-done
  46.8 0.0 copy-done.4
  46.8 0.5 copy-done.6
  47.3 5.3 %other_products_02.1 = (f32[2,1024,512]{2,1,0:T(8,128)S(1)}, s32[8]{0:T(128)S(1)}) custom-call(s32[4]{0:T(128)S(1)} %copy-done.4, s32[4,4]{1,0:T(4,128)S(1)} %copy-done.2, s32[1]{0:T(128)S(6)} %copy.17.partner, bf16[16,128]{1,0:T(8,128)(2,1)} %collective-permute-done.5.tick, bf16[512,1536]{1,0:T(8,128)(2,1)S(1)} %copy-done.6, ...), custom_call_target="tpu_custom_call" | custom-call | flops 9999999827968 | bytes 10000000000 | tf_op jit(solution)/shard_map/other_products_02/pallas_call | solution.py:640
  52.6 0.0 collective-permute-done.9.same
  52.6 0.0 collective-permute-done.10.cross
  52.6 4.9 %other_products_13.1.kb = f32[2,1024,512]{2,1,0:T(8,128)S(1)} custom-call(s32[4]{0:T(128)S(1)} %copy-done.4, s32[4,4]{1,0:T(4,128)S(1)} %copy-done.2, s32[8]{0:T(128)S(1)} %get-tuple-element.46.label, bf16[512,1536]{1,0:T(8,128)(2,1)S(1)} %copy-done.6, bf16[512,1536]{1,0:T(8,128)(2,1)S(1)} %get-tuple-element.37.h1, ...), custom_call_target="tpu_custom_call" | custom-call | flops 9999999827968 | bytes 10000000000 | tf_op jit(solution)/shard_map/other_products_13/pallas_call | solution.py:651
  57.6 1.7 %collective-permute-done.4.rest = bf16[2,192,512]{2,1,0:T(8,128)(2,1)} collective-permute-done((bf16[2,192,512]{2,1,0:T(8,128)(2,1)}, bf16[2,192,512]{2,1,0:T(8,128)(2,1)}, u32[]{:S(2)}, u32[]{:S(2)}) %collective-permute-start.4) | collective-permute-done | bytes 393248 | tf_op jit(solution)/shard_map/ppermute | solution.py:463
  59.3 0.0 collective-permute-done.11.far
  59.3 2.9 %traces.1 = f32[32,1,128]{2,1,0:T(1,128)S(1)} custom-call(bf16[2,192,512]{2,1,0:T(8,128)(2,1)} %collective-permute-done.4.rest, s32[4]{0:T(128)S(1)} %copy-done.4, s32[8]{0:T(128)S(1)} %get-tuple-element.46.label, f32[2,1024,512]{2,1,0:T(8,128)S(1)} %get-tuple-element.47.ka, f32[2,1024,512]{2,1,0:T(8,128)S(1)} %other_products_13.1.kb, ...), custom_call_target="tpu_custom_call" | custom-call | flops 9999999827968 | bytes 10000000000 | tf_op jit(solution)/shard_map/traces/pallas_call | solution.py:664
  62.2 9.4 %all_to_all.5 = f32[32,1,128]{2,1,0:T(1,128)S(1)} all-to-all(f32[32,1,128]{2,1,0:T(1,128)S(1)} %traces.1), channel_id=1, replica_groups=mesh['src'=2,'snk'=4,'mom'=4] {'src','snk','mom'}, dimensions={0} | all-to-all | bytes 32768 | tf_op jit(solution)/shard_map/all_to_all | solution.py:673
  71.6 0.1 reduce_sum.11
  71.7 0.7 reshape.11
  (9 shorter events, 0.0 us)
Async XLA Ops:
  0.0 19.7 %collective-permute-start.2 = (bf16[4,1024,128]{2,1,0:T(8,128)(2,1)}, bf16[4,1024,128]{2,1,0:T(8,128)(2,1)}, u32[]{:S(2)}, u32[]{:S(2)}) collective-permute-start(bf16[4,1024,128]{2,1,0:T(8,128)(2,1)} %bitcast.5), channel_id=1, source_target_pairs={{0,1},{1,0},{2,3},{3,2},{4,5},{5,4},{6,7},{7,6},{8,9},{9,8},{10,11... | collective-permute-start | bytes 3145736 | tf_op jit(solution)/shard_map/ppermute | solution.py:459
  0.5 26.7 %collective-permute-start.3 = (bf16[4,1024,128]{2,1,0:T(8,128)(2,1)}, bf16[4,1024,128]{2,1,0:T(8,128)(2,1)}, u32[]{:S(2)}, u32[]{:S(2)}) collective-permute-start(bf16[4,1024,128]{2,1,0:T(8,128)(2,1)} %bitcast.6), channel_id=1, source_target_pairs={{0,2},{1,3},{2,0},{3,1},{4,6},{5,7},{6,4},{7,5},{8,10},{9,11},{10,... | collective-permute-start | bytes 3145736 | tf_op jit(solution)/shard_map/ppermute | solution.py:459
  7.0 32.2 %collective-permute-start = (bf16[2,320,512]{2,1,0:T(8,128)(2,1)}, bf16[2,320,512]{2,1,0:T(8,128)(2,1)}, u32[]{:S(2)}, u32[]{:S(2)}) collective-permute-start(bf16[2,320,512]{2,1,0:T(8,128)(2,1)} %get-tuple-element.27), channel_id=1, source_target_pairs={{0,8},{4,12},{8,0},{12,4},{1,9},{5,13},{9,1},{13,5},{2,10},{6,14},... | collective-permute-start | bytes 1966088 | tf_op jit(solution)/shard_map/ppermute | solution.py:463
  9.7 21.4 %collective-permute-start.1 = (bf16[2,192,512]{2,1,0:T(8,128)(2,1)}, bf16[2,192,512]{2,1,0:T(8,128)(2,1)}, u32[]{:S(2)}, u32[]{:S(2)}) collective-permute-start(bf16[2,192,512]{2,1,0:T(8,128)(2,1)} %get-tuple-element.28.near), channel_id=1, source_target_pairs={{16,0},{17,1},{18,2},{19,3},{0,16},{1,17},{2,18},{3,19},{20,4},{21... | collective-permute-start | bytes 1179656 | tf_op jit(solution)/shard_map/ppermute | solution.py:471
  11.2 4.9 %collective-permute-start.5 = (bf16[16,128]{1,0:T(8,128)(2,1)}, bf16[16,128]{1,0:T(8,128)(2,1)}, u32[]{:S(2)}, u32[]{:S(2)}) collective-permute-start(bf16[16,128]{1,0:T(8,128)(2,1)} %get-tuple-element.35), channel_id=1, source_target_pairs={{0,1},{1,0},{2,3},{3,2},{4,5},{5,4},{6,7},{7,6},{8,9},{9,8},{10,11... | collective-permute-start | bytes 12296 | tf_op jit(solution)/shard_map/ppermute | solution.py:459
  16.1 5.1 %copy-start.2 = (s32[4,4]{1,0:T(4,128)S(1)}, s32[4,4]{1,0:T(4,128)}, u32[]{:S(2)}) copy-start(s32[4,4]{1,0:T(4,128)} %gamma.11) | copy-start | bytes 196
  16.1 5.1 %copy-start.5 = (bf16[1024,1024]{1,0:T(8,128)(2,1)S(1)}, bf16[1024,1024]{1,0:T(8,128)(2,1)}, u32[]{:S(2)}) copy-start(bf16[1024,1024]{1,0:T(8,128)(2,1)} %get-tuple-element.29.y_ref) | copy-start | bytes 6291460
  16.1 5.1 %copy-start.7 = (bf16[16,128]{1,0:T(8,128)(2,1)S(1)}, bf16[16,128]{1,0:T(8,128)(2,1)}, u32[]{:S(2)}) copy-start(bf16[16,128]{1,0:T(8,128)(2,1)} %get-tuple-element.30.after) | copy-start | bytes 12292
  19.1 24.8 %collective-permute-start.7 = (bf16[2048,128]{1,0:T(8,128)(2,1)}, bf16[2048,128]{1,0:T(8,128)(2,1)}, u32[]{:S(2)}, u32[]{:S(2)}) collective-permute-start(bf16[2048,128]{1,0:T(8,128)(2,1)} %get-tuple-element.42), channel_id=1, source_target_pairs={{16,0},{17,1},{18,2},{19,3},{0,16},{1,17},{2,18},{3,19},{20,4},{21... | collective-permute-start | bytes 1572872 | tf_op jit(solution)/shard_map/ppermute | solution.py:471
  19.7 25.9 %collective-permute-start.8 = (bf16[2080,128]{1,0:T(8,128)(2,1)}, bf16[2080,128]{1,0:T(8,128)(2,1)}, u32[]{:S(2)}, u32[]{:S(2)}) collective-permute-start(bf16[2080,128]{1,0:T(8,128)(2,1)} %get-tuple-element.43), channel_id=1, source_target_pairs={{18,0},{19,1},{16,2},{17,3},{2,16},{3,17},{0,18},{1,19},{22,4},{23... | collective-permute-start | bytes 1597448 | tf_op jit(solution)/shard_map/ppermute | solution.py:471
  27.7 3.4 %copy-start.1 = (bf16[2,192,512]{2,1,0:T(8,128)(2,1)S(1)}, bf16[2,192,512]{2,1,0:T(8,128)(2,1)}, u32[]{:S(2)}) copy-start(bf16[2,192,512]{2,1,0:T(8,128)(2,1)} %get-tuple-element.28.near) | copy-start | bytes 1179652
  27.7 3.4 %copy-start.3 = (s32[4]{0:T(128)S(1)}, s32[4]{0:T(128)}, u32[]{:S(2)}) copy-start(s32[4]{0:T(128)} %seps.13) | copy-start | bytes 52
  31.0 9.7 %collective-permute-start.6 = (bf16[4,1024,128]{2,1,0:T(8,128)(2,1)}, bf16[4,1024,128]{2,1,0:T(8,128)(2,1)}, u32[]{:S(2)}, u32[]{:S(2)}) collective-permute-start(bf16[4,1024,128]{2,1,0:T(8,128)(2,1)} %get-tuple-element.32.source.near), channel_id=1, source_target_pairs={{0,1},{1,0},{2,3},{3,2},{4,5},{5,4},{6,7},{7,6},{8,9},{9,8},{10,11... | collective-permute-start | bytes 3145736 | tf_op jit(solution)/shard_map/ppermute | solution.py:459
  39.2 20.1 %collective-permute-start.4 = (bf16[2,192,512]{2,1,0:T(8,128)(2,1)}, bf16[2,192,512]{2,1,0:T(8,128)(2,1)}, u32[]{:S(2)}, u32[]{:S(2)}) collective-permute-start(bf16[2,192,512]{2,1,0:T(8,128)(2,1)} %get-tuple-element.34), channel_id=1, source_target_pairs={{0,8},{4,12},{8,0},{12,4},{1,9},{5,13},{9,1},{13,5},{2,10},{6,14},... | collective-permute-start | bytes 1179656 | tf_op jit(solution)/shard_map/ppermute | solution.py:463
  39.2 20.1 %collective-permute-start.11 = (bf16[2,320,512]{2,1,0:T(8,128)(2,1)}, bf16[2,320,512]{2,1,0:T(8,128)(2,1)}, u32[]{:S(2)}, u32[]{:S(2)}) collective-permute-start(bf16[2,320,512]{2,1,0:T(8,128)(2,1)} %get-tuple-element.48.near), channel_id=1, source_target_pairs={{16,0},{17,1},{18,2},{19,3},{0,16},{1,17},{2,18},{3,19},{20,4},{21... | collective-permute-start | bytes 1966088 | tf_op jit(solution)/shard_map/ppermute | solution.py:471
  45.6 1.2 %copy-start = (bf16[4,1,4,2,128,128]{5,4,3,2,1,0:T(8,128)(2,1)S(1)}, bf16[4,1,4,2,128,128]{5,4,3,2,1,0:T(8,128)(2,1)}, u32[]{:S(2)}) copy-start(bf16[4,1,4,2,128,128]{5,4,3,2,1,0:T(8,128)(2,1)} %param.6) | copy-start | bytes 3145732
  45.6 1.2 %copy-start.4 = (s32[4]{0:T(128)S(1)}, s32[4]{0:T(128)}, u32[]{:S(2)}) copy-start(s32[4]{0:T(128)} %seps.13) | copy-start | bytes 52
  45.6 1.7 %copy-start.6 = (bf16[512,1536]{1,0:T(8,128)(2,1)S(1)}, bf16[512,1536]{1,0:T(8,128)(2,1)}, u32[]{:S(2)}) copy-start(bf16[512,1536]{1,0:T(8,128)(2,1)} %get-tuple-element.36.h0) | copy-start | bytes 4718596
  46.2 6.4 %collective-permute-start.9 = (bf16[2048,128]{1,0:T(8,128)(2,1)}, bf16[2048,128]{1,0:T(8,128)(2,1)}, u32[]{:S(2)}, u32[]{:S(2)}) collective-permute-start(bf16[2048,128]{1,0:T(8,128)(2,1)} %get-tuple-element.44.same), channel_id=1, source_target_pairs={{0,1},{1,0},{2,3},{3,2},{4,5},{5,4},{6,7},{7,6},{8,9},{9,8},{10,11... | collective-permute-start | bytes 1572872 | tf_op jit(solution)/shard_map/ppermute | solution.py:459
  46.2 6.4 %collective-permute-start.10 = (bf16[2080,128]{1,0:T(8,128)(2,1)}, bf16[2080,128]{1,0:T(8,128)(2,1)}, u32[]{:S(2)}, u32[]{:S(2)}) collective-permute-start(bf16[2080,128]{1,0:T(8,128)(2,1)} %get-tuple-element.45.cross), channel_id=1, source_target_pairs={{0,1},{1,0},{2,3},{3,2},{4,5},{5,4},{6,7},{7,6},{8,9},{9,8},{10,11... | collective-permute-start | bytes 1597448 | tf_op jit(solution)/shard_map/ppermute | solution.py:459
